TPU v7x, 32 devices: a whole 2x2x4 slice. The times are simulated.
32 devices in a mesh: space: 4 (over z), ens: 8 (over y, x, core).
Axes of the slice: x: 2, y: 2, z: 4, core: 2. Of those that a mesh axis runs over, the one named last changes fastest.
Arguments:
- starting_speed_field: float32 [64, 64, 2048], P('ens', 'space'), may hold values from -6 to 6
- sample_fluidity_exponent: float32 [64, 64, 2048], P('ens', 'space'), may hold values from -1.5 to 0.5
- observed: float32 [1024], P('space'), may hold values from -6 to 6
- obs_noise: float32 [64, 1024], P('ens', 'space'), may hold values from -3 to 3
- obs_var: float32 [1024], P('space'), may hold values from 0.5 to 4
- probe_cells: int32 [1024], P('space'), may hold values from 0 to 32767
- pair_cells: int32 [4, 32], P('space'), may hold values from 0 to 255
- pair_probes: int32 [4, 32], P('space'), may hold values from 0 to 5, as said below
- pair_taper: int32 [4, 32], P('space'), may hold values from 1 to 256
- pair_counts: int32 [4], P('space'), may hold values from 8 to 32, as said below
- probe_taper: int32 [4, 2, 6], P('space'), may hold values from 1 to 256
Outputs:
- prior_speed_prediction: float32 [64, 64, 2048], P('ens', 'space')
- posterior_fluidity_exponent: float32 [64, 64, 2048], P('ens', 'space')
- weighted_innovation_matrix: float32 [64, 1024], P('ens', 'space')
Inputs may be any that keep to these rules, and one draw needn't show every extreme that they name: `pair_probes`: each pair slot names a probe block of the slab or of a neighbour slab, never one outside the channel: slab 0 uses 2 to 5 and the last slab 0 to 3. `pair_counts`: slots at or beyond a slab's count are padding; some slab has all 32 slots live.
All inputs are finite; a program needn't handle non-finite values.
Results may differ from a plain program's by a relative error of at most 0.000096.
Values sent between devices are 32-bit elements; how exact they have to be, the bound alone decides.
No kernel may reach another device: no remote copies, remote signals or barrier semaphores. Data moves between devices by JAX's collectives and lax.ppermute only.
A program may use at most 64 MiB of HBM per device.

v0:
```python
import functools

import jax
import jax.numpy as jnp
from jax import lax
from jax.experimental import pallas as pl
from jax.experimental.pallas import tpu as pltpu
from jax.sharding import PartitionSpec as P

LANES = 128
ROWS = 8
NZ = 64
HALF_DT = 0.5 * 0.08

VMEM = pl.BlockSpec(memory_space=pltpu.VMEM)
SMEM = pl.BlockSpec(memory_space=pltpu.SMEM)
HBM = pl.BlockSpec(memory_space=pltpu.HBM)
ANY = pl.BlockSpec(memory_space=pl.ANY)


def stay(array):
    return pltpu.with_memory_space_constraint(array, pltpu.HBM)


def to_rows(array):
    members, planes, cells = array.shape
    split = array.reshape(members, planes // ROWS, ROWS, cells // LANES, LANES)
    return split.transpose(0, 1, 3, 2, 4).reshape(-1, LANES)


def from_rows(rows, shape):
    members, planes, cells = shape
    split = rows.reshape(members, planes // ROWS, cells // LANES, ROWS, LANES)
    return split.transpose(0, 1, 3, 2, 4).reshape(shape)


def row_of(plane, tile, tiles):
    return (plane // ROWS * tiles + tile) * ROWS + plane % ROWS


def pack_kernel(planes, tiles, cells_hbm, taper_hbm, u_hbm, t_hbm, noise_hbm, observed_hbm, var_hbm,
                low_ref, high_ref, obs_ref, pick_hbm,
                cells_ref, taper_ref, u_ref, t_ref, noise_ref, row_ref, pick_ref, sems):
    stride = planes * tiles
    blocks = noise_ref.shape[1] // LANES
    copies = [
        pltpu.make_async_copy(source, target, sems.at[at])
        for at, (source, target) in enumerate((
            (cells_hbm, cells_ref),
            (t_hbm, t_ref),
            (u_hbm, u_ref),
            (taper_hbm, taper_ref),
            (noise_hbm, noise_ref),
            (observed_hbm, row_ref.at[0:1]),
            (var_hbm, row_ref.at[1:2]),
        ))
    ]
    for copy in copies:
        copy.start()
    copies[0].wait()
    copies[1].wait()
    for slot in range(pick_ref.shape[0]):
        block = cells_ref[0, slot]
        pick_ref[slot] = t_ref[pl.ds(row_of(block // tiles, block % tiles, tiles), ROWS, stride=stride), :]
    picked = pltpu.make_async_copy(pick_ref, pick_hbm, sems.at[len(copies)])
    picked.start()
    for kind, source in ((1, t_ref), (0, u_ref)):
        if kind == 0:
            copies[2].wait()
        for out_ref, first in ((high_ref, planes - 2), (low_ref, 0)):
            for depth in range(2):
                for tile in range(tiles):
                    out_ref[(kind * 2 + depth) * tiles + tile] = source[
                        pl.ds(row_of(first + depth, tile, tiles), ROWS, stride=stride), :
                    ]
    for copy in copies[3:]:
        copy.wait()
    own, window = taper_ref.shape[1:]
    rows = [row_ref[kind : kind + 1, b * LANES : (b + 1) * LANES] for kind in range(2) for b in range(blocks)]
    rows.append(jnp.ones((1, LANES), jnp.float32))
    for i in range(own):
        for j in range(window):
            rows.append(jnp.full((1, LANES), taper_ref[0, i, j].astype(jnp.float32), jnp.float32))
    for ref, first in ((low_ref, 4 * tiles), (high_ref, 4 * tiles), (obs_ref, 0)):
        for b in range(blocks):
            ref[first + b] = noise_ref[:, b * LANES : (b + 1) * LANES]
        for at, row in enumerate(rows):
            ref[first + blocks + at // ROWS, at % ROWS : at % ROWS + 1, :] = row
    picked.wait()


def rot(value, by):
    return pltpu.roll(value, by % LANES, 1)


def lane_masks():
    lane = lax.broadcasted_iota(jnp.int32, (ROWS, LANES), 1)
    height = lane & (NZ - 1)
    return lane < NZ, height == 0, height == NZ - 1


def coefficients(masks, low, here, high):
    first_half, floor, roof = masks
    tiles = len(here)
    turned = [rot(value, NZ) for value in here]
    out = []
    for tile in range(tiles):
        mid = here[tile]
        near = mid + turned[tile]
        far = mid + jnp.where(first_half, turned[tile - 1], turned[(tile + 1) % tiles])
        up = mid + jnp.where(roof, HALF_DT, rot(mid, -1))
        down = mid + jnp.where(floor, HALF_DT, rot(mid, 1))
        below = mid + low[tile]
        above = mid + high[tile]
        diag = 1.0 - ((near + far) + (up + down) + (below + above))
        out.append((diag, near, far, jnp.where(roof, 0.0, up), jnp.where(floor, 0.0, down), below, above))
    return out


def step(masks, weights, low, here, high):
    first_half = masks[0]
    tiles = len(here)
    turned = [rot(value, NZ) for value in here]
    out = []
    for tile in range(tiles):
        diag, near, far, up, down, below, above = weights[tile]
        mid = here[tile]
        beyond = jnp.where(first_half, turned[tile - 1], turned[(tile + 1) % tiles])
        out.append(
            (diag * mid + near * turned[tile])
            + (far * beyond + up * rot(mid, -1))
            + (down * rot(mid, 1) + below * low[tile])
            + above * high[tile]
        )
    return out


def plane_of(ref, at, tiles):
    return [ref[at * tiles + tile] for tile in range(tiles)]


def put(ref, at, values):
    for tile, value in enumerate(values):
        ref[at * len(values) + tile] = value


def inner_kernel(planes, tiles, u_hbm, t_hbm, u2_ref, edge_ref,
                 u_ref, t_ref, u0, hv, u1, held, sems):
    stride = planes * tiles
    masks = lane_masks()
    copies = [pltpu.make_async_copy(u_hbm, u_ref, sems.at[0]), pltpu.make_async_copy(t_hbm, t_ref, sems.at[1])]
    for copy in copies:
        copy.start()
    for copy in copies:
        copy.wait()

    def load(x, _):
        base = (x // ROWS) * tiles * ROWS + x % ROWS
        for tile in range(tiles):
            rows = pl.ds(base + tile * ROWS, ROWS, stride=stride)
            u0[x * tiles + tile] = u_ref[rows, :]
            hv[x * tiles + tile] = HALF_DT * jnp.exp(t_ref[rows, :])
        return 0

    lax.fori_loop(0, planes, load, 0)

    def first_step(x, _):
        weights = coefficients(masks, *[plane_of(hv, x + d, tiles) for d in (-1, 0, 1)])
        for tile in range(tiles):
            for kind in range(5):
                held[kind, x * tiles + tile] = weights[tile][kind]
        put(u1, x, step(masks, weights, *[plane_of(u0, x + d, tiles) for d in (-1, 0, 1)]))
        return 0

    lax.fori_loop(1, planes - 1, first_step, 0)

    def second_step(x, _):
        weights = []
        for tile in range(tiles):
            at = x * tiles + tile
            here = hv[at]
            weights.append([held[kind, at] for kind in range(5)] + [here + hv[at - tiles], here + hv[at + tiles]])
        put(u2_ref, x, step(masks, weights, *[plane_of(u1, x + d, tiles) for d in (-1, 0, 1)]))
        return 0

    lax.fori_loop(2, planes - 2, second_step, 0)
    last = planes - 1
    at = 0
    for ref, kept in ((u0, (0, 1, last - 1, last)), (hv, (0, 1, 2, last - 2, last - 1, last)),
                      (u1, (1, 2, last - 2, last - 1))):
        for x in kept:
            put(edge_ref, at, plane_of(ref, x, tiles))
            at += 1


def outer_kernel(planes, tiles, probe_hbm, before_ref, after_ref, edge_ref, inner_ref, before_2_hbm, after_2_hbm,
                 u2_ref, sent_ref, probe_ref, sem):
    probe_copy = pltpu.make_async_copy(probe_hbm, probe_ref, sem)
    probe_copy.start()
    masks = lane_masks()
    blocks = sent_ref.shape[2] // LANES
    mark = 4 * tiles + blocks + 2 * blocks // ROWS
    mark_row = 2 * blocks % ROWS
    edge = [plane_of(edge_ref, at, tiles) for at in range(14)]
    last = planes - 1
    for ref, own_u, own_v, own_1, where in (
        (before_ref, edge[0:2], edge[4:7], edge[10:12], (0, 1)),
        (after_ref, edge[3:1:-1], edge[9:6:-1], edge[13:11:-1], (last, last - 1)),
    ):
        order = (0, 1) if ref is before_ref else (1, 0)
        u = [plane_of(ref, d, tiles) for d in order] + own_u
        v = [[HALF_DT * jnp.exp(t) for t in plane_of(ref, 2 + d, tiles)] for d in order] + own_v
        live = ref[mark, mark_row : mark_row + 1, :]
        weights = [coefficients(masks, v[d], v[d + 1], v[d + 2]) for d in range(3)]
        next_u = [step(masks, weights[d], u[d], u[d + 1], u[d + 2]) for d in range(2)]
        next_u[0] = [value * live for value in next_u[0]]
        next_u = next_u + own_1
        for d in range(2):
            put(u2_ref, where[d], step(masks, weights[d + 1], next_u[d], next_u[d + 1], next_u[d + 2]))

    probe_copy.wait()
    lane = lax.broadcasted_iota(jnp.int32, (ROWS, LANES), 1)
    for part in range(blocks):
        found = jnp.zeros((ROWS, LANES), jnp.float32)
        for p in range(LANES):
            cell = probe_ref[part * LANES + p]
            turned = pltpu.roll(u2_ref[cell >> 7], (p - cell) & (LANES - 1), 1)
            found = jnp.where(lane == p, turned, found)

        def send(device, _):
            sent_ref[device, :, part * LANES : (part + 1) * LANES] = found
            return 0

        lax.fori_loop(0, sent_ref.shape[0], send, 0)


def halves(value):
    high = value.astype(jnp.bfloat16)
    return high, (value - high.astype(jnp.float32)).astype(jnp.bfloat16)


def between_kernel(planes, tiles, u2_ref, theta_hbm, out_ref, split_ref, theta_ref, sem):
    copy = pltpu.make_async_copy(theta_hbm, theta_ref, sem)
    copy.start()
    stride = planes * tiles
    members = theta_ref.shape[0] * ROWS

    def store(x, _):
        base = (x // ROWS) * tiles * ROWS + x % ROWS
        for tile in range(tiles):
            out_ref[pl.ds(base + tile * ROWS, ROWS, stride=stride), :] = u2_ref[x * tiles + tile]
        return 0

    lax.fori_loop(0, planes, store, 0)
    copy.wait()

    def split(slot, _):
        high, low = halves(theta_ref[:, slot].reshape(members, LANES))
        split_ref[slot, :members, :] = high
        split_ref[slot, members:, :] = low
        return 0

    lax.fori_loop(0, split_ref.shape[0], split, 0)


def dot_lanes(left, right):
    return lax.dot_general(left, right, (((1,), (1,)), ((), ())), precision=lax.Precision.HIGHEST,
                           preferred_element_type=jnp.float32)


def dot_rows(left, right):
    return lax.dot_general(left, right, (((1,), (0,)), ((), ())), precision=lax.Precision.HIGHEST,
                           preferred_element_type=jnp.float32)


def update_kernel(slabs, groups, planes, tiles, place_ref, count_ref, cells_hbm, probes_hbm, level_hbm,
                  pred_ref, obs_refs, split_ref, t_ref, post_ref, gain_ref,
                  reach, cells_ref, probes_ref, level_ref, sems):
    members = groups * ROWS
    share = 1.0 / (members - 1)
    copies = [
        pltpu.make_async_copy(source, target, sems.at[at])
        for at, (source, target) in enumerate((
            (cells_hbm, cells_ref), (probes_hbm, probes_ref), (level_hbm, level_ref)))
    ]
    for copy in copies:
        copy.start()
    slab, group = place_ref[0], place_ref[1]
    blocks = gain_ref.shape[1] // LANES
    window = 3 * blocks
    post_ref[...] = t_ref[...]

    def wide(row):
        return row[:, :members] if members <= LANES else jnp.concatenate([row] * (members // LANES), axis=1)

    anomaly, scaled, variance, matches = [], [], [], []
    for d in range(5):
        wanted = slab + d - 2
        at = jnp.clip(wanted, 0, slabs - 1)
        live = jnp.where((wanted >= 0) & (wanted < slabs), 1.0, 0.0)
        predicted = pred_ref[pl.ds(at * groups, groups)].reshape(members, blocks * LANES)
        mean = jnp.sum(predicted, axis=0, keepdims=True) / members
        anomaly.append((predicted - mean) * live)
        mine = pred_ref[at * groups + group]
        ref, first = obs_refs[d]
        for b in range(blocks):
            cut = slice(b * LANES, (b + 1) * LANES)
            observed = ref[first + blocks, b : b + 1, :]
            variance.append(ref[first + blocks, blocks + b : blocks + b + 1, :] + (1.0 - live))
            scaled.append((observed + ref[first + b] - mine[:, cut]) / variance[-1] * live)
            matches.append(dot_lanes(scaled[-1], anomaly[d][:, cut]))
    for d in range(1, 4):
        ref, first = obs_refs[d]
        for i in range(blocks):
            cut = slice(i * LANES, (i + 1) * LANES)
            total = jnp.zeros((ROWS, members), jnp.float32)
            for j in range(window):
                at = 2 * blocks + 1 + i * window + j
                level = ref[first + blocks + at // ROWS, at % ROWS : at % ROWS + 1, :] / 256.0 * share
                total = total + wide(level) * matches[(d - 1) * blocks + j]
            correction = dot_rows(total, anomaly[d][:, cut])
            gain = scaled[d * blocks + i] - correction / variance[d * blocks + i]
            if d == 2:
                gain_ref[:, cut] = gain
            high, low = halves(dot_lanes(gain, anomaly[d][:, cut]))
            both = jnp.concatenate([high.astype(jnp.float32), low.astype(jnp.float32)], axis=0)
            reach[(d - 1) * blocks + i] = jnp.concatenate([both, both], axis=1).astype(jnp.bfloat16)
    for copy in copies:
        copy.wait()
    for slot in range(split_ref.shape[0]):
        weight = jnp.where(slot < count_ref[0], level_ref[0, slot].astype(jnp.float32) / 256.0, 0.0) * share
        both = lax.dot_general(reach[probes_ref[0, slot]], split_ref[slot],
                               (((1,), (0,)), ((), ())), preferred_element_type=jnp.float32)
        change = (both[:ROWS] + both[ROWS:]) * weight
        block = cells_ref[0, slot]
        rows = pl.ds(row_of(block // tiles, block % tiles, tiles), ROWS, stride=planes * tiles)
        post_ref[rows, :] = post_ref[rows, :] + change


def shards(
    starting_speed_field,
    sample_fluidity_exponent,
    observed,
    obs_noise,
    obs_var,
    probe_cells,
    pair_cells,
    pair_probes,
    pair_taper,
    pair_counts,
    probe_taper,
):
    shape = starting_speed_field.shape
    members, planes, cells = shape
    tiles = cells // LANES
    slots = pair_cells.shape[1]
    probes = obs_noise.shape[1]
    blocks = probes // LANES
    slabs, groups = lax.axis_size("space"), lax.axis_size("ens")
    f32, i32 = jnp.float32, jnp.int32
    u_rows = to_rows(starting_speed_field)
    t_rows = to_rows(sample_fluidity_exponent)
    obs_tiles = blocks - (-(2 * blocks + 1 + probe_taper.shape[1] * probe_taper.shape[2]) // ROWS)
    edge = jax.ShapeDtypeStruct((4 * tiles + obs_tiles, ROWS, LANES), f32)
    obs_shape = jax.ShapeDtypeStruct((obs_tiles, ROWS, LANES), f32)
    params = pltpu.CompilerParams(vmem_limit_bytes=48 * 1024 * 1024)
    field = pltpu.VMEM(u_rows.shape, f32)
    stack = pltpu.VMEM((planes * tiles, ROWS, LANES), f32)
    low, high, obs, picked = pl.pallas_call(
        functools.partial(pack_kernel, planes, tiles),
        out_shape=(edge, edge, obs_shape, jax.ShapeDtypeStruct((slots, ROWS, LANES), f32)),
        in_specs=[HBM] * 7,
        out_specs=(VMEM, VMEM, VMEM, HBM),
        scratch_shapes=[
            pltpu.SMEM(pair_cells.shape, i32),
            pltpu.SMEM(probe_taper.shape, i32),
            field,
            field,
            pltpu.VMEM((ROWS, probes), f32),
            pltpu.VMEM((2, probes), f32),
            pltpu.VMEM((slots, ROWS, LANES), f32),
            pltpu.SemaphoreType.DMA((8,)),
        ],
        compiler_params=params,
        name="pack",
    )(*map(stay, (pair_cells, probe_taper, u_rows, t_rows, obs_noise, observed.reshape(1, -1), obs_var.reshape(1, -1))))
    upward = [(i, i + 1) for i in range(slabs - 1)]
    before = lax.ppermute(high, "space", upward)
    after = lax.ppermute(low, "space", [(j, i) for i, j in upward])
    if slabs == 4:
        before_2 = after_2 = lax.ppermute(obs, "space", [(i, (i + 2) % 4) for i in range(4)])
    else:
        upward_2 = [(i, i + 2) for i in range(slabs - 2)]
        before_2 = lax.ppermute(obs, "space", upward_2)
        after_2 = lax.ppermute(obs, "space", [(j, i) for i, j in upward_2])
    theta_all = lax.all_gather(picked, "ens")
    inner, edges = pl.pallas_call(
        functools.partial(inner_kernel, planes, tiles),
        out_shape=(
            jax.ShapeDtypeStruct((planes * tiles, ROWS, LANES), f32),
            jax.ShapeDtypeStruct((14 * tiles, ROWS, LANES), f32),
        ),
        in_specs=[HBM] * 2,
        out_specs=(VMEM,) * 2,
        scratch_shapes=[
            field,
            field,
            stack,
            stack,
            stack,
            pltpu.VMEM((5, planes * tiles, ROWS, LANES), f32),
            pltpu.SemaphoreType.DMA((2,)),
        ],
        compiler_params=params,
        cost_estimate=pl.CostEstimate(flops=20_000_000, bytes_accessed=20_000_000, transcendentals=0),
        name="inner_planes",
    )(stay(u_rows), stay(t_rows))
    u2, sent = pl.pallas_call(
        functools.partial(outer_kernel, planes, tiles),
        out_shape=(
            jax.ShapeDtypeStruct((planes * tiles, ROWS, LANES), f32),
            jax.ShapeDtypeStruct((slabs * groups, members, probes), f32),
        ),
        in_specs=[HBM] + [VMEM] * 4 + [ANY] * 2,
        out_specs=(VMEM,) * 2,
        scratch_shapes=[pltpu.SMEM(probe_cells.shape, i32), pltpu.SemaphoreType.DMA(())],
        input_output_aliases={4: 0},
        compiler_params=params,
        name="outer_planes",
    )(stay(probe_cells), before, after, edges, inner, before_2, after_2)
    pred_all = lax.all_to_all(sent, ("space", "ens"), 0, 0)
    u2_rows, split = pl.pallas_call(
        functools.partial(between_kernel, planes, tiles),
        out_shape=(
            jax.ShapeDtypeStruct(u_rows.shape, f32),
            jax.ShapeDtypeStruct((slots, 2 * groups * ROWS, LANES), jnp.bfloat16),
        ),
        in_specs=[VMEM, HBM],
        out_specs=(VMEM,) * 2,
        scratch_shapes=[pltpu.VMEM(theta_all.shape, f32), pltpu.SemaphoreType.DMA(())],
        compiler_params=params,
        cost_estimate=pl.CostEstimate(flops=1_000_000, bytes_accessed=8_000_000, transcendentals=0),
        name="between",
    )(u2, stay(theta_all))
    place = jnp.stack([lax.axis_index("space"), lax.axis_index("ens")]).astype(i32)

    def update(place_ref, count_ref, cells_ref, probes_ref, level_ref, pred_ref, before_2_ref, before_ref, obs_ref,
               after_ref, after_2_ref, *rest):
        seen = ((before_2_ref, 0), (before_ref, 4 * tiles), (obs_ref, 0), (after_ref, 4 * tiles), (after_2_ref, 0))
        update_kernel(slabs, groups, planes, tiles, place_ref, count_ref, cells_ref, probes_ref, level_ref,
                      pred_ref, seen, *rest)

    post_rows, gain = pl.pallas_call(
        update,
        out_shape=(
            jax.ShapeDtypeStruct(u_rows.shape, f32),
            jax.ShapeDtypeStruct((members, probes), f32),
        ),
        in_specs=[SMEM] * 2 + [HBM] * 3 + [VMEM] * 8,
        out_specs=(VMEM,) * 2,
        scratch_shapes=[
            pltpu.VMEM((probe_taper.shape[2], 2 * ROWS, 2 * groups * ROWS), jnp.bfloat16),
            pltpu.SMEM(pair_cells.shape, i32),
            pltpu.SMEM(pair_cells.shape, i32),
            pltpu.SMEM(pair_cells.shape, i32),
            pltpu.SemaphoreType.DMA((3,)),
        ],
        compiler_params=params,
        name="update",
    )(place, pair_counts, *map(stay, (pair_cells, pair_probes, pair_taper)), pred_all, before_2, before, obs, after,
      after_2, split, t_rows)
    return (from_rows(u2_rows, shape), from_rows(post_rows, shape), gain)


def solution(mesh):
    return jax.shard_map(
        shards,
        mesh=mesh,
        in_specs=(
            P("ens", "space", None),
            P("ens", "space", None),
            P("space"),
            P("ens", "space"),
            P("space"),
            P("space"),
            P("space", None),
            P("space", None),
            P("space", None),
            P("space"),
            P("space", None, None),
        ),
        out_specs=(P("ens", "space", None), P("ens", "space", None), P("ens", "space")),
        check_vma=False,
    )
```

profile of v0, /device:TPU:0, one launch (start us, length us, event | category | flops | bytes accessed | tf_op | source)
XLA Modules:
  0.0 55.6 jit_solution(6692866012943802386)
XLA Ops:
  7.2 0.0 all-gather.3.cloned.1.call-start
  7.2 2.3 %pack.1 = (f32[69,8,128]{2,1,0:T(8,128)S(1)}, f32[69,8,128]{2,1,0:T(8,128)S(1)}, f32[5,8,128]{2,1,0:T(8,128)S(1)}, f32[32,8,128]{2,1,0:T(8,128)}) custom-call(s32[1,32]{1,0:T(1,128)} %cells_ref.1, s32[1,2,6]{2,1,0:T(2,128)} %taper_hbm.1, f32[2048,128]{1,0:T(8,128)} %bitcast.28, f32[2048,128]{1,0:T(8,128)} %bitcast.25, f32[8,256]{1,0:T(8,128)} %noise_hbm.1, ...), custom_call_target="tpu_custom_call" | custom-call | tf_op jit(solution)/shard_map/pack/pallas_call | solution.py:369
  9.5 0.0 all-gather.3.cloned.1.call-update
  9.6 4.9 %collective-permute-start = (f32[69,8,128]{2,1,0:T(8,128)S(1)}, f32[69,8,128]{2,1,0:T(8,128)S(1)}, u32[]{:S(2)}, u32[]{:S(2)}) collective-permute-start(f32[69,8,128]{2,1,0:T(8,128)S(1)} %get-tuple-element.15), channel_id=1, source_target_pairs={{0,8},{8,16},{16,24},{1,9},{9,17},{17,25},{2,10},{10,18},{18,26},{... | collective-permute-start | bytes 847880 | tf_op jit(solution)/shard_map/ppermute | solution.py:388
  14.5 1.3 %collective-permute-start.1 = (f32[69,8,128]{2,1,0:T(8,128)S(1)}, f32[69,8,128]{2,1,0:T(8,128)S(1)}, u32[]{:S(2)}, u32[]{:S(2)}) collective-permute-start(f32[69,8,128]{2,1,0:T(8,128)S(1)} %get-tuple-element.16), channel_id=1, source_target_pairs={{8,0},{16,8},{24,16},{9,1},{17,9},{25,17},{10,2},{18,10},{26,18},{... | collective-permute-start | bytes 847880 | tf_op jit(solution)/shard_map/ppermute | solution.py:389
  15.8 3.7 %collective-permute-start.2 = (f32[5,8,128]{2,1,0:T(8,128)S(1)}, f32[5,8,128]{2,1,0:T(8,128)S(1)}, u32[]{:S(2)}, u32[]{:S(2)}) collective-permute-start(f32[5,8,128]{2,1,0:T(8,128)S(1)} %get-tuple-element.19.obs_ref), channel_id=1, source_target_pairs={{0,16},{8,24},{16,0},{24,8},{1,17},{9,25},{17,1},{25,9},{2,18},{10... | collective-permute-start | bytes 61448 | tf_op jit(solution)/shard_map/ppermute | solution.py:391
  19.5 7.1 %inner_planes.1 = (f32[256,8,128]{2,1,0:T(8,128)S(1)}, f32[224,8,128]{2,1,0:T(8,128)S(1)}) custom-call(f32[2048,128]{1,0:T(8,128)} %bitcast.29, f32[2048,128]{1,0:T(8,128)} %bitcast.26), custom_call_target="tpu_custom_call" | custom-call | flops 20000000 | bytes 20000000 | tf_op jit(solution)/shard_map/inner_planes/pallas_call | solution.py:397
  26.6 0.0 collective-permute-done.2.before_2_hbm.after_2_hbm.before_2_ref.after_2_ref
  26.6 0.0 collective-permute-done.before_ref
  26.6 0.0 collective-permute-done.1.after_ref
  26.7 2.6 %outer_planes.1 = (f32[256,8,128]{2,1,0:T(8,128)S(1)}, f32[32,8,256]{2,1,0:T(8,128)}) custom-call(s32[256]{0:T(256)} %probe_hbm.1, f32[69,8,128]{2,1,0:T(8,128)S(1)} %collective-permute-done.before_ref, f32[69,8,128]{2,1,0:T(8,128)S(1)} %collective-permute-done.1.after_ref, ...), custom_call_target="tpu_custom_call", output_to_operand_aliasing={{0}: (4, {})} | custom-call | tf_op jit(solution)/shard_map/outer_planes/pallas_call | solution.py:418
  29.3 3.8 %all-to-all-start = ((f32[32,8,256]{2,1,0:T(8,128)}), f32[32,8,256]{2,1,0:T(8,128)S(1)}, u32[]{:S(2)}, u32[]{:S(2)}) async-start(f32[32,8,256]{2,1,0:T(8,128)} %get-tuple-element.23), calls=%async_computation | async-start | bytes 524288 | tf_op jit(solution)/shard_map/all_to_all | solution.py:431
  33.8 0.1 pad_add_fusion.place_ref
  33.9 2.8 %all-gather.3.cloned.1.call-done = f32[256,8,128]{2,1,0:T(8,128)} async-done(((f32[32,8,128]{2,1,0:T(8,128)}), f32[256,8,128]{2,1,0:T(8,128)}) %all-gather.3.cloned.1.call-update) | async-done | bytes 1048592 | tf_op jit(solution)/shard_map/all_gather | solution.py:396
  36.7 0.0 copy-start
  36.7 2.6 %between.1 = (f32[2048,128]{1,0:T(8,128)}, bf16[32,128,128]{2,1,0:T(8,128)(2,1)S(1)}) custom-call(f32[256,8,128]{2,1,0:T(8,128)S(1)} %get-tuple-element.20.u2_ref, f32[8,32,8,128]{3,2,1,0:T(8,128)} %bitcast.30), custom_call_target="tpu_custom_call" | custom-call | flops 1000000 | bytes 8000000 | tf_op jit(solution)/shard_map/between/pallas_call | solution.py:432
  39.3 0.0 copy-start.1
  39.3 1.0 %copy-done.1 = bf16[32,128,128]{2,1,0:T(8,128)(2,1)} copy-done((bf16[32,128,128]{2,1,0:T(8,128)(2,1)}, bf16[32,128,128]{2,1,0:T(8,128)(2,1)S(1)}, u32[]{:S(2)}) %copy-start.1) | copy-done | bytes 1048600
  40.3 3.5 %all-to-all-done.pred_ref = f32[32,8,256]{2,1,0:T(8,128)S(1)} async-done(((f32[32,8,256]{2,1,0:T(8,128)}), f32[32,8,256]{2,1,0:T(8,128)S(1)}, u32[]{:S(2)}, u32[]{:S(2)}) %all-to-all-start) | async-done | bytes 262176 | tf_op jit(solution)/shard_map/all_to_all | solution.py:431
  43.8 0.0 copy-done
  43.8 0.0 copy-start.2
  43.8 1.2 %copy-done.2 = bf16[32,128,128]{2,1,0:T(8,128)(2,1)S(1)} copy-done((bf16[32,128,128]{2,1,0:T(8,128)(2,1)S(1)}, bf16[32,128,128]{2,1,0:T(8,128)(2,1)}, u32[]{:S(2)}) %copy-start.2) | copy-done | bytes 1048600
  45.0 3.8 %update.1 = (f32[2048,128]{1,0:T(8,128)}, f32[8,256]{1,0:T(8,128)}) custom-call(s32[2]{0:T(128)S(1)} %pad_add_fusion.place_ref, s32[1]{0:T(128)S(6)} %copy.16.count_ref, s32[1,32]{1,0:T(1,128)} %cells_ref.1, s32[1,32]{1,0:T(1,128)} %probes_ref.1, s32[1,32]{1,0:T(1,128)} %level_ref.1, f32[32,8,256]{2,1,0:T(8,128)S(1)} %all-to-all-done.pred_ref, ...), custom_call_target="tpu_custom_call" | custom-call | tf_op jit(solution)/shard_map/update/pallas_call | solution.py:453
Async XLA Ops:
  7.2 29.5 %all-gather.3.cloned.1.call-start = ((), (), s32[]{:S(2)}) async-start(), calls=%async_computation.1 | async-start | bytes 1179648 | tf_op jit(solution)/shard_map/all_gather | solution.py:396
  9.6 17.1 %collective-permute-start = (f32[69,8,128]{2,1,0:T(8,128)S(1)}, f32[69,8,128]{2,1,0:T(8,128)S(1)}, u32[]{:S(2)}, u32[]{:S(2)}) collective-permute-start(f32[69,8,128]{2,1,0:T(8,128)S(1)} %get-tuple-element.15), channel_id=1, source_target_pairs={{0,8},{8,16},{16,24},{1,9},{9,17},{17,25},{2,10},{10,18},{18,26},{... | collective-permute-start | bytes 847880 | tf_op jit(solution)/shard_map/ppermute | solution.py:388
  14.5 12.1 %collective-permute-start.1 = (f32[69,8,128]{2,1,0:T(8,128)S(1)}, f32[69,8,128]{2,1,0:T(8,128)S(1)}, u32[]{:S(2)}, u32[]{:S(2)}) collective-permute-start(f32[69,8,128]{2,1,0:T(8,128)S(1)} %get-tuple-element.16), channel_id=1, source_target_pairs={{8,0},{16,8},{24,16},{9,1},{17,9},{25,17},{10,2},{18,10},{26,18},{... | collective-permute-start | bytes 847880 | tf_op jit(solution)/shard_map/ppermute | solution.py:389
  15.8 10.8 %collective-permute-start.2 = (f32[5,8,128]{2,1,0:T(8,128)S(1)}, f32[5,8,128]{2,1,0:T(8,128)S(1)}, u32[]{:S(2)}, u32[]{:S(2)}) collective-permute-start(f32[5,8,128]{2,1,0:T(8,128)S(1)} %get-tuple-element.19.obs_ref), channel_id=1, source_target_pairs={{0,16},{8,24},{16,0},{24,8},{1,17},{9,25},{17,1},{25,9},{2,18},{10... | collective-permute-start | bytes 61448 | tf_op jit(solution)/shard_map/ppermute | solution.py:391
  29.3 14.5 %all-to-all-start = ((f32[32,8,256]{2,1,0:T(8,128)}), f32[32,8,256]{2,1,0:T(8,128)S(1)}, u32[]{:S(2)}, u32[]{:S(2)}) async-start(f32[32,8,256]{2,1,0:T(8,128)} %get-tuple-element.23), calls=%async_computation | async-start | bytes 524288 | tf_op jit(solution)/shard_map/all_to_all | solution.py:431
  36.7 7.1 %copy-start = (f32[8,16,2048]{2,1,0:T(8,128)S(1)}, f32[8,16,2048]{2,1,0:T(8,128)}, u32[]{:S(2)}) copy-start(f32[8,16,2048]{2,1,0:T(8,128)} %param.12) | copy-start | bytes 3145732
  39.3 1.0 %copy-start.1 = (bf16[32,128,128]{2,1,0:T(8,128)(2,1)}, bf16[32,128,128]{2,1,0:T(8,128)(2,1)S(1)}, u32[]{:S(2)}) copy-start(bf16[32,128,128]{2,1,0:T(8,128)(2,1)S(1)} %get-tuple-element.24.rest_0_) | copy-start | bytes 3145732
  43.8 1.2 %copy-start.2 = (bf16[32,128,128]{2,1,0:T(8,128)(2,1)S(1)}, bf16[32,128,128]{2,1,0:T(8,128)(2,1)}, u32[]{:S(2)}) copy-start(bf16[32,128,128]{2,1,0:T(8,128)(2,1)} %copy-done.1) | copy-start | bytes 3145732
Sparse Core Ops, SparseCore 0:
  10.5 26.1 all-gather.2
where the time goes:
time: 56 us; the launch traced here: 55.6 us
  Pallas kernels  18.4 us (33%)
  between operations  14.8 us (26%)
  starting transfers between devices  13.8 us (25%)
  waiting for transfers between devices  6.3 us (11%)
  local copies, waits for them, and re-layouts  2.19 us (4%)
    pallas_call x1, Pallas kernels, shards(): pl.pallas_call(functools.partial(inner_kernel, planes, tiles), out_shape=...  7.09 us
    ppermute x1, starting transfers between devices, shards(): before = lax.ppermute(high, 'space', upward)  4.95 us
    all_to_all x1, starting transfers between devices, shards(): pred_all = lax.all_to_all(sent, ('space', 'ens'), 0, 0)  3.85 us
    pallas_call x1, Pallas kernels, shards(): pl.pallas_call(update, out_shape=(jax.ShapeDtypeStruct(u_rows.shape, f32)...  3.76 us
    ppermute x1, starting transfers between devices, shards(): lax.ppermute(obs, 'space', [(i, (i + 2) % 4) for i in range(4)])  3.71 us
    all_to_all x1, waiting for transfers between devices, shards(): pred_all = lax.all_to_all(sent, ('space', 'ens'), 0, 0)  3.46 us
    all_gather x1, waiting for transfers between devices, shards(): theta_all = lax.all_gather(picked, 'ens')  2.81 us
    pallas_call x1, Pallas kernels, shards(): pl.pallas_call(functools.partial(outer_kernel, planes, tiles), out_shape=...  2.64 us
  transfers between devices with their start and end apart: 5, of which 2 were waited for; matrix products, arithmetic and copies ran while one was open for 0% of the time, Pallas kernels for 22%

commit v1 on v0

--- a/solution.py
+++ b/solution.py
@@ -39,8 +39,8 @@
 
 
 def pack_kernel(planes, tiles, cells_hbm, taper_hbm, u_hbm, t_hbm, noise_hbm, observed_hbm, var_hbm,
-                low_ref, high_ref, obs_ref, pick_hbm,
-                cells_ref, taper_ref, u_ref, t_ref, noise_ref, row_ref, pick_ref, sems):
+                low_ref, high_ref, obs_ref, pick_hbm, u_ref, t_ref,
+                cells_ref, taper_ref, noise_ref, row_ref, pick_ref, sems):
     stride = planes * tiles
     blocks = noise_ref.shape[1] // LANES
     copies = [
@@ -62,8 +62,12 @@
     for slot in range(pick_ref.shape[0]):
         block = cells_ref[0, slot]
         pick_ref[slot] = t_ref[pl.ds(row_of(block // tiles, block % tiles, tiles), ROWS, stride=stride), :]
-    picked = pltpu.make_async_copy(pick_ref, pick_hbm, sems.at[len(copies)])
-    picked.start()
+    picked = [
+        pltpu.make_async_copy(pick_ref, pick_hbm.at[device], sems.at[len(copies) + device])
+        for device in range(pick_hbm.shape[0])
+    ]
+    for copy in picked:
+        copy.start()
     for kind, source in ((1, t_ref), (0, u_ref)):
         if kind == 0:
             copies[2].wait()
@@ -86,7 +90,8 @@
             ref[first + b] = noise_ref[:, b * LANES : (b + 1) * LANES]
         for at, row in enumerate(rows):
             ref[first + blocks + at // ROWS, at % ROWS : at % ROWS + 1, :] = row
-    picked.wait()
+    for copy in picked:
+        copy.wait()
 
 
 def rot(value, by):
@@ -144,15 +149,9 @@
         ref[at * len(values) + tile] = value
 
 
-def inner_kernel(planes, tiles, u_hbm, t_hbm, u2_ref, edge_ref,
-                 u_ref, t_ref, u0, hv, u1, held, sems):
+def inner_kernel(planes, tiles, u_ref, t_ref, u2_ref, edge_ref, u0, hv, u1, held):
     stride = planes * tiles
     masks = lane_masks()
-    copies = [pltpu.make_async_copy(u_hbm, u_ref, sems.at[0]), pltpu.make_async_copy(t_hbm, t_ref, sems.at[1])]
-    for copy in copies:
-        copy.start()
-    for copy in copies:
-        copy.wait()
 
     def load(x, _):
         base = (x // ROWS) * tiles * ROWS + x % ROWS
@@ -363,23 +362,27 @@
     obs_tiles = blocks - (-(2 * blocks + 1 + probe_taper.shape[1] * probe_taper.shape[2]) // ROWS)
     edge = jax.ShapeDtypeStruct((4 * tiles + obs_tiles, ROWS, LANES), f32)
     obs_shape = jax.ShapeDtypeStruct((obs_tiles, ROWS, LANES), f32)
-    params = pltpu.CompilerParams(vmem_limit_bytes=48 * 1024 * 1024)
-    field = pltpu.VMEM(u_rows.shape, f32)
+    params = pltpu.CompilerParams(vmem_limit_bytes=32 * 1024 * 1024)
     stack = pltpu.VMEM((planes * tiles, ROWS, LANES), f32)
-    low, high, obs, picked = pl.pallas_call(
+    low, high, obs, picked, u_near, t_near = pl.pallas_call(
         functools.partial(pack_kernel, planes, tiles),
-        out_shape=(edge, edge, obs_shape, jax.ShapeDtypeStruct((slots, ROWS, LANES), f32)),
+        out_shape=(
+            edge,
+            edge,
+            obs_shape,
+            jax.ShapeDtypeStruct((groups, slots, ROWS, LANES), f32),
+            jax.ShapeDtypeStruct(u_rows.shape, f32),
+            jax.ShapeDtypeStruct(u_rows.shape, f32),
+        ),
         in_specs=[HBM] * 7,
-        out_specs=(VMEM, VMEM, VMEM, HBM),
+        out_specs=(VMEM, VMEM, VMEM, HBM, VMEM, VMEM),
         scratch_shapes=[
             pltpu.SMEM(pair_cells.shape, i32),
             pltpu.SMEM(probe_taper.shape, i32),
-            field,
-            field,
             pltpu.VMEM((ROWS, probes), f32),
             pltpu.VMEM((2, probes), f32),
             pltpu.VMEM((slots, ROWS, LANES), f32),
-            pltpu.SemaphoreType.DMA((8,)),
+            pltpu.SemaphoreType.DMA((7 + groups,)),
         ],
         compiler_params=params,
         name="pack",
@@ -393,28 +396,20 @@
         upward_2 = [(i, i + 2) for i in range(slabs - 2)]
         before_2 = lax.ppermute(obs, "space", upward_2)
         after_2 = lax.ppermute(obs, "space", [(j, i) for i, j in upward_2])
-    theta_all = lax.all_gather(picked, "ens")
+    theta_all = lax.all_to_all(picked, "ens", 0, 0)
     inner, edges = pl.pallas_call(
         functools.partial(inner_kernel, planes, tiles),
         out_shape=(
             jax.ShapeDtypeStruct((planes * tiles, ROWS, LANES), f32),
             jax.ShapeDtypeStruct((14 * tiles, ROWS, LANES), f32),
         ),
-        in_specs=[HBM] * 2,
+        in_specs=[VMEM] * 2,
         out_specs=(VMEM,) * 2,
-        scratch_shapes=[
-            field,
-            field,
-            stack,
-            stack,
-            stack,
-            pltpu.VMEM((5, planes * tiles, ROWS, LANES), f32),
-            pltpu.SemaphoreType.DMA((2,)),
-        ],
+        scratch_shapes=[stack, stack, stack, pltpu.VMEM((5, planes * tiles, ROWS, LANES), f32)],
         compiler_params=params,
         cost_estimate=pl.CostEstimate(flops=20_000_000, bytes_accessed=20_000_000, transcendentals=0),
         name="inner_planes",
-    )(stay(u_rows), stay(t_rows))
+    )(u_near, t_near)
     u2, sent = pl.pallas_call(
         functools.partial(outer_kernel, planes, tiles),
         out_shape=(
@@ -468,7 +463,7 @@
         compiler_params=params,
         name="update",
     )(place, pair_counts, *map(stay, (pair_cells, pair_probes, pair_taper)), pred_all, before_2, before, obs, after,
-      after_2, split, t_rows)
+      after_2, split, t_near)
     return (from_rows(u2_rows, shape), from_rows(post_rows, shape), gain)
 
 

time: 56 us -> 48.2 us (0.86)
  between operations: 14.8 us -> 1.37 us
  starting transfers between devices: 13.8 us -> 18 us
  local copies, waits for them, and re-layouts: 2.19 us -> 4.38 us
  Pallas kernels: 18.4 us -> 17.1 us
  waiting for transfers between devices: 6.3 us -> 6.91 us
    all_to_all x0 -> x1, starting transfers between devices: none -> 5.17 us  [shards(): theta_all = lax.all_to_all(picked, 'ens', 0, 0)]
    all_to_all x1, waiting for transfers between devices: 3.46 us -> 6.36 us  [shards(): pred_all = lax.all_to_all(sent, ('space', 'ens'), 0, 0)]
    all_gather x1 -> x0, waiting for transfers between devices: 2.81 us -> none  [shards(): theta_all = lax.all_gather(picked, 'ens')]
    unnamed x6 -> x8, local copies, waits for them, and re-layouts: 2.19 us -> 4.38 us
    pallas_call x1, Pallas kernels: 7.09 us -> 5.49 us  [shards(): pl.pallas_call(functools.partial(inner_kernel, planes, tiles), out_shape=...]
    ppermute x1, starting transfers between devices: 4.95 us -> 4.05 us  [shards(): before = lax.ppermute(high, 'space', upward)]
where the time goes in v1:
time: 48.2 us; the launch traced here: 47.8 us
  starting transfers between devices  18 us (37%)
  Pallas kernels  17.1 us (35%)
  waiting for transfers between devices  6.91 us (14%)
  local copies, waits for them, and re-layouts  4.38 us (9%)
  between operations  1.37 us (3%)
    all_to_all x1, waiting for transfers between devices, shards(): pred_all = lax.all_to_all(sent, ('space', 'ens'), 0, 0)  6.36 us
    pallas_call x1, Pallas kernels, shards(): pl.pallas_call(functools.partial(inner_kernel, planes, tiles), out_shape=...  5.49 us
    all_to_all x1, starting transfers between devices, shards(): theta_all = lax.all_to_all(picked, 'ens', 0, 0)  5.17 us
    unnamed x8, local copies, waits for them, and re-layouts  4.38 us
    ppermute x1, starting transfers between devices, shards(): before = lax.ppermute(high, 'space', upward)  4.05 us
    all_to_all x1, starting transfers between devices, shards(): pred_all = lax.all_to_all(sent, ('space', 'ens'), 0, 0)  3.76 us
    pallas_call x1, Pallas kernels, shards(): pl.pallas_call(update, out_shape=(jax.ShapeDtypeStruct(u_rows.shape, f32)...  3.76 us
    ppermute x1, starting transfers between devices, shards(): lax.ppermute(obs, 'space', [(i, (i + 2) % 4) for i in range(4)])  3.71 us
  transfers between devices with their start and end apart: 5, of which 2 were waited for; matrix products, arithmetic and copies ran while one was open for 0% of the time, Pallas kernels for 22%

profile of v1, /device:TPU:0, one launch (start us, length us, event | category | flops | bytes accessed | tf_op | source)
XLA Modules:
  0.0 47.8 jit_solution(2131799563104804478)
XLA Ops:
  0.6 2.7 %pack.1 = (f32[69,8,128]{2,1,0:T(8,128)S(1)}, f32[69,8,128]{2,1,0:T(8,128)S(1)}, f32[5,8,128]{2,1,0:T(8,128)S(1)}, f32[8,32,8,128]{3,2,1,0:T(8,128)}, f32[2048,128]{1,0:T(8,128)S(1)}, /*index=5*/f32[2048,128]{1,0:T(8,128)S(1)}) custom-call(s32[1,32]{1,0:T(1,128)} %cells_ref.1, s32[1,2,6]{2,1,0:T(2,128)} %taper_hbm.1, f32[2048,128]{1,0:T(8,128)} %bitcast.24, ...), custom_call_target="tpu_custom_call" | custom-call | tf_op jit(solution)/shard_map/pack/pallas_call | solution.py:367
  3.3 0.0 copy-start
  3.3 1.0 %copy-done = f32[2048,128]{1,0:T(8,128)} copy-done((f32[2048,128]{1,0:T(8,128)}, f32[2048,128]{1,0:T(8,128)S(1)}, u32[]{:S(2)}) %copy-start) | copy-done | bytes 1048600
  4.3 5.2 %all-to-all-start = ((f32[8,32,8,128]{3,2,1,0:T(8,128)}), f32[8,32,8,128]{3,2,1,0:T(8,128)}, u32[]{:S(2)}, u32[]{:S(2)}) async-start(f32[8,32,8,128]{3,2,1,0:T(8,128)} %get-tuple-element.25), calls=%async_computation | async-start | bytes 2097152 | tf_op jit(solution)/shard_map/all_to_all | solution.py:399
  9.5 4.0 %collective-permute-start = (f32[69,8,128]{2,1,0:T(8,128)S(1)}, f32[69,8,128]{2,1,0:T(8,128)S(1)}, u32[]{:S(2)}, u32[]{:S(2)}) collective-permute-start(f32[69,8,128]{2,1,0:T(8,128)S(1)} %get-tuple-element.17), channel_id=1, source_target_pairs={{0,8},{8,16},{16,24},{1,9},{9,17},{17,25},{2,10},{10,18},{18,26},{... | collective-permute-start | bytes 847880 | tf_op jit(solution)/shard_map/ppermute | solution.py:391
  13.5 1.3 %collective-permute-start.1 = (f32[69,8,128]{2,1,0:T(8,128)S(1)}, f32[69,8,128]{2,1,0:T(8,128)S(1)}, u32[]{:S(2)}, u32[]{:S(2)}) collective-permute-start(f32[69,8,128]{2,1,0:T(8,128)S(1)} %get-tuple-element.18), channel_id=1, source_target_pairs={{8,0},{16,8},{24,16},{9,1},{17,9},{25,17},{10,2},{18,10},{26,18},{... | collective-permute-start | bytes 847880 | tf_op jit(solution)/shard_map/ppermute | solution.py:392
  14.8 3.7 %collective-permute-start.2 = (f32[5,8,128]{2,1,0:T(8,128)S(1)}, f32[5,8,128]{2,1,0:T(8,128)S(1)}, u32[]{:S(2)}, u32[]{:S(2)}) collective-permute-start(f32[5,8,128]{2,1,0:T(8,128)S(1)} %get-tuple-element.23.obs_ref), channel_id=1, source_target_pairs={{0,16},{8,24},{16,0},{24,8},{1,17},{9,25},{17,1},{25,9},{2,18},{10... | collective-permute-start | bytes 61448 | tf_op jit(solution)/shard_map/ppermute | solution.py:394
  18.5 0.0 copy-start.1
  18.5 1.2 %copy-done.1 = f32[2048,128]{1,0:T(8,128)S(1)} copy-done((f32[2048,128]{1,0:T(8,128)S(1)}, f32[2048,128]{1,0:T(8,128)}, u32[]{:S(2)}) %copy-start.1) | copy-done | bytes 1048600
  19.8 5.5 %inner_planes.1 = (f32[256,8,128]{2,1,0:T(8,128)S(1)}, f32[224,8,128]{2,1,0:T(8,128)S(1)}) custom-call(f32[2048,128]{1,0:T(8,128)S(1)} %copy-done.1, f32[2048,128]{1,0:T(8,128)S(1)} %get-tuple-element.20.t_ref.rest_1_), custom_call_target="tpu_custom_call" | custom-call | flops 20000000 | bytes 20000000 | tf_op jit(solution)/shard_map/inner_planes/pallas_call | solution.py:400
  25.2 0.5 %collective-permute-done.2.before_2_hbm.after_2_hbm.before_2_ref.after_2_ref = f32[5,8,128]{2,1,0:T(8,128)S(1)} collective-permute-done((f32[5,8,128]{2,1,0:T(8,128)S(1)}, f32[5,8,128]{2,1,0:T(8,128)S(1)}, u32[]{:S(2)}, u32[]{:S(2)}) %collective-permute-start.2) | collective-permute-done | bytes 20512 | tf_op jit(solution)/shard_map/ppermute | solution.py:394
  25.8 0.0 collective-permute-done.before_ref
  25.8 0.0 collective-permute-done.1.after_ref
  25.8 2.6 %outer_planes.1 = (f32[256,8,128]{2,1,0:T(8,128)S(1)}, f32[32,8,256]{2,1,0:T(8,128)}) custom-call(s32[256]{0:T(256)} %probe_hbm.1, f32[69,8,128]{2,1,0:T(8,128)S(1)} %collective-permute-done.before_ref, f32[69,8,128]{2,1,0:T(8,128)S(1)} %collective-permute-done.1.after_ref, ...), custom_call_target="tpu_custom_call", output_to_operand_aliasing={{0}: (4, {})} | custom-call | tf_op jit(solution)/shard_map/outer_planes/pallas_call | solution.py:413
  28.4 0.0 all-to-all-done.theta_hbm
  28.5 3.8 %all-to-all-start.1 = ((f32[32,8,256]{2,1,0:T(8,128)}), f32[32,8,256]{2,1,0:T(8,128)S(1)}, u32[]{:S(2)}, u32[]{:S(2)}) async-start(f32[32,8,256]{2,1,0:T(8,128)} %get-tuple-element.27), calls=%async_computation.1 | async-start | bytes 524288 | tf_op jit(solution)/shard_map/all_to_all | solution.py:426
  32.9 0.1 pad_add_fusion.place_ref
  33.0 2.5 %between.1 = (f32[2048,128]{1,0:T(8,128)}, bf16[32,128,128]{2,1,0:T(8,128)(2,1)S(1)}) custom-call(f32[256,8,128]{2,1,0:T(8,128)S(1)} %get-tuple-element.24.u2_ref, f32[8,32,8,128]{3,2,1,0:T(8,128)} %all-to-all-done.theta_hbm), custom_call_target="tpu_custom_call" | custom-call | flops 1000000 | bytes 8000000 | tf_op jit(solution)/shard_map/between/pallas_call | solution.py:427
  35.5 0.0 copy-start.2
  35.5 1.0 %copy-done.2 = bf16[32,128,128]{2,1,0:T(8,128)(2,1)} copy-done((bf16[32,128,128]{2,1,0:T(8,128)(2,1)}, bf16[32,128,128]{2,1,0:T(8,128)(2,1)S(1)}, u32[]{:S(2)}) %copy-start.2) | copy-done | bytes 1048600
  36.5 6.4 %all-to-all-done.1.pred_ref = f32[32,8,256]{2,1,0:T(8,128)S(1)} async-done(((f32[32,8,256]{2,1,0:T(8,128)}), f32[32,8,256]{2,1,0:T(8,128)S(1)}, u32[]{:S(2)}, u32[]{:S(2)}) %all-to-all-start.1) | async-done | bytes 262176 | tf_op jit(solution)/shard_map/all_to_all | solution.py:426
  42.8 0.0 copy-start.3
  42.8 1.2 %copy-done.3 = bf16[32,128,128]{2,1,0:T(8,128)(2,1)S(1)} copy-done((bf16[32,128,128]{2,1,0:T(8,128)(2,1)S(1)}, bf16[32,128,128]{2,1,0:T(8,128)(2,1)}, u32[]{:S(2)}) %copy-start.3) | copy-done | bytes 1048600
  44.1 3.8 %update.1 = (f32[2048,128]{1,0:T(8,128)}, f32[8,256]{1,0:T(8,128)}) custom-call(s32[2]{0:T(128)S(1)} %pad_add_fusion.place_ref, s32[1]{0:T(128)S(6)} %copy.16.count_ref, s32[1,32]{1,0:T(1,128)} %cells_ref.1, s32[1,32]{1,0:T(1,128)} %probes_ref.1, s32[1,32]{1,0:T(1,128)} %level_ref.1, f32[32,8,256]{2,1,0:T(8,128)S(1)} %all-to-all-done.1.pred_ref, ...), custom_call_target="tpu_custom_call" | custom-call | tf_op jit(solution)/shard_map/update/pallas_call | solution.py:448
Async XLA Ops:
  3.3 1.0 %copy-start = (f32[2048,128]{1,0:T(8,128)}, f32[2048,128]{1,0:T(8,128)S(1)}, u32[]{:S(2)}) copy-start(f32[2048,128]{1,0:T(8,128)S(1)} %get-tuple-element.19.u_ref) | copy-start | bytes 3145732
  4.3 24.2 %all-to-all-start = ((f32[8,32,8,128]{3,2,1,0:T(8,128)}), f32[8,32,8,128]{3,2,1,0:T(8,128)}, u32[]{:S(2)}, u32[]{:S(2)}) async-start(f32[8,32,8,128]{3,2,1,0:T(8,128)} %get-tuple-element.25), calls=%async_computation | async-start | bytes 2097152 | tf_op jit(solution)/shard_map/all_to_all | solution.py:399
  9.5 16.3 %collective-permute-start = (f32[69,8,128]{2,1,0:T(8,128)S(1)}, f32[69,8,128]{2,1,0:T(8,128)S(1)}, u32[]{:S(2)}, u32[]{:S(2)}) collective-permute-start(f32[69,8,128]{2,1,0:T(8,128)S(1)} %get-tuple-element.17), channel_id=1, source_target_pairs={{0,8},{8,16},{16,24},{1,9},{9,17},{17,25},{2,10},{10,18},{18,26},{... | collective-permute-start | bytes 847880 | tf_op jit(solution)/shard_map/ppermute | solution.py:391
  13.5 12.3 %collective-permute-start.1 = (f32[69,8,128]{2,1,0:T(8,128)S(1)}, f32[69,8,128]{2,1,0:T(8,128)S(1)}, u32[]{:S(2)}, u32[]{:S(2)}) collective-permute-start(f32[69,8,128]{2,1,0:T(8,128)S(1)} %get-tuple-element.18), channel_id=1, source_target_pairs={{8,0},{16,8},{24,16},{9,1},{17,9},{25,17},{10,2},{18,10},{26,18},{... | collective-permute-start | bytes 847880 | tf_op jit(solution)/shard_map/ppermute | solution.py:392
  14.8 11.0 %collective-permute-start.2 = (f32[5,8,128]{2,1,0:T(8,128)S(1)}, f32[5,8,128]{2,1,0:T(8,128)S(1)}, u32[]{:S(2)}, u32[]{:S(2)}) collective-permute-start(f32[5,8,128]{2,1,0:T(8,128)S(1)} %get-tuple-element.23.obs_ref), channel_id=1, source_target_pairs={{0,16},{8,24},{16,0},{24,8},{1,17},{9,25},{17,1},{25,9},{2,18},{10... | collective-permute-start | bytes 61448 | tf_op jit(solution)/shard_map/ppermute | solution.py:394
  18.5 1.2 %copy-start.1 = (f32[2048,128]{1,0:T(8,128)S(1)}, f32[2048,128]{1,0:T(8,128)}, u32[]{:S(2)}) copy-start(f32[2048,128]{1,0:T(8,128)} %copy-done) | copy-start | bytes 3145732
  28.5 14.4 %all-to-all-start.1 = ((f32[32,8,256]{2,1,0:T(8,128)}), f32[32,8,256]{2,1,0:T(8,128)S(1)}, u32[]{:S(2)}, u32[]{:S(2)}) async-start(f32[32,8,256]{2,1,0:T(8,128)} %get-tuple-element.27), calls=%async_computation.1 | async-start | bytes 524288 | tf_op jit(solution)/shard_map/all_to_all | solution.py:426
  35.5 1.0 %copy-start.2 = (bf16[32,128,128]{2,1,0:T(8,128)(2,1)}, bf16[32,128,128]{2,1,0:T(8,128)(2,1)S(1)}, u32[]{:S(2)}) copy-start(bf16[32,128,128]{2,1,0:T(8,128)(2,1)S(1)} %get-tuple-element.28.rest_0_) | copy-start | bytes 3145732
  42.8 1.2 %copy-start.3 = (bf16[32,128,128]{2,1,0:T(8,128)(2,1)S(1)}, bf16[32,128,128]{2,1,0:T(8,128)(2,1)}, u32[]{:S(2)}) copy-start(bf16[32,128,128]{2,1,0:T(8,128)(2,1)} %copy-done.2) | copy-start | bytes 3145732

commit v2 on v0

--- a/solution.py
+++ b/solution.py
@@ -38,15 +38,13 @@
     return (plane // ROWS * tiles + tile) * ROWS + plane % ROWS
 
 
-def pack_kernel(planes, tiles, cells_hbm, taper_hbm, u_hbm, t_hbm, noise_hbm, observed_hbm, var_hbm,
-                low_ref, high_ref, obs_ref, pick_hbm,
-                cells_ref, taper_ref, u_ref, t_ref, noise_ref, row_ref, pick_ref, sems):
+def pack_kernel(planes, tiles, taper_hbm, u_hbm, t_hbm, noise_hbm, observed_hbm, var_hbm,
+                low_ref, high_ref, obs_ref, t_ref, taper_ref, u_ref, noise_ref, row_ref, sems):
     stride = planes * tiles
     blocks = noise_ref.shape[1] // LANES
     copies = [
         pltpu.make_async_copy(source, target, sems.at[at])
         for at, (source, target) in enumerate((
-            (cells_hbm, cells_ref),
             (t_hbm, t_ref),
             (u_hbm, u_ref),
             (taper_hbm, taper_ref),
@@ -57,23 +55,15 @@
     ]
     for copy in copies:
         copy.start()
-    copies[0].wait()
-    copies[1].wait()
-    for slot in range(pick_ref.shape[0]):
-        block = cells_ref[0, slot]
-        pick_ref[slot] = t_ref[pl.ds(row_of(block // tiles, block % tiles, tiles), ROWS, stride=stride), :]
-    picked = pltpu.make_async_copy(pick_ref, pick_hbm, sems.at[len(copies)])
-    picked.start()
     for kind, source in ((1, t_ref), (0, u_ref)):
-        if kind == 0:
-            copies[2].wait()
+        copies[1 - kind].wait()
         for out_ref, first in ((high_ref, planes - 2), (low_ref, 0)):
             for depth in range(2):
                 for tile in range(tiles):
                     out_ref[(kind * 2 + depth) * tiles + tile] = source[
                         pl.ds(row_of(first + depth, tile, tiles), ROWS, stride=stride), :
                     ]
-    for copy in copies[3:]:
+    for copy in copies[2:]:
         copy.wait()
     own, window = taper_ref.shape[1:]
     rows = [row_ref[kind : kind + 1, b * LANES : (b + 1) * LANES] for kind in range(2) for b in range(blocks)]
@@ -86,7 +76,25 @@
             ref[first + b] = noise_ref[:, b * LANES : (b + 1) * LANES]
         for at, row in enumerate(rows):
             ref[first + blocks + at // ROWS, at % ROWS : at % ROWS + 1, :] = row
-    picked.wait()
+
+
+def pick_kernel(planes, tiles, cells_hbm, t_ref, pick_hbm, done_ref, cells_ref, pick_ref, sems):
+    copy = pltpu.make_async_copy(cells_hbm, cells_ref, sems.at[0])
+    copy.start()
+    done_ref[...] = jnp.zeros(done_ref.shape, jnp.float32)
+    copy.wait()
+    for slot in range(pick_ref.shape[0]):
+        block = cells_ref[0, slot]
+        row = row_of(block // tiles, block % tiles, tiles)
+        pick_ref[slot] = t_ref[pl.ds(row, ROWS, stride=planes * tiles), :]
+    copies = [
+        pltpu.make_async_copy(pick_ref, pick_hbm.at[device], sems.at[1 + device])
+        for device in range(pick_hbm.shape[0])
+    ]
+    for copy in copies:
+        copy.start()
+    for copy in copies:
+        copy.wait()
 
 
 def rot(value, by):
@@ -144,46 +152,56 @@
         ref[at * len(values) + tile] = value
 
 
-def inner_kernel(planes, tiles, u_hbm, t_hbm, u2_ref, edge_ref,
-                 u_ref, t_ref, u0, hv, u1, held, sems):
+def each(first, last, unroll, body):
+    count = (last - first) // unroll
+
+    def several(at, _):
+        for d in range(unroll):
+            body(first + at * unroll + d)
+        return 0
+
+    lax.fori_loop(0, count, several, 0)
+    for x in range(first + count * unroll, last):
+        body(x)
+
+
+def inner_kernel(planes, tiles, u_hbm, t_ref, after_pick, u2_ref, edge_ref, u_ref, u0, hv, u1, held, sem):
     stride = planes * tiles
     masks = lane_masks()
-    copies = [pltpu.make_async_copy(u_hbm, u_ref, sems.at[0]), pltpu.make_async_copy(t_hbm, t_ref, sems.at[1])]
-    for copy in copies:
-        copy.start()
-    for copy in copies:
-        copy.wait()
-
-    def load(x, _):
-        base = (x // ROWS) * tiles * ROWS + x % ROWS
+    copy = pltpu.make_async_copy(u_hbm, u_ref, sem)
+    copy.start()
+
+    def rows_at(x, tile):
+        return pl.ds((x // ROWS) * tiles * ROWS + x % ROWS + tile * ROWS, ROWS, stride=stride)
+
+    def load_t(x):
         for tile in range(tiles):
-            rows = pl.ds(base + tile * ROWS, ROWS, stride=stride)
-            u0[x * tiles + tile] = u_ref[rows, :]
-            hv[x * tiles + tile] = HALF_DT * jnp.exp(t_ref[rows, :])
-        return 0
-
-    lax.fori_loop(0, planes, load, 0)
-
-    def first_step(x, _):
+            hv[x * tiles + tile] = HALF_DT * jnp.exp(t_ref[rows_at(x, tile), :])
+
+    def load_u(x):
+        for tile in range(tiles):
+            u0[x * tiles + tile] = u_ref[rows_at(x, tile), :]
+
+    def first_step(x):
         weights = coefficients(masks, *[plane_of(hv, x + d, tiles) for d in (-1, 0, 1)])
         for tile in range(tiles):
             for kind in range(5):
                 held[kind, x * tiles + tile] = weights[tile][kind]
         put(u1, x, step(masks, weights, *[plane_of(u0, x + d, tiles) for d in (-1, 0, 1)]))
-        return 0
-
-    lax.fori_loop(1, planes - 1, first_step, 0)
-
-    def second_step(x, _):
+
+    def second_step(x):
         weights = []
         for tile in range(tiles):
             at = x * tiles + tile
             here = hv[at]
             weights.append([held[kind, at] for kind in range(5)] + [here + hv[at - tiles], here + hv[at + tiles]])
         put(u2_ref, x, step(masks, weights, *[plane_of(u1, x + d, tiles) for d in (-1, 0, 1)]))
-        return 0
-
-    lax.fori_loop(2, planes - 2, second_step, 0)
+
+    each(0, planes, 4, load_t)
+    copy.wait()
+    each(0, planes, 4, load_u)
+    each(1, planes - 1, 7, first_step)
+    each(2, planes - 2, 6, second_step)
     last = planes - 1
     at = 0
     for ref, kept in ((u0, (0, 1, last - 1, last)), (hv, (0, 1, 2, last - 2, last - 1, last)),
@@ -274,21 +292,21 @@
 
 
 def update_kernel(slabs, groups, planes, tiles, place_ref, count_ref, cells_hbm, probes_hbm, level_hbm,
-                  pred_ref, obs_refs, split_ref, t_ref, post_ref, gain_ref,
-                  reach, cells_ref, probes_ref, level_ref, sems):
+                  pred_ref, obs_refs, split_hbm, t_hbm, post_ref, gain_ref,
+                  reach, cells_ref, probes_ref, level_ref, split_ref, sems):
     members = groups * ROWS
     share = 1.0 / (members - 1)
     copies = [
         pltpu.make_async_copy(source, target, sems.at[at])
         for at, (source, target) in enumerate((
-            (cells_hbm, cells_ref), (probes_hbm, probes_ref), (level_hbm, level_ref)))
+            (cells_hbm, cells_ref), (probes_hbm, probes_ref), (level_hbm, level_ref),
+            (split_hbm, split_ref), (t_hbm, post_ref)))
     ]
     for copy in copies:
         copy.start()
     slab, group = place_ref[0], place_ref[1]
     blocks = gain_ref.shape[1] // LANES
     window = 3 * blocks
-    post_ref[...] = t_ref[...]
 
     def wide(row):
         return row[:, :members] if members <= LANES else jnp.concatenate([row] * (members // LANES), axis=1)
@@ -363,27 +381,23 @@
     obs_tiles = blocks - (-(2 * blocks + 1 + probe_taper.shape[1] * probe_taper.shape[2]) // ROWS)
     edge = jax.ShapeDtypeStruct((4 * tiles + obs_tiles, ROWS, LANES), f32)
     obs_shape = jax.ShapeDtypeStruct((obs_tiles, ROWS, LANES), f32)
-    params = pltpu.CompilerParams(vmem_limit_bytes=48 * 1024 * 1024)
-    field = pltpu.VMEM(u_rows.shape, f32)
+    params = pltpu.CompilerParams(vmem_limit_bytes=32 * 1024 * 1024)
     stack = pltpu.VMEM((planes * tiles, ROWS, LANES), f32)
-    low, high, obs, picked = pl.pallas_call(
+    low, high, obs, t_near = pl.pallas_call(
         functools.partial(pack_kernel, planes, tiles),
-        out_shape=(edge, edge, obs_shape, jax.ShapeDtypeStruct((slots, ROWS, LANES), f32)),
-        in_specs=[HBM] * 7,
-        out_specs=(VMEM, VMEM, VMEM, HBM),
+        out_shape=(edge, edge, obs_shape, jax.ShapeDtypeStruct(u_rows.shape, f32)),
+        in_specs=[HBM] * 6,
+        out_specs=(VMEM,) * 4,
         scratch_shapes=[
-            pltpu.SMEM(pair_cells.shape, i32),
             pltpu.SMEM(probe_taper.shape, i32),
-            field,
-            field,
+            pltpu.VMEM(u_rows.shape, f32),
             pltpu.VMEM((ROWS, probes), f32),
             pltpu.VMEM((2, probes), f32),
-            pltpu.VMEM((slots, ROWS, LANES), f32),
-            pltpu.SemaphoreType.DMA((8,)),
+            pltpu.SemaphoreType.DMA((6,)),
         ],
         compiler_params=params,
         name="pack",
-    )(*map(stay, (pair_cells, probe_taper, u_rows, t_rows, obs_noise, observed.reshape(1, -1), obs_var.reshape(1, -1))))
+    )(*map(stay, (probe_taper, u_rows, t_rows, obs_noise, observed.reshape(1, -1), obs_var.reshape(1, -1))))
     upward = [(i, i + 1) for i in range(slabs - 1)]
     before = lax.ppermute(high, "space", upward)
     after = lax.ppermute(low, "space", [(j, i) for i, j in upward])
@@ -393,28 +407,43 @@
         upward_2 = [(i, i + 2) for i in range(slabs - 2)]
         before_2 = lax.ppermute(obs, "space", upward_2)
         after_2 = lax.ppermute(obs, "space", [(j, i) for i, j in upward_2])
-    theta_all = lax.all_gather(picked, "ens")
+    picked, after_pick = pl.pallas_call(
+        functools.partial(pick_kernel, planes, tiles),
+        out_shape=(
+            pltpu.HBM((groups, slots, ROWS, LANES), f32),
+            jax.ShapeDtypeStruct((ROWS, LANES), f32),
+        ),
+        in_specs=[HBM, VMEM],
+        out_specs=(HBM, VMEM),
+        scratch_shapes=[
+            pltpu.SMEM(pair_cells.shape, i32),
+            pltpu.VMEM((slots, ROWS, LANES), f32),
+            pltpu.SemaphoreType.DMA((1 + groups,)),
+        ],
+        compiler_params=params,
+        name="pick",
+    )(stay(pair_cells), t_near)
+    theta_all = lax.all_to_all(picked, "ens", 0, 0)
     inner, edges = pl.pallas_call(
         functools.partial(inner_kernel, planes, tiles),
         out_shape=(
             jax.ShapeDtypeStruct((planes * tiles, ROWS, LANES), f32),
             jax.ShapeDtypeStruct((14 * tiles, ROWS, LANES), f32),
         ),
-        in_specs=[HBM] * 2,
+        in_specs=[HBM, VMEM, VMEM],
         out_specs=(VMEM,) * 2,
         scratch_shapes=[
-            field,
-            field,
+            pltpu.VMEM(u_rows.shape, f32),
             stack,
             stack,
             stack,
             pltpu.VMEM((5, planes * tiles, ROWS, LANES), f32),
-            pltpu.SemaphoreType.DMA((2,)),
+            pltpu.SemaphoreType.DMA(()),
         ],
         compiler_params=params,
         cost_estimate=pl.CostEstimate(flops=20_000_000, bytes_accessed=20_000_000, transcendentals=0),
         name="inner_planes",
-    )(stay(u_rows), stay(t_rows))
+    )(stay(u_rows), t_near, after_pick)
     u2, sent = pl.pallas_call(
         functools.partial(outer_kernel, planes, tiles),
         out_shape=(
@@ -433,7 +462,7 @@
         functools.partial(between_kernel, planes, tiles),
         out_shape=(
             jax.ShapeDtypeStruct(u_rows.shape, f32),
-            jax.ShapeDtypeStruct((slots, 2 * groups * ROWS, LANES), jnp.bfloat16),
+            pltpu.HBM((slots, 2 * groups * ROWS, LANES), jnp.bfloat16),
         ),
         in_specs=[VMEM, HBM],
         out_specs=(VMEM,) * 2,
@@ -456,19 +485,20 @@
             jax.ShapeDtypeStruct(u_rows.shape, f32),
             jax.ShapeDtypeStruct((members, probes), f32),
         ),
-        in_specs=[SMEM] * 2 + [HBM] * 3 + [VMEM] * 8,
+        in_specs=[SMEM] * 2 + [HBM] * 3 + [VMEM] * 6 + [HBM] * 2,
         out_specs=(VMEM,) * 2,
         scratch_shapes=[
             pltpu.VMEM((probe_taper.shape[2], 2 * ROWS, 2 * groups * ROWS), jnp.bfloat16),
             pltpu.SMEM(pair_cells.shape, i32),
             pltpu.SMEM(pair_cells.shape, i32),
             pltpu.SMEM(pair_cells.shape, i32),
-            pltpu.SemaphoreType.DMA((3,)),
+            pltpu.VMEM(split.shape, jnp.bfloat16),
+            pltpu.SemaphoreType.DMA((5,)),
         ],
         compiler_params=params,
         name="update",
     )(place, pair_counts, *map(stay, (pair_cells, pair_probes, pair_taper)), pred_all, before_2, before, obs, after,
-      after_2, split, t_rows)
+      after_2, stay(split), stay(t_rows))
     return (from_rows(u2_rows, shape), from_rows(post_rows, shape), gain)
 
 

time: 56 us -> 47.6 us (0.85)
  between operations: 14.8 us -> 1.36 us
  starting transfers between devices: 13.8 us -> 18 us
  waiting for transfers between devices: 6.3 us -> 9.94 us
  local copies, waits for them, and re-layouts: 2.19 us -> 0 us
  Pallas kernels: 18.4 us -> 17.8 us
    all_to_all x0 -> x1, starting transfers between devices: none -> 5.18 us  [shards(): theta_all = lax.all_to_all(picked, 'ens', 0, 0)]
    all_to_all x1, waiting for transfers between devices: 3.46 us -> 6.96 us  [shards(): pred_all = lax.all_to_all(sent, ('space', 'ens'), 0, 0)]
    ppermute x1, waiting for transfers between devices: 0.01 us -> 2.97 us  [shards(): lax.ppermute(obs, 'space', [(i, (i + 2) % 4) for i in range(4)])]
    pallas_call x1, Pallas kernels: 7.09 us -> 4.28 us  [shards(): pl.pallas_call(functools.partial(inner_kernel, planes, tiles), out_shape=...]
    all_gather x1 -> x0, waiting for transfers between devices: 2.81 us -> none  [shards(): theta_all = lax.all_gather(picked, 'ens')]
    unnamed x6 -> x0, local copies, waits for them, and re-layouts: 2.19 us -> none
    pallas_call x0 -> x1, Pallas kernels: none -> 2.08 us  [shards(): pl.pallas_call(functools.partial(pick_kernel, planes, tiles), out_shape=(...]
    ppermute x1, starting transfers between devices: 4.95 us -> 4.04 us  [shards(): before = lax.ppermute(high, 'space', upward)]
  transfers between devices with their start and end apart: 5 -> 5, of which waited for: 2 -> 2; matrix products, arithmetic and copies ran while one was open for 0% -> 0% of each run, Pallas kernels for 22% -> 21%
where the time goes in v2:
time: 47.6 us; the launch traced here: 47.1 us
  starting transfers between devices  18 us (38%)
  Pallas kernels  17.8 us (37%)
  waiting for transfers between devices  9.94 us (21%)
  between operations  1.36 us (3%)
    all_to_all x1, waiting for transfers between devices, shards(): pred_all = lax.all_to_all(sent, ('space', 'ens'), 0, 0)  6.96 us
    all_to_all x1, starting transfers between devices, shards(): theta_all = lax.all_to_all(picked, 'ens', 0, 0)  5.18 us
    pallas_call x1, Pallas kernels, shards(): pl.pallas_call(functools.partial(inner_kernel, planes, tiles), out_shape=...  4.28 us
    pallas_call x1, Pallas kernels, shards(): pl.pallas_call(update, out_shape=(jax.ShapeDtypeStruct(u_rows.shape, f32)...  4.1 us
    ppermute x1, starting transfers between devices, shards(): before = lax.ppermute(high, 'space', upward)  4.04 us
    all_to_all x1, starting transfers between devices, shards(): pred_all = lax.all_to_all(sent, ('space', 'ens'), 0, 0)  3.76 us
    ppermute x1, starting transfers between devices, shards(): lax.ppermute(obs, 'space', [(i, (i + 2) % 4) for i in range(4)])  3.71 us
    ppermute x1, waiting for transfers between devices, shards(): lax.ppermute(obs, 'space', [(i, (i + 2) % 4) for i in range(4)])  2.97 us
  transfers between devices with their start and end apart: 5, of which 2 were waited for; matrix products, arithmetic and copies ran while one was open for 0% of the time, Pallas kernels for 21%

profile of v2, /device:TPU:0, one launch (start us, length us, event | category | flops | bytes accessed | tf_op | source)
XLA Modules:
  0.0 47.1 jit_solution(16164739974985549767)
XLA Ops:
  0.6 1.8 %pack.1 = (f32[69,8,128]{2,1,0:T(8,128)S(1)}, f32[69,8,128]{2,1,0:T(8,128)S(1)}, f32[5,8,128]{2,1,0:T(8,128)S(1)}, f32[2048,128]{1,0:T(8,128)S(1)}) custom-call(s32[1,2,6]{2,1,0:T(2,128)} %taper_hbm.1, f32[2048,128]{1,0:T(8,128)} %bitcast.24, f32[2048,128]{1,0:T(8,128)} %bitcast.26, f32[8,256]{1,0:T(8,128)} %noise_hbm.1, f32[1,256]{1,0:T(1,128)} %bitcast.28, ...), custom_call_target="tpu_custom_call" | custom-call | tf_op jit(solution)/shard_map/pack/pallas_call | solution.py:386
  2.4 2.1 %pick.1 = (f32[8,32,8,128]{3,2,1,0:T(8,128)}, f32[8,128]{1,0:T(8,128)S(1)}) custom-call(s32[1,32]{1,0:T(1,128)} %cells_ref.1, f32[2048,128]{1,0:T(8,128)S(1)} %get-tuple-element.19.t_ref), custom_call_target="tpu_custom_call" | custom-call | tf_op jit(solution)/shard_map/pick/pallas_call | solution.py:410
  4.5 5.2 %all-to-all-start = ((f32[8,32,8,128]{3,2,1,0:T(8,128)}), f32[8,32,8,128]{3,2,1,0:T(8,128)}, u32[]{:S(2)}, u32[]{:S(2)}) async-start(f32[8,32,8,128]{3,2,1,0:T(8,128)} %get-tuple-element.25), calls=%async_computation | async-start | bytes 2097152 | tf_op jit(solution)/shard_map/all_to_all | solution.py:426
  9.7 4.0 %collective-permute-start = (f32[69,8,128]{2,1,0:T(8,128)S(1)}, f32[69,8,128]{2,1,0:T(8,128)S(1)}, u32[]{:S(2)}, u32[]{:S(2)}) collective-permute-start(f32[69,8,128]{2,1,0:T(8,128)S(1)} %get-tuple-element.17), channel_id=1, source_target_pairs={{0,8},{8,16},{16,24},{1,9},{9,17},{17,25},{2,10},{10,18},{18,26},{... | collective-permute-start | bytes 847880 | tf_op jit(solution)/shard_map/ppermute | solution.py:402
  13.7 1.3 %collective-permute-start.1 = (f32[69,8,128]{2,1,0:T(8,128)S(1)}, f32[69,8,128]{2,1,0:T(8,128)S(1)}, u32[]{:S(2)}, u32[]{:S(2)}) collective-permute-start(f32[69,8,128]{2,1,0:T(8,128)S(1)} %get-tuple-element.18), channel_id=1, source_target_pairs={{8,0},{16,8},{24,16},{9,1},{17,9},{25,17},{10,2},{18,10},{26,18},{... | collective-permute-start | bytes 847880 | tf_op jit(solution)/shard_map/ppermute | solution.py:403
  15.0 3.7 %collective-permute-start.2 = (f32[5,8,128]{2,1,0:T(8,128)S(1)}, f32[5,8,128]{2,1,0:T(8,128)S(1)}, u32[]{:S(2)}, u32[]{:S(2)}) collective-permute-start(f32[5,8,128]{2,1,0:T(8,128)S(1)} %get-tuple-element.23.obs_ref), channel_id=1, source_target_pairs={{0,16},{8,24},{16,0},{24,8},{1,17},{9,25},{17,1},{25,9},{2,18},{10... | collective-permute-start | bytes 61448 | tf_op jit(solution)/shard_map/ppermute | solution.py:405
  18.8 4.3 %inner_planes.1 = (f32[256,8,128]{2,1,0:T(8,128)S(1)}, f32[224,8,128]{2,1,0:T(8,128)S(1)}) custom-call(f32[2048,128]{1,0:T(8,128)} %bitcast.25, f32[2048,128]{1,0:T(8,128)S(1)} %get-tuple-element.19.t_ref, f32[8,128]{1,0:T(8,128)S(1)} %get-tuple-element.20.after_pick), custom_call_target="tpu_custom_call" | custom-call | flops 20000000 | bytes 20000000 | tf_op jit(solution)/shard_map/inner_planes/pallas_call | solution.py:427
  23.0 3.0 %collective-permute-done.2.before_2_hbm.after_2_hbm.before_2_ref.after_2_ref = f32[5,8,128]{2,1,0:T(8,128)S(1)} collective-permute-done((f32[5,8,128]{2,1,0:T(8,128)S(1)}, f32[5,8,128]{2,1,0:T(8,128)S(1)}, u32[]{:S(2)}, u32[]{:S(2)}) %collective-permute-start.2) | collective-permute-done | bytes 20512 | tf_op jit(solution)/shard_map/ppermute | solution.py:405
  26.0 0.0 collective-permute-done.before_ref
  26.0 0.0 collective-permute-done.1.after_ref
  26.0 2.6 %outer_planes.1 = (f32[256,8,128]{2,1,0:T(8,128)S(1)}, f32[32,8,256]{2,1,0:T(8,128)}) custom-call(s32[256]{0:T(256)} %probe_hbm.1, f32[69,8,128]{2,1,0:T(8,128)S(1)} %collective-permute-done.before_ref, f32[69,8,128]{2,1,0:T(8,128)S(1)} %collective-permute-done.1.after_ref, ...), custom_call_target="tpu_custom_call", output_to_operand_aliasing={{0}: (4, {})} | custom-call | tf_op jit(solution)/shard_map/outer_planes/pallas_call | solution.py:447
  28.6 0.0 all-to-all-done.theta_hbm
  28.7 3.8 %all-to-all-start.1 = ((f32[32,8,256]{2,1,0:T(8,128)}), f32[32,8,256]{2,1,0:T(8,128)S(1)}, u32[]{:S(2)}, u32[]{:S(2)}) async-start(f32[32,8,256]{2,1,0:T(8,128)} %get-tuple-element.27), calls=%async_computation.1 | async-start | bytes 524288 | tf_op jit(solution)/shard_map/all_to_all | solution.py:460
  33.1 0.1 pad_add_fusion.place_ref
  33.2 2.9 %between.1 = (f32[2048,128]{1,0:T(8,128)}, bf16[32,128,128]{2,1,0:T(8,128)(2,1)}) custom-call(f32[256,8,128]{2,1,0:T(8,128)S(1)} %get-tuple-element.24.u2_ref, f32[8,32,8,128]{3,2,1,0:T(8,128)} %all-to-all-done.theta_hbm), custom_call_target="tpu_custom_call" | custom-call | flops 1000000 | bytes 8000000 | tf_op jit(solution)/shard_map/between/pallas_call | solution.py:461
  36.1 7.0 %all-to-all-done.1.pred_ref = f32[32,8,256]{2,1,0:T(8,128)S(1)} async-done(((f32[32,8,256]{2,1,0:T(8,128)}), f32[32,8,256]{2,1,0:T(8,128)S(1)}, u32[]{:S(2)}, u32[]{:S(2)}) %all-to-all-start.1) | async-done | bytes 262176 | tf_op jit(solution)/shard_map/all_to_all | solution.py:460
  43.0 4.1 %update.1 = (f32[2048,128]{1,0:T(8,128)}, f32[8,256]{1,0:T(8,128)}) custom-call(s32[2]{0:T(128)S(1)} %pad_add_fusion.place_ref, s32[1]{0:T(128)S(6)} %copy.16.count_ref, s32[1,32]{1,0:T(1,128)} %cells_ref.1, s32[1,32]{1,0:T(1,128)} %probes_ref.1, s32[1,32]{1,0:T(1,128)} %level_ref.1, f32[32,8,256]{2,1,0:T(8,128)S(1)} %all-to-all-done.1.pred_ref, ...), custom_call_target="tpu_custom_call" | custom-call | tf_op jit(solution)/shard_map/update/pallas_call | solution.py:482
Async XLA Ops:
  4.5 24.1 %all-to-all-start = ((f32[8,32,8,128]{3,2,1,0:T(8,128)}), f32[8,32,8,128]{3,2,1,0:T(8,128)}, u32[]{:S(2)}, u32[]{:S(2)}) async-start(f32[8,32,8,128]{3,2,1,0:T(8,128)} %get-tuple-element.25), calls=%async_computation | async-start | bytes 2097152 | tf_op jit(solution)/shard_map/all_to_all | solution.py:426
  9.7 16.3 %collective-permute-start = (f32[69,8,128]{2,1,0:T(8,128)S(1)}, f32[69,8,128]{2,1,0:T(8,128)S(1)}, u32[]{:S(2)}, u32[]{:S(2)}) collective-permute-start(f32[69,8,128]{2,1,0:T(8,128)S(1)} %get-tuple-element.17), channel_id=1, source_target_pairs={{0,8},{8,16},{16,24},{1,9},{9,17},{17,25},{2,10},{10,18},{18,26},{... | collective-permute-start | bytes 847880 | tf_op jit(solution)/shard_map/ppermute | solution.py:402
  13.7 12.3 %collective-permute-start.1 = (f32[69,8,128]{2,1,0:T(8,128)S(1)}, f32[69,8,128]{2,1,0:T(8,128)S(1)}, u32[]{:S(2)}, u32[]{:S(2)}) collective-permute-start(f32[69,8,128]{2,1,0:T(8,128)S(1)} %get-tuple-element.18), channel_id=1, source_target_pairs={{8,0},{16,8},{24,16},{9,1},{17,9},{25,17},{10,2},{18,10},{26,18},{... | collective-permute-start | bytes 847880 | tf_op jit(solution)/shard_map/ppermute | solution.py:403
  15.0 11.0 %collective-permute-start.2 = (f32[5,8,128]{2,1,0:T(8,128)S(1)}, f32[5,8,128]{2,1,0:T(8,128)S(1)}, u32[]{:S(2)}, u32[]{:S(2)}) collective-permute-start(f32[5,8,128]{2,1,0:T(8,128)S(1)} %get-tuple-element.23.obs_ref), channel_id=1, source_target_pairs={{0,16},{8,24},{16,0},{24,8},{1,17},{9,25},{17,1},{25,9},{2,18},{10... | collective-permute-start | bytes 61448 | tf_op jit(solution)/shard_map/ppermute | solution.py:405
  28.7 14.4 %all-to-all-start.1 = ((f32[32,8,256]{2,1,0:T(8,128)}), f32[32,8,256]{2,1,0:T(8,128)S(1)}, u32[]{:S(2)}, u32[]{:S(2)}) async-start(f32[32,8,256]{2,1,0:T(8,128)} %get-tuple-element.27), calls=%async_computation.1 | async-start | bytes 524288 | tf_op jit(solution)/shard_map/all_to_all | solution.py:460

commit v3 on v2

--- a/solution.py
+++ b/solution.py
@@ -15,7 +15,6 @@
 VMEM = pl.BlockSpec(memory_space=pltpu.VMEM)
 SMEM = pl.BlockSpec(memory_space=pltpu.SMEM)
 HBM = pl.BlockSpec(memory_space=pltpu.HBM)
-ANY = pl.BlockSpec(memory_space=pl.ANY)
 
 
 def stay(array):
@@ -38,13 +37,15 @@
     return (plane // ROWS * tiles + tile) * ROWS + plane % ROWS
 
 
-def pack_kernel(planes, tiles, taper_hbm, u_hbm, t_hbm, noise_hbm, observed_hbm, var_hbm,
-                low_ref, high_ref, obs_ref, t_ref, taper_ref, u_ref, noise_ref, row_ref, sems):
+def pack_kernel(planes, tiles, cells_hbm, taper_hbm, u_hbm, t_hbm, noise_hbm, observed_hbm, var_hbm,
+                low_ref, high_ref, obs_ref, t_ref, pick_hbm,
+                cells_ref, taper_ref, u_ref, noise_ref, row_ref, pick_ref, sems):
     stride = planes * tiles
     blocks = noise_ref.shape[1] // LANES
     copies = [
         pltpu.make_async_copy(source, target, sems.at[at])
         for at, (source, target) in enumerate((
+            (cells_hbm, cells_ref),
             (t_hbm, t_ref),
             (u_hbm, u_ref),
             (taper_hbm, taper_ref),
@@ -55,45 +56,41 @@
     ]
     for copy in copies:
         copy.start()
+    copies[0].wait()
+    copies[1].wait()
+    for slot in range(pick_ref.shape[0]):
+        block = cells_ref[0, slot]
+        row = row_of(block // tiles, block % tiles, tiles)
+        pick_ref[slot] = t_ref[pl.ds(row, ROWS, stride=stride), :]
+    picks = [
+        pltpu.make_async_copy(pick_ref, pick_hbm.at[device], sems.at[len(copies) + device])
+        for device in range(pick_hbm.shape[0])
+    ]
+    for copy in picks:
+        copy.start()
     for kind, source in ((1, t_ref), (0, u_ref)):
-        copies[1 - kind].wait()
+        if kind == 0:
+            copies[2].wait()
         for out_ref, first in ((high_ref, planes - 2), (low_ref, 0)):
             for depth in range(2):
                 for tile in range(tiles):
                     out_ref[(kind * 2 + depth) * tiles + tile] = source[
                         pl.ds(row_of(first + depth, tile, tiles), ROWS, stride=stride), :
                     ]
-    for copy in copies[2:]:
+    for ref in (low_ref, high_ref):
+        ref[4 * tiles] = jnp.ones((ROWS, LANES), jnp.float32)
+    for copy in copies[3:]:
         copy.wait()
     own, window = taper_ref.shape[1:]
     rows = [row_ref[kind : kind + 1, b * LANES : (b + 1) * LANES] for kind in range(2) for b in range(blocks)]
-    rows.append(jnp.ones((1, LANES), jnp.float32))
     for i in range(own):
         for j in range(window):
             rows.append(jnp.full((1, LANES), taper_ref[0, i, j].astype(jnp.float32), jnp.float32))
-    for ref, first in ((low_ref, 4 * tiles), (high_ref, 4 * tiles), (obs_ref, 0)):
-        for b in range(blocks):
-            ref[first + b] = noise_ref[:, b * LANES : (b + 1) * LANES]
-        for at, row in enumerate(rows):
-            ref[first + blocks + at // ROWS, at % ROWS : at % ROWS + 1, :] = row
-
-
-def pick_kernel(planes, tiles, cells_hbm, t_ref, pick_hbm, done_ref, cells_ref, pick_ref, sems):
-    copy = pltpu.make_async_copy(cells_hbm, cells_ref, sems.at[0])
-    copy.start()
-    done_ref[...] = jnp.zeros(done_ref.shape, jnp.float32)
-    copy.wait()
-    for slot in range(pick_ref.shape[0]):
-        block = cells_ref[0, slot]
-        row = row_of(block // tiles, block % tiles, tiles)
-        pick_ref[slot] = t_ref[pl.ds(row, ROWS, stride=planes * tiles), :]
-    copies = [
-        pltpu.make_async_copy(pick_ref, pick_hbm.at[device], sems.at[1 + device])
-        for device in range(pick_hbm.shape[0])
-    ]
-    for copy in copies:
-        copy.start()
-    for copy in copies:
+    for b in range(blocks):
+        obs_ref[b] = noise_ref[:, b * LANES : (b + 1) * LANES]
+    for at, row in enumerate(rows):
+        obs_ref[blocks + at // ROWS, at % ROWS : at % ROWS + 1, :] = row
+    for copy in picks:
         copy.wait()
 
 
@@ -165,7 +162,7 @@
         body(x)
 
 
-def inner_kernel(planes, tiles, u_hbm, t_ref, after_pick, u2_ref, edge_ref, u_ref, u0, hv, u1, held, sem):
+def inner_kernel(planes, tiles, u_hbm, t_ref, u2_ref, edge_ref, u_ref, u0, hv, u1, held, sem):
     stride = planes * tiles
     masks = lane_masks()
     copy = pltpu.make_async_copy(u_hbm, u_ref, sem)
@@ -211,14 +208,12 @@
             at += 1
 
 
-def outer_kernel(planes, tiles, probe_hbm, before_ref, after_ref, edge_ref, inner_ref, before_2_hbm, after_2_hbm,
+def outer_kernel(planes, tiles, probe_hbm, before_ref, after_ref, edge_ref, inner_ref, obs_ref,
                  u2_ref, sent_ref, probe_ref, sem):
     probe_copy = pltpu.make_async_copy(probe_hbm, probe_ref, sem)
     probe_copy.start()
     masks = lane_masks()
-    blocks = sent_ref.shape[2] // LANES
-    mark = 4 * tiles + blocks + 2 * blocks // ROWS
-    mark_row = 2 * blocks % ROWS
+    blocks = probe_ref.shape[0] // LANES
     edge = [plane_of(edge_ref, at, tiles) for at in range(14)]
     last = planes - 1
     for ref, own_u, own_v, own_1, where in (
@@ -228,7 +223,7 @@
         order = (0, 1) if ref is before_ref else (1, 0)
         u = [plane_of(ref, d, tiles) for d in order] + own_u
         v = [[HALF_DT * jnp.exp(t) for t in plane_of(ref, 2 + d, tiles)] for d in order] + own_v
-        live = ref[mark, mark_row : mark_row + 1, :]
+        live = ref[4 * tiles]
         weights = [coefficients(masks, v[d], v[d + 1], v[d + 2]) for d in range(3)]
         next_u = [step(masks, weights[d], u[d], u[d + 1], u[d + 2]) for d in range(2)]
         next_u[0] = [value * live for value in next_u[0]]
@@ -245,11 +240,25 @@
             turned = pltpu.roll(u2_ref[cell >> 7], (p - cell) & (LANES - 1), 1)
             found = jnp.where(lane == p, turned, found)
 
-        def send(device, _):
-            sent_ref[device, :, part * LANES : (part + 1) * LANES] = found
-            return 0
-
-        lax.fori_loop(0, sent_ref.shape[0], send, 0)
+        observed = obs_ref[blocks, part : part + 1, :]
+        variance = obs_ref[blocks, blocks + part : blocks + part + 1, :]
+        scaled = (observed + obs_ref[part] - found) / variance
+        for slab in range(sent_ref.shape[0]):
+            sent_ref[slab, part] = found
+            sent_ref[slab, blocks + part] = scaled
+    for slab in range(sent_ref.shape[0]):
+        for at in range(blocks, obs_ref.shape[0]):
+            sent_ref[slab, blocks + at] = obs_ref[at]
+
+
+def spread_kernel(place_ref, got_ref, sent_ref):
+    slabs, (groups, windows, blocks) = got_ref.shape[0], sent_ref.shape[:3]
+    for window in range(windows):
+        at = window if windows == slabs else jnp.clip(place_ref[0] + window - 2, 0, slabs - 1)
+        for b in range(blocks):
+            value = got_ref[at, b]
+            for group in range(groups):
+                sent_ref[group, window, b] = value
 
 
 def halves(value):
@@ -281,19 +290,23 @@
     lax.fori_loop(0, split_ref.shape[0], split, 0)
 
 
-def dot_lanes(left, right):
-    return lax.dot_general(left, right, (((1,), (1,)), ((), ())), precision=lax.Precision.HIGHEST,
-                           preferred_element_type=jnp.float32)
-
-
-def dot_rows(left, right):
-    return lax.dot_general(left, right, (((1,), (0,)), ((), ())), precision=lax.Precision.HIGHEST,
-                           preferred_element_type=jnp.float32)
-
-
-def update_kernel(slabs, groups, planes, tiles, place_ref, count_ref, cells_hbm, probes_hbm, level_hbm,
-                  pred_ref, obs_refs, split_hbm, t_hbm, post_ref, gain_ref,
+def stacked(value):
+    high, low = halves(value)
+    return jnp.concatenate([high.astype(jnp.float32), low.astype(jnp.float32)], axis=0).astype(jnp.bfloat16)
+
+
+def fold(both):
+    return both[:ROWS] + both[ROWS:]
+
+
+def dot(left, right, over):
+    return lax.dot_general(left, right, (((1,), (over,)), ((), ())), preferred_element_type=jnp.float32)
+
+
+def update_kernel(slabs, planes, tiles, place_ref, count_ref, cells_hbm, probes_hbm, level_hbm,
+                  pred_ref, got_ref, split_hbm, t_hbm, post_ref, gain_ref,
                   reach, cells_ref, probes_ref, level_ref, split_ref, sems):
+    groups, windows, blocks = pred_ref.shape[:3]
     members = groups * ROWS
     share = 1.0 / (members - 1)
     copies = [
@@ -304,52 +317,48 @@
     ]
     for copy in copies:
         copy.start()
-    slab, group = place_ref[0], place_ref[1]
-    blocks = gain_ref.shape[1] // LANES
-    window = 3 * blocks
+    slab = place_ref[0]
 
     def wide(row):
         return row[:, :members] if members <= LANES else jnp.concatenate([row] * (members // LANES), axis=1)
 
-    anomaly, scaled, variance, matches = [], [], [], []
+    anomaly, scaled, matches, places = [], [], [], []
     for d in range(5):
         wanted = slab + d - 2
         at = jnp.clip(wanted, 0, slabs - 1)
         live = jnp.where((wanted >= 0) & (wanted < slabs), 1.0, 0.0)
-        predicted = pred_ref[pl.ds(at * groups, groups)].reshape(members, blocks * LANES)
-        mean = jnp.sum(predicted, axis=0, keepdims=True) / members
-        anomaly.append((predicted - mean) * live)
-        mine = pred_ref[at * groups + group]
-        ref, first = obs_refs[d]
+        places.append(at)
         for b in range(blocks):
-            cut = slice(b * LANES, (b + 1) * LANES)
-            observed = ref[first + blocks, b : b + 1, :]
-            variance.append(ref[first + blocks, blocks + b : blocks + b + 1, :] + (1.0 - live))
-            scaled.append((observed + ref[first + b] - mine[:, cut]) / variance[-1] * live)
-            matches.append(dot_lanes(scaled[-1], anomaly[d][:, cut]))
+            predicted = pred_ref[:, at if windows == slabs else d, b].reshape(members, LANES)
+            mean = jnp.sum(predicted, axis=0, keepdims=True) / members
+            anomaly.append(halves((predicted - mean) * live))
+            scaled.append(got_ref[at, blocks + b] * live)
+            left = stacked(scaled[-1])
+            high, low = anomaly[-1]
+            matches.append(fold(dot(left, high, 1) + dot(left, low, 1)))
     for d in range(1, 4):
-        ref, first = obs_refs[d]
         for i in range(blocks):
-            cut = slice(i * LANES, (i + 1) * LANES)
             total = jnp.zeros((ROWS, members), jnp.float32)
-            for j in range(window):
-                at = 2 * blocks + 1 + i * window + j
-                level = ref[first + blocks + at // ROWS, at % ROWS : at % ROWS + 1, :] / 256.0 * share
+            for j in range(3 * blocks):
+                at = 2 * blocks + i * 3 * blocks + j
+                level = got_ref[places[d], 2 * blocks + at // ROWS, at % ROWS : at % ROWS + 1, :] / 256.0 * share
                 total = total + wide(level) * matches[(d - 1) * blocks + j]
-            correction = dot_rows(total, anomaly[d][:, cut])
-            gain = scaled[d * blocks + i] - correction / variance[d * blocks + i]
+            high, low = anomaly[d * blocks + i]
+            left = stacked(total)
+            correction = fold(dot(left, high, 0) + dot(left, low, 0))
+            at = blocks + i
+            variance = got_ref[places[d], 2 * blocks + at // ROWS, at % ROWS : at % ROWS + 1, :]
+            gain = scaled[d * blocks + i] - correction / variance
             if d == 2:
-                gain_ref[:, cut] = gain
-            high, low = halves(dot_lanes(gain, anomaly[d][:, cut]))
-            both = jnp.concatenate([high.astype(jnp.float32), low.astype(jnp.float32)], axis=0)
-            reach[(d - 1) * blocks + i] = jnp.concatenate([both, both], axis=1).astype(jnp.bfloat16)
+                gain_ref[:, i * LANES : (i + 1) * LANES] = gain
+            left = stacked(gain)
+            both = stacked(fold(dot(left, high, 1) + dot(left, low, 1)))
+            reach[(d - 1) * blocks + i] = jnp.concatenate([both, both], axis=1)
     for copy in copies:
         copy.wait()
     for slot in range(split_ref.shape[0]):
         weight = jnp.where(slot < count_ref[0], level_ref[0, slot].astype(jnp.float32) / 256.0, 0.0) * share
-        both = lax.dot_general(reach[probes_ref[0, slot]], split_ref[slot],
-                               (((1,), (0,)), ((), ())), preferred_element_type=jnp.float32)
-        change = (both[:ROWS] + both[ROWS:]) * weight
+        change = fold(dot(reach[probes_ref[0, slot]], split_ref[slot], 0)) * weight
         block = cells_ref[0, slot]
         rows = pl.ds(row_of(block // tiles, block % tiles, tiles), ROWS, stride=planes * tiles)
         post_ref[rows, :] = post_ref[rows, :] + change
@@ -378,51 +387,37 @@
     f32, i32 = jnp.float32, jnp.int32
     u_rows = to_rows(starting_speed_field)
     t_rows = to_rows(sample_fluidity_exponent)
-    obs_tiles = blocks - (-(2 * blocks + 1 + probe_taper.shape[1] * probe_taper.shape[2]) // ROWS)
-    edge = jax.ShapeDtypeStruct((4 * tiles + obs_tiles, ROWS, LANES), f32)
+    obs_tiles = blocks - (-(2 * blocks + probe_taper.shape[1] * probe_taper.shape[2]) // ROWS)
+    edge = jax.ShapeDtypeStruct((4 * tiles + 1, ROWS, LANES), f32)
     obs_shape = jax.ShapeDtypeStruct((obs_tiles, ROWS, LANES), f32)
     params = pltpu.CompilerParams(vmem_limit_bytes=32 * 1024 * 1024)
     stack = pltpu.VMEM((planes * tiles, ROWS, LANES), f32)
-    low, high, obs, t_near = pl.pallas_call(
+    low, high, obs, t_near, picked = pl.pallas_call(
         functools.partial(pack_kernel, planes, tiles),
-        out_shape=(edge, edge, obs_shape, jax.ShapeDtypeStruct(u_rows.shape, f32)),
-        in_specs=[HBM] * 6,
-        out_specs=(VMEM,) * 4,
+        out_shape=(
+            edge,
+            edge,
+            obs_shape,
+            jax.ShapeDtypeStruct(u_rows.shape, f32),
+            pltpu.HBM((groups, slots, ROWS, LANES), f32),
+        ),
+        in_specs=[HBM] * 7,
+        out_specs=(VMEM,) * 4 + (HBM,),
         scratch_shapes=[
+            pltpu.SMEM(pair_cells.shape, i32),
             pltpu.SMEM(probe_taper.shape, i32),
             pltpu.VMEM(u_rows.shape, f32),
             pltpu.VMEM((ROWS, probes), f32),
             pltpu.VMEM((2, probes), f32),
-            pltpu.SemaphoreType.DMA((6,)),
+            pltpu.VMEM((slots, ROWS, LANES), f32),
+            pltpu.SemaphoreType.DMA((7 + groups,)),
         ],
         compiler_params=params,
         name="pack",
-    )(*map(stay, (probe_taper, u_rows, t_rows, obs_noise, observed.reshape(1, -1), obs_var.reshape(1, -1))))
+    )(*map(stay, (pair_cells, probe_taper, u_rows, t_rows, obs_noise, observed.reshape(1, -1), obs_var.reshape(1, -1))))
     upward = [(i, i + 1) for i in range(slabs - 1)]
     before = lax.ppermute(high, "space", upward)
     after = lax.ppermute(low, "space", [(j, i) for i, j in upward])
-    if slabs == 4:
-        before_2 = after_2 = lax.ppermute(obs, "space", [(i, (i + 2) % 4) for i in range(4)])
-    else:
-        upward_2 = [(i, i + 2) for i in range(slabs - 2)]
-        before_2 = lax.ppermute(obs, "space", upward_2)
-        after_2 = lax.ppermute(obs, "space", [(j, i) for i, j in upward_2])
-    picked, after_pick = pl.pallas_call(
-        functools.partial(pick_kernel, planes, tiles),
-        out_shape=(
-            pltpu.HBM((groups, slots, ROWS, LANES), f32),
-            jax.ShapeDtypeStruct((ROWS, LANES), f32),
-        ),
-        in_specs=[HBM, VMEM],
-        out_specs=(HBM, VMEM),
-        scratch_shapes=[
-            pltpu.SMEM(pair_cells.shape, i32),
-            pltpu.VMEM((slots, ROWS, LANES), f32),
-            pltpu.SemaphoreType.DMA((1 + groups,)),
-        ],
-        compiler_params=params,
-        name="pick",
-    )(stay(pair_cells), t_near)
     theta_all = lax.all_to_all(picked, "ens", 0, 0)
     inner, edges = pl.pallas_call(
         functools.partial(inner_kernel, planes, tiles),
@@ -430,7 +425,7 @@
             jax.ShapeDtypeStruct((planes * tiles, ROWS, LANES), f32),
             jax.ShapeDtypeStruct((14 * tiles, ROWS, LANES), f32),
         ),
-        in_specs=[HBM, VMEM, VMEM],
+        in_specs=[HBM, VMEM],
         out_specs=(VMEM,) * 2,
         scratch_shapes=[
             pltpu.VMEM(u_rows.shape, f32),
@@ -443,21 +438,32 @@
         compiler_params=params,
         cost_estimate=pl.CostEstimate(flops=20_000_000, bytes_accessed=20_000_000, transcendentals=0),
         name="inner_planes",
-    )(stay(u_rows), t_near, after_pick)
+    )(stay(u_rows), t_near)
     u2, sent = pl.pallas_call(
         functools.partial(outer_kernel, planes, tiles),
         out_shape=(
             jax.ShapeDtypeStruct((planes * tiles, ROWS, LANES), f32),
-            jax.ShapeDtypeStruct((slabs * groups, members, probes), f32),
+            jax.ShapeDtypeStruct((slabs, blocks + obs_tiles, ROWS, LANES), f32),
         ),
-        in_specs=[HBM] + [VMEM] * 4 + [ANY] * 2,
+        in_specs=[HBM] + [VMEM] * 5,
         out_specs=(VMEM,) * 2,
         scratch_shapes=[pltpu.SMEM(probe_cells.shape, i32), pltpu.SemaphoreType.DMA(())],
         input_output_aliases={4: 0},
         compiler_params=params,
         name="outer_planes",
-    )(stay(probe_cells), before, after, edges, inner, before_2, after_2)
-    pred_all = lax.all_to_all(sent, ("space", "ens"), 0, 0)
+    )(stay(probe_cells), before, after, edges, inner, obs)
+    got = lax.all_to_all(sent, "space", 0, 0)
+    place = lax.axis_index("space").astype(i32).reshape(1)
+    windows = min(slabs, 5)
+    spread = pl.pallas_call(
+        spread_kernel,
+        out_shape=jax.ShapeDtypeStruct((groups, windows, blocks, ROWS, LANES), f32),
+        in_specs=[SMEM, VMEM],
+        out_specs=VMEM,
+        compiler_params=params,
+        name="spread",
+    )(place, got)
+    pred_all = lax.all_to_all(spread, "ens", 0, 0)
     u2_rows, split = pl.pallas_call(
         functools.partial(between_kernel, planes, tiles),
         out_shape=(
@@ -471,21 +477,13 @@
         cost_estimate=pl.CostEstimate(flops=1_000_000, bytes_accessed=8_000_000, transcendentals=0),
         name="between",
     )(u2, stay(theta_all))
-    place = jnp.stack([lax.axis_index("space"), lax.axis_index("ens")]).astype(i32)
-
-    def update(place_ref, count_ref, cells_ref, probes_ref, level_ref, pred_ref, before_2_ref, before_ref, obs_ref,
-               after_ref, after_2_ref, *rest):
-        seen = ((before_2_ref, 0), (before_ref, 4 * tiles), (obs_ref, 0), (after_ref, 4 * tiles), (after_2_ref, 0))
-        update_kernel(slabs, groups, planes, tiles, place_ref, count_ref, cells_ref, probes_ref, level_ref,
-                      pred_ref, seen, *rest)
-
     post_rows, gain = pl.pallas_call(
-        update,
+        functools.partial(update_kernel, slabs, planes, tiles),
         out_shape=(
             jax.ShapeDtypeStruct(u_rows.shape, f32),
             jax.ShapeDtypeStruct((members, probes), f32),
         ),
-        in_specs=[SMEM] * 2 + [HBM] * 3 + [VMEM] * 6 + [HBM] * 2,
+        in_specs=[SMEM] * 2 + [HBM] * 3 + [VMEM] * 2 + [HBM] * 2,
         out_specs=(VMEM,) * 2,
         scratch_shapes=[
             pltpu.VMEM((probe_taper.shape[2], 2 * ROWS, 2 * groups * ROWS), jnp.bfloat16),
@@ -497,8 +495,8 @@
         ],
         compiler_params=params,
         name="update",
-    )(place, pair_counts, *map(stay, (pair_cells, pair_probes, pair_taper)), pred_all, before_2, before, obs, after,
-      after_2, stay(split), stay(t_rows))
+    )(place, pair_counts, *map(stay, (pair_cells, pair_probes, pair_taper)), pred_all, got,
+      stay(split), stay(t_rows))
     return (from_rows(u2_rows, shape), from_rows(post_rows, shape), gain)
 
 

time: 47.6 us -> 62.4 us (1.31)
  waiting for transfers between devices: 9.94 us -> 22.2 us
  blocking collectives: 0 us -> 9.48 us
  starting transfers between devices: 18 us -> 13.4 us
  Pallas kernels: 17.8 us -> 15.6 us
    all_to_all x1, waiting for transfers between devices: 0.01 us -> 14.7 us  [shards(): theta_all = lax.all_to_all(picked, 'ens', 0, 0)]
    all_to_all x0 -> x1, blocking collectives: none -> 9.48 us  [shards(): got = lax.all_to_all(sent, 'space', 0, 0)]
    ppermute x1, waiting for transfers between devices: 0.01 us -> 4.13 us  [shards(): after = lax.ppermute(low, 'space', [(j, i) for i, j in upward])]
    ppermute x1 -> x0, starting transfers between devices: 3.71 us -> none  [shards(): lax.ppermute(obs, 'space', [(i, (i + 2) % 4) for i in range(4)])]
    all_to_all x1, waiting for transfers between devices: 6.96 us -> 3.33 us  [shards(): pred_all = lax.all_to_all(spread, 'ens', 0, 0)]
    ppermute x1 -> x0, waiting for transfers between devices: 2.97 us -> none  [shards(): lax.ppermute(obs, 'space', [(i, (i + 2) % 4) for i in range(4)])]
    pallas_call x2, Pallas kernels: 6.19 us -> 4.16 us  [the longest x1 3.43 us: shards(): pl.pallas_call(functools.partial(update_kernel, slabs, planes, tiles), ou...]
    all_to_all x1, starting transfers between devices: 5.18 us -> 3.72 us  [shards(): theta_all = lax.all_to_all(picked, 'ens', 0, 0)]
  transfers between devices with their start and end apart: 5 -> 4, of which waited for: 2 -> 3; matrix products, arithmetic and copies ran while one was open for 0% -> 0% of each run, Pallas kernels for 21% -> 13%
where the time goes in v3:
time: 62.4 us; the launch traced here: 61.9 us
  waiting for transfers between devices  22.2 us (36%)
  Pallas kernels  15.6 us (25%)
  starting transfers between devices  13.4 us (21%)
  blocking collectives  9.48 us (15%)
  between operations  1.35 us (2%)
    all_to_all x1, waiting for transfers between devices, shards(): theta_all = lax.all_to_all(picked, 'ens', 0, 0)  14.7 us
    all_to_all x1, blocking collectives, shards(): got = lax.all_to_all(sent, 'space', 0, 0)  9.48 us
    ppermute x1, starting transfers between devices, shards(): before = lax.ppermute(high, 'space', upward)  4.94 us
    pallas_call x1, Pallas kernels, shards(): pl.pallas_call(functools.partial(inner_kernel, planes, tiles), out_shape=...  4.28 us
    ppermute x1, waiting for transfers between devices, shards(): after = lax.ppermute(low, 'space', [(j, i) for i, j in upward])  4.13 us
    all_to_all x1, starting transfers between devices, shards(): theta_all = lax.all_to_all(picked, 'ens', 0, 0)  3.72 us
    pallas_call x1, Pallas kernels, shards(): pl.pallas_call(functools.partial(update_kernel, slabs, planes, tiles), ou...  3.43 us
    all_to_all x1, starting transfers between devices, shards(): pred_all = lax.all_to_all(spread, 'ens', 0, 0)  3.41 us
  transfers between devices with their start and end apart: 4, of which 3 were waited for; matrix products, arithmetic and copies ran while one was open for 0% of the time, Pallas kernels for 13%

profile of v3, /device:TPU:0, one launch (start us, length us, event | category | flops | bytes accessed | tf_op | source)
XLA Modules:
  0.0 61.9 jit_solution(3073935279914710617)
XLA Ops:
  0.6 2.7 %pack.1 = (f32[65,8,128]{2,1,0:T(8,128)S(1)}, f32[65,8,128]{2,1,0:T(8,128)S(1)}, f32[4,8,128]{2,1,0:T(8,128)S(1)}, f32[2048,128]{1,0:T(8,128)S(1)}, f32[8,32,8,128]{3,2,1,0:T(8,128)}) custom-call(s32[1,32]{1,0:T(1,128)} %cells_hbm.3, s32[1,2,6]{2,1,0:T(2,128)} %taper_hbm.1, f32[2048,128]{1,0:T(8,128)} %bitcast.23, f32[2048,128]{1,0:T(8,128)} %bitcast.25, ...), custom_call_target="tpu_custom_call" | custom-call | tf_op jit(solution)/shard_map/pack/pallas_call | solution.py:395
  3.3 4.9 %collective-permute-start = (f32[65,8,128]{2,1,0:T(8,128)S(1)}, f32[65,8,128]{2,1,0:T(8,128)S(1)}, u32[]{:S(2)}, u32[]{:S(2)}) collective-permute-start(f32[65,8,128]{2,1,0:T(8,128)S(1)} %get-tuple-element.16), channel_id=1, source_target_pairs={{0,8},{8,16},{16,24},{1,9},{9,17},{17,25},{2,10},{10,18},{18,26},{... | collective-permute-start | bytes 798728 | tf_op jit(solution)/shard_map/ppermute | solution.py:419
  8.3 1.3 %collective-permute-start.1 = (f32[65,8,128]{2,1,0:T(8,128)S(1)}, f32[65,8,128]{2,1,0:T(8,128)S(1)}, u32[]{:S(2)}, u32[]{:S(2)}) collective-permute-start(f32[65,8,128]{2,1,0:T(8,128)S(1)} %get-tuple-element.17), channel_id=1, source_target_pairs={{8,0},{16,8},{24,16},{9,1},{17,9},{25,17},{10,2},{18,10},{26,18},{... | collective-permute-start | bytes 798728 | tf_op jit(solution)/shard_map/ppermute | solution.py:420
  9.6 4.3 %inner_planes.1 = (f32[256,8,128]{2,1,0:T(8,128)S(1)}, f32[224,8,128]{2,1,0:T(8,128)S(1)}) custom-call(f32[2048,128]{1,0:T(8,128)} %bitcast.24, f32[2048,128]{1,0:T(8,128)S(1)} %get-tuple-element.18.t_ref), custom_call_target="tpu_custom_call" | custom-call | flops 20000000 | bytes 20000000 | tf_op jit(solution)/shard_map/inner_planes/pallas_call | solution.py:422
  13.9 0.0 collective-permute-done.before_ref
  13.9 4.1 %collective-permute-done.1.after_ref = f32[65,8,128]{2,1,0:T(8,128)S(1)} collective-permute-done((f32[65,8,128]{2,1,0:T(8,128)S(1)}, f32[65,8,128]{2,1,0:T(8,128)S(1)}, u32[]{:S(2)}, u32[]{:S(2)}) %collective-permute-start.1) | collective-permute-done | bytes 266272 | tf_op jit(solution)/shard_map/ppermute | solution.py:420
  18.0 1.6 %outer_planes.1 = (f32[256,8,128]{2,1,0:T(8,128)S(1)}, f32[4,6,8,128]{3,2,1,0:T(8,128)S(1)}) custom-call(s32[256]{0:T(256)} %probe_hbm.1, f32[65,8,128]{2,1,0:T(8,128)S(1)} %collective-permute-done.before_ref, f32[65,8,128]{2,1,0:T(8,128)S(1)} %collective-permute-done.1.after_ref, ...), custom_call_target="tpu_custom_call", output_to_operand_aliasing={{0}: (4, {})} | custom-call | tf_op jit(solution)/shard_map/outer_planes/pallas_call | solution.py:442
  19.6 9.5 %all_to_all.15.got_ref = f32[4,6,8,128]{3,2,1,0:T(8,128)S(1)} all-to-all(f32[4,6,8,128]{3,2,1,0:T(8,128)S(1)} %get-tuple-element.25), channel_id=1, replica_groups=mesh['space'=4,'ens'=8] {'space'}, dimensions={0} | all-to-all | bytes 196608 | tf_op jit(solution)/shard_map/all_to_all | solution.py:455
  29.1 3.7 %all-to-all-start = ((f32[8,32,8,128]{3,2,1,0:T(8,128)}), f32[8,32,8,128]{3,2,1,0:T(8,128)S(1)}, u32[]{:S(2)}, u32[]{:S(2)}) async-start(f32[8,32,8,128]{3,2,1,0:T(8,128)} %get-tuple-element.23), calls=%async_computation | async-start | bytes 2097152 | tf_op jit(solution)/shard_map/all_to_all | solution.py:421
  32.8 0.7 %spread.1 = f32[8,4,2,8,128]{4,3,2,1,0:T(8,128)} custom-call(s32[1]{0:T(128)} %bitcast.13.place_ref, f32[4,6,8,128]{3,2,1,0:T(8,128)S(1)} %all_to_all.15.got_ref), custom_call_target="tpu_custom_call" | custom-call | tf_op jit(solution)/shard_map/spread/pallas_call | solution.py:458
  33.5 14.7 %all-to-all-done.theta_hbm = f32[8,32,8,128]{3,2,1,0:T(8,128)S(1)} async-done(((f32[8,32,8,128]{3,2,1,0:T(8,128)}), f32[8,32,8,128]{3,2,1,0:T(8,128)S(1)}, u32[]{:S(2)}, u32[]{:S(2)}) %all-to-all-start) | async-done | bytes 1048608 | tf_op jit(solution)/shard_map/all_to_all | solution.py:421
  48.2 0.0 copy-start
  48.2 3.4 %all-to-all-start.2 = ((f32[8,4,2,8,128]{4,3,2,1,0:T(8,128)}), f32[8,4,2,8,128]{4,3,2,1,0:T(8,128)S(1)}, u32[]{:S(2)}, u32[]{:S(2)}) async-start(f32[8,4,2,8,128]{4,3,2,1,0:T(8,128)} %spread.1), calls=%async_computation.2 | async-start | bytes 524288 | tf_op jit(solution)/shard_map/all_to_all | solution.py:466
  52.3 0.0 copy-done
  52.3 2.9 %between.1 = (f32[2048,128]{1,0:T(8,128)}, bf16[32,128,128]{2,1,0:T(8,128)(2,1)}) custom-call(f32[256,8,128]{2,1,0:T(8,128)S(1)} %get-tuple-element.22.u2_ref, f32[8,32,8,128]{3,2,1,0:T(8,128)} %copy-done), custom_call_target="tpu_custom_call" | custom-call | flops 1000000 | bytes 8000000 | tf_op jit(solution)/shard_map/between/pallas_call | solution.py:467
  55.2 3.3 %all-to-all-done.2.pred_ref = f32[8,4,2,8,128]{4,3,2,1,0:T(8,128)S(1)} async-done(((f32[8,4,2,8,128]{4,3,2,1,0:T(8,128)}), f32[8,4,2,8,128]{4,3,2,1,0:T(8,128)S(1)}, u32[]{:S(2)}, u32[]{:S(2)}) %all-to-all-start.2) | async-done | bytes 262176 | tf_op jit(solution)/shard_map/all_to_all | solution.py:466
  58.5 3.4 %update.1 = (f32[2048,128]{1,0:T(8,128)}, f32[8,256]{1,0:T(8,128)}) custom-call(s32[1]{0:T(128)} %bitcast.13.place_ref, s32[1]{0:T(128)S(6)} %copy.16.count_ref, s32[1,32]{1,0:T(1,128)} %cells_hbm.3, s32[1,32]{1,0:T(1,128)} %probes_hbm.1, s32[1,32]{1,0:T(1,128)} %level_hbm.1, f32[8,4,2,8,128]{4,3,2,1,0:T(8,128)S(1)} %all-to-all-done.2.pred_ref, ...), custom_call_target="tpu_custom_call" | custom-call | tf_op jit(solution)/shard_map/update/pallas_call | solution.py:480
Async XLA Ops:
  3.3 10.6 %collective-permute-start = (f32[65,8,128]{2,1,0:T(8,128)S(1)}, f32[65,8,128]{2,1,0:T(8,128)S(1)}, u32[]{:S(2)}, u32[]{:S(2)}) collective-permute-start(f32[65,8,128]{2,1,0:T(8,128)S(1)} %get-tuple-element.16), channel_id=1, source_target_pairs={{0,8},{8,16},{16,24},{1,9},{9,17},{17,25},{2,10},{10,18},{18,26},{... | collective-permute-start | bytes 798728 | tf_op jit(solution)/shard_map/ppermute | solution.py:419
  8.3 9.7 %collective-permute-start.1 = (f32[65,8,128]{2,1,0:T(8,128)S(1)}, f32[65,8,128]{2,1,0:T(8,128)S(1)}, u32[]{:S(2)}, u32[]{:S(2)}) collective-permute-start(f32[65,8,128]{2,1,0:T(8,128)S(1)} %get-tuple-element.17), channel_id=1, source_target_pairs={{8,0},{16,8},{24,16},{9,1},{17,9},{25,17},{10,2},{18,10},{26,18},{... | collective-permute-start | bytes 798728 | tf_op jit(solution)/shard_map/ppermute | solution.py:420
  29.1 19.1 %all-to-all-start = ((f32[8,32,8,128]{3,2,1,0:T(8,128)}), f32[8,32,8,128]{3,2,1,0:T(8,128)S(1)}, u32[]{:S(2)}, u32[]{:S(2)}) async-start(f32[8,32,8,128]{3,2,1,0:T(8,128)} %get-tuple-element.23), calls=%async_computation | async-start | bytes 2097152 | tf_op jit(solution)/shard_map/all_to_all | solution.py:421
  48.2 4.1 %copy-start = (f32[8,32,8,128]{3,2,1,0:T(8,128)}, f32[8,32,8,128]{3,2,1,0:T(8,128)S(1)}, u32[]{:S(2)}) copy-start(f32[8,32,8,128]{3,2,1,0:T(8,128)S(1)} %all-to-all-done.theta_hbm) | copy-start | bytes 3145732
  48.2 10.3 %all-to-all-start.2 = ((f32[8,4,2,8,128]{4,3,2,1,0:T(8,128)}), f32[8,4,2,8,128]{4,3,2,1,0:T(8,128)S(1)}, u32[]{:S(2)}, u32[]{:S(2)}) async-start(f32[8,4,2,8,128]{4,3,2,1,0:T(8,128)} %spread.1), calls=%async_computation.2 | async-start | bytes 524288 | tf_op jit(solution)/shard_map/all_to_all | solution.py:466

commit v4 on v3

--- a/solution.py
+++ b/solution.py
@@ -90,6 +90,9 @@
         obs_ref[b] = noise_ref[:, b * LANES : (b + 1) * LANES]
     for at, row in enumerate(rows):
         obs_ref[blocks + at // ROWS, at % ROWS : at % ROWS + 1, :] = row
+    for ref in (low_ref, high_ref):
+        for at in range(obs_ref.shape[0]):
+            ref[4 * tiles + 1 + at] = obs_ref[at]
     for copy in picks:
         copy.wait()
 
@@ -208,7 +211,7 @@
             at += 1
 
 
-def outer_kernel(planes, tiles, probe_hbm, before_ref, after_ref, edge_ref, inner_ref, obs_ref,
+def outer_kernel(planes, tiles, probe_hbm, before_ref, after_ref, edge_ref, inner_ref,
                  u2_ref, sent_ref, probe_ref, sem):
     probe_copy = pltpu.make_async_copy(probe_hbm, probe_ref, sem)
     probe_copy.start()
@@ -240,25 +243,12 @@
             turned = pltpu.roll(u2_ref[cell >> 7], (p - cell) & (LANES - 1), 1)
             found = jnp.where(lane == p, turned, found)
 
-        observed = obs_ref[blocks, part : part + 1, :]
-        variance = obs_ref[blocks, blocks + part : blocks + part + 1, :]
-        scaled = (observed + obs_ref[part] - found) / variance
-        for slab in range(sent_ref.shape[0]):
-            sent_ref[slab, part] = found
-            sent_ref[slab, blocks + part] = scaled
-    for slab in range(sent_ref.shape[0]):
-        for at in range(blocks, obs_ref.shape[0]):
-            sent_ref[slab, blocks + at] = obs_ref[at]
-
-
-def spread_kernel(place_ref, got_ref, sent_ref):
-    slabs, (groups, windows, blocks) = got_ref.shape[0], sent_ref.shape[:3]
-    for window in range(windows):
-        at = window if windows == slabs else jnp.clip(place_ref[0] + window - 2, 0, slabs - 1)
-        for b in range(blocks):
-            value = got_ref[at, b]
-            for group in range(groups):
-                sent_ref[group, window, b] = value
+        def send(at, _):
+            for d in range(ROWS):
+                sent_ref[at * ROWS + d, part] = found
+            return 0
+
+        lax.fori_loop(0, sent_ref.shape[0] // ROWS, send, 0)
 
 
 def halves(value):
@@ -266,11 +256,16 @@
     return high, (value - high.astype(jnp.float32)).astype(jnp.bfloat16)
 
 
-def between_kernel(planes, tiles, u2_ref, theta_hbm, out_ref, split_ref, theta_ref, sem):
-    copy = pltpu.make_async_copy(theta_hbm, theta_ref, sem)
-    copy.start()
+def between_kernel(planes, tiles, place_ref, u2_ref, same_hbm, other_hbm, out_ref, split_ref, same_ref, other_ref, sems):
+    copies = [
+        pltpu.make_async_copy(same_hbm, same_ref, sems.at[0]),
+        pltpu.make_async_copy(other_hbm, other_ref, sems.at[1]),
+    ]
+    for copy in copies:
+        copy.start()
     stride = planes * tiles
-    members = theta_ref.shape[0] * ROWS
+    members = 2 * same_ref.shape[0] * ROWS
+    first_core = jnp.where(place_ref[2] == 0, 1.0, 0.0)
 
     def store(x, _):
         base = (x // ROWS) * tiles * ROWS + x % ROWS
@@ -279,10 +274,15 @@
         return 0
 
     lax.fori_loop(0, planes, store, 0)
-    copy.wait()
+    for copy in copies:
+        copy.wait()
 
     def split(slot, _):
-        high, low = halves(theta_ref[:, slot].reshape(members, LANES))
+        parts = []
+        for chip in range(same_ref.shape[0]):
+            same, other = same_ref[chip, slot], other_ref[chip, slot]
+            parts += [jnp.where(first_core > 0.5, same, other), jnp.where(first_core > 0.5, other, same)]
+        high, low = halves(jnp.concatenate(parts, axis=0))
         split_ref[slot, :members, :] = high
         split_ref[slot, members:, :] = low
         return 0
@@ -304,9 +304,9 @@
 
 
 def update_kernel(slabs, planes, tiles, place_ref, count_ref, cells_hbm, probes_hbm, level_hbm,
-                  pred_ref, got_ref, split_hbm, t_hbm, post_ref, gain_ref,
-                  reach, cells_ref, probes_ref, level_ref, split_ref, sems):
-    groups, windows, blocks = pred_ref.shape[:3]
+                  pred_ref, before_2_ref, before_ref, own_ref, after_ref, after_2_ref, split_hbm, t_hbm,
+                  post_ref, gain_ref, reach, cells_ref, probes_ref, level_ref, split_ref, sems):
+    groups, blocks = pred_ref.shape[0] // slabs, pred_ref.shape[1]
     members = groups * ROWS
     share = 1.0 / (members - 1)
     copies = [
@@ -317,22 +317,29 @@
     ]
     for copy in copies:
         copy.start()
-    slab = place_ref[0]
+    slab, group = place_ref[0], place_ref[1]
+    halo = 4 * tiles + 1
+    seen = ((before_2_ref, 0), (before_ref, halo), (own_ref, 0), (after_ref, halo), (after_2_ref, 0))
+
+    def extra(d, at):
+        ref, first = seen[d]
+        return ref[first + blocks + at // ROWS, at % ROWS : at % ROWS + 1, :]
 
     def wide(row):
         return row[:, :members] if members <= LANES else jnp.concatenate([row] * (members // LANES), axis=1)
 
-    anomaly, scaled, matches, places = [], [], [], []
+    anomaly, scaled, variance, matches = [], [], [], []
     for d in range(5):
         wanted = slab + d - 2
         at = jnp.clip(wanted, 0, slabs - 1)
         live = jnp.where((wanted >= 0) & (wanted < slabs), 1.0, 0.0)
-        places.append(at)
         for b in range(blocks):
-            predicted = pred_ref[:, at if windows == slabs else d, b].reshape(members, LANES)
+            predicted = pred_ref[pl.ds(at * groups, groups), b].reshape(members, LANES)
             mean = jnp.sum(predicted, axis=0, keepdims=True) / members
             anomaly.append(halves((predicted - mean) * live))
-            scaled.append(got_ref[at, blocks + b] * live)
+            variance.append(extra(d, blocks + b) + (1.0 - live))
+            noise = seen[d][0][seen[d][1] + b]
+            scaled.append((extra(d, b) + noise - pred_ref[at * groups + group, b]) / variance[-1] * live)
             left = stacked(scaled[-1])
             high, low = anomaly[-1]
             matches.append(fold(dot(left, high, 1) + dot(left, low, 1)))
@@ -340,15 +347,12 @@
         for i in range(blocks):
             total = jnp.zeros((ROWS, members), jnp.float32)
             for j in range(3 * blocks):
-                at = 2 * blocks + i * 3 * blocks + j
-                level = got_ref[places[d], 2 * blocks + at // ROWS, at % ROWS : at % ROWS + 1, :] / 256.0 * share
+                level = extra(d, 2 * blocks + i * 3 * blocks + j) / 256.0 * share
                 total = total + wide(level) * matches[(d - 1) * blocks + j]
             high, low = anomaly[d * blocks + i]
             left = stacked(total)
             correction = fold(dot(left, high, 0) + dot(left, low, 0))
-            at = blocks + i
-            variance = got_ref[places[d], 2 * blocks + at // ROWS, at % ROWS : at % ROWS + 1, :]
-            gain = scaled[d * blocks + i] - correction / variance
+            gain = scaled[d * blocks + i] - correction / variance[d * blocks + i]
             if d == 2:
                 gain_ref[:, i * LANES : (i + 1) * LANES] = gain
             left = stacked(gain)
@@ -383,12 +387,13 @@
     slots = pair_cells.shape[1]
     probes = obs_noise.shape[1]
     blocks = probes // LANES
-    slabs, groups = lax.axis_size("space"), lax.axis_size("ens")
+    slabs, chips = lax.axis_size("space"), lax.axis_size("chip")
+    groups = 2 * chips
     f32, i32 = jnp.float32, jnp.int32
     u_rows = to_rows(starting_speed_field)
     t_rows = to_rows(sample_fluidity_exponent)
     obs_tiles = blocks - (-(2 * blocks + probe_taper.shape[1] * probe_taper.shape[2]) // ROWS)
-    edge = jax.ShapeDtypeStruct((4 * tiles + 1, ROWS, LANES), f32)
+    edge = jax.ShapeDtypeStruct((4 * tiles + 1 + obs_tiles, ROWS, LANES), f32)
     obs_shape = jax.ShapeDtypeStruct((obs_tiles, ROWS, LANES), f32)
     params = pltpu.CompilerParams(vmem_limit_bytes=32 * 1024 * 1024)
     stack = pltpu.VMEM((planes * tiles, ROWS, LANES), f32)
@@ -399,7 +404,7 @@
             edge,
             obs_shape,
             jax.ShapeDtypeStruct(u_rows.shape, f32),
-            pltpu.HBM((groups, slots, ROWS, LANES), f32),
+            pltpu.HBM((chips, slots, ROWS, LANES), f32),
         ),
         in_specs=[HBM] * 7,
         out_specs=(VMEM,) * 4 + (HBM,),
@@ -410,7 +415,7 @@
             pltpu.VMEM((ROWS, probes), f32),
             pltpu.VMEM((2, probes), f32),
             pltpu.VMEM((slots, ROWS, LANES), f32),
-            pltpu.SemaphoreType.DMA((7 + groups,)),
+            pltpu.SemaphoreType.DMA((7 + chips,)),
         ],
         compiler_params=params,
         name="pack",
@@ -418,7 +423,14 @@
     upward = [(i, i + 1) for i in range(slabs - 1)]
     before = lax.ppermute(high, "space", upward)
     after = lax.ppermute(low, "space", [(j, i) for i, j in upward])
-    theta_all = lax.all_to_all(picked, "ens", 0, 0)
+    if slabs == 4:
+        before_2 = after_2 = lax.ppermute(obs, "space", [(i, (i + 2) % 4) for i in range(4)])
+    else:
+        upward_2 = [(i, i + 2) for i in range(slabs - 2)]
+        before_2 = lax.ppermute(obs, "space", upward_2)
+        after_2 = lax.ppermute(obs, "space", [(j, i) for i, j in upward_2])
+    theta_same = lax.all_to_all(picked, "chip", 0, 0)
+    theta_other = lax.ppermute(theta_same, "core", [(0, 1), (1, 0)])
     inner, edges = pl.pallas_call(
         functools.partial(inner_kernel, planes, tiles),
         out_shape=(
@@ -443,47 +455,38 @@
         functools.partial(outer_kernel, planes, tiles),
         out_shape=(
             jax.ShapeDtypeStruct((planes * tiles, ROWS, LANES), f32),
-            jax.ShapeDtypeStruct((slabs, blocks + obs_tiles, ROWS, LANES), f32),
+            jax.ShapeDtypeStruct((slabs * groups, blocks, ROWS, LANES), f32),
         ),
-        in_specs=[HBM] + [VMEM] * 5,
+        in_specs=[HBM] + [VMEM] * 4,
         out_specs=(VMEM,) * 2,
         scratch_shapes=[pltpu.SMEM(probe_cells.shape, i32), pltpu.SemaphoreType.DMA(())],
         input_output_aliases={4: 0},
         compiler_params=params,
         name="outer_planes",
-    )(stay(probe_cells), before, after, edges, inner, obs)
-    got = lax.all_to_all(sent, "space", 0, 0)
-    place = lax.axis_index("space").astype(i32).reshape(1)
-    windows = min(slabs, 5)
-    spread = pl.pallas_call(
-        spread_kernel,
-        out_shape=jax.ShapeDtypeStruct((groups, windows, blocks, ROWS, LANES), f32),
-        in_specs=[SMEM, VMEM],
-        out_specs=VMEM,
-        compiler_params=params,
-        name="spread",
-    )(place, got)
-    pred_all = lax.all_to_all(spread, "ens", 0, 0)
+    )(stay(probe_cells), before, after, edges, inner)
+    pred_all = lax.all_to_all(sent, ("space", "chip", "core"), 0, 0)
+    group = lax.axis_index(("chip", "core"))
+    place = jnp.stack([lax.axis_index("space"), group, lax.axis_index("core")]).astype(i32)
     u2_rows, split = pl.pallas_call(
         functools.partial(between_kernel, planes, tiles),
         out_shape=(
             jax.ShapeDtypeStruct(u_rows.shape, f32),
             pltpu.HBM((slots, 2 * groups * ROWS, LANES), jnp.bfloat16),
         ),
-        in_specs=[VMEM, HBM],
+        in_specs=[SMEM, VMEM, HBM, HBM],
         out_specs=(VMEM,) * 2,
-        scratch_shapes=[pltpu.VMEM(theta_all.shape, f32), pltpu.SemaphoreType.DMA(())],
+        scratch_shapes=[pltpu.VMEM(picked.shape, f32)] * 2 + [pltpu.SemaphoreType.DMA((2,))],
         compiler_params=params,
         cost_estimate=pl.CostEstimate(flops=1_000_000, bytes_accessed=8_000_000, transcendentals=0),
         name="between",
-    )(u2, stay(theta_all))
+    )(place, u2, stay(theta_same), stay(theta_other))
     post_rows, gain = pl.pallas_call(
         functools.partial(update_kernel, slabs, planes, tiles),
         out_shape=(
             jax.ShapeDtypeStruct(u_rows.shape, f32),
             jax.ShapeDtypeStruct((members, probes), f32),
         ),
-        in_specs=[SMEM] * 2 + [HBM] * 3 + [VMEM] * 2 + [HBM] * 2,
+        in_specs=[SMEM] * 2 + [HBM] * 3 + [VMEM] * 6 + [HBM] * 2,
         out_specs=(VMEM,) * 2,
         scratch_shapes=[
             pltpu.VMEM((probe_taper.shape[2], 2 * ROWS, 2 * groups * ROWS), jnp.bfloat16),
@@ -495,20 +498,23 @@
         ],
         compiler_params=params,
         name="update",
-    )(place, pair_counts, *map(stay, (pair_cells, pair_probes, pair_taper)), pred_all, got,
-      stay(split), stay(t_rows))
+    )(place, pair_counts, *map(stay, (pair_cells, pair_probes, pair_taper)), pred_all,
+      before_2, before, obs, after, after_2, stay(split), stay(t_rows))
     return (from_rows(u2_rows, shape), from_rows(post_rows, shape), gain)
 
 
 def solution(mesh):
+    slabs, groups = mesh.devices.shape
+    split = jax.sharding.Mesh(mesh.devices.reshape(slabs, groups // 2, 2), ("space", "chip", "core"))
+    members = ("chip", "core")
     return jax.shard_map(
         shards,
-        mesh=mesh,
+        mesh=split,
         in_specs=(
-            P("ens", "space", None),
-            P("ens", "space", None),
+            P(members, "space", None),
+            P(members, "space", None),
             P("space"),
-            P("ens", "space"),
+            P(members, "space"),
             P("space"),
             P("space"),
             P("space", None),
@@ -517,6 +523,6 @@
             P("space"),
             P("space", None, None),
         ),
-        out_specs=(P("ens", "space", None), P("ens", "space", None), P("ens", "space")),
+        out_specs=(P(members, "space", None), P(members, "space", None), P(members, "space")),
         check_vma=False,
     )

time: 62.4 us -> 45.1 us (0.72)
  waiting for transfers between devices: 22.2 us -> 8.57 us
  blocking collectives: 9.48 us -> 0 us
  starting transfers between devices: 13.4 us -> 18.1 us
  Pallas kernels: 15.6 us -> 16.6 us
    all_to_all x2, waiting for transfers between devices: 18 us -> 4.38 us  [the longest x1 3.31 us: shards(): theta_same = lax.all_to_all(picked, 'chip', 0, 0)]
    all_to_all x1 -> x0, blocking collectives: 9.48 us -> none  [shards(): got = lax.all_to_all(sent, 'space', 0, 0)]
    ppermute x0 -> x2, waiting for transfers between devices: none -> 3.18 us  [the longest x1 3.18 us: shards(): lax.ppermute(obs, 'space', [(i, (i + 2) % 4) for i in range(4)])]
    ppermute x1, waiting for transfers between devices: 4.13 us -> 1.01 us  [shards(): after = lax.ppermute(low, 'space', [(j, i) for i, j in upward])]
    all_to_all x2, starting transfers between devices: 7.13 us -> 10.1 us  [the longest x1 5.18 us: shards(): theta_same = lax.all_to_all(picked, 'chip', 0, 0)]
    ppermute x0 -> x2, starting transfers between devices: none -> 2.74 us  [the longest x1 2.74 us: shards(): lax.ppermute(obs, 'space', [(i, (i + 2) % 4) for i in range(4)])]
    ppermute x1, starting transfers between devices: 4.94 us -> 3.93 us  [shards(): before = lax.ppermute(high, 'space', upward)]
    pallas_call x1, Pallas kernels: 1.57 us -> 2.36 us  [shards(): pl.pallas_call(functools.partial(outer_kernel, planes, tiles), out_shape=...]
  transfers between devices with their start and end apart: 4 -> 6, of which waited for: 3 -> 4; matrix products, arithmetic and copies ran while one was open for 0% -> 0% of each run, Pallas kernels for 13% -> 23%
where the time goes in v4:
time: 45.1 us; the launch traced here: 44.7 us
  starting transfers between devices  18.1 us (40%)
  Pallas kernels  16.6 us (37%)
  waiting for transfers between devices  8.57 us (19%)
  between operations  1.36 us (3%)
    all_to_all x1, starting transfers between devices, shards(): theta_same = lax.all_to_all(picked, 'chip', 0, 0)  5.18 us
    all_to_all x1, starting transfers between devices, shards(): pred_all = lax.all_to_all(sent, ('space', 'chip', 'core'), 0, 0)  4.97 us
    pallas_call x1, Pallas kernels, shards(): pl.pallas_call(functools.partial(inner_kernel, planes, tiles), out_shape=...  4.46 us
    ppermute x1, starting transfers between devices, shards(): before = lax.ppermute(high, 'space', upward)  3.93 us
    pallas_call x1, Pallas kernels, shards(): pl.pallas_call(functools.partial(update_kernel, slabs, planes, tiles), ou...  3.87 us
    pallas_call x1, Pallas kernels, shards(): pl.pallas_call(functools.partial(between_kernel, planes, tiles), out_shap...  3.42 us
    all_to_all x1, waiting for transfers between devices, shards(): theta_same = lax.all_to_all(picked, 'chip', 0, 0)  3.31 us
    ppermute x1, waiting for transfers between devices, shards(): lax.ppermute(obs, 'space', [(i, (i + 2) % 4) for i in range(4)])  3.18 us
  transfers between devices with their start and end apart: 6, of which 4 were waited for; matrix products, arithmetic and copies ran while one was open for 0% of the time, Pallas kernels for 23%

profile of v4, /device:TPU:0, one launch (start us, length us, event | category | flops | bytes accessed | tf_op | source)
XLA Modules:
  0.0 44.7 jit_solution(209538058014781228)
XLA Ops:
  0.6 2.5 %pack.1 = (f32[69,8,128]{2,1,0:T(8,128)S(1)}, f32[69,8,128]{2,1,0:T(8,128)S(1)}, f32[4,8,128]{2,1,0:T(8,128)S(1)}, f32[2048,128]{1,0:T(8,128)S(1)}, f32[4,32,8,128]{3,2,1,0:T(8,128)}) custom-call(s32[1,32]{1,0:T(1,128)} %cells_hbm.3, s32[1,2,6]{2,1,0:T(2,128)} %taper_hbm.1, f32[2048,128]{1,0:T(8,128)} %bitcast.25, f32[2048,128]{1,0:T(8,128)} %bitcast.27, ...), custom_call_target="tpu_custom_call" | custom-call | tf_op jit(solution)/shard_map/pack/pallas_call | solution.py:400
  3.1 5.2 %all-to-all-start = ((f32[4,32,8,128]{3,2,1,0:T(8,128)}), f32[4,32,8,128]{3,2,1,0:T(8,128)}, u32[]{:S(2)}, u32[]{:S(2)}) async-start(f32[4,32,8,128]{3,2,1,0:T(8,128)} %get-tuple-element.22), calls=%async_computation | async-start | bytes 1048576 | tf_op jit(solution)/shard_map/all_to_all | solution.py:432
  8.3 3.9 %collective-permute-start = (f32[69,8,128]{2,1,0:T(8,128)S(1)}, f32[69,8,128]{2,1,0:T(8,128)S(1)}, u32[]{:S(2)}, u32[]{:S(2)}) collective-permute-start(f32[69,8,128]{2,1,0:T(8,128)S(1)} %get-tuple-element.16), channel_id=1, source_target_pairs={{0,8},{8,16},{16,24},{1,9},{9,17},{17,25},{2,10},{10,18},{18,26},{... | collective-permute-start | bytes 847880 | tf_op jit(solution)/shard_map/ppermute | solution.py:424
  12.2 1.3 %collective-permute-start.1 = (f32[69,8,128]{2,1,0:T(8,128)S(1)}, f32[69,8,128]{2,1,0:T(8,128)S(1)}, u32[]{:S(2)}, u32[]{:S(2)}) collective-permute-start(f32[69,8,128]{2,1,0:T(8,128)S(1)} %get-tuple-element.17), channel_id=1, source_target_pairs={{8,0},{16,8},{24,16},{9,1},{17,9},{25,17},{10,2},{18,10},{26,18},{... | collective-permute-start | bytes 847880 | tf_op jit(solution)/shard_map/ppermute | solution.py:425
  13.5 3.3 %all-to-all-done.same_hbm = f32[4,32,8,128]{3,2,1,0:T(8,128)} async-done(((f32[4,32,8,128]{3,2,1,0:T(8,128)}), f32[4,32,8,128]{3,2,1,0:T(8,128)}, u32[]{:S(2)}, u32[]{:S(2)}) %all-to-all-start) | async-done | bytes 524320 | tf_op jit(solution)/shard_map/all_to_all | solution.py:432
  16.8 0.0 collective-permute-start.2
  16.8 4.5 %inner_planes.1 = (f32[256,8,128]{2,1,0:T(8,128)S(1)}, f32[224,8,128]{2,1,0:T(8,128)S(1)}) custom-call(f32[2048,128]{1,0:T(8,128)} %bitcast.26, f32[2048,128]{1,0:T(8,128)S(1)} %get-tuple-element.18.t_ref), custom_call_target="tpu_custom_call" | custom-call | flops 20000000 | bytes 20000000 | tf_op jit(solution)/shard_map/inner_planes/pallas_call | solution.py:434
  21.3 0.0 collective-permute-done.before_ref
  21.3 1.0 %collective-permute-done.1.after_ref = f32[69,8,128]{2,1,0:T(8,128)S(1)} collective-permute-done((f32[69,8,128]{2,1,0:T(8,128)S(1)}, f32[69,8,128]{2,1,0:T(8,128)S(1)}, u32[]{:S(2)}, u32[]{:S(2)}) %collective-permute-start.1) | collective-permute-done | bytes 282656 | tf_op jit(solution)/shard_map/ppermute | solution.py:425
  22.3 2.4 %outer_planes.1 = (f32[256,8,128]{2,1,0:T(8,128)S(1)}, f32[32,2,8,128]{3,2,1,0:T(8,128)}) custom-call(s32[256]{0:T(256)} %probe_hbm.1, f32[69,8,128]{2,1,0:T(8,128)S(1)} %collective-permute-done.before_ref, f32[69,8,128]{2,1,0:T(8,128)S(1)} %collective-permute-done.1.after_ref, ...), custom_call_target="tpu_custom_call", output_to_operand_aliasing={{0}: (4, {})} | custom-call | tf_op jit(solution)/shard_map/outer_planes/pallas_call | solution.py:454
  24.7 5.0 %all-to-all-start.1 = ((f32[32,2,8,128]{3,2,1,0:T(8,128)}), f32[32,2,8,128]{3,2,1,0:T(8,128)S(1)}, u32[]{:S(2)}, u32[]{:S(2)}) async-start(f32[32,2,8,128]{3,2,1,0:T(8,128)} %get-tuple-element.24), calls=%async_computation.1 | async-start | bytes 524288 | tf_op jit(solution)/shard_map/all_to_all | solution.py:467
  29.7 2.7 %collective-permute-start.3 = (f32[4,8,128]{2,1,0:T(8,128)S(1)}, f32[4,8,128]{2,1,0:T(8,128)S(1)}, u32[]{:S(2)}, u32[]{:S(2)}) collective-permute-start(f32[4,8,128]{2,1,0:T(8,128)S(1)} %get-tuple-element.25.own_ref), channel_id=1, source_target_pairs={{0,16},{8,24},{16,0},{24,8},{1,17},{9,25},{17,1},{25,9},{2,18},{10... | collective-permute-start | bytes 49160 | tf_op jit(solution)/shard_map/ppermute | solution.py:427
  32.4 0.1 pad_add_fusion.place_ref
  33.1 0.0 collective-permute-done.2.other_hbm
  33.1 3.4 %between.1 = (f32[2048,128]{1,0:T(8,128)}, bf16[32,128,128]{2,1,0:T(8,128)(2,1)}) custom-call(s32[3]{0:T(128)S(1)} %pad_add_fusion.place_ref, f32[256,8,128]{2,1,0:T(8,128)S(1)} %get-tuple-element.21.u2_ref, f32[4,32,8,128]{3,2,1,0:T(8,128)} %all-to-all-done.same_hbm, f32[4,32,8,128]{3,2,1,0:T(8,128)} %collective-permute-done.2.other_hbm), custom_call_target="tpu_custom_call" | custom-call | flops 1000000 | bytes 8000000 | tf_op jit(solution)/shard_map/between/pallas_call | solution.py:470
  36.6 3.2 %collective-permute-done.3.before_2_ref.after_2_ref = f32[4,8,128]{2,1,0:T(8,128)S(1)} collective-permute-done((f32[4,8,128]{2,1,0:T(8,128)S(1)}, f32[4,8,128]{2,1,0:T(8,128)S(1)}, u32[]{:S(2)}, u32[]{:S(2)}) %collective-permute-start.3) | collective-permute-done | bytes 16416 | tf_op jit(solution)/shard_map/ppermute | solution.py:427
  39.7 1.1 %all-to-all-done.1.pred_ref = f32[32,2,8,128]{3,2,1,0:T(8,128)S(1)} async-done(((f32[32,2,8,128]{3,2,1,0:T(8,128)}), f32[32,2,8,128]{3,2,1,0:T(8,128)S(1)}, u32[]{:S(2)}, u32[]{:S(2)}) %all-to-all-start.1) | async-done | bytes 262176 | tf_op jit(solution)/shard_map/all_to_all | solution.py:467
  40.8 3.9 %update.1 = (f32[2048,128]{1,0:T(8,128)}, f32[8,256]{1,0:T(8,128)}) custom-call(s32[3]{0:T(128)S(1)} %pad_add_fusion.place_ref, s32[1]{0:T(128)S(6)} %copy.16.count_ref, s32[1,32]{1,0:T(1,128)} %cells_hbm.3, s32[1,32]{1,0:T(1,128)} %probes_hbm.1, s32[1,32]{1,0:T(1,128)} %level_hbm.1, f32[32,2,8,128]{3,2,1,0:T(8,128)S(1)} %all-to-all-done.1.pred_ref, ...), custom_call_target="tpu_custom_call" | custom-call | tf_op jit(solution)/shard_map/update/pallas_call | solution.py:483
Async XLA Ops:
  3.1 13.7 %all-to-all-start = ((f32[4,32,8,128]{3,2,1,0:T(8,128)}), f32[4,32,8,128]{3,2,1,0:T(8,128)}, u32[]{:S(2)}, u32[]{:S(2)}) async-start(f32[4,32,8,128]{3,2,1,0:T(8,128)} %get-tuple-element.22), calls=%async_computation | async-start | bytes 1048576 | tf_op jit(solution)/shard_map/all_to_all | solution.py:432
  8.3 13.0 %collective-permute-start = (f32[69,8,128]{2,1,0:T(8,128)S(1)}, f32[69,8,128]{2,1,0:T(8,128)S(1)}, u32[]{:S(2)}, u32[]{:S(2)}) collective-permute-start(f32[69,8,128]{2,1,0:T(8,128)S(1)} %get-tuple-element.16), channel_id=1, source_target_pairs={{0,8},{8,16},{16,24},{1,9},{9,17},{17,25},{2,10},{10,18},{18,26},{... | collective-permute-start | bytes 847880 | tf_op jit(solution)/shard_map/ppermute | solution.py:424
  12.2 10.1 %collective-permute-start.1 = (f32[69,8,128]{2,1,0:T(8,128)S(1)}, f32[69,8,128]{2,1,0:T(8,128)S(1)}, u32[]{:S(2)}, u32[]{:S(2)}) collective-permute-start(f32[69,8,128]{2,1,0:T(8,128)S(1)} %get-tuple-element.17), channel_id=1, source_target_pairs={{8,0},{16,8},{24,16},{9,1},{17,9},{25,17},{10,2},{18,10},{26,18},{... | collective-permute-start | bytes 847880 | tf_op jit(solution)/shard_map/ppermute | solution.py:425
  16.8 16.3 %collective-permute-start.2 = (f32[4,32,8,128]{3,2,1,0:T(8,128)}, f32[4,32,8,128]{3,2,1,0:T(8,128)}, u32[]{:S(2)}, u32[]{:S(2)}) collective-permute-start(f32[4,32,8,128]{3,2,1,0:T(8,128)} %all-to-all-done.same_hbm), channel_id=1, source_target_pairs={{0,1},{1,0},{2,3},{3,2},{4,5},{5,4},{6,7},{7,6},{8,9},{9,8},{10,11... | collective-permute-start | bytes 1572872 | tf_op jit(solution)/shard_map/ppermute | solution.py:433
  24.7 16.1 %all-to-all-start.1 = ((f32[32,2,8,128]{3,2,1,0:T(8,128)}), f32[32,2,8,128]{3,2,1,0:T(8,128)S(1)}, u32[]{:S(2)}, u32[]{:S(2)}) async-start(f32[32,2,8,128]{3,2,1,0:T(8,128)} %get-tuple-element.24), calls=%async_computation.1 | async-start | bytes 524288 | tf_op jit(solution)/shard_map/all_to_all | solution.py:467
  29.7 10.1 %collective-permute-start.3 = (f32[4,8,128]{2,1,0:T(8,128)S(1)}, f32[4,8,128]{2,1,0:T(8,128)S(1)}, u32[]{:S(2)}, u32[]{:S(2)}) collective-permute-start(f32[4,8,128]{2,1,0:T(8,128)S(1)} %get-tuple-element.25.own_ref), channel_id=1, source_target_pairs={{0,16},{8,24},{16,0},{24,8},{1,17},{9,25},{17,1},{25,9},{2,18},{10... | collective-permute-start | bytes 49160 | tf_op jit(solution)/shard_map/ppermute | solution.py:427

commit v5 on v4

--- a/solution.py
+++ b/solution.py
@@ -211,8 +211,8 @@
             at += 1
 
 
-def outer_kernel(planes, tiles, probe_hbm, before_ref, after_ref, edge_ref, inner_ref,
-                 u2_ref, sent_ref, probe_ref, sem):
+def outer_kernel(planes, tiles, probe_hbm, before_ref, after_ref, edge_ref, inner_ref, same_in,
+                 u2_ref, sent_ref, same_out, probe_ref, sem):
     probe_copy = pltpu.make_async_copy(probe_hbm, probe_ref, sem)
     probe_copy.start()
     masks = lane_masks()
@@ -256,38 +256,32 @@
     return high, (value - high.astype(jnp.float32)).astype(jnp.bfloat16)
 
 
-def between_kernel(planes, tiles, place_ref, u2_ref, same_hbm, other_hbm, out_ref, split_ref, same_ref, other_ref, sems):
+def between_kernel(planes, tiles, u2_ref, same_hbm, other_hbm, out_ref, split_ref, theta_ref, sems):
+    chips = same_hbm.shape[0]
     copies = [
-        pltpu.make_async_copy(same_hbm, same_ref, sems.at[0]),
-        pltpu.make_async_copy(other_hbm, other_ref, sems.at[1]),
+        pltpu.make_async_copy(same_hbm, theta_ref.at[pl.ds(0, chips)], sems.at[0]),
+        pltpu.make_async_copy(other_hbm, theta_ref.at[pl.ds(chips, chips)], sems.at[1]),
     ]
     for copy in copies:
         copy.start()
     stride = planes * tiles
-    members = 2 * same_ref.shape[0] * ROWS
-    first_core = jnp.where(place_ref[2] == 0, 1.0, 0.0)
-
-    def store(x, _):
-        base = (x // ROWS) * tiles * ROWS + x % ROWS
+    members = theta_ref.shape[0] * ROWS
+
+    def store(x):
         for tile in range(tiles):
-            out_ref[pl.ds(base + tile * ROWS, ROWS, stride=stride), :] = u2_ref[x * tiles + tile]
-        return 0
-
-    lax.fori_loop(0, planes, store, 0)
+            rows = pl.ds((x // ROWS) * tiles * ROWS + x % ROWS + tile * ROWS, ROWS, stride=stride)
+            out_ref[rows, :] = u2_ref[x * tiles + tile]
+
+    each(0, planes, 4, store)
     for copy in copies:
         copy.wait()
 
-    def split(slot, _):
-        parts = []
-        for chip in range(same_ref.shape[0]):
-            same, other = same_ref[chip, slot], other_ref[chip, slot]
-            parts += [jnp.where(first_core > 0.5, same, other), jnp.where(first_core > 0.5, other, same)]
-        high, low = halves(jnp.concatenate(parts, axis=0))
+    def split(slot):
+        high, low = halves(theta_ref[:, slot].reshape(members, LANES))
         split_ref[slot, :members, :] = high
         split_ref[slot, members:, :] = low
-        return 0
-
-    lax.fori_loop(0, split_ref.shape[0], split, 0)
+
+    each(0, split_ref.shape[0], 4, split)
 
 
 def stacked(value):
@@ -304,10 +298,10 @@
 
 
 def update_kernel(slabs, planes, tiles, place_ref, count_ref, cells_hbm, probes_hbm, level_hbm,
-                  pred_ref, before_2_ref, before_ref, own_ref, after_ref, after_2_ref, split_hbm, t_hbm,
+                  near_ref, far_ref, before_2_ref, before_ref, own_ref, after_ref, after_2_ref, split_hbm, t_hbm,
                   post_ref, gain_ref, reach, cells_ref, probes_ref, level_ref, split_ref, sems):
-    groups, blocks = pred_ref.shape[0] // slabs, pred_ref.shape[1]
-    members = groups * ROWS
+    chips, blocks = near_ref.shape[0] // slabs, near_ref.shape[1]
+    members = 2 * chips * ROWS
     share = 1.0 / (members - 1)
     copies = [
         pltpu.make_async_copy(source, target, sems.at[at])
@@ -317,7 +311,7 @@
     ]
     for copy in copies:
         copy.start()
-    slab, group = place_ref[0], place_ref[1]
+    slab, chip = place_ref[0], place_ref[1]
     halo = 4 * tiles + 1
     seen = ((before_2_ref, 0), (before_ref, halo), (own_ref, 0), (after_ref, halo), (after_2_ref, 0))
 
@@ -334,12 +328,14 @@
         at = jnp.clip(wanted, 0, slabs - 1)
         live = jnp.where((wanted >= 0) & (wanted < slabs), 1.0, 0.0)
         for b in range(blocks):
-            predicted = pred_ref[pl.ds(at * groups, groups), b].reshape(members, LANES)
+            predicted = jnp.concatenate(
+                [ref[pl.ds(at * chips, chips), b].reshape(members // 2, LANES) for ref in (near_ref, far_ref)], axis=0
+            )
             mean = jnp.sum(predicted, axis=0, keepdims=True) / members
             anomaly.append(halves((predicted - mean) * live))
             variance.append(extra(d, blocks + b) + (1.0 - live))
             noise = seen[d][0][seen[d][1] + b]
-            scaled.append((extra(d, b) + noise - pred_ref[at * groups + group, b]) / variance[-1] * live)
+            scaled.append((extra(d, b) + noise - near_ref[at * chips + chip, b]) / variance[-1] * live)
             left = stacked(scaled[-1])
             high, low = anomaly[-1]
             matches.append(fold(dot(left, high, 1) + dot(left, low, 1)))
@@ -430,7 +426,6 @@
         before_2 = lax.ppermute(obs, "space", upward_2)
         after_2 = lax.ppermute(obs, "space", [(j, i) for i, j in upward_2])
     theta_same = lax.all_to_all(picked, "chip", 0, 0)
-    theta_other = lax.ppermute(theta_same, "core", [(0, 1), (1, 0)])
     inner, edges = pl.pallas_call(
         functools.partial(inner_kernel, planes, tiles),
         out_shape=(
@@ -448,45 +443,49 @@
             pltpu.SemaphoreType.DMA(()),
         ],
         compiler_params=params,
-        cost_estimate=pl.CostEstimate(flops=20_000_000, bytes_accessed=20_000_000, transcendentals=0),
+        cost_estimate=pl.CostEstimate(flops=0, bytes_accessed=15_000_000, transcendentals=0),
         name="inner_planes",
     )(stay(u_rows), t_near)
-    u2, sent = pl.pallas_call(
+    u2, sent, theta_same = pl.pallas_call(
         functools.partial(outer_kernel, planes, tiles),
         out_shape=(
             jax.ShapeDtypeStruct((planes * tiles, ROWS, LANES), f32),
-            jax.ShapeDtypeStruct((slabs * groups, blocks, ROWS, LANES), f32),
+            jax.ShapeDtypeStruct((slabs * chips, blocks, ROWS, LANES), f32),
+            pltpu.HBM(picked.shape, f32),
         ),
-        in_specs=[HBM] + [VMEM] * 4,
-        out_specs=(VMEM,) * 2,
+        in_specs=[HBM] + [VMEM] * 4 + [HBM],
+        out_specs=(VMEM, VMEM, HBM),
         scratch_shapes=[pltpu.SMEM(probe_cells.shape, i32), pltpu.SemaphoreType.DMA(())],
-        input_output_aliases={4: 0},
+        input_output_aliases={4: 0, 5: 2},
         compiler_params=params,
+        cost_estimate=pl.CostEstimate(flops=0, bytes_accessed=26_000_000, transcendentals=0),
         name="outer_planes",
-    )(stay(probe_cells), before, after, edges, inner)
-    pred_all = lax.all_to_all(sent, ("space", "chip", "core"), 0, 0)
-    group = lax.axis_index(("chip", "core"))
-    place = jnp.stack([lax.axis_index("space"), group, lax.axis_index("core")]).astype(i32)
+    )(stay(probe_cells), before, after, edges, inner, stay(theta_same))
+    pred_near = lax.all_to_all(sent, ("space", "chip"), 0, 0)
+    swap = [(0, 1), (1, 0)]
+    theta_other = lax.ppermute(theta_same, "core", swap)
+    pred_far = lax.ppermute(pred_near, "core", swap)
+    place = jnp.stack([lax.axis_index("space"), lax.axis_index("chip")]).astype(i32)
     u2_rows, split = pl.pallas_call(
         functools.partial(between_kernel, planes, tiles),
         out_shape=(
             jax.ShapeDtypeStruct(u_rows.shape, f32),
             pltpu.HBM((slots, 2 * groups * ROWS, LANES), jnp.bfloat16),
         ),
-        in_specs=[SMEM, VMEM, HBM, HBM],
+        in_specs=[VMEM, HBM, HBM],
         out_specs=(VMEM,) * 2,
-        scratch_shapes=[pltpu.VMEM(picked.shape, f32)] * 2 + [pltpu.SemaphoreType.DMA((2,))],
+        scratch_shapes=[pltpu.VMEM((groups, slots, ROWS, LANES), f32), pltpu.SemaphoreType.DMA((2,))],
         compiler_params=params,
         cost_estimate=pl.CostEstimate(flops=1_000_000, bytes_accessed=8_000_000, transcendentals=0),
         name="between",
-    )(place, u2, stay(theta_same), stay(theta_other))
+    )(u2, stay(theta_same), stay(theta_other))
     post_rows, gain = pl.pallas_call(
         functools.partial(update_kernel, slabs, planes, tiles),
         out_shape=(
             jax.ShapeDtypeStruct(u_rows.shape, f32),
             jax.ShapeDtypeStruct((members, probes), f32),
         ),
-        in_specs=[SMEM] * 2 + [HBM] * 3 + [VMEM] * 6 + [HBM] * 2,
+        in_specs=[SMEM] * 2 + [HBM] * 3 + [VMEM] * 7 + [HBM] * 2,
         out_specs=(VMEM,) * 2,
         scratch_shapes=[
             pltpu.VMEM((probe_taper.shape[2], 2 * ROWS, 2 * groups * ROWS), jnp.bfloat16),
@@ -498,7 +497,7 @@
         ],
         compiler_params=params,
         name="update",
-    )(place, pair_counts, *map(stay, (pair_cells, pair_probes, pair_taper)), pred_all,
+    )(place, pair_counts, *map(stay, (pair_cells, pair_probes, pair_taper)), pred_near, pred_far,
       before_2, before, obs, after, after_2, stay(split), stay(t_rows))
     return (from_rows(u2_rows, shape), from_rows(post_rows, shape), gain)
 

time: 45.1 us -> 48.5 us (1.075)
  blocking collectives: 0 us -> 13.9 us
  starting transfers between devices: 18.1 us -> 11.4 us
  waiting for transfers between devices: 8.57 us -> 3.59 us
  local copies, waits for them, and re-layouts: 0 us -> 2.89 us
  Pallas kernels: 16.6 us -> 14.9 us
    all_to_all x0 -> x1, blocking collectives: none -> 13.9 us  [shards(): pred_near = lax.all_to_all(sent, ('space', 'chip'), 0, 0)]
    all_to_all x1 -> x0, starting transfers between devices: 4.97 us -> none  [shards(): pred_all = lax.all_to_all(sent, ('space', 'chip', 'core'), 0, 0)]
    all_to_all x1, waiting for transfers between devices: 3.31 us -> 0.01 us  [shards(): theta_same = lax.all_to_all(picked, 'chip', 0, 0)]
    ppermute x1, waiting for transfers between devices: 3.18 us -> 0.01 us  [shards(): lax.ppermute(obs, 'space', [(i, (i + 2) % 4) for i in range(4)])]
    unnamed x0 -> x6, local copies, waits for them, and re-layouts: none -> 2.89 us
    ppermute x1, waiting for transfers between devices: 1.01 us -> 3.58 us  [shards(): after = lax.ppermute(low, 'space', [(j, i) for i, j in upward])]
    ppermute x1, starting transfers between devices: 2.74 us -> 0.91 us  [shards(): lax.ppermute(obs, 'space', [(i, (i + 2) % 4) for i in range(4)])]
    all_to_all x1 -> x0, waiting for transfers between devices: 1.07 us -> none  [shards(): pred_all = lax.all_to_all(sent, ('space', 'chip', 'core'), 0, 0)]
  transfers between devices with their start and end apart: 6 -> 6, of which waited for: 4 -> 1; matrix products, arithmetic and copies ran while one was open for 0% -> 0% of each run, Pallas kernels for 23% -> 14%
where the time goes in v5:
time: 48.5 us; the launch traced here: 48.1 us
  Pallas kernels  14.9 us (31%)
  blocking collectives  13.9 us (29%)
  starting transfers between devices  11.4 us (24%)
  waiting for transfers between devices  3.59 us (7%)
  local copies, waits for them, and re-layouts  2.89 us (6%)
  between operations  1.38 us (3%)
    all_to_all x1, blocking collectives, shards(): pred_near = lax.all_to_all(sent, ('space', 'chip'), 0, 0)  13.9 us
    all_to_all x1, starting transfers between devices, shards(): theta_same = lax.all_to_all(picked, 'chip', 0, 0)  5.18 us
    pallas_call x1, Pallas kernels, shards(): pl.pallas_call(functools.partial(inner_kernel, planes, tiles), out_shape=...  4.28 us
    ppermute x1, starting transfers between devices, shards(): before = lax.ppermute(high, 'space', upward)  3.93 us
    pallas_call x1, Pallas kernels, shards(): pl.pallas_call(functools.partial(update_kernel, slabs, planes, tiles), ou...  3.88 us
    ppermute x1, waiting for transfers between devices, shards(): after = lax.ppermute(low, 'space', [(j, i) for i, j in upward])  3.58 us
    unnamed x6, local copies, waits for them, and re-layouts  2.89 us
    pallas_call x1, Pallas kernels, shards(): pl.pallas_call(functools.partial(between_kernel, planes, tiles), out_shap...  2.68 us
  transfers between devices with their start and end apart: 6, of which 1 were waited for; matrix products, arithmetic and copies ran while one was open for 0% of the time, Pallas kernels for 14%

profile of v5, /device:TPU:0, one launch (start us, length us, event | category | flops | bytes accessed | tf_op | source)
XLA Modules:
  0.0 48.1 jit_solution(16970921929968292466)
XLA Ops:
  0.6 2.5 %pack.1 = (f32[69,8,128]{2,1,0:T(8,128)S(1)}, f32[69,8,128]{2,1,0:T(8,128)S(1)}, f32[4,8,128]{2,1,0:T(8,128)S(1)}, f32[2048,128]{1,0:T(8,128)S(1)}, f32[4,32,8,128]{3,2,1,0:T(8,128)}) custom-call(s32[1,32]{1,0:T(1,128)} %cells_hbm.3, s32[1,2,6]{2,1,0:T(2,128)} %taper_hbm.1, f32[2048,128]{1,0:T(8,128)} %bitcast.24, f32[2048,128]{1,0:T(8,128)} %bitcast.26, ...), custom_call_target="tpu_custom_call" | custom-call | tf_op jit(solution)/shard_map/pack/pallas_call | solution.py:396
  3.1 5.2 %all-to-all-start = ((f32[4,32,8,128]{3,2,1,0:T(8,128)}), f32[4,32,8,128]{3,2,1,0:T(8,128)}, u32[]{:S(2)}, u32[]{:S(2)}) async-start(f32[4,32,8,128]{3,2,1,0:T(8,128)} %get-tuple-element.22), calls=%async_computation | async-start | bytes 1048576 | tf_op jit(solution)/shard_map/all_to_all | solution.py:428
  8.3 3.9 %collective-permute-start = (f32[69,8,128]{2,1,0:T(8,128)S(1)}, f32[69,8,128]{2,1,0:T(8,128)S(1)}, u32[]{:S(2)}, u32[]{:S(2)}) collective-permute-start(f32[69,8,128]{2,1,0:T(8,128)S(1)} %get-tuple-element.17), channel_id=1, source_target_pairs={{0,8},{8,16},{16,24},{1,9},{9,17},{17,25},{2,10},{10,18},{18,26},{... | collective-permute-start | bytes 847880 | tf_op jit(solution)/shard_map/ppermute | solution.py:420
  12.2 1.3 %collective-permute-start.1 = (f32[69,8,128]{2,1,0:T(8,128)S(1)}, f32[69,8,128]{2,1,0:T(8,128)S(1)}, u32[]{:S(2)}, u32[]{:S(2)}) collective-permute-start(f32[69,8,128]{2,1,0:T(8,128)S(1)} %get-tuple-element.18), channel_id=1, source_target_pairs={{8,0},{16,8},{24,16},{9,1},{17,9},{25,17},{10,2},{18,10},{26,18},{... | collective-permute-start | bytes 847880 | tf_op jit(solution)/shard_map/ppermute | solution.py:421
  13.5 4.3 %inner_planes.1 = (f32[256,8,128]{2,1,0:T(8,128)S(1)}, f32[224,8,128]{2,1,0:T(8,128)S(1)}) custom-call(f32[2048,128]{1,0:T(8,128)} %bitcast.25, f32[2048,128]{1,0:T(8,128)S(1)} %get-tuple-element.19.t_ref), custom_call_target="tpu_custom_call" | custom-call | bytes 15000000 | tf_op jit(solution)/shard_map/inner_planes/pallas_call | solution.py:429
  17.8 0.0 copy-start
  17.8 0.9 %copy-done = f32[224,8,128]{2,1,0:T(8,128)} copy-done((f32[224,8,128]{2,1,0:T(8,128)}, f32[224,8,128]{2,1,0:T(8,128)S(1)}, u32[]{:S(2)}) %copy-start) | copy-done | bytes 917528
  18.7 0.0 collective-permute-done.before_ref
  18.8 3.6 %collective-permute-done.1.after_ref = f32[69,8,128]{2,1,0:T(8,128)S(1)} collective-permute-done((f32[69,8,128]{2,1,0:T(8,128)S(1)}, f32[69,8,128]{2,1,0:T(8,128)S(1)}, u32[]{:S(2)}, u32[]{:S(2)}) %collective-permute-start.1) | collective-permute-done | bytes 282656 | tf_op jit(solution)/shard_map/ppermute | solution.py:421
  22.3 0.0 all-to-all-done.same_in
  22.3 0.0 copy-start.1
  22.3 1.2 %copy-done.1 = f32[224,8,128]{2,1,0:T(8,128)S(1)} copy-done((f32[224,8,128]{2,1,0:T(8,128)S(1)}, f32[224,8,128]{2,1,0:T(8,128)}, u32[]{:S(2)}) %copy-start.1) | copy-done | bytes 917528
  23.5 1.6 %outer_planes.1 = (f32[256,8,128]{2,1,0:T(8,128)S(1)}, f32[16,2,8,128]{3,2,1,0:T(8,128)S(1)}, f32[4,32,8,128]{3,2,1,0:T(8,128)}) custom-call(s32[256]{0:T(256)} %probe_hbm.1, f32[69,8,128]{2,1,0:T(8,128)S(1)} %collective-permute-done.before_ref, f32[69,8,128]{2,1,0:T(8,128)S(1)} %collective-permute-done.1.after_ref, ...), custom_call_target="tpu_custom_call", output_to_operand_aliasing={{0}: (4, {}), {2}: (5, {})} | custom-call | bytes 26000000 | tf_op jit(solution)/shard_map/outer_planes/pallas_call | solution.py:449
  25.1 0.1 collective-permute-start.2
  25.2 13.9 %all_to_all.10.near_ref = f32[16,2,8,128]{3,2,1,0:T(8,128)S(1)} all-to-all(f32[16,2,8,128]{3,2,1,0:T(8,128)S(1)} %get-tuple-element.26), channel_id=1, replica_groups=mesh['space'=4,'chip'=4,'core'=2] {'space','chip'}, dimensions={0} | all-to-all | bytes 262144 | tf_op jit(solution)/shard_map/all_to_all | solution.py:464
  39.0 0.0 collective-permute-start.3
  39.0 0.9 %collective-permute-start.4 = (f32[4,8,128]{2,1,0:T(8,128)S(1)}, f32[4,8,128]{2,1,0:T(8,128)S(1)}, u32[]{:S(2)}, u32[]{:S(2)}) collective-permute-start(f32[4,8,128]{2,1,0:T(8,128)S(1)} %get-tuple-element.27.own_ref), channel_id=1, source_target_pairs={{0,16},{8,24},{16,0},{24,8},{1,17},{9,25},{17,1},{25,9},{2,18},{10... | collective-permute-start | bytes 49160 | tf_op jit(solution)/shard_map/ppermute | solution.py:423
  40.0 0.1 pad_add_fusion.place_ref
  40.7 0.0 collective-permute-done.2.other_hbm
  40.7 0.0 copy-start.2
  40.7 0.8 %copy-done.2 = f32[4,32,8,128]{3,2,1,0:T(8,128)} copy-done((f32[4,32,8,128]{3,2,1,0:T(8,128)}, f32[4,32,8,128]{3,2,1,0:T(8,128)S(1)}, u32[]{:S(2)}) %copy-start.2) | copy-done | bytes 524312
  41.5 2.7 %between.1 = (f32[2048,128]{1,0:T(8,128)}, bf16[32,128,128]{2,1,0:T(8,128)(2,1)}) custom-call(f32[256,8,128]{2,1,0:T(8,128)S(1)} %get-tuple-element.23.u2_ref, f32[4,32,8,128]{3,2,1,0:T(8,128)} %get-tuple-element.24.same_hbm, f32[4,32,8,128]{3,2,1,0:T(8,128)} %copy-done.2), custom_call_target="tpu_custom_call" | custom-call | flops 1000000 | bytes 8000000 | tf_op jit(solution)/shard_map/between/pallas_call | solution.py:469
  44.2 0.0 collective-permute-done.4.before_2_ref.after_2_ref
  44.2 0.0 collective-permute-done.3.far_ref
  44.2 3.9 %update.1 = (f32[2048,128]{1,0:T(8,128)}, f32[8,256]{1,0:T(8,128)}) custom-call(s32[2]{0:T(128)S(1)} %pad_add_fusion.place_ref, s32[1]{0:T(128)S(6)} %copy.18.count_ref, s32[1,32]{1,0:T(1,128)} %cells_hbm.3, s32[1,32]{1,0:T(1,128)} %probes_hbm.1, s32[1,32]{1,0:T(1,128)} %level_hbm.1, f32[16,2,8,128]{3,2,1,0:T(8,128)S(1)} %all_to_all.10.near_ref, ...), custom_call_target="tpu_custom_call" | custom-call | tf_op jit(solution)/shard_map/update/pallas_call | solution.py:482
Async XLA Ops:
  3.1 19.2 %all-to-all-start = ((f32[4,32,8,128]{3,2,1,0:T(8,128)}), f32[4,32,8,128]{3,2,1,0:T(8,128)}, u32[]{:S(2)}, u32[]{:S(2)}) async-start(f32[4,32,8,128]{3,2,1,0:T(8,128)} %get-tuple-element.22), calls=%async_computation | async-start | bytes 1048576 | tf_op jit(solution)/shard_map/all_to_all | solution.py:428
  8.3 10.5 %collective-permute-start = (f32[69,8,128]{2,1,0:T(8,128)S(1)}, f32[69,8,128]{2,1,0:T(8,128)S(1)}, u32[]{:S(2)}, u32[]{:S(2)}) collective-permute-start(f32[69,8,128]{2,1,0:T(8,128)S(1)} %get-tuple-element.17), channel_id=1, source_target_pairs={{0,8},{8,16},{16,24},{1,9},{9,17},{17,25},{2,10},{10,18},{18,26},{... | collective-permute-start | bytes 847880 | tf_op jit(solution)/shard_map/ppermute | solution.py:420
  12.2 10.1 %collective-permute-start.1 = (f32[69,8,128]{2,1,0:T(8,128)S(1)}, f32[69,8,128]{2,1,0:T(8,128)S(1)}, u32[]{:S(2)}, u32[]{:S(2)}) collective-permute-start(f32[69,8,128]{2,1,0:T(8,128)S(1)} %get-tuple-element.18), channel_id=1, source_target_pairs={{8,0},{16,8},{24,16},{9,1},{17,9},{25,17},{10,2},{18,10},{26,18},{... | collective-permute-start | bytes 847880 | tf_op jit(solution)/shard_map/ppermute | solution.py:421
  17.8 0.9 %copy-start = (f32[224,8,128]{2,1,0:T(8,128)}, f32[224,8,128]{2,1,0:T(8,128)S(1)}, u32[]{:S(2)}) copy-start(f32[224,8,128]{2,1,0:T(8,128)S(1)} %get-tuple-element.20.edge_ref) | copy-start | bytes 2752516
  22.3 1.2 %copy-start.1 = (f32[224,8,128]{2,1,0:T(8,128)S(1)}, f32[224,8,128]{2,1,0:T(8,128)}, u32[]{:S(2)}) copy-start(f32[224,8,128]{2,1,0:T(8,128)} %copy-done) | copy-start | bytes 2752516
  25.1 15.6 %collective-permute-start.2 = (f32[4,32,8,128]{3,2,1,0:T(8,128)}, f32[4,32,8,128]{3,2,1,0:T(8,128)S(1)}, u32[]{:S(2)}, u32[]{:S(2)}) collective-permute-start(f32[4,32,8,128]{3,2,1,0:T(8,128)} %get-tuple-element.24.same_hbm), channel_id=1, source_target_pairs={{0,1},{1,0},{2,3},{3,2},{4,5},{5,4},{6,7},{7,6},{8,9},{9,8},{10,11... | collective-permute-start | bytes 1572872 | tf_op jit(solution)/shard_map/ppermute | solution.py:466
  39.0 5.2 %collective-permute-start.3 = (f32[16,2,8,128]{3,2,1,0:T(8,128)S(1)}, f32[16,2,8,128]{3,2,1,0:T(8,128)S(1)}, u32[]{:S(2)}, u32[]{:S(2)}) collective-permute-start(f32[16,2,8,128]{3,2,1,0:T(8,128)S(1)} %all_to_all.10.near_ref), channel_id=1, source_target_pairs={{0,1},{1,0},{2,3},{3,2},{4,5},{5,4},{6,7},{7,6},{8,9},{9,8},{10,11... | collective-permute-start | bytes 393224 | tf_op jit(solution)/shard_map/ppermute | solution.py:467
  39.0 5.1 %collective-permute-start.4 = (f32[4,8,128]{2,1,0:T(8,128)S(1)}, f32[4,8,128]{2,1,0:T(8,128)S(1)}, u32[]{:S(2)}, u32[]{:S(2)}) collective-permute-start(f32[4,8,128]{2,1,0:T(8,128)S(1)} %get-tuple-element.27.own_ref), channel_id=1, source_target_pairs={{0,16},{8,24},{16,0},{24,8},{1,17},{9,25},{17,1},{25,9},{2,18},{10... | collective-permute-start | bytes 49160 | tf_op jit(solution)/shard_map/ppermute | solution.py:423
  40.7 0.8 %copy-start.2 = (f32[4,32,8,128]{3,2,1,0:T(8,128)}, f32[4,32,8,128]{3,2,1,0:T(8,128)S(1)}, u32[]{:S(2)}) copy-start(f32[4,32,8,128]{3,2,1,0:T(8,128)S(1)} %collective-permute-done.2.other_hbm) | copy-start | bytes 1572868

commit v6 on v5

--- a/solution.py
+++ b/solution.py
@@ -256,16 +256,16 @@
     return high, (value - high.astype(jnp.float32)).astype(jnp.bfloat16)
 
 
-def between_kernel(planes, tiles, u2_ref, same_hbm, other_hbm, out_ref, split_ref, theta_ref, sems):
-    chips = same_hbm.shape[0]
+def between_kernel(planes, tiles, place_ref, u2_ref, same_hbm, other_hbm, out_ref, split_ref, theta_ref, sems):
+    core = place_ref[2]
     copies = [
-        pltpu.make_async_copy(same_hbm, theta_ref.at[pl.ds(0, chips)], sems.at[0]),
-        pltpu.make_async_copy(other_hbm, theta_ref.at[pl.ds(chips, chips)], sems.at[1]),
+        pltpu.make_async_copy(same_hbm, theta_ref.at[:, core], sems.at[0]),
+        pltpu.make_async_copy(other_hbm, theta_ref.at[:, 1 - core], sems.at[1]),
     ]
     for copy in copies:
         copy.start()
     stride = planes * tiles
-    members = theta_ref.shape[0] * ROWS
+    members = 2 * theta_ref.shape[0] * ROWS
 
     def store(x):
         for tile in range(tiles):
@@ -277,7 +277,7 @@
         copy.wait()
 
     def split(slot):
-        high, low = halves(theta_ref[:, slot].reshape(members, LANES))
+        high, low = halves(theta_ref[:, :, slot].reshape(members, LANES))
         split_ref[slot, :members, :] = high
         split_ref[slot, members:, :] = low
 
@@ -298,10 +298,10 @@
 
 
 def update_kernel(slabs, planes, tiles, place_ref, count_ref, cells_hbm, probes_hbm, level_hbm,
-                  near_ref, far_ref, before_2_ref, before_ref, own_ref, after_ref, after_2_ref, split_hbm, t_hbm,
+                  pred_ref, before_2_ref, before_ref, own_ref, after_ref, after_2_ref, split_hbm, t_hbm,
                   post_ref, gain_ref, reach, cells_ref, probes_ref, level_ref, split_ref, sems):
-    chips, blocks = near_ref.shape[0] // slabs, near_ref.shape[1]
-    members = 2 * chips * ROWS
+    groups, blocks = pred_ref.shape[0] // slabs, pred_ref.shape[1]
+    members = groups * ROWS
     share = 1.0 / (members - 1)
     copies = [
         pltpu.make_async_copy(source, target, sems.at[at])
@@ -311,7 +311,7 @@
     ]
     for copy in copies:
         copy.start()
-    slab, chip = place_ref[0], place_ref[1]
+    slab, group = place_ref[0], place_ref[1]
     halo = 4 * tiles + 1
     seen = ((before_2_ref, 0), (before_ref, halo), (own_ref, 0), (after_ref, halo), (after_2_ref, 0))
 
@@ -328,14 +328,12 @@
         at = jnp.clip(wanted, 0, slabs - 1)
         live = jnp.where((wanted >= 0) & (wanted < slabs), 1.0, 0.0)
         for b in range(blocks):
-            predicted = jnp.concatenate(
-                [ref[pl.ds(at * chips, chips), b].reshape(members // 2, LANES) for ref in (near_ref, far_ref)], axis=0
-            )
+            predicted = pred_ref[pl.ds(at * groups, groups), b].reshape(members, LANES)
             mean = jnp.sum(predicted, axis=0, keepdims=True) / members
             anomaly.append(halves((predicted - mean) * live))
             variance.append(extra(d, blocks + b) + (1.0 - live))
             noise = seen[d][0][seen[d][1] + b]
-            scaled.append((extra(d, b) + noise - near_ref[at * chips + chip, b]) / variance[-1] * live)
+            scaled.append((extra(d, b) + noise - pred_ref[at * groups + group, b]) / variance[-1] * live)
             left = stacked(scaled[-1])
             high, low = anomaly[-1]
             matches.append(fold(dot(left, high, 1) + dot(left, low, 1)))
@@ -443,14 +441,14 @@
             pltpu.SemaphoreType.DMA(()),
         ],
         compiler_params=params,
-        cost_estimate=pl.CostEstimate(flops=0, bytes_accessed=15_000_000, transcendentals=0),
+        cost_estimate=pl.CostEstimate(flops=0, bytes_accessed=400_000_000, transcendentals=0),
         name="inner_planes",
     )(stay(u_rows), t_near)
     u2, sent, theta_same = pl.pallas_call(
         functools.partial(outer_kernel, planes, tiles),
         out_shape=(
             jax.ShapeDtypeStruct((planes * tiles, ROWS, LANES), f32),
-            jax.ShapeDtypeStruct((slabs * chips, blocks, ROWS, LANES), f32),
+            jax.ShapeDtypeStruct((slabs * groups, blocks, ROWS, LANES), f32),
             pltpu.HBM(picked.shape, f32),
         ),
         in_specs=[HBM] + [VMEM] * 4 + [HBM],
@@ -461,31 +459,29 @@
         cost_estimate=pl.CostEstimate(flops=0, bytes_accessed=26_000_000, transcendentals=0),
         name="outer_planes",
     )(stay(probe_cells), before, after, edges, inner, stay(theta_same))
-    pred_near = lax.all_to_all(sent, ("space", "chip"), 0, 0)
-    swap = [(0, 1), (1, 0)]
-    theta_other = lax.ppermute(theta_same, "core", swap)
-    pred_far = lax.ppermute(pred_near, "core", swap)
-    place = jnp.stack([lax.axis_index("space"), lax.axis_index("chip")]).astype(i32)
+    pred_all = lax.all_to_all(sent, ("space", "chip", "core"), 0, 0)
+    theta_other = lax.ppermute(theta_same, "core", [(0, 1), (1, 0)])
+    place = jnp.stack([lax.axis_index("space"), lax.axis_index(("chip", "core")), lax.axis_index("core")]).astype(i32)
     u2_rows, split = pl.pallas_call(
         functools.partial(between_kernel, planes, tiles),
         out_shape=(
             jax.ShapeDtypeStruct(u_rows.shape, f32),
             pltpu.HBM((slots, 2 * groups * ROWS, LANES), jnp.bfloat16),
         ),
-        in_specs=[VMEM, HBM, HBM],
+        in_specs=[SMEM, VMEM, HBM, HBM],
         out_specs=(VMEM,) * 2,
-        scratch_shapes=[pltpu.VMEM((groups, slots, ROWS, LANES), f32), pltpu.SemaphoreType.DMA((2,))],
+        scratch_shapes=[pltpu.VMEM((chips, 2, slots, ROWS, LANES), f32), pltpu.SemaphoreType.DMA((2,))],
         compiler_params=params,
         cost_estimate=pl.CostEstimate(flops=1_000_000, bytes_accessed=8_000_000, transcendentals=0),
         name="between",
-    )(u2, stay(theta_same), stay(theta_other))
+    )(place, u2, stay(theta_same), stay(theta_other))
     post_rows, gain = pl.pallas_call(
         functools.partial(update_kernel, slabs, planes, tiles),
         out_shape=(
             jax.ShapeDtypeStruct(u_rows.shape, f32),
             jax.ShapeDtypeStruct((members, probes), f32),
         ),
-        in_specs=[SMEM] * 2 + [HBM] * 3 + [VMEM] * 7 + [HBM] * 2,
+        in_specs=[SMEM] * 2 + [HBM] * 3 + [VMEM] * 6 + [HBM] * 2,
         out_specs=(VMEM,) * 2,
         scratch_shapes=[
             pltpu.VMEM((probe_taper.shape[2], 2 * ROWS, 2 * groups * ROWS), jnp.bfloat16),
@@ -497,7 +493,7 @@
         ],
         compiler_params=params,
         name="update",
-    )(place, pair_counts, *map(stay, (pair_cells, pair_probes, pair_taper)), pred_near, pred_far,
+    )(place, pair_counts, *map(stay, (pair_cells, pair_probes, pair_taper)), pred_all,
       before_2, before, obs, after, after_2, stay(split), stay(t_rows))
     return (from_rows(u2_rows, shape), from_rows(post_rows, shape), gain)
 

time: 48.5 us -> 46.5 us (0.959)
  blocking collectives: 13.9 us -> 0 us
  starting transfers between devices: 11.4 us -> 18.3 us
  waiting for transfers between devices: 3.59 us -> 7.06 us
  Pallas kernels: 14.9 us -> 16.4 us
    all_to_all x1 -> x0, blocking collectives: 13.9 us -> none  [shards(): pred_near = lax.all_to_all(sent, ('space', 'chip'), 0, 0)]
    all_to_all x0 -> x1, starting transfers between devices: none -> 5.07 us  [shards(): pred_all = lax.all_to_all(sent, ('space', 'chip', 'core'), 0, 0)]
    ppermute x1, waiting for transfers between devices: 0.01 us -> 2.58 us  [shards(): lax.ppermute(obs, 'space', [(i, (i + 2) % 4) for i in range(4)])]
    ppermute x1, starting transfers between devices: 0.91 us -> 2.74 us  [shards(): lax.ppermute(obs, 'space', [(i, (i + 2) % 4) for i in range(4)])]
    all_to_all x0 -> x1, waiting for transfers between devices: none -> 1.07 us  [shards(): pred_all = lax.all_to_all(sent, ('space', 'chip', 'core'), 0, 0)]
    pallas_call x1, Pallas kernels: 1.58 us -> 2.36 us  [shards(): pl.pallas_call(functools.partial(outer_kernel, planes, tiles), out_shape=...]
    pallas_call x1, Pallas kernels: 2.68 us -> 3.22 us  [shards(): pl.pallas_call(functools.partial(between_kernel, planes, tiles), out_shap...]
  transfers between devices with their start and end apart: 6 -> 6, of which waited for: 1 -> 3; matrix products, arithmetic and copies ran while one was open for 0% -> 0% of each run, Pallas kernels for 14% -> 17%
where the time goes in v6:
time: 46.5 us; the launch traced here: 46.1 us
  starting transfers between devices  18.3 us (39%)
  Pallas kernels  16.4 us (35%)
  waiting for transfers between devices  7.06 us (15%)
  local copies, waits for them, and re-layouts  2.89 us (6%)
  between operations  1.38 us (3%)
    all_to_all x1, starting transfers between devices, shards(): theta_same = lax.all_to_all(picked, 'chip', 0, 0)  5.18 us
    all_to_all x1, starting transfers between devices, shards(): pred_all = lax.all_to_all(sent, ('space', 'chip', 'core'), 0, 0)  5.07 us
    pallas_call x1, Pallas kernels, shards(): pl.pallas_call(functools.partial(inner_kernel, planes, tiles), out_shape=...  4.46 us
    ppermute x1, starting transfers between devices, shards(): before = lax.ppermute(high, 'space', upward)  3.92 us
    pallas_call x1, Pallas kernels, shards(): pl.pallas_call(functools.partial(update_kernel, slabs, planes, tiles), ou...  3.87 us
    ppermute x1, waiting for transfers between devices, shards(): after = lax.ppermute(low, 'space', [(j, i) for i, j in upward])  3.4 us
    pallas_call x1, Pallas kernels, shards(): pl.pallas_call(functools.partial(between_kernel, planes, tiles), out_shap...  3.22 us
    unnamed x6, local copies, waits for them, and re-layouts  2.89 us
  transfers between devices with their start and end apart: 6, of which 3 were waited for; matrix products, arithmetic and copies ran while one was open for 0% of the time, Pallas kernels for 17%

profile of v6, /device:TPU:0, one launch (start us, length us, event | category | flops | bytes accessed | tf_op | source)
XLA Modules:
  0.0 46.1 jit_solution(3721785860242280469)
XLA Ops:
  0.6 2.5 %pack.1 = (f32[69,8,128]{2,1,0:T(8,128)S(1)}, f32[69,8,128]{2,1,0:T(8,128)S(1)}, f32[4,8,128]{2,1,0:T(8,128)S(1)}, f32[2048,128]{1,0:T(8,128)S(1)}, f32[4,32,8,128]{3,2,1,0:T(8,128)}) custom-call(s32[1,32]{1,0:T(1,128)} %cells_hbm.3, s32[1,2,6]{2,1,0:T(2,128)} %taper_hbm.1, f32[2048,128]{1,0:T(8,128)} %bitcast.25, f32[2048,128]{1,0:T(8,128)} %bitcast.27, ...), custom_call_target="tpu_custom_call" | custom-call | tf_op jit(solution)/shard_map/pack/pallas_call | solution.py:394
  3.1 5.2 %all-to-all-start = ((f32[4,32,8,128]{3,2,1,0:T(8,128)}), f32[4,32,8,128]{3,2,1,0:T(8,128)}, u32[]{:S(2)}, u32[]{:S(2)}) async-start(f32[4,32,8,128]{3,2,1,0:T(8,128)} %get-tuple-element.22), calls=%async_computation | async-start | bytes 1048576 | tf_op jit(solution)/shard_map/all_to_all | solution.py:426
  8.3 3.9 %collective-permute-start = (f32[69,8,128]{2,1,0:T(8,128)S(1)}, f32[69,8,128]{2,1,0:T(8,128)S(1)}, u32[]{:S(2)}, u32[]{:S(2)}) collective-permute-start(f32[69,8,128]{2,1,0:T(8,128)S(1)} %get-tuple-element.17), channel_id=1, source_target_pairs={{0,8},{8,16},{16,24},{1,9},{9,17},{17,25},{2,10},{10,18},{18,26},{... | collective-permute-start | bytes 847880 | tf_op jit(solution)/shard_map/ppermute | solution.py:418
  12.2 1.3 %collective-permute-start.1 = (f32[69,8,128]{2,1,0:T(8,128)S(1)}, f32[69,8,128]{2,1,0:T(8,128)S(1)}, u32[]{:S(2)}, u32[]{:S(2)}) collective-permute-start(f32[69,8,128]{2,1,0:T(8,128)S(1)} %get-tuple-element.18), channel_id=1, source_target_pairs={{8,0},{16,8},{24,16},{9,1},{17,9},{25,17},{10,2},{18,10},{26,18},{... | collective-permute-start | bytes 847880 | tf_op jit(solution)/shard_map/ppermute | solution.py:419
  13.5 4.5 %inner_planes.1 = (f32[256,8,128]{2,1,0:T(8,128)S(1)}, f32[224,8,128]{2,1,0:T(8,128)S(1)}) custom-call(f32[2048,128]{1,0:T(8,128)} %bitcast.26, f32[2048,128]{1,0:T(8,128)S(1)} %get-tuple-element.19.t_ref), custom_call_target="tpu_custom_call" | custom-call | bytes 400000000 | tf_op jit(solution)/shard_map/inner_planes/pallas_call | solution.py:427
  18.0 0.0 copy-start
  18.0 0.9 %copy-done = f32[224,8,128]{2,1,0:T(8,128)} copy-done((f32[224,8,128]{2,1,0:T(8,128)}, f32[224,8,128]{2,1,0:T(8,128)S(1)}, u32[]{:S(2)}) %copy-start) | copy-done | bytes 917528
  18.9 0.0 collective-permute-done.before_ref
  18.9 3.4 %collective-permute-done.1.after_ref = f32[69,8,128]{2,1,0:T(8,128)S(1)} collective-permute-done((f32[69,8,128]{2,1,0:T(8,128)S(1)}, f32[69,8,128]{2,1,0:T(8,128)S(1)}, u32[]{:S(2)}, u32[]{:S(2)}) %collective-permute-start.1) | collective-permute-done | bytes 282656 | tf_op jit(solution)/shard_map/ppermute | solution.py:419
  22.3 0.0 all-to-all-done.same_in
  22.3 0.0 copy-start.1
  22.3 1.2 %copy-done.1 = f32[224,8,128]{2,1,0:T(8,128)S(1)} copy-done((f32[224,8,128]{2,1,0:T(8,128)S(1)}, f32[224,8,128]{2,1,0:T(8,128)}, u32[]{:S(2)}) %copy-start.1) | copy-done | bytes 917528
  23.5 2.4 %outer_planes.1 = (f32[256,8,128]{2,1,0:T(8,128)S(1)}, f32[32,2,8,128]{3,2,1,0:T(8,128)}, f32[4,32,8,128]{3,2,1,0:T(8,128)}) custom-call(s32[256]{0:T(256)} %probe_hbm.1, f32[69,8,128]{2,1,0:T(8,128)S(1)} %collective-permute-done.before_ref, f32[69,8,128]{2,1,0:T(8,128)S(1)} %collective-permute-done.1.after_ref, ...), custom_call_target="tpu_custom_call", output_to_operand_aliasing={{0}: (4, {}), {2}: (5, {})} | custom-call | bytes 26000000 | tf_op jit(solution)/shard_map/outer_planes/pallas_call | solution.py:447
  25.9 0.1 collective-permute-start.2
  26.0 5.1 %all-to-all-start.1 = ((f32[32,2,8,128]{3,2,1,0:T(8,128)}), f32[32,2,8,128]{3,2,1,0:T(8,128)S(1)}, u32[]{:S(2)}, u32[]{:S(2)}) async-start(f32[32,2,8,128]{3,2,1,0:T(8,128)} %get-tuple-element.26), calls=%async_computation.1 | async-start | bytes 524288 | tf_op jit(solution)/shard_map/all_to_all | solution.py:462
  31.0 2.7 %collective-permute-start.3 = (f32[4,8,128]{2,1,0:T(8,128)S(1)}, f32[4,8,128]{2,1,0:T(8,128)S(1)}, u32[]{:S(2)}, u32[]{:S(2)}) collective-permute-start(f32[4,8,128]{2,1,0:T(8,128)S(1)} %get-tuple-element.27.own_ref), channel_id=1, source_target_pairs={{0,16},{8,24},{16,0},{24,8},{1,17},{9,25},{17,1},{25,9},{2,18},{10... | collective-permute-start | bytes 49160 | tf_op jit(solution)/shard_map/ppermute | solution.py:421
  33.8 0.1 pad_add_fusion.place_ref
  34.5 0.0 collective-permute-done.2.other_hbm
  34.5 0.0 copy-start.2
  34.5 0.8 %copy-done.2 = f32[4,32,8,128]{3,2,1,0:T(8,128)} copy-done((f32[4,32,8,128]{3,2,1,0:T(8,128)}, f32[4,32,8,128]{3,2,1,0:T(8,128)S(1)}, u32[]{:S(2)}) %copy-start.2) | copy-done | bytes 524312
  35.3 3.2 %between.1 = (f32[2048,128]{1,0:T(8,128)}, bf16[32,128,128]{2,1,0:T(8,128)(2,1)}) custom-call(s32[3]{0:T(128)S(1)} %pad_add_fusion.place_ref, f32[256,8,128]{2,1,0:T(8,128)S(1)} %get-tuple-element.23.u2_ref, f32[4,32,8,128]{3,2,1,0:T(8,128)} %get-tuple-element.24.same_hbm, f32[4,32,8,128]{3,2,1,0:T(8,128)} %copy-done.2), custom_call_target="tpu_custom_call" | custom-call | flops 1000000 | bytes 8000000 | tf_op jit(solution)/shard_map/between/pallas_call | solution.py:465
  38.5 2.6 %collective-permute-done.3.before_2_ref.after_2_ref = f32[4,8,128]{2,1,0:T(8,128)S(1)} collective-permute-done((f32[4,8,128]{2,1,0:T(8,128)S(1)}, f32[4,8,128]{2,1,0:T(8,128)S(1)}, u32[]{:S(2)}, u32[]{:S(2)}) %collective-permute-start.3) | collective-permute-done | bytes 16416 | tf_op jit(solution)/shard_map/ppermute | solution.py:421
  41.1 1.1 %all-to-all-done.1.pred_ref = f32[32,2,8,128]{3,2,1,0:T(8,128)S(1)} async-done(((f32[32,2,8,128]{3,2,1,0:T(8,128)}), f32[32,2,8,128]{3,2,1,0:T(8,128)S(1)}, u32[]{:S(2)}, u32[]{:S(2)}) %all-to-all-start.1) | async-done | bytes 262176 | tf_op jit(solution)/shard_map/all_to_all | solution.py:462
  42.2 3.9 %update.1 = (f32[2048,128]{1,0:T(8,128)}, f32[8,256]{1,0:T(8,128)}) custom-call(s32[3]{0:T(128)S(1)} %pad_add_fusion.place_ref, s32[1]{0:T(128)S(6)} %copy.18.count_ref, s32[1,32]{1,0:T(1,128)} %cells_hbm.3, s32[1,32]{1,0:T(1,128)} %probes_hbm.1, s32[1,32]{1,0:T(1,128)} %level_hbm.1, f32[32,2,8,128]{3,2,1,0:T(8,128)S(1)} %all-to-all-done.1.pred_ref, ...), custom_call_target="tpu_custom_call" | custom-call | tf_op jit(solution)/shard_map/update/pallas_call | solution.py:478
Async XLA Ops:
  3.1 19.2 %all-to-all-start = ((f32[4,32,8,128]{3,2,1,0:T(8,128)}), f32[4,32,8,128]{3,2,1,0:T(8,128)}, u32[]{:S(2)}, u32[]{:S(2)}) async-start(f32[4,32,8,128]{3,2,1,0:T(8,128)} %get-tuple-element.22), calls=%async_computation | async-start | bytes 1048576 | tf_op jit(solution)/shard_map/all_to_all | solution.py:426
  8.3 10.6 %collective-permute-start = (f32[69,8,128]{2,1,0:T(8,128)S(1)}, f32[69,8,128]{2,1,0:T(8,128)S(1)}, u32[]{:S(2)}, u32[]{:S(2)}) collective-permute-start(f32[69,8,128]{2,1,0:T(8,128)S(1)} %get-tuple-element.17), channel_id=1, source_target_pairs={{0,8},{8,16},{16,24},{1,9},{9,17},{17,25},{2,10},{10,18},{18,26},{... | collective-permute-start | bytes 847880 | tf_op jit(solution)/shard_map/ppermute | solution.py:418
  12.2 10.1 %collective-permute-start.1 = (f32[69,8,128]{2,1,0:T(8,128)S(1)}, f32[69,8,128]{2,1,0:T(8,128)S(1)}, u32[]{:S(2)}, u32[]{:S(2)}) collective-permute-start(f32[69,8,128]{2,1,0:T(8,128)S(1)} %get-tuple-element.18), channel_id=1, source_target_pairs={{8,0},{16,8},{24,16},{9,1},{17,9},{25,17},{10,2},{18,10},{26,18},{... | collective-permute-start | bytes 847880 | tf_op jit(solution)/shard_map/ppermute | solution.py:419
  18.0 0.9 %copy-start = (f32[224,8,128]{2,1,0:T(8,128)}, f32[224,8,128]{2,1,0:T(8,128)S(1)}, u32[]{:S(2)}) copy-start(f32[224,8,128]{2,1,0:T(8,128)S(1)} %get-tuple-element.20.edge_ref) | copy-start | bytes 2752516
  22.3 1.2 %copy-start.1 = (f32[224,8,128]{2,1,0:T(8,128)S(1)}, f32[224,8,128]{2,1,0:T(8,128)}, u32[]{:S(2)}) copy-start(f32[224,8,128]{2,1,0:T(8,128)} %copy-done) | copy-start | bytes 2752516
  25.9 8.6 %collective-permute-start.2 = (f32[4,32,8,128]{3,2,1,0:T(8,128)}, f32[4,32,8,128]{3,2,1,0:T(8,128)S(1)}, u32[]{:S(2)}, u32[]{:S(2)}) collective-permute-start(f32[4,32,8,128]{3,2,1,0:T(8,128)} %get-tuple-element.24.same_hbm), channel_id=1, source_target_pairs={{0,1},{1,0},{2,3},{3,2},{4,5},{5,4},{6,7},{7,6},{8,9},{9,8},{10,11... | collective-permute-start | bytes 1572872 | tf_op jit(solution)/shard_map/ppermute | solution.py:463
  26.0 16.2 %all-to-all-start.1 = ((f32[32,2,8,128]{3,2,1,0:T(8,128)}), f32[32,2,8,128]{3,2,1,0:T(8,128)S(1)}, u32[]{:S(2)}, u32[]{:S(2)}) async-start(f32[32,2,8,128]{3,2,1,0:T(8,128)} %get-tuple-element.26), calls=%async_computation.1 | async-start | bytes 524288 | tf_op jit(solution)/shard_map/all_to_all | solution.py:462
  31.0 10.1 %collective-permute-start.3 = (f32[4,8,128]{2,1,0:T(8,128)S(1)}, f32[4,8,128]{2,1,0:T(8,128)S(1)}, u32[]{:S(2)}, u32[]{:S(2)}) collective-permute-start(f32[4,8,128]{2,1,0:T(8,128)S(1)} %get-tuple-element.27.own_ref), channel_id=1, source_target_pairs={{0,16},{8,24},{16,0},{24,8},{1,17},{9,25},{17,1},{25,9},{2,18},{10... | collective-permute-start | bytes 49160 | tf_op jit(solution)/shard_map/ppermute | solution.py:421
  34.5 0.8 %copy-start.2 = (f32[4,32,8,128]{3,2,1,0:T(8,128)}, f32[4,32,8,128]{3,2,1,0:T(8,128)S(1)}, u32[]{:S(2)}) copy-start(f32[4,32,8,128]{3,2,1,0:T(8,128)S(1)} %collective-permute-done.2.other_hbm) | copy-start | bytes 1572868

commit v7 on v6

--- a/solution.py
+++ b/solution.py
@@ -15,6 +15,7 @@
 VMEM = pl.BlockSpec(memory_space=pltpu.VMEM)
 SMEM = pl.BlockSpec(memory_space=pltpu.SMEM)
 HBM = pl.BlockSpec(memory_space=pltpu.HBM)
+ANY = pl.BlockSpec(memory_space=pl.ANY)
 
 
 def stay(array):
@@ -37,15 +38,13 @@
     return (plane // ROWS * tiles + tile) * ROWS + plane % ROWS
 
 
-def pack_kernel(planes, tiles, cells_hbm, taper_hbm, u_hbm, t_hbm, noise_hbm, observed_hbm, var_hbm,
-                low_ref, high_ref, obs_ref, t_ref, pick_hbm,
-                cells_ref, taper_ref, u_ref, noise_ref, row_ref, pick_ref, sems):
+def pack_kernel(planes, tiles, taper_hbm, u_hbm, t_hbm, noise_hbm, observed_hbm, var_hbm,
+                low_ref, high_ref, obs_ref, t_ref, taper_ref, u_ref, noise_ref, row_ref, sems):
     stride = planes * tiles
     blocks = noise_ref.shape[1] // LANES
     copies = [
         pltpu.make_async_copy(source, target, sems.at[at])
         for at, (source, target) in enumerate((
-            (cells_hbm, cells_ref),
             (t_hbm, t_ref),
             (u_hbm, u_ref),
             (taper_hbm, taper_ref),
@@ -56,21 +55,8 @@
     ]
     for copy in copies:
         copy.start()
-    copies[0].wait()
-    copies[1].wait()
-    for slot in range(pick_ref.shape[0]):
-        block = cells_ref[0, slot]
-        row = row_of(block // tiles, block % tiles, tiles)
-        pick_ref[slot] = t_ref[pl.ds(row, ROWS, stride=stride), :]
-    picks = [
-        pltpu.make_async_copy(pick_ref, pick_hbm.at[device], sems.at[len(copies) + device])
-        for device in range(pick_hbm.shape[0])
-    ]
-    for copy in picks:
-        copy.start()
     for kind, source in ((1, t_ref), (0, u_ref)):
-        if kind == 0:
-            copies[2].wait()
+        copies[1 - kind].wait()
         for out_ref, first in ((high_ref, planes - 2), (low_ref, 0)):
             for depth in range(2):
                 for tile in range(tiles):
@@ -79,7 +65,7 @@
                     ]
     for ref in (low_ref, high_ref):
         ref[4 * tiles] = jnp.ones((ROWS, LANES), jnp.float32)
-    for copy in copies[3:]:
+    for copy in copies[2:]:
         copy.wait()
     own, window = taper_ref.shape[1:]
     rows = [row_ref[kind : kind + 1, b * LANES : (b + 1) * LANES] for kind in range(2) for b in range(blocks)]
@@ -93,8 +79,6 @@
     for ref in (low_ref, high_ref):
         for at in range(obs_ref.shape[0]):
             ref[4 * tiles + 1 + at] = obs_ref[at]
-    for copy in picks:
-        copy.wait()
 
 
 def rot(value, by):
@@ -165,10 +149,14 @@
         body(x)
 
 
-def inner_kernel(planes, tiles, u_hbm, t_ref, u2_ref, edge_ref, u_ref, u0, hv, u1, held, sem):
+def inner_kernel(planes, tiles, u_hbm, cells_hbm, t_ref, u2_ref, edge_ref, pick_hbm,
+                 u_ref, u0, hv, u1, held, cells_ref, pick_ref, sems):
     stride = planes * tiles
     masks = lane_masks()
-    copy = pltpu.make_async_copy(u_hbm, u_ref, sem)
+    copy = pltpu.make_async_copy(u_hbm, u_ref, sems.at[0])
+    cells_copy = pltpu.make_async_copy(cells_hbm, cells_ref, sems.at[1])
+    picked = pltpu.make_async_copy(pick_ref, pick_hbm, sems.at[2])
+    cells_copy.start()
     copy.start()
 
     def rows_at(x, tile):
@@ -198,6 +186,12 @@
         put(u2_ref, x, step(masks, weights, *[plane_of(u1, x + d, tiles) for d in (-1, 0, 1)]))
 
     each(0, planes, 4, load_t)
+    cells_copy.wait()
+    for slot in range(pick_ref.shape[0]):
+        block = cells_ref[0, slot]
+        row = row_of(block // tiles, block % tiles, tiles)
+        pick_ref[slot] = t_ref[pl.ds(row, ROWS, stride=stride), :]
+    picked.start()
     copy.wait()
     each(0, planes, 4, load_u)
     each(1, planes - 1, 7, first_step)
@@ -209,11 +203,12 @@
         for x in kept:
             put(edge_ref, at, plane_of(ref, x, tiles))
             at += 1
-
-
-def outer_kernel(planes, tiles, probe_hbm, before_ref, after_ref, edge_ref, inner_ref, same_in,
-                 u2_ref, sent_ref, same_out, probe_ref, sem):
-    probe_copy = pltpu.make_async_copy(probe_hbm, probe_ref, sem)
+    picked.wait()
+
+
+def outer_kernel(planes, tiles, probe_hbm, before_ref, after_ref, edge_ref, inner_ref,
+                 u2_ref, sent_hbm, probe_ref, found_ref, sems):
+    probe_copy = pltpu.make_async_copy(probe_hbm, probe_ref, sems.at[0])
     probe_copy.start()
     masks = lane_masks()
     blocks = probe_ref.shape[0] // LANES
@@ -243,12 +238,14 @@
             turned = pltpu.roll(u2_ref[cell >> 7], (p - cell) & (LANES - 1), 1)
             found = jnp.where(lane == p, turned, found)
 
-        def send(at, _):
-            for d in range(ROWS):
-                sent_ref[at * ROWS + d, part] = found
-            return 0
-
-        lax.fori_loop(0, sent_ref.shape[0] // ROWS, send, 0)
+        found_ref[part] = found
+
+    def send(device, _):
+        pltpu.make_async_copy(found_ref, sent_hbm.at[device], sems.at[1]).start()
+        return 0
+
+    lax.fori_loop(0, sent_hbm.shape[0], send, 0)
+    pltpu.make_async_copy(sent_hbm, sent_hbm, sems.at[1]).wait()
 
 
 def halves(value):
@@ -256,23 +253,32 @@
     return high, (value - high.astype(jnp.float32)).astype(jnp.bfloat16)
 
 
-def between_kernel(planes, tiles, place_ref, u2_ref, same_hbm, other_hbm, out_ref, split_ref, theta_ref, sems):
-    core = place_ref[2]
-    copies = [
-        pltpu.make_async_copy(same_hbm, theta_ref.at[:, core], sems.at[0]),
-        pltpu.make_async_copy(other_hbm, theta_ref.at[:, 1 - core], sems.at[1]),
-    ]
+def store_kernel(planes, tiles, u2_ref, *refs):
+    *parts, out_ref, same_hbm, sems = refs
+    copies = [pltpu.make_async_copy(part, same_hbm.at[at], sems.at[at]) for at, part in enumerate(parts)]
     for copy in copies:
         copy.start()
-    stride = planes * tiles
-    members = 2 * theta_ref.shape[0] * ROWS
 
     def store(x):
         for tile in range(tiles):
-            rows = pl.ds((x // ROWS) * tiles * ROWS + x % ROWS + tile * ROWS, ROWS, stride=stride)
+            rows = pl.ds((x // ROWS) * tiles * ROWS + x % ROWS + tile * ROWS, ROWS, stride=planes * tiles)
             out_ref[rows, :] = u2_ref[x * tiles + tile]
 
     each(0, planes, 4, store)
+    for copy in copies:
+        copy.wait()
+
+
+def split_kernel(by_xor, place_ref, same_hbm, other_hbm, split_ref, theta_ref, sems):
+    chip, core = place_ref[2], place_ref[3]
+    members = 2 * theta_ref.shape[0] * ROWS
+    copies = []
+    for at in range(same_hbm.shape[0]):
+        where = chip ^ at if by_xor else at
+        copies.append(pltpu.make_async_copy(same_hbm.at[at], theta_ref.at[where, core], sems.at[2 * at]))
+        copies.append(pltpu.make_async_copy(other_hbm.at[at], theta_ref.at[where, 1 - core], sems.at[2 * at + 1]))
+    for copy in copies:
+        copy.start()
     for copy in copies:
         copy.wait()
 
@@ -391,29 +397,26 @@
     obs_shape = jax.ShapeDtypeStruct((obs_tiles, ROWS, LANES), f32)
     params = pltpu.CompilerParams(vmem_limit_bytes=32 * 1024 * 1024)
     stack = pltpu.VMEM((planes * tiles, ROWS, LANES), f32)
-    low, high, obs, t_near, picked = pl.pallas_call(
+    low, high, obs, t_near = pl.pallas_call(
         functools.partial(pack_kernel, planes, tiles),
         out_shape=(
             edge,
             edge,
             obs_shape,
             jax.ShapeDtypeStruct(u_rows.shape, f32),
-            pltpu.HBM((chips, slots, ROWS, LANES), f32),
         ),
-        in_specs=[HBM] * 7,
-        out_specs=(VMEM,) * 4 + (HBM,),
+        in_specs=[HBM] * 6,
+        out_specs=(VMEM,) * 4,
         scratch_shapes=[
-            pltpu.SMEM(pair_cells.shape, i32),
             pltpu.SMEM(probe_taper.shape, i32),
             pltpu.VMEM(u_rows.shape, f32),
             pltpu.VMEM((ROWS, probes), f32),
             pltpu.VMEM((2, probes), f32),
-            pltpu.VMEM((slots, ROWS, LANES), f32),
-            pltpu.SemaphoreType.DMA((7 + chips,)),
+            pltpu.SemaphoreType.DMA((6,)),
         ],
         compiler_params=params,
         name="pack",
-    )(*map(stay, (pair_cells, probe_taper, u_rows, t_rows, obs_noise, observed.reshape(1, -1), obs_var.reshape(1, -1))))
+    )(*map(stay, (probe_taper, u_rows, t_rows, obs_noise, observed.reshape(1, -1), obs_var.reshape(1, -1))))
     upward = [(i, i + 1) for i in range(slabs - 1)]
     before = lax.ppermute(high, "space", upward)
     after = lax.ppermute(low, "space", [(j, i) for i, j in upward])
@@ -423,58 +426,79 @@
         upward_2 = [(i, i + 2) for i in range(slabs - 2)]
         before_2 = lax.ppermute(obs, "space", upward_2)
         after_2 = lax.ppermute(obs, "space", [(j, i) for i, j in upward_2])
-    theta_same = lax.all_to_all(picked, "chip", 0, 0)
-    inner, edges = pl.pallas_call(
+    inner, edges, picked = pl.pallas_call(
         functools.partial(inner_kernel, planes, tiles),
         out_shape=(
             jax.ShapeDtypeStruct((planes * tiles, ROWS, LANES), f32),
             jax.ShapeDtypeStruct((14 * tiles, ROWS, LANES), f32),
+            pltpu.HBM((slots, ROWS, LANES), f32),
         ),
-        in_specs=[HBM, VMEM],
-        out_specs=(VMEM,) * 2,
+        in_specs=[HBM, HBM, VMEM],
+        out_specs=(VMEM, VMEM, HBM),
         scratch_shapes=[
             pltpu.VMEM(u_rows.shape, f32),
             stack,
             stack,
             stack,
             pltpu.VMEM((5, planes * tiles, ROWS, LANES), f32),
-            pltpu.SemaphoreType.DMA(()),
+            pltpu.SMEM(pair_cells.shape, i32),
+            pltpu.VMEM((slots, ROWS, LANES), f32),
+            pltpu.SemaphoreType.DMA((3,)),
         ],
         compiler_params=params,
-        cost_estimate=pl.CostEstimate(flops=0, bytes_accessed=400_000_000, transcendentals=0),
+        cost_estimate=pl.CostEstimate(flops=0, bytes_accessed=15_000_000, transcendentals=0),
         name="inner_planes",
-    )(stay(u_rows), t_near)
-    u2, sent, theta_same = pl.pallas_call(
+    )(stay(u_rows), stay(pair_cells), t_near)
+    by_xor = chips <= 4 and chips & (chips - 1) == 0
+    if by_xor:
+        parts = [picked]
+        for d in range(1, chips):
+            parts.append(lax.ppermute(picked, "chip", [(i, i ^ d) for i in range(chips)]))
+    else:
+        spread = lax.all_to_all(jnp.broadcast_to(picked, (chips, *picked.shape)), "chip", 0, 0)
+        parts = [spread[i] for i in range(chips)]
+    u2, sent = pl.pallas_call(
         functools.partial(outer_kernel, planes, tiles),
         out_shape=(
             jax.ShapeDtypeStruct((planes * tiles, ROWS, LANES), f32),
-            jax.ShapeDtypeStruct((slabs * groups, blocks, ROWS, LANES), f32),
-            pltpu.HBM(picked.shape, f32),
+            pltpu.HBM((slabs * groups, blocks, ROWS, LANES), f32),
         ),
-        in_specs=[HBM] + [VMEM] * 4 + [HBM],
-        out_specs=(VMEM, VMEM, HBM),
-        scratch_shapes=[pltpu.SMEM(probe_cells.shape, i32), pltpu.SemaphoreType.DMA(())],
-        input_output_aliases={4: 0, 5: 2},
+        in_specs=[HBM] + [VMEM] * 4,
+        out_specs=(VMEM, HBM),
+        scratch_shapes=[
+            pltpu.SMEM(probe_cells.shape, i32),
+            pltpu.VMEM((blocks, ROWS, LANES), f32),
+            pltpu.SemaphoreType.DMA((2,)),
+        ],
+        input_output_aliases={4: 0},
         compiler_params=params,
         cost_estimate=pl.CostEstimate(flops=0, bytes_accessed=26_000_000, transcendentals=0),
         name="outer_planes",
-    )(stay(probe_cells), before, after, edges, inner, stay(theta_same))
+    )(stay(probe_cells), before, after, edges, inner)
     pred_all = lax.all_to_all(sent, ("space", "chip", "core"), 0, 0)
+    u2_rows, theta_same = pl.pallas_call(
+        functools.partial(store_kernel, planes, tiles),
+        out_shape=(jax.ShapeDtypeStruct(u_rows.shape, f32), pltpu.HBM((chips, slots, ROWS, LANES), f32)),
+        in_specs=[VMEM] + [ANY] * chips,
+        out_specs=(VMEM, HBM),
+        scratch_shapes=[pltpu.SemaphoreType.DMA((chips,))],
+        compiler_params=params,
+        cost_estimate=pl.CostEstimate(flops=0, bytes_accessed=8_000_000, transcendentals=0),
+        name="store",
+    )(u2, *parts)
     theta_other = lax.ppermute(theta_same, "core", [(0, 1), (1, 0)])
-    place = jnp.stack([lax.axis_index("space"), lax.axis_index(("chip", "core")), lax.axis_index("core")]).astype(i32)
-    u2_rows, split = pl.pallas_call(
-        functools.partial(between_kernel, planes, tiles),
-        out_shape=(
-            jax.ShapeDtypeStruct(u_rows.shape, f32),
-            pltpu.HBM((slots, 2 * groups * ROWS, LANES), jnp.bfloat16),
-        ),
-        in_specs=[SMEM, VMEM, HBM, HBM],
-        out_specs=(VMEM,) * 2,
-        scratch_shapes=[pltpu.VMEM((chips, 2, slots, ROWS, LANES), f32), pltpu.SemaphoreType.DMA((2,))],
+    where = [lax.axis_index(axes) for axes in ("space", ("chip", "core"), "chip", "core")]
+    place = jnp.stack(where).astype(i32)
+    split = pl.pallas_call(
+        functools.partial(split_kernel, by_xor),
+        out_shape=pltpu.HBM((slots, 2 * groups * ROWS, LANES), jnp.bfloat16),
+        in_specs=[SMEM, HBM, ANY],
+        out_specs=VMEM,
+        scratch_shapes=[pltpu.VMEM((chips, 2, slots, ROWS, LANES), f32), pltpu.SemaphoreType.DMA((2 * chips,))],
         compiler_params=params,
-        cost_estimate=pl.CostEstimate(flops=1_000_000, bytes_accessed=8_000_000, transcendentals=0),
-        name="between",
-    )(place, u2, stay(theta_same), stay(theta_other))
+        cost_estimate=pl.CostEstimate(flops=0, bytes_accessed=5_000_000, transcendentals=0),
+        name="split",
+    )(place, stay(theta_same), theta_other)
     post_rows, gain = pl.pallas_call(
         functools.partial(update_kernel, slabs, planes, tiles),
         out_shape=(

time: 46.5 us -> 45.2 us (0.972)
  local copies, waits for them, and re-layouts: 2.89 us -> 0.01 us
  Pallas kernels: 16.4 us -> 17.3 us
  waiting for transfers between devices: 7.06 us -> 7.53 us
    all_to_all x1 -> x0, starting transfers between devices: 5.18 us -> none  [shards(): theta_same = lax.all_to_all(picked, 'chip', 0, 0)]
    ppermute x0 -> x3, starting transfers between devices: none -> 3.55 us  [shards(): lax.ppermute(picked, 'chip', [(i, i ^ d) for i in range(chips)])]
    unnamed x6 -> x2, local copies, waits for them, and re-layouts: 2.89 us -> 0.01 us
    ppermute x1, waiting for transfers between devices: 3.4 us -> 0.93 us  [shards(): after = lax.ppermute(low, 'space', [(j, i) for i, j in upward])]
    ppermute x0 -> x3, waiting for transfers between devices: none -> 2.14 us  [shards(): lax.ppermute(picked, 'chip', [(i, i ^ d) for i in range(chips)])]
    pallas_call x1 -> x2, Pallas kernels: 3.22 us -> 4.99 us  [the longest x1 3.21 us: shards(): pl.pallas_call(functools.partial(split_kernel, by_xor), out_shape=pltpu.H...]
    ppermute x1, starting transfers between devices: 3.92 us -> 4.95 us  [shards(): before = lax.ppermute(high, 'space', upward)]
    all_to_all x1, starting transfers between devices: 5.07 us -> 5.97 us  [shards(): pred_all = lax.all_to_all(sent, ('space', 'chip', 'core'), 0, 0)]
  transfers between devices with their start and end apart: 6 -> 8, of which waited for: 3 -> 5; matrix products, arithmetic and copies ran while one was open for 0% -> 0% of each run, Pallas kernels for 17% -> 22%
where the time goes in v7:
time: 45.2 us; the launch traced here: 44.9 us
  starting transfers between devices  18.6 us (41%)
  Pallas kernels  17.3 us (38%)
  waiting for transfers between devices  7.53 us (17%)
  between operations  1.38 us (3%)
    all_to_all x1, starting transfers between devices, shards(): pred_all = lax.all_to_all(sent, ('space', 'chip', 'core'), 0, 0)  5.97 us
    ppermute x1, starting transfers between devices, shards(): before = lax.ppermute(high, 'space', upward)  4.95 us
    pallas_call x1, Pallas kernels, shards(): pl.pallas_call(functools.partial(inner_kernel, planes, tiles), out_shape=...  4.31 us
    pallas_call x1, Pallas kernels, shards(): pl.pallas_call(functools.partial(update_kernel, slabs, planes, tiles), ou...  3.87 us
    ppermute x3, starting transfers between devices, shards(): lax.ppermute(picked, 'chip', [(i, i ^ d) for i in range(chips)])  3.55 us
    ppermute x1, waiting for transfers between devices, shards(): lax.ppermute(obs, 'space', [(i, (i + 2) % 4) for i in range(4)])  3.39 us
    pallas_call x1, Pallas kernels, shards(): pl.pallas_call(functools.partial(split_kernel, by_xor), out_shape=pltpu.H...  3.21 us
    ppermute x1, starting transfers between devices, shards(): lax.ppermute(obs, 'space', [(i, (i + 2) % 4) for i in range(4)])  2.74 us
  transfers between devices with their start and end apart: 8, of which 5 were waited for; matrix products, arithmetic and copies ran while one was open for 0% of the time, Pallas kernels for 22%

profile of v7, /device:TPU:0, one launch (start us, length us, event | category | flops | bytes accessed | tf_op | source)
XLA Modules:
  0.0 44.9 jit_solution(8346314148064133480)
XLA Ops:
  0.6 1.8 %pack.1 = (f32[69,8,128]{2,1,0:T(8,128)S(1)}, f32[69,8,128]{2,1,0:T(8,128)S(1)}, f32[4,8,128]{2,1,0:T(8,128)S(1)}, f32[2048,128]{1,0:T(8,128)S(1)}) custom-call(s32[1,2,6]{2,1,0:T(2,128)} %taper_hbm.1, f32[2048,128]{1,0:T(8,128)} %bitcast.26, f32[2048,128]{1,0:T(8,128)} %bitcast.28, f32[8,256]{1,0:T(8,128)} %noise_hbm.1, f32[1,256]{1,0:T(1,128)} %bitcast.30, ...), custom_call_target="tpu_custom_call" | custom-call | tf_op jit(solution)/shard_map/pack/pallas_call | solution.py:400
  2.4 4.9 %collective-permute-start = (f32[69,8,128]{2,1,0:T(8,128)S(1)}, f32[69,8,128]{2,1,0:T(8,128)S(1)}, u32[]{:S(2)}, u32[]{:S(2)}) collective-permute-start(f32[69,8,128]{2,1,0:T(8,128)S(1)} %get-tuple-element.16), channel_id=1, source_target_pairs={{0,8},{8,16},{16,24},{1,9},{9,17},{17,25},{2,10},{10,18},{18,26},{... | collective-permute-start | bytes 847880 | tf_op jit(solution)/shard_map/ppermute | solution.py:421
  7.4 1.3 %collective-permute-start.1 = (f32[69,8,128]{2,1,0:T(8,128)S(1)}, f32[69,8,128]{2,1,0:T(8,128)S(1)}, u32[]{:S(2)}, u32[]{:S(2)}) collective-permute-start(f32[69,8,128]{2,1,0:T(8,128)S(1)} %get-tuple-element.17), channel_id=1, source_target_pairs={{8,0},{16,8},{24,16},{9,1},{17,9},{25,17},{10,2},{18,10},{26,18},{... | collective-permute-start | bytes 847880 | tf_op jit(solution)/shard_map/ppermute | solution.py:422
  8.7 4.3 %inner_planes.1 = (f32[256,8,128]{2,1,0:T(8,128)S(1)}, f32[224,8,128]{2,1,0:T(8,128)S(1)}, f32[32,8,128]{2,1,0:T(8,128)}) custom-call(f32[2048,128]{1,0:T(8,128)} %bitcast.27, s32[1,32]{1,0:T(1,128)} %cells_hbm.3, f32[2048,128]{1,0:T(8,128)S(1)} %get-tuple-element.18.t_ref), custom_call_target="tpu_custom_call" | custom-call | bytes 15000000 | tf_op jit(solution)/shard_map/inner_planes/pallas_call | solution.py:429
  13.0 2.5 %collective-permute-start.4 = (f32[32,8,128]{2,1,0:T(8,128)}, f32[32,8,128]{2,1,0:T(8,128)S(1)}, u32[]{:S(2)}, u32[]{:S(2)}) collective-permute-start(f32[32,8,128]{2,1,0:T(8,128)} %get-tuple-element.22.refs_0_), channel_id=1, source_target_pairs={{0,6},{2,4},{4,2},{6,0},{1,7},{3,5},{5,3},{7,1},{8,14},{10,12},{12... | collective-permute-start | bytes 393224 | tf_op jit(solution)/shard_map/ppermute | solution.py:456
  15.5 0.5 %collective-permute-start.3 = (f32[32,8,128]{2,1,0:T(8,128)}, f32[32,8,128]{2,1,0:T(8,128)S(1)}, u32[]{:S(2)}, u32[]{:S(2)}) collective-permute-start(f32[32,8,128]{2,1,0:T(8,128)} %get-tuple-element.22.refs_0_), channel_id=1, source_target_pairs={{0,4},{2,6},{4,0},{6,2},{1,5},{3,7},{5,1},{7,3},{8,12},{10,14},{12... | collective-permute-start | bytes 393224 | tf_op jit(solution)/shard_map/ppermute | solution.py:456
  16.0 0.5 %collective-permute-start.2 = (f32[32,8,128]{2,1,0:T(8,128)}, f32[32,8,128]{2,1,0:T(8,128)S(1)}, u32[]{:S(2)}, u32[]{:S(2)}) collective-permute-start(f32[32,8,128]{2,1,0:T(8,128)} %get-tuple-element.22.refs_0_), channel_id=1, source_target_pairs={{0,2},{2,0},{4,6},{6,4},{1,3},{3,1},{5,7},{7,5},{8,10},{10,8},{12,... | collective-permute-start | bytes 393224 | tf_op jit(solution)/shard_map/ppermute | solution.py:456
  16.5 0.0 collective-permute-done.before_ref
  16.5 0.9 %collective-permute-done.1.after_ref = f32[69,8,128]{2,1,0:T(8,128)S(1)} collective-permute-done((f32[69,8,128]{2,1,0:T(8,128)S(1)}, f32[69,8,128]{2,1,0:T(8,128)S(1)}, u32[]{:S(2)}, u32[]{:S(2)}) %collective-permute-start.1) | collective-permute-done | bytes 282656 | tf_op jit(solution)/shard_map/ppermute | solution.py:422
  17.5 0.0 copy-start
  17.5 2.4 %outer_planes.1 = (f32[256,8,128]{2,1,0:T(8,128)S(1)}, f32[32,2,8,128]{3,2,1,0:T(8,128)}) custom-call(s32[256]{0:T(256)} %probe_hbm.1, f32[69,8,128]{2,1,0:T(8,128)S(1)} %collective-permute-done.before_ref, f32[69,8,128]{2,1,0:T(8,128)S(1)} %collective-permute-done.1.after_ref, ...), custom_call_target="tpu_custom_call", output_to_operand_aliasing={{0}: (4, {})} | custom-call | bytes 26000000 | tf_op jit(solution)/shard_map/outer_planes/pallas_call | solution.py:460
  19.8 0.0 collective-permute-done.4.refs_3_
  19.9 2.1 %collective-permute-done.3.refs_2_ = f32[32,8,128]{2,1,0:T(8,128)S(1)} collective-permute-done((f32[32,8,128]{2,1,0:T(8,128)}, f32[32,8,128]{2,1,0:T(8,128)S(1)}, u32[]{:S(2)}, u32[]{:S(2)}) %collective-permute-start.3) | collective-permute-done | bytes 131104 | tf_op jit(solution)/shard_map/ppermute | solution.py:456
  21.9 0.1 collective-permute-done.2.refs_1_
  22.0 0.0 copy-done
  22.0 1.8 %store.1 = (f32[2048,128]{1,0:T(8,128)}, f32[4,32,8,128]{3,2,1,0:T(8,128)}) custom-call(f32[256,8,128]{2,1,0:T(8,128)S(1)} %get-tuple-element.21.u2_ref, f32[32,8,128]{2,1,0:T(8,128)S(1)} %copy-done, f32[32,8,128]{2,1,0:T(8,128)S(1)} %collective-permute-done.2.refs_1_, f32[32,8,128]{2,1,0:T(8,128)S(1)} %collective-permute-done.3.refs_2_, ...), custom_call_target="tpu_custom_call" | custom-call | bytes 8000000 | tf_op jit(solution)/shard_map/store/pallas_call | solution.py:479
  23.8 0.1 collective-permute-start.6
  23.9 6.0 %all-to-all-start = ((f32[32,2,8,128]{3,2,1,0:T(8,128)}), f32[32,2,8,128]{3,2,1,0:T(8,128)S(1)}, u32[]{:S(2)}, u32[]{:S(2)}) async-start(f32[32,2,8,128]{3,2,1,0:T(8,128)} %get-tuple-element.24), calls=%async_computation | async-start | bytes 524288 | tf_op jit(solution)/shard_map/all_to_all | solution.py:478
  29.9 2.7 %collective-permute-start.5 = (f32[4,8,128]{2,1,0:T(8,128)S(1)}, f32[4,8,128]{2,1,0:T(8,128)S(1)}, u32[]{:S(2)}, u32[]{:S(2)}) collective-permute-start(f32[4,8,128]{2,1,0:T(8,128)S(1)} %get-tuple-element.25.own_ref), channel_id=1, source_target_pairs={{0,16},{8,24},{16,0},{24,8},{1,17},{9,25},{17,1},{25,9},{2,18},{10... | collective-permute-start | bytes 49160 | tf_op jit(solution)/shard_map/ppermute | solution.py:424
  32.6 0.1 pad_add_fusion.place_ref
  33.3 0.0 collective-permute-done.6.other_hbm
  33.3 3.2 %split.1.split_hbm = bf16[32,128,128]{2,1,0:T(8,128)(2,1)} custom-call(s32[4]{0:T(128)S(1)} %pad_add_fusion.place_ref, f32[4,32,8,128]{3,2,1,0:T(8,128)} %get-tuple-element.26.same_hbm, f32[4,32,8,128]{3,2,1,0:T(8,128)S(1)} %collective-permute-done.6.other_hbm), custom_call_target="tpu_custom_call" | custom-call | bytes 5000000 | tf_op jit(solution)/shard_map/split/pallas_call | solution.py:492
  36.5 3.4 %collective-permute-done.5.before_2_ref.after_2_ref = f32[4,8,128]{2,1,0:T(8,128)S(1)} collective-permute-done((f32[4,8,128]{2,1,0:T(8,128)S(1)}, f32[4,8,128]{2,1,0:T(8,128)S(1)}, u32[]{:S(2)}, u32[]{:S(2)}) %collective-permute-start.5) | collective-permute-done | bytes 16416 | tf_op jit(solution)/shard_map/ppermute | solution.py:424
  39.9 1.1 %all-to-all-done.pred_ref = f32[32,2,8,128]{3,2,1,0:T(8,128)S(1)} async-done(((f32[32,2,8,128]{3,2,1,0:T(8,128)}), f32[32,2,8,128]{3,2,1,0:T(8,128)S(1)}, u32[]{:S(2)}, u32[]{:S(2)}) %all-to-all-start) | async-done | bytes 262176 | tf_op jit(solution)/shard_map/all_to_all | solution.py:478
  41.0 3.9 %update.1 = (f32[2048,128]{1,0:T(8,128)}, f32[8,256]{1,0:T(8,128)}) custom-call(s32[4]{0:T(128)S(1)} %pad_add_fusion.place_ref, s32[1]{0:T(128)S(6)} %copy.16.count_ref, s32[1,32]{1,0:T(1,128)} %cells_hbm.3, s32[1,32]{1,0:T(1,128)} %probes_hbm.1, s32[1,32]{1,0:T(1,128)} %level_hbm.1, f32[32,2,8,128]{3,2,1,0:T(8,128)S(1)} %all-to-all-done.pred_ref, ...), custom_call_target="tpu_custom_call" | custom-call | tf_op jit(solution)/shard_map/update/pallas_call | solution.py:502
Async XLA Ops:
  2.4 14.1 %collective-permute-start = (f32[69,8,128]{2,1,0:T(8,128)S(1)}, f32[69,8,128]{2,1,0:T(8,128)S(1)}, u32[]{:S(2)}, u32[]{:S(2)}) collective-permute-start(f32[69,8,128]{2,1,0:T(8,128)S(1)} %get-tuple-element.16), channel_id=1, source_target_pairs={{0,8},{8,16},{16,24},{1,9},{9,17},{17,25},{2,10},{10,18},{18,26},{... | collective-permute-start | bytes 847880 | tf_op jit(solution)/shard_map/ppermute | solution.py:421
  7.4 10.1 %collective-permute-start.1 = (f32[69,8,128]{2,1,0:T(8,128)S(1)}, f32[69,8,128]{2,1,0:T(8,128)S(1)}, u32[]{:S(2)}, u32[]{:S(2)}) collective-permute-start(f32[69,8,128]{2,1,0:T(8,128)S(1)} %get-tuple-element.17), channel_id=1, source_target_pairs={{8,0},{16,8},{24,16},{9,1},{17,9},{25,17},{10,2},{18,10},{26,18},{... | collective-permute-start | bytes 847880 | tf_op jit(solution)/shard_map/ppermute | solution.py:422
  13.0 6.9 %collective-permute-start.4 = (f32[32,8,128]{2,1,0:T(8,128)}, f32[32,8,128]{2,1,0:T(8,128)S(1)}, u32[]{:S(2)}, u32[]{:S(2)}) collective-permute-start(f32[32,8,128]{2,1,0:T(8,128)} %get-tuple-element.22.refs_0_), channel_id=1, source_target_pairs={{0,6},{2,4},{4,2},{6,0},{1,7},{3,5},{5,3},{7,1},{8,14},{10,12},{12... | collective-permute-start | bytes 393224 | tf_op jit(solution)/shard_map/ppermute | solution.py:456
  15.5 6.4 %collective-permute-start.3 = (f32[32,8,128]{2,1,0:T(8,128)}, f32[32,8,128]{2,1,0:T(8,128)S(1)}, u32[]{:S(2)}, u32[]{:S(2)}) collective-permute-start(f32[32,8,128]{2,1,0:T(8,128)} %get-tuple-element.22.refs_0_), channel_id=1, source_target_pairs={{0,4},{2,6},{4,0},{6,2},{1,5},{3,7},{5,1},{7,3},{8,12},{10,14},{12... | collective-permute-start | bytes 393224 | tf_op jit(solution)/shard_map/ppermute | solution.py:456
  16.0 6.0 %collective-permute-start.2 = (f32[32,8,128]{2,1,0:T(8,128)}, f32[32,8,128]{2,1,0:T(8,128)S(1)}, u32[]{:S(2)}, u32[]{:S(2)}) collective-permute-start(f32[32,8,128]{2,1,0:T(8,128)} %get-tuple-element.22.refs_0_), channel_id=1, source_target_pairs={{0,2},{2,0},{4,6},{6,4},{1,3},{3,1},{5,7},{7,5},{8,10},{10,8},{12,... | collective-permute-start | bytes 393224 | tf_op jit(solution)/shard_map/ppermute | solution.py:456
  17.5 4.5 %copy-start = (f32[32,8,128]{2,1,0:T(8,128)S(1)}, f32[32,8,128]{2,1,0:T(8,128)}, u32[]{:S(2)}) copy-start(f32[32,8,128]{2,1,0:T(8,128)} %get-tuple-element.22.refs_0_) | copy-start | bytes 393220
  23.8 9.5 %collective-permute-start.6 = (f32[4,32,8,128]{3,2,1,0:T(8,128)}, f32[4,32,8,128]{3,2,1,0:T(8,128)S(1)}, u32[]{:S(2)}, u32[]{:S(2)}) collective-permute-start(f32[4,32,8,128]{3,2,1,0:T(8,128)} %get-tuple-element.26.same_hbm), channel_id=1, source_target_pairs={{0,1},{1,0},{2,3},{3,2},{4,5},{5,4},{6,7},{7,6},{8,9},{9,8},{10,11... | collective-permute-start | bytes 1572872 | tf_op jit(solution)/shard_map/ppermute | solution.py:489
  23.9 17.1 %all-to-all-start = ((f32[32,2,8,128]{3,2,1,0:T(8,128)}), f32[32,2,8,128]{3,2,1,0:T(8,128)S(1)}, u32[]{:S(2)}, u32[]{:S(2)}) async-start(f32[32,2,8,128]{3,2,1,0:T(8,128)} %get-tuple-element.24), calls=%async_computation | async-start | bytes 524288 | tf_op jit(solution)/shard_map/all_to_all | solution.py:478
  29.9 10.1 %collective-permute-start.5 = (f32[4,8,128]{2,1,0:T(8,128)S(1)}, f32[4,8,128]{2,1,0:T(8,128)S(1)}, u32[]{:S(2)}, u32[]{:S(2)}) collective-permute-start(f32[4,8,128]{2,1,0:T(8,128)S(1)} %get-tuple-element.25.own_ref), channel_id=1, source_target_pairs={{0,16},{8,24},{16,0},{24,8},{1,17},{9,25},{17,1},{25,9},{2,18},{10... | collective-permute-start | bytes 49160 | tf_op jit(solution)/shard_map/ppermute | solution.py:424

commit v8 on v7

--- a/solution.py
+++ b/solution.py
@@ -207,11 +207,15 @@
 
 
 def outer_kernel(planes, tiles, probe_hbm, before_ref, after_ref, edge_ref, inner_ref,
-                 u2_ref, sent_hbm, probe_ref, found_ref, sems):
+                 u2_ref, sent_hbm, seen_ref, probe_ref, found_ref, sems):
     probe_copy = pltpu.make_async_copy(probe_hbm, probe_ref, sems.at[0])
     probe_copy.start()
     masks = lane_masks()
     blocks = probe_ref.shape[0] // LANES
+    count = seen_ref.shape[0] // 2
+    for at in range(count):
+        seen_ref[at] = before_ref[4 * tiles + 1 + at]
+        seen_ref[count + at] = after_ref[4 * tiles + 1 + at]
     edge = [plane_of(edge_ref, at, tiles) for at in range(14)]
     last = planes - 1
     for ref, own_u, own_v, own_1, where in (
@@ -254,10 +258,7 @@
 
 
 def store_kernel(planes, tiles, u2_ref, *refs):
-    *parts, out_ref, same_hbm, sems = refs
-    copies = [pltpu.make_async_copy(part, same_hbm.at[at], sems.at[at]) for at, part in enumerate(parts)]
-    for copy in copies:
-        copy.start()
+    out_ref = refs[len(refs) // 2]
 
     def store(x):
         for tile in range(tiles):
@@ -265,18 +266,20 @@
             out_ref[rows, :] = u2_ref[x * tiles + tile]
 
     each(0, planes, 4, store)
-    for copy in copies:
-        copy.wait()
-
-
-def split_kernel(by_xor, place_ref, same_hbm, other_hbm, split_ref, theta_ref, sems):
+
+
+def split_kernel(by_xor, chips, place_ref, *refs):
+    *parts, split_ref, theta_ref, sems = refs
     chip, core = place_ref[2], place_ref[3]
+    same, other = parts[: len(parts) // 2], parts[len(parts) // 2 :]
+    if not by_xor:
+        same, other = ([ref.at[at] for at in range(chips)] for (ref,) in (same, other))
     members = 2 * theta_ref.shape[0] * ROWS
     copies = []
-    for at in range(same_hbm.shape[0]):
+    for at in range(chips):
         where = chip ^ at if by_xor else at
-        copies.append(pltpu.make_async_copy(same_hbm.at[at], theta_ref.at[where, core], sems.at[2 * at]))
-        copies.append(pltpu.make_async_copy(other_hbm.at[at], theta_ref.at[where, 1 - core], sems.at[2 * at + 1]))
+        copies.append(pltpu.make_async_copy(same[at], theta_ref.at[where, core], sems.at[2 * at]))
+        copies.append(pltpu.make_async_copy(other[at], theta_ref.at[where, 1 - core], sems.at[2 * at + 1]))
     for copy in copies:
         copy.start()
     for copy in copies:
@@ -304,7 +307,7 @@
 
 
 def update_kernel(slabs, planes, tiles, place_ref, count_ref, cells_hbm, probes_hbm, level_hbm,
-                  pred_ref, before_2_ref, before_ref, own_ref, after_ref, after_2_ref, split_hbm, t_hbm,
+                  pred_ref, before_2_ref, seen_ref, own_ref, after_2_ref, split_hbm, t_hbm,
                   post_ref, gain_ref, reach, cells_ref, probes_ref, level_ref, split_ref, sems):
     groups, blocks = pred_ref.shape[0] // slabs, pred_ref.shape[1]
     members = groups * ROWS
@@ -318,8 +321,7 @@
     for copy in copies:
         copy.start()
     slab, group = place_ref[0], place_ref[1]
-    halo = 4 * tiles + 1
-    seen = ((before_2_ref, 0), (before_ref, halo), (own_ref, 0), (after_ref, halo), (after_2_ref, 0))
+    seen = ((before_2_ref, 0), (seen_ref, 0), (own_ref, 0), (seen_ref, seen_ref.shape[0] // 2), (after_2_ref, 0))
 
     def extra(d, at):
         ref, first = seen[d]
@@ -417,6 +419,7 @@
         compiler_params=params,
         name="pack",
     )(*map(stay, (probe_taper, u_rows, t_rows, obs_noise, observed.reshape(1, -1), obs_var.reshape(1, -1))))
+    little = pl.CostEstimate(flops=1000, bytes_accessed=1000, transcendentals=0)
     upward = [(i, i + 1) for i in range(slabs - 1)]
     before = lax.ppermute(high, "space", upward)
     after = lax.ppermute(low, "space", [(j, i) for i, j in upward])
@@ -455,16 +458,16 @@
         for d in range(1, chips):
             parts.append(lax.ppermute(picked, "chip", [(i, i ^ d) for i in range(chips)]))
     else:
-        spread = lax.all_to_all(jnp.broadcast_to(picked, (chips, *picked.shape)), "chip", 0, 0)
-        parts = [spread[i] for i in range(chips)]
-    u2, sent = pl.pallas_call(
+        parts = [lax.all_to_all(jnp.broadcast_to(picked, (chips, *picked.shape)), "chip", 0, 0)]
+    u2, sent, seen = pl.pallas_call(
         functools.partial(outer_kernel, planes, tiles),
         out_shape=(
             jax.ShapeDtypeStruct((planes * tiles, ROWS, LANES), f32),
             pltpu.HBM((slabs * groups, blocks, ROWS, LANES), f32),
+            jax.ShapeDtypeStruct((2 * obs_tiles, ROWS, LANES), f32),
         ),
         in_specs=[HBM] + [VMEM] * 4,
-        out_specs=(VMEM, HBM),
+        out_specs=(VMEM, HBM, VMEM),
         scratch_shapes=[
             pltpu.SMEM(probe_cells.shape, i32),
             pltpu.VMEM((blocks, ROWS, LANES), f32),
@@ -476,36 +479,36 @@
         name="outer_planes",
     )(stay(probe_cells), before, after, edges, inner)
     pred_all = lax.all_to_all(sent, ("space", "chip", "core"), 0, 0)
-    u2_rows, theta_same = pl.pallas_call(
+    u2_rows, *parts = pl.pallas_call(
         functools.partial(store_kernel, planes, tiles),
-        out_shape=(jax.ShapeDtypeStruct(u_rows.shape, f32), pltpu.HBM((chips, slots, ROWS, LANES), f32)),
-        in_specs=[VMEM] + [ANY] * chips,
-        out_specs=(VMEM, HBM),
-        scratch_shapes=[pltpu.SemaphoreType.DMA((chips,))],
+        out_shape=(jax.ShapeDtypeStruct(u_rows.shape, f32), *(jax.ShapeDtypeStruct(part.shape, f32) for part in parts)),
+        in_specs=[VMEM] + [ANY] * len(parts),
+        out_specs=(VMEM,) + (ANY,) * len(parts),
+        input_output_aliases={1 + at: 1 + at for at in range(len(parts))},
         compiler_params=params,
-        cost_estimate=pl.CostEstimate(flops=0, bytes_accessed=8_000_000, transcendentals=0),
+        cost_estimate=little,
         name="store",
     )(u2, *parts)
-    theta_other = lax.ppermute(theta_same, "core", [(0, 1), (1, 0)])
+    swapped = [lax.ppermute(part, "core", [(0, 1), (1, 0)]) for part in parts]
     where = [lax.axis_index(axes) for axes in ("space", ("chip", "core"), "chip", "core")]
     place = jnp.stack(where).astype(i32)
     split = pl.pallas_call(
-        functools.partial(split_kernel, by_xor),
+        functools.partial(split_kernel, by_xor, chips),
         out_shape=pltpu.HBM((slots, 2 * groups * ROWS, LANES), jnp.bfloat16),
-        in_specs=[SMEM, HBM, ANY],
+        in_specs=[SMEM] + [ANY] * (2 * len(parts)),
         out_specs=VMEM,
         scratch_shapes=[pltpu.VMEM((chips, 2, slots, ROWS, LANES), f32), pltpu.SemaphoreType.DMA((2 * chips,))],
         compiler_params=params,
-        cost_estimate=pl.CostEstimate(flops=0, bytes_accessed=5_000_000, transcendentals=0),
+        cost_estimate=little,
         name="split",
-    )(place, stay(theta_same), theta_other)
+    )(place, *parts, *swapped)
     post_rows, gain = pl.pallas_call(
         functools.partial(update_kernel, slabs, planes, tiles),
         out_shape=(
             jax.ShapeDtypeStruct(u_rows.shape, f32),
             jax.ShapeDtypeStruct((members, probes), f32),
         ),
-        in_specs=[SMEM] * 2 + [HBM] * 3 + [VMEM] * 6 + [HBM] * 2,
+        in_specs=[SMEM] * 2 + [HBM] * 3 + [VMEM] * 5 + [HBM] * 2,
         out_specs=(VMEM,) * 2,
         scratch_shapes=[
             pltpu.VMEM((probe_taper.shape[2], 2 * ROWS, 2 * groups * ROWS), jnp.bfloat16),
@@ -518,7 +521,7 @@
         compiler_params=params,
         name="update",
     )(place, pair_counts, *map(stay, (pair_cells, pair_probes, pair_taper)), pred_all,
-      before_2, before, obs, after, after_2, stay(split), stay(t_rows))
+      before_2, seen, obs, after_2, stay(split), stay(t_rows))
     return (from_rows(u2_rows, shape), from_rows(post_rows, shape), gain)
 
 

time: 45.2 us -> 50.5 us (1.12)
  waiting for transfers between devices: 7.53 us -> 13.2 us
  starting transfers between devices: 18.6 us -> 18 us
    ppermute x3, waiting for transfers between devices: 2.14 us -> 8.67 us  [shards(): lax.ppermute(picked, 'chip', [(i, i ^ d) for i in range(chips)])]
    ppermute x1, waiting for transfers between devices: 3.39 us -> 0.01 us  [shards(): lax.ppermute(obs, 'space', [(i, (i + 2) % 4) for i in range(4)])]
    ppermute x1, waiting for transfers between devices: 0.93 us -> 4.13 us  [shards(): after = lax.ppermute(low, 'space', [(j, i) for i, j in upward])]
    all_to_all x1, starting transfers between devices: 5.97 us -> 4.83 us  [shards(): pred_all = lax.all_to_all(sent, ('space', 'chip', 'core'), 0, 0)]
    all_to_all x1, waiting for transfers between devices: 1.07 us -> 0.01 us  [shards(): pred_all = lax.all_to_all(sent, ('space', 'chip', 'core'), 0, 0)]
    ppermute x1 -> x4, starting transfers between devices: 0.07 us -> 1.02 us  [shards(): swapped = [lax.ppermute(part, 'core', [(0, 1), (1, 0)]) for part in parts]]
    pallas_call x1, Pallas kernels: 2.37 us -> 2.91 us  [shards(): pl.pallas_call(functools.partial(outer_kernel, planes, tiles), out_shape=...]
  transfers between devices with their start and end apart: 8 -> 11, of which waited for: 5 -> 5; matrix products, arithmetic and copies ran while one was open for 0% -> 0% of each run, Pallas kernels for 22% -> 18%
where the time goes in v8:
time: 50.5 us; the launch traced here: 50.1 us
  starting transfers between devices  18 us (36%)
  Pallas kernels  17.5 us (35%)
  waiting for transfers between devices  13.2 us (26%)
  between operations  1.41 us (3%)
    ppermute x3, waiting for transfers between devices, shards(): lax.ppermute(picked, 'chip', [(i, i ^ d) for i in range(chips)])  8.67 us
    ppermute x1, starting transfers between devices, shards(): before = lax.ppermute(high, 'space', upward)  4.95 us
    all_to_all x1, starting transfers between devices, shards(): pred_all = lax.all_to_all(sent, ('space', 'chip', 'core'), 0, 0)  4.83 us
    pallas_call x1, Pallas kernels, shards(): pl.pallas_call(functools.partial(inner_kernel, planes, tiles), out_shape=...  4.31 us
    ppermute x1, waiting for transfers between devices, shards(): after = lax.ppermute(low, 'space', [(j, i) for i, j in upward])  4.13 us
    pallas_call x1, Pallas kernels, shards(): pl.pallas_call(functools.partial(update_kernel, slabs, planes, tiles), ou...  3.81 us
    ppermute x3, starting transfers between devices, shards(): lax.ppermute(picked, 'chip', [(i, i ^ d) for i in range(chips)])  3.55 us
    pallas_call x1, Pallas kernels, shards(): pl.pallas_call(functools.partial(split_kernel, by_xor, chips), out_shape=...  3.11 us
  transfers between devices with their start and end apart: 11, of which 5 were waited for; matrix products, arithmetic and copies ran while one was open for 0% of the time, Pallas kernels for 18%

profile of v8, /device:TPU:0, one launch (start us, length us, event | category | flops | bytes accessed | tf_op | source)
XLA Modules:
  0.0 50.1 jit_solution(10096556693819214025)
XLA Ops:
  0.6 1.8 %pack.1 = (f32[69,8,128]{2,1,0:T(8,128)S(1)}, f32[69,8,128]{2,1,0:T(8,128)S(1)}, f32[4,8,128]{2,1,0:T(8,128)S(1)}, f32[2048,128]{1,0:T(8,128)S(1)}) custom-call(s32[1,2,6]{2,1,0:T(2,128)} %taper_hbm.1, f32[2048,128]{1,0:T(8,128)} %bitcast.26, f32[2048,128]{1,0:T(8,128)} %bitcast.28, f32[8,256]{1,0:T(8,128)} %noise_hbm.1, f32[1,256]{1,0:T(1,128)} %bitcast.30, ...), custom_call_target="tpu_custom_call" | custom-call | tf_op jit(solution)/shard_map/pack/pallas_call | solution.py:402
  2.4 4.9 %collective-permute-start = (f32[69,8,128]{2,1,0:T(8,128)S(1)}, f32[69,8,128]{2,1,0:T(8,128)S(1)}, u32[]{:S(2)}, u32[]{:S(2)}) collective-permute-start(f32[69,8,128]{2,1,0:T(8,128)S(1)} %get-tuple-element.20), channel_id=1, source_target_pairs={{0,8},{8,16},{16,24},{1,9},{9,17},{17,25},{2,10},{10,18},{18,26},{... | collective-permute-start | bytes 847880 | tf_op jit(solution)/shard_map/ppermute | solution.py:424
  7.4 1.3 %collective-permute-start.1 = (f32[69,8,128]{2,1,0:T(8,128)S(1)}, f32[69,8,128]{2,1,0:T(8,128)S(1)}, u32[]{:S(2)}, u32[]{:S(2)}) collective-permute-start(f32[69,8,128]{2,1,0:T(8,128)S(1)} %get-tuple-element.21), channel_id=1, source_target_pairs={{8,0},{16,8},{24,16},{9,1},{17,9},{25,17},{10,2},{18,10},{26,18},{... | collective-permute-start | bytes 847880 | tf_op jit(solution)/shard_map/ppermute | solution.py:425
  8.7 4.3 %inner_planes.1 = (f32[256,8,128]{2,1,0:T(8,128)S(1)}, f32[224,8,128]{2,1,0:T(8,128)S(1)}, f32[32,8,128]{2,1,0:T(8,128)}) custom-call(f32[2048,128]{1,0:T(8,128)} %bitcast.27, s32[1,32]{1,0:T(1,128)} %cells_hbm.3, f32[2048,128]{1,0:T(8,128)S(1)} %get-tuple-element.22.t_ref), custom_call_target="tpu_custom_call" | custom-call | bytes 15000000 | tf_op jit(solution)/shard_map/inner_planes/pallas_call | solution.py:432
  13.0 0.4 collective-permute-done.before_ref
  13.3 4.1 %collective-permute-done.1.after_ref = f32[69,8,128]{2,1,0:T(8,128)S(1)} collective-permute-done((f32[69,8,128]{2,1,0:T(8,128)S(1)}, f32[69,8,128]{2,1,0:T(8,128)S(1)}, u32[]{:S(2)}, u32[]{:S(2)}) %collective-permute-start.1) | collective-permute-done | bytes 282656 | tf_op jit(solution)/shard_map/ppermute | solution.py:425
  17.5 2.9 %outer_planes.1 = (f32[256,8,128]{2,1,0:T(8,128)S(1)}, f32[32,2,8,128]{3,2,1,0:T(8,128)}, f32[8,8,128]{2,1,0:T(8,128)S(1)}) custom-call(s32[256]{0:T(256)} %probe_hbm.1, f32[69,8,128]{2,1,0:T(8,128)S(1)} %collective-permute-done.before_ref, f32[69,8,128]{2,1,0:T(8,128)S(1)} %collective-permute-done.1.after_ref, ...), custom_call_target="tpu_custom_call", output_to_operand_aliasing={{0}: (4, {})} | custom-call | bytes 26000000 | tf_op jit(solution)/shard_map/outer_planes/pallas_call | solution.py:462
  20.4 0.0 copy-start
  20.4 4.8 %all-to-all-start = ((f32[32,2,8,128]{3,2,1,0:T(8,128)}), f32[32,2,8,128]{3,2,1,0:T(8,128)S(1)}, u32[]{:S(2)}, u32[]{:S(2)}) async-start(f32[32,2,8,128]{3,2,1,0:T(8,128)} %get-tuple-element.28), calls=%async_computation | async-start | bytes 524288 | tf_op jit(solution)/shard_map/all_to_all | solution.py:481
  25.2 0.0 copy-done
  25.2 1.8 %collective-permute-start.2 = (f32[32,8,128]{2,1,0:T(8,128)S(1)}, f32[32,8,128]{2,1,0:T(8,128)S(1)}, u32[]{:S(2)}, u32[]{:S(2)}) collective-permute-start(f32[32,8,128]{2,1,0:T(8,128)S(1)} %copy-done), channel_id=1, source_target_pairs={{0,2},{2,0},{4,6},{6,4},{1,3},{3,1},{5,7},{7,5},{8,10},{10,8},{12,... | collective-permute-start | bytes 393224 | tf_op jit(solution)/shard_map/ppermute | solution.py:459
  27.1 1.5 %collective-permute-start.3 = (f32[32,8,128]{2,1,0:T(8,128)S(1)}, f32[32,8,128]{2,1,0:T(8,128)S(1)}, u32[]{:S(2)}, u32[]{:S(2)}) collective-permute-start(f32[32,8,128]{2,1,0:T(8,128)S(1)} %copy-done), channel_id=1, source_target_pairs={{0,4},{2,6},{4,0},{6,2},{1,5},{3,7},{5,1},{7,3},{8,12},{10,14},{12... | collective-permute-start | bytes 393224 | tf_op jit(solution)/shard_map/ppermute | solution.py:459
  28.5 0.3 collective-permute-start.4
  28.8 5.1 %collective-permute-done.2.refs_1_ = f32[32,8,128]{2,1,0:T(8,128)S(1)} collective-permute-done((f32[32,8,128]{2,1,0:T(8,128)S(1)}, f32[32,8,128]{2,1,0:T(8,128)S(1)}, u32[]{:S(2)}, u32[]{:S(2)}) %collective-permute-start.2) | collective-permute-done | bytes 131104 | tf_op jit(solution)/shard_map/ppermute | solution.py:459
  33.9 0.5 %collective-permute-done.3.refs_2_ = f32[32,8,128]{2,1,0:T(8,128)S(1)} collective-permute-done((f32[32,8,128]{2,1,0:T(8,128)S(1)}, f32[32,8,128]{2,1,0:T(8,128)S(1)}, u32[]{:S(2)}, u32[]{:S(2)}) %collective-permute-start.3) | collective-permute-done | bytes 131104 | tf_op jit(solution)/shard_map/ppermute | solution.py:459
  34.4 3.0 %collective-permute-done.4.refs_3_ = f32[32,8,128]{2,1,0:T(8,128)S(1)} collective-permute-done((f32[32,8,128]{2,1,0:T(8,128)S(1)}, f32[32,8,128]{2,1,0:T(8,128)S(1)}, u32[]{:S(2)}, u32[]{:S(2)}) %collective-permute-start.4) | collective-permute-done | bytes 131104 | tf_op jit(solution)/shard_map/ppermute | solution.py:459
  37.5 1.6 %store.1 = (f32[2048,128]{1,0:T(8,128)}, f32[32,8,128]{2,1,0:T(8,128)S(1)}, f32[32,8,128]{2,1,0:T(8,128)S(1)}, f32[32,8,128]{2,1,0:T(8,128)S(1)}, f32[32,8,128]{2,1,0:T(8,128)S(1)}) custom-call(f32[256,8,128]{2,1,0:T(8,128)S(1)} %get-tuple-element.25.u2_ref, ...), custom_call_target="tpu_custom_call", output_to_operand_aliasing={{1}: (1, {}), {2}: (2, {}), {3}: (3, {}), {4}: (4, {})} | custom-call | flops 1000 | bytes 1000 | tf_op jit(solution)/shard_map/store/pallas_call | solution.py:482
  39.1 0.0 collective-permute-start.6
  39.1 0.5 %collective-permute-start.7 = (f32[32,8,128]{2,1,0:T(8,128)S(1)}, f32[32,8,128]{2,1,0:T(8,128)S(1)}, u32[]{:S(2)}, u32[]{:S(2)}) collective-permute-start(f32[32,8,128]{2,1,0:T(8,128)S(1)} %get-tuple-element.32.refs_1_), channel_id=1, source_target_pairs={{0,1},{1,0},{2,3},{3,2},{4,5},{5,4},{6,7},{7,6},{8,9},{9,8},{10,11... | collective-permute-start | bytes 393224 | tf_op jit(solution)/shard_map/ppermute | solution.py:492
  39.6 0.0 collective-permute-start.8
  39.6 0.5 %collective-permute-start.9 = (f32[32,8,128]{2,1,0:T(8,128)S(1)}, f32[32,8,128]{2,1,0:T(8,128)S(1)}, u32[]{:S(2)}, u32[]{:S(2)}) collective-permute-start(f32[32,8,128]{2,1,0:T(8,128)S(1)} %get-tuple-element.34.refs_3_), channel_id=1, source_target_pairs={{0,1},{1,0},{2,3},{3,2},{4,5},{5,4},{6,7},{7,6},{8,9},{9,8},{10,11... | collective-permute-start | bytes 393224 | tf_op jit(solution)/shard_map/ppermute | solution.py:492
  40.1 2.3 %collective-permute-start.5 = (f32[4,8,128]{2,1,0:T(8,128)S(1)}, f32[4,8,128]{2,1,0:T(8,128)S(1)}, u32[]{:S(2)}, u32[]{:S(2)}) collective-permute-start(f32[4,8,128]{2,1,0:T(8,128)S(1)} %get-tuple-element.29.own_ref), channel_id=1, source_target_pairs={{0,16},{8,24},{16,0},{24,8},{1,17},{9,25},{17,1},{25,9},{2,18},{10... | collective-permute-start | bytes 49160 | tf_op jit(solution)/shard_map/ppermute | solution.py:427
  42.4 0.1 pad_add_fusion.place_ref
  43.2 0.0 collective-permute-done.6.refs_4_
  43.2 0.0 collective-permute-done.7.refs_5_
  43.2 0.0 collective-permute-done.8.refs_6_
  43.2 0.0 collective-permute-done.9.refs_7_
  43.2 3.1 %split.1.split_hbm = bf16[32,128,128]{2,1,0:T(8,128)(2,1)} custom-call(s32[4]{0:T(128)S(1)} %pad_add_fusion.place_ref, f32[32,8,128]{2,1,0:T(8,128)S(1)} %get-tuple-element.31.refs_0_, f32[32,8,128]{2,1,0:T(8,128)S(1)} %get-tuple-element.32.refs_1_, f32[32,8,128]{2,1,0:T(8,128)S(1)} %get-tuple-element.33.refs_2_, ...), custom_call_target="tpu_custom_call" | custom-call | flops 1000 | bytes 1000 | tf_op jit(solution)/shard_map/split/pallas_call | solution.py:495
  46.3 0.0 collective-permute-done.5.before_2_ref.after_2_ref
  46.3 0.0 all-to-all-done.pred_ref
  46.3 3.8 %update.1 = (f32[2048,128]{1,0:T(8,128)}, f32[8,256]{1,0:T(8,128)}) custom-call(s32[4]{0:T(128)S(1)} %pad_add_fusion.place_ref, s32[1]{0:T(128)S(6)} %copy.24.count_ref, s32[1,32]{1,0:T(1,128)} %cells_hbm.3, s32[1,32]{1,0:T(1,128)} %probes_hbm.1, s32[1,32]{1,0:T(1,128)} %level_hbm.1, f32[32,2,8,128]{3,2,1,0:T(8,128)S(1)} %all-to-all-done.pred_ref, ...), custom_call_target="tpu_custom_call" | custom-call | tf_op jit(solution)/shard_map/update/pallas_call | solution.py:505
Async XLA Ops:
  2.4 10.9 %collective-permute-start = (f32[69,8,128]{2,1,0:T(8,128)S(1)}, f32[69,8,128]{2,1,0:T(8,128)S(1)}, u32[]{:S(2)}, u32[]{:S(2)}) collective-permute-start(f32[69,8,128]{2,1,0:T(8,128)S(1)} %get-tuple-element.20), channel_id=1, source_target_pairs={{0,8},{8,16},{16,24},{1,9},{9,17},{17,25},{2,10},{10,18},{18,26},{... | collective-permute-start | bytes 847880 | tf_op jit(solution)/shard_map/ppermute | solution.py:424
  7.4 10.1 %collective-permute-start.1 = (f32[69,8,128]{2,1,0:T(8,128)S(1)}, f32[69,8,128]{2,1,0:T(8,128)S(1)}, u32[]{:S(2)}, u32[]{:S(2)}) collective-permute-start(f32[69,8,128]{2,1,0:T(8,128)S(1)} %get-tuple-element.21), channel_id=1, source_target_pairs={{8,0},{16,8},{24,16},{9,1},{17,9},{25,17},{10,2},{18,10},{26,18},{... | collective-permute-start | bytes 847880 | tf_op jit(solution)/shard_map/ppermute | solution.py:425
  20.4 4.9 %copy-start = (f32[32,8,128]{2,1,0:T(8,128)S(1)}, f32[32,8,128]{2,1,0:T(8,128)}, u32[]{:S(2)}) copy-start(f32[32,8,128]{2,1,0:T(8,128)} %get-tuple-element.26.refs_0_) | copy-start | bytes 393220
  20.4 25.9 %all-to-all-start = ((f32[32,2,8,128]{3,2,1,0:T(8,128)}), f32[32,2,8,128]{3,2,1,0:T(8,128)S(1)}, u32[]{:S(2)}, u32[]{:S(2)}) async-start(f32[32,2,8,128]{3,2,1,0:T(8,128)} %get-tuple-element.28), calls=%async_computation | async-start | bytes 524288 | tf_op jit(solution)/shard_map/all_to_all | solution.py:481
  25.2 8.7 %collective-permute-start.2 = (f32[32,8,128]{2,1,0:T(8,128)S(1)}, f32[32,8,128]{2,1,0:T(8,128)S(1)}, u32[]{:S(2)}, u32[]{:S(2)}) collective-permute-start(f32[32,8,128]{2,1,0:T(8,128)S(1)} %copy-done), channel_id=1, source_target_pairs={{0,2},{2,0},{4,6},{6,4},{1,3},{3,1},{5,7},{7,5},{8,10},{10,8},{12,... | collective-permute-start | bytes 393224 | tf_op jit(solution)/shard_map/ppermute | solution.py:459
  27.1 7.4 %collective-permute-start.3 = (f32[32,8,128]{2,1,0:T(8,128)S(1)}, f32[32,8,128]{2,1,0:T(8,128)S(1)}, u32[]{:S(2)}, u32[]{:S(2)}) collective-permute-start(f32[32,8,128]{2,1,0:T(8,128)S(1)} %copy-done), channel_id=1, source_target_pairs={{0,4},{2,6},{4,0},{6,2},{1,5},{3,7},{5,1},{7,3},{8,12},{10,14},{12... | collective-permute-start | bytes 393224 | tf_op jit(solution)/shard_map/ppermute | solution.py:459
  28.5 8.9 %collective-permute-start.4 = (f32[32,8,128]{2,1,0:T(8,128)S(1)}, f32[32,8,128]{2,1,0:T(8,128)S(1)}, u32[]{:S(2)}, u32[]{:S(2)}) collective-permute-start(f32[32,8,128]{2,1,0:T(8,128)S(1)} %copy-done), channel_id=1, source_target_pairs={{0,6},{2,4},{4,2},{6,0},{1,7},{3,5},{5,3},{7,1},{8,14},{10,12},{12... | collective-permute-start | bytes 393224 | tf_op jit(solution)/shard_map/ppermute | solution.py:459
  39.1 4.1 %collective-permute-start.6 = (f32[32,8,128]{2,1,0:T(8,128)S(1)}, f32[32,8,128]{2,1,0:T(8,128)S(1)}, u32[]{:S(2)}, u32[]{:S(2)}) collective-permute-start(f32[32,8,128]{2,1,0:T(8,128)S(1)} %get-tuple-element.31.refs_0_), channel_id=1, source_target_pairs={{0,1},{1,0},{2,3},{3,2},{4,5},{5,4},{6,7},{7,6},{8,9},{9,8},{10,11... | collective-permute-start | bytes 393224 | tf_op jit(solution)/shard_map/ppermute | solution.py:492
  39.1 4.1 %collective-permute-start.7 = (f32[32,8,128]{2,1,0:T(8,128)S(1)}, f32[32,8,128]{2,1,0:T(8,128)S(1)}, u32[]{:S(2)}, u32[]{:S(2)}) collective-permute-start(f32[32,8,128]{2,1,0:T(8,128)S(1)} %get-tuple-element.32.refs_1_), channel_id=1, source_target_pairs={{0,1},{1,0},{2,3},{3,2},{4,5},{5,4},{6,7},{7,6},{8,9},{9,8},{10,11... | collective-permute-start | bytes 393224 | tf_op jit(solution)/shard_map/ppermute | solution.py:492
  39.6 3.6 %collective-permute-start.8 = (f32[32,8,128]{2,1,0:T(8,128)S(1)}, f32[32,8,128]{2,1,0:T(8,128)S(1)}, u32[]{:S(2)}, u32[]{:S(2)}) collective-permute-start(f32[32,8,128]{2,1,0:T(8,128)S(1)} %get-tuple-element.33.refs_2_), channel_id=1, source_target_pairs={{0,1},{1,0},{2,3},{3,2},{4,5},{5,4},{6,7},{7,6},{8,9},{9,8},{10,11... | collective-permute-start | bytes 393224 | tf_op jit(solution)/shard_map/ppermute | solution.py:492
  39.6 3.6 %collective-permute-start.9 = (f32[32,8,128]{2,1,0:T(8,128)S(1)}, f32[32,8,128]{2,1,0:T(8,128)S(1)}, u32[]{:S(2)}, u32[]{:S(2)}) collective-permute-start(f32[32,8,128]{2,1,0:T(8,128)S(1)} %get-tuple-element.34.refs_3_), channel_id=1, source_target_pairs={{0,1},{1,0},{2,3},{3,2},{4,5},{5,4},{6,7},{7,6},{8,9},{9,8},{10,11... | collective-permute-start | bytes 393224 | tf_op jit(solution)/shard_map/ppermute | solution.py:492
  40.1 6.2 %collective-permute-start.5 = (f32[4,8,128]{2,1,0:T(8,128)S(1)}, f32[4,8,128]{2,1,0:T(8,128)S(1)}, u32[]{:S(2)}, u32[]{:S(2)}) collective-permute-start(f32[4,8,128]{2,1,0:T(8,128)S(1)} %get-tuple-element.29.own_ref), channel_id=1, source_target_pairs={{0,16},{8,24},{16,0},{24,8},{1,17},{9,25},{17,1},{25,9},{2,18},{10... | collective-permute-start | bytes 49160 | tf_op jit(solution)/shard_map/ppermute | solution.py:427

commit v9 on v8

--- a/solution.py
+++ b/solution.py
@@ -38,8 +38,9 @@
     return (plane // ROWS * tiles + tile) * ROWS + plane % ROWS
 
 
-def pack_kernel(planes, tiles, taper_hbm, u_hbm, t_hbm, noise_hbm, observed_hbm, var_hbm,
-                low_ref, high_ref, obs_ref, t_ref, taper_ref, u_ref, noise_ref, row_ref, sems):
+def pack_kernel(planes, tiles, taper_hbm, u_hbm, t_hbm, noise_hbm, observed_hbm, var_hbm, cells_hbm,
+                low_ref, high_ref, obs_ref, t_ref, pick_hbm,
+                taper_ref, u_ref, noise_ref, row_ref, cells_ref, pick_ref, sems):
     stride = planes * tiles
     blocks = noise_ref.shape[1] // LANES
     copies = [
@@ -51,12 +52,22 @@
             (noise_hbm, noise_ref),
             (observed_hbm, row_ref.at[0:1]),
             (var_hbm, row_ref.at[1:2]),
+            (cells_hbm, cells_ref),
         ))
     ]
     for copy in copies:
         copy.start()
+    copies[0].wait()
+    copies[6].wait()
+    for slot in range(pick_ref.shape[0]):
+        block = cells_ref[0, slot]
+        row = row_of(block // tiles, block % tiles, tiles)
+        pick_ref[slot] = t_ref[pl.ds(row, ROWS, stride=stride), :]
+    picked = pltpu.make_async_copy(pick_ref, pick_hbm, sems.at[7])
+    picked.start()
     for kind, source in ((1, t_ref), (0, u_ref)):
-        copies[1 - kind].wait()
+        if kind == 0:
+            copies[1].wait()
         for out_ref, first in ((high_ref, planes - 2), (low_ref, 0)):
             for depth in range(2):
                 for tile in range(tiles):
@@ -65,7 +76,7 @@
                     ]
     for ref in (low_ref, high_ref):
         ref[4 * tiles] = jnp.ones((ROWS, LANES), jnp.float32)
-    for copy in copies[2:]:
+    for copy in copies[2:6]:
         copy.wait()
     own, window = taper_ref.shape[1:]
     rows = [row_ref[kind : kind + 1, b * LANES : (b + 1) * LANES] for kind in range(2) for b in range(blocks)]
@@ -79,6 +90,7 @@
     for ref in (low_ref, high_ref):
         for at in range(obs_ref.shape[0]):
             ref[4 * tiles + 1 + at] = obs_ref[at]
+    picked.wait()
 
 
 def rot(value, by):
@@ -149,14 +161,10 @@
         body(x)
 
 
-def inner_kernel(planes, tiles, u_hbm, cells_hbm, t_ref, u2_ref, edge_ref, pick_hbm,
-                 u_ref, u0, hv, u1, held, cells_ref, pick_ref, sems):
+def inner_kernel(planes, tiles, u_hbm, t_ref, u2_ref, edge_ref, u_ref, u0, hv, u1, held, sem):
     stride = planes * tiles
     masks = lane_masks()
-    copy = pltpu.make_async_copy(u_hbm, u_ref, sems.at[0])
-    cells_copy = pltpu.make_async_copy(cells_hbm, cells_ref, sems.at[1])
-    picked = pltpu.make_async_copy(pick_ref, pick_hbm, sems.at[2])
-    cells_copy.start()
+    copy = pltpu.make_async_copy(u_hbm, u_ref, sem)
     copy.start()
 
     def rows_at(x, tile):
@@ -186,12 +194,6 @@
         put(u2_ref, x, step(masks, weights, *[plane_of(u1, x + d, tiles) for d in (-1, 0, 1)]))
 
     each(0, planes, 4, load_t)
-    cells_copy.wait()
-    for slot in range(pick_ref.shape[0]):
-        block = cells_ref[0, slot]
-        row = row_of(block // tiles, block % tiles, tiles)
-        pick_ref[slot] = t_ref[pl.ds(row, ROWS, stride=stride), :]
-    picked.start()
     copy.wait()
     each(0, planes, 4, load_u)
     each(1, planes - 1, 7, first_step)
@@ -203,12 +205,11 @@
         for x in kept:
             put(edge_ref, at, plane_of(ref, x, tiles))
             at += 1
-    picked.wait()
 
 
 def outer_kernel(planes, tiles, probe_hbm, before_ref, after_ref, edge_ref, inner_ref,
-                 u2_ref, sent_hbm, seen_ref, probe_ref, found_ref, sems):
-    probe_copy = pltpu.make_async_copy(probe_hbm, probe_ref, sems.at[0])
+                 u2_ref, found_ref, seen_ref, probe_ref, sem):
+    probe_copy = pltpu.make_async_copy(probe_hbm, probe_ref, sem)
     probe_copy.start()
     masks = lane_masks()
     blocks = probe_ref.shape[0] // LANES
@@ -244,12 +245,16 @@
 
         found_ref[part] = found
 
+
+def send_kernel(found_ref, *refs):
+    sent_hbm, sem = refs[-2:]
+
     def send(device, _):
-        pltpu.make_async_copy(found_ref, sent_hbm.at[device], sems.at[1]).start()
+        pltpu.make_async_copy(found_ref, sent_hbm.at[device], sem).start()
         return 0
 
     lax.fori_loop(0, sent_hbm.shape[0], send, 0)
-    pltpu.make_async_copy(sent_hbm, sent_hbm, sems.at[1]).wait()
+    pltpu.make_async_copy(sent_hbm, sent_hbm, sem).wait()
 
 
 def halves(value):
@@ -399,26 +404,29 @@
     obs_shape = jax.ShapeDtypeStruct((obs_tiles, ROWS, LANES), f32)
     params = pltpu.CompilerParams(vmem_limit_bytes=32 * 1024 * 1024)
     stack = pltpu.VMEM((planes * tiles, ROWS, LANES), f32)
-    low, high, obs, t_near = pl.pallas_call(
+    low, high, obs, t_near, picked = pl.pallas_call(
         functools.partial(pack_kernel, planes, tiles),
         out_shape=(
             edge,
             edge,
             obs_shape,
             jax.ShapeDtypeStruct(u_rows.shape, f32),
+            pltpu.HBM((slots, ROWS, LANES), f32),
         ),
-        in_specs=[HBM] * 6,
-        out_specs=(VMEM,) * 4,
+        in_specs=[HBM] * 7,
+        out_specs=(VMEM,) * 4 + (HBM,),
         scratch_shapes=[
             pltpu.SMEM(probe_taper.shape, i32),
             pltpu.VMEM(u_rows.shape, f32),
             pltpu.VMEM((ROWS, probes), f32),
             pltpu.VMEM((2, probes), f32),
-            pltpu.SemaphoreType.DMA((6,)),
+            pltpu.SMEM(pair_cells.shape, i32),
+            pltpu.VMEM((slots, ROWS, LANES), f32),
+            pltpu.SemaphoreType.DMA((8,)),
         ],
         compiler_params=params,
         name="pack",
-    )(*map(stay, (probe_taper, u_rows, t_rows, obs_noise, observed.reshape(1, -1), obs_var.reshape(1, -1))))
+    )(*map(stay, (probe_taper, u_rows, t_rows, obs_noise, observed.reshape(1, -1), obs_var.reshape(1, -1), pair_cells)))
     little = pl.CostEstimate(flops=1000, bytes_accessed=1000, transcendentals=0)
     upward = [(i, i + 1) for i in range(slabs - 1)]
     before = lax.ppermute(high, "space", upward)
@@ -429,29 +437,26 @@
         upward_2 = [(i, i + 2) for i in range(slabs - 2)]
         before_2 = lax.ppermute(obs, "space", upward_2)
         after_2 = lax.ppermute(obs, "space", [(j, i) for i, j in upward_2])
-    inner, edges, picked = pl.pallas_call(
+    inner, edges = pl.pallas_call(
         functools.partial(inner_kernel, planes, tiles),
         out_shape=(
             jax.ShapeDtypeStruct((planes * tiles, ROWS, LANES), f32),
             jax.ShapeDtypeStruct((14 * tiles, ROWS, LANES), f32),
-            pltpu.HBM((slots, ROWS, LANES), f32),
         ),
-        in_specs=[HBM, HBM, VMEM],
-        out_specs=(VMEM, VMEM, HBM),
+        in_specs=[HBM, VMEM],
+        out_specs=(VMEM, VMEM),
         scratch_shapes=[
             pltpu.VMEM(u_rows.shape, f32),
             stack,
             stack,
             stack,
             pltpu.VMEM((5, planes * tiles, ROWS, LANES), f32),
-            pltpu.SMEM(pair_cells.shape, i32),
-            pltpu.VMEM((slots, ROWS, LANES), f32),
-            pltpu.SemaphoreType.DMA((3,)),
+            pltpu.SemaphoreType.DMA(()),
         ],
         compiler_params=params,
         cost_estimate=pl.CostEstimate(flops=0, bytes_accessed=15_000_000, transcendentals=0),
         name="inner_planes",
-    )(stay(u_rows), stay(pair_cells), t_near)
+    )(stay(u_rows), t_near)
     by_xor = chips <= 4 and chips & (chips - 1) == 0
     if by_xor:
         parts = [picked]
@@ -459,25 +464,34 @@
             parts.append(lax.ppermute(picked, "chip", [(i, i ^ d) for i in range(chips)]))
     else:
         parts = [lax.all_to_all(jnp.broadcast_to(picked, (chips, *picked.shape)), "chip", 0, 0)]
-    u2, sent, seen = pl.pallas_call(
+    u2, found, seen = pl.pallas_call(
         functools.partial(outer_kernel, planes, tiles),
         out_shape=(
             jax.ShapeDtypeStruct((planes * tiles, ROWS, LANES), f32),
-            pltpu.HBM((slabs * groups, blocks, ROWS, LANES), f32),
+            jax.ShapeDtypeStruct((blocks, ROWS, LANES), f32),
             jax.ShapeDtypeStruct((2 * obs_tiles, ROWS, LANES), f32),
         ),
         in_specs=[HBM] + [VMEM] * 4,
-        out_specs=(VMEM, HBM, VMEM),
+        out_specs=(VMEM,) * 3,
         scratch_shapes=[
             pltpu.SMEM(probe_cells.shape, i32),
-            pltpu.VMEM((blocks, ROWS, LANES), f32),
-            pltpu.SemaphoreType.DMA((2,)),
+            pltpu.SemaphoreType.DMA(()),
         ],
         input_output_aliases={4: 0},
         compiler_params=params,
-        cost_estimate=pl.CostEstimate(flops=0, bytes_accessed=26_000_000, transcendentals=0),
+        cost_estimate=little,
         name="outer_planes",
     )(stay(probe_cells), before, after, edges, inner)
+    sent = pl.pallas_call(
+        send_kernel,
+        out_shape=pltpu.HBM((slabs * groups, blocks, ROWS, LANES), f32),
+        in_specs=[VMEM] + [ANY] * len(parts),
+        out_specs=HBM,
+        scratch_shapes=[pltpu.SemaphoreType.DMA(())],
+        compiler_params=params,
+        cost_estimate=little,
+        name="send",
+    )(found, *parts)
     pred_all = lax.all_to_all(sent, ("space", "chip", "core"), 0, 0)
     u2_rows, *parts = pl.pallas_call(
         functools.partial(store_kernel, planes, tiles),

time: 50.5 us -> 42.3 us (0.84)
  waiting for transfers between devices: 13.2 us -> 2.94 us
  starting transfers between devices: 18 us -> 19.5 us
  Pallas kernels: 17.5 us -> 18.1 us
    ppermute x3, waiting for transfers between devices: 8.67 us -> 0.01 us  [shards(): lax.ppermute(picked, 'chip', [(i, i ^ d) for i in range(chips)])]
    ppermute x1, waiting for transfers between devices: 4.13 us -> 0.94 us  [shards(): after = lax.ppermute(low, 'space', [(j, i) for i, j in upward])]
    all_to_all x1, starting transfers between devices: 4.83 us -> 6 us  [shards(): pred_all = lax.all_to_all(sent, ('space', 'chip', 'core'), 0, 0)]
    all_to_all x1, waiting for transfers between devices: 0.01 us -> 1.07 us  [shards(): pred_all = lax.all_to_all(sent, ('space', 'chip', 'core'), 0, 0)]
    ppermute x1, waiting for transfers between devices: 0.01 us -> 0.9 us  [shards(): lax.ppermute(obs, 'space', [(i, (i + 2) % 4) for i in range(4)])]
    pallas_call x0 -> x1, Pallas kernels: none -> 0.81 us  [shards(): pl.pallas_call(send_kernel, out_shape=pltpu.HBM((slabs * groups, blocks,...]
    pallas_call x1, Pallas kernels: 2.91 us -> 2.1 us  [shards(): pl.pallas_call(functools.partial(outer_kernel, planes, tiles), out_shape=...]
    pallas_call x1, Pallas kernels: 1.78 us -> 2.35 us  [shards(): pl.pallas_call(functools.partial(pack_kernel, planes, tiles), out_shape=(...]
  transfers between devices with their start and end apart: 11 -> 11, of which waited for: 5 -> 3; matrix products, arithmetic and copies ran while one was open for 0% -> 0% of each run, Pallas kernels for 18% -> 26%
where the time goes in v9:
time: 42.3 us; the launch traced here: 42 us
  starting transfers between devices  19.5 us (46%)
  Pallas kernels  18.1 us (43%)
  waiting for transfers between devices  2.94 us (7%)
  between operations  1.43 us (3%)
    all_to_all x1, starting transfers between devices, shards(): pred_all = lax.all_to_all(sent, ('space', 'chip', 'core'), 0, 0)  6 us
    ppermute x1, starting transfers between devices, shards(): before = lax.ppermute(high, 'space', upward)  4.95 us
    pallas_call x1, Pallas kernels, shards(): pl.pallas_call(functools.partial(inner_kernel, planes, tiles), out_shape=...  4.28 us
    pallas_call x1, Pallas kernels, shards(): pl.pallas_call(functools.partial(update_kernel, slabs, planes, tiles), ou...  3.8 us
    ppermute x3, starting transfers between devices, shards(): lax.ppermute(picked, 'chip', [(i, i ^ d) for i in range(chips)])  3.55 us
    pallas_call x1, Pallas kernels, shards(): pl.pallas_call(functools.partial(split_kernel, by_xor, chips), out_shape=...  3.11 us
    ppermute x1, starting transfers between devices, shards(): lax.ppermute(obs, 'space', [(i, (i + 2) % 4) for i in range(4)])  2.67 us
    pallas_call x1, Pallas kernels, shards(): pl.pallas_call(functools.partial(pack_kernel, planes, tiles), out_shape=(...  2.35 us
  transfers between devices with their start and end apart: 11, of which 3 were waited for; matrix products, arithmetic and copies ran while one was open for 0% of the time, Pallas kernels for 26%

profile of v9, /device:TPU:0, one launch (start us, length us, event | category | flops | bytes accessed | tf_op | source)
XLA Modules:
  0.0 42.0 jit_solution(16984674208483539907)
XLA Ops:
  0.6 2.4 %pack.1 = (f32[69,8,128]{2,1,0:T(8,128)S(1)}, f32[69,8,128]{2,1,0:T(8,128)S(1)}, f32[4,8,128]{2,1,0:T(8,128)S(1)}, f32[2048,128]{1,0:T(8,128)S(1)}, f32[32,8,128]{2,1,0:T(8,128)}) custom-call(s32[1,2,6]{2,1,0:T(2,128)} %taper_hbm.1, f32[2048,128]{1,0:T(8,128)} %bitcast.26, f32[2048,128]{1,0:T(8,128)} %bitcast.28, f32[8,256]{1,0:T(8,128)} %noise_hbm.1, ...), custom_call_target="tpu_custom_call" | custom-call | tf_op jit(solution)/shard_map/pack/pallas_call | solution.py:407
  3.0 4.9 %collective-permute-start = (f32[69,8,128]{2,1,0:T(8,128)S(1)}, f32[69,8,128]{2,1,0:T(8,128)S(1)}, u32[]{:S(2)}, u32[]{:S(2)}) collective-permute-start(f32[69,8,128]{2,1,0:T(8,128)S(1)} %get-tuple-element.20), channel_id=1, source_target_pairs={{0,8},{8,16},{16,24},{1,9},{9,17},{17,25},{2,10},{10,18},{18,26},{... | collective-permute-start | bytes 847880 | tf_op jit(solution)/shard_map/ppermute | solution.py:432
  7.9 1.3 %collective-permute-start.1 = (f32[69,8,128]{2,1,0:T(8,128)S(1)}, f32[69,8,128]{2,1,0:T(8,128)S(1)}, u32[]{:S(2)}, u32[]{:S(2)}) collective-permute-start(f32[69,8,128]{2,1,0:T(8,128)S(1)} %get-tuple-element.21), channel_id=1, source_target_pairs={{8,0},{16,8},{24,16},{9,1},{17,9},{25,17},{10,2},{18,10},{26,18},{... | collective-permute-start | bytes 847880 | tf_op jit(solution)/shard_map/ppermute | solution.py:433
  9.2 1.6 %collective-permute-start.2 = (f32[32,8,128]{2,1,0:T(8,128)}, f32[32,8,128]{2,1,0:T(8,128)S(1)}, u32[]{:S(2)}, u32[]{:S(2)}) collective-permute-start(f32[32,8,128]{2,1,0:T(8,128)} %get-tuple-element.26.refs_0_), channel_id=1, source_target_pairs={{0,2},{2,0},{4,6},{6,4},{1,3},{3,1},{5,7},{7,5},{8,10},{10,8},{12,... | collective-permute-start | bytes 393224 | tf_op jit(solution)/shard_map/ppermute | solution.py:464
  10.8 1.5 %collective-permute-start.3 = (f32[32,8,128]{2,1,0:T(8,128)}, f32[32,8,128]{2,1,0:T(8,128)S(1)}, u32[]{:S(2)}, u32[]{:S(2)}) collective-permute-start(f32[32,8,128]{2,1,0:T(8,128)} %get-tuple-element.26.refs_0_), channel_id=1, source_target_pairs={{0,4},{2,6},{4,0},{6,2},{1,5},{3,7},{5,1},{7,3},{8,12},{10,14},{12... | collective-permute-start | bytes 393224 | tf_op jit(solution)/shard_map/ppermute | solution.py:464
  12.3 0.5 %collective-permute-start.4 = (f32[32,8,128]{2,1,0:T(8,128)}, f32[32,8,128]{2,1,0:T(8,128)S(1)}, u32[]{:S(2)}, u32[]{:S(2)}) collective-permute-start(f32[32,8,128]{2,1,0:T(8,128)} %get-tuple-element.26.refs_0_), channel_id=1, source_target_pairs={{0,6},{2,4},{4,2},{6,0},{1,7},{3,5},{5,3},{7,1},{8,14},{10,12},{12... | collective-permute-start | bytes 393224 | tf_op jit(solution)/shard_map/ppermute | solution.py:464
  12.8 4.3 %inner_planes.1 = (f32[256,8,128]{2,1,0:T(8,128)S(1)}, f32[224,8,128]{2,1,0:T(8,128)S(1)}) custom-call(f32[2048,128]{1,0:T(8,128)} %bitcast.27, f32[2048,128]{1,0:T(8,128)S(1)} %get-tuple-element.22.t_ref), custom_call_target="tpu_custom_call" | custom-call | bytes 15000000 | tf_op jit(solution)/shard_map/inner_planes/pallas_call | solution.py:440
  17.1 0.0 collective-permute-done.before_ref
  17.1 0.9 %collective-permute-done.1.after_ref = f32[69,8,128]{2,1,0:T(8,128)S(1)} collective-permute-done((f32[69,8,128]{2,1,0:T(8,128)S(1)}, f32[69,8,128]{2,1,0:T(8,128)S(1)}, u32[]{:S(2)}, u32[]{:S(2)}) %collective-permute-start.1) | collective-permute-done | bytes 282656 | tf_op jit(solution)/shard_map/ppermute | solution.py:433
  18.0 0.0 copy-start
  18.0 2.1 %outer_planes.1 = (f32[256,8,128]{2,1,0:T(8,128)S(1)}, f32[2,8,128]{2,1,0:T(8,128)S(1)}, f32[8,8,128]{2,1,0:T(8,128)S(1)}) custom-call(s32[256]{0:T(256)} %probe_hbm.1, f32[69,8,128]{2,1,0:T(8,128)S(1)} %collective-permute-done.before_ref, f32[69,8,128]{2,1,0:T(8,128)S(1)} %collective-permute-done.1.after_ref, ...), custom_call_target="tpu_custom_call", output_to_operand_aliasing={{0}: (4, {})} | custom-call | flops 1000 | bytes 1000 | tf_op jit(solution)/shard_map/outer_planes/pallas_call | solution.py:467
  20.2 0.0 collective-permute-done.2.refs_1_
  20.2 0.0 collective-permute-done.3.refs_2_
  20.2 0.0 collective-permute-done.4.refs_3_
  20.2 0.0 copy-done
  20.2 0.8 %send.1 = f32[32,2,8,128]{3,2,1,0:T(8,128)} custom-call(f32[2,8,128]{2,1,0:T(8,128)S(1)} %get-tuple-element.28.found_ref, f32[32,8,128]{2,1,0:T(8,128)S(1)} %copy-done, f32[32,8,128]{2,1,0:T(8,128)S(1)} %collective-permute-done.2.refs_1_, f32[32,8,128]{2,1,0:T(8,128)S(1)} %collective-permute-done.3.refs_2_, f32[32,8,128]{2,1,0:T(8,128)S(1)} %collective-permute-done.4.refs_3_), custom_call_target="tpu_custom_call" | custom-call | flops 1000 | bytes 1000 | tf_op jit(solution)/shard_map/send/pallas_call | solution.py:485
  21.0 6.0 %all-to-all-start = ((f32[32,2,8,128]{3,2,1,0:T(8,128)}), f32[32,2,8,128]{3,2,1,0:T(8,128)S(1)}, u32[]{:S(2)}, u32[]{:S(2)}) async-start(f32[32,2,8,128]{3,2,1,0:T(8,128)} %send.1), calls=%async_computation | async-start | bytes 524288 | tf_op jit(solution)/shard_map/all_to_all | solution.py:495
  27.0 1.6 %store.1 = (f32[2048,128]{1,0:T(8,128)}, f32[32,8,128]{2,1,0:T(8,128)S(1)}, f32[32,8,128]{2,1,0:T(8,128)S(1)}, f32[32,8,128]{2,1,0:T(8,128)S(1)}, f32[32,8,128]{2,1,0:T(8,128)S(1)}) custom-call(f32[256,8,128]{2,1,0:T(8,128)S(1)} %get-tuple-element.25.u2_ref, ...), custom_call_target="tpu_custom_call", output_to_operand_aliasing={{1}: (1, {}), {2}: (2, {}), {3}: (3, {}), {4}: (4, {})} | custom-call | flops 1000 | bytes 1000 | tf_op jit(solution)/shard_map/store/pallas_call | solution.py:496
  28.6 0.3 collective-permute-start.6
  28.9 0.3 collective-permute-start.7
  29.1 0.3 collective-permute-start.8
  29.4 0.3 collective-permute-start.9
  29.6 2.7 %collective-permute-start.5 = (f32[4,8,128]{2,1,0:T(8,128)S(1)}, f32[4,8,128]{2,1,0:T(8,128)S(1)}, u32[]{:S(2)}, u32[]{:S(2)}) collective-permute-start(f32[4,8,128]{2,1,0:T(8,128)S(1)} %get-tuple-element.29.own_ref), channel_id=1, source_target_pairs={{0,16},{8,24},{16,0},{24,8},{1,17},{9,25},{17,1},{25,9},{2,18},{10... | collective-permute-start | bytes 49160 | tf_op jit(solution)/shard_map/ppermute | solution.py:435
  32.3 0.1 pad_add_fusion.place_ref
  33.0 0.0 collective-permute-done.6.refs_4_
  33.1 0.0 collective-permute-done.7.refs_5_
  33.1 0.0 collective-permute-done.8.refs_6_
  33.1 0.0 collective-permute-done.9.refs_7_
  33.1 3.1 %split.1.split_hbm = bf16[32,128,128]{2,1,0:T(8,128)(2,1)} custom-call(s32[4]{0:T(128)S(1)} %pad_add_fusion.place_ref, f32[32,8,128]{2,1,0:T(8,128)S(1)} %get-tuple-element.31.refs_0_, f32[32,8,128]{2,1,0:T(8,128)S(1)} %get-tuple-element.32.refs_1_, f32[32,8,128]{2,1,0:T(8,128)S(1)} %get-tuple-element.33.refs_2_, ...), custom_call_target="tpu_custom_call" | custom-call | flops 1000 | bytes 1000 | tf_op jit(solution)/shard_map/split/pallas_call | solution.py:509
  36.2 0.9 %collective-permute-done.5.before_2_ref.after_2_ref = f32[4,8,128]{2,1,0:T(8,128)S(1)} collective-permute-done((f32[4,8,128]{2,1,0:T(8,128)S(1)}, f32[4,8,128]{2,1,0:T(8,128)S(1)}, u32[]{:S(2)}, u32[]{:S(2)}) %collective-permute-start.5) | collective-permute-done | bytes 16416 | tf_op jit(solution)/shard_map/ppermute | solution.py:435
  37.1 1.1 %all-to-all-done.pred_ref = f32[32,2,8,128]{3,2,1,0:T(8,128)S(1)} async-done(((f32[32,2,8,128]{3,2,1,0:T(8,128)}), f32[32,2,8,128]{3,2,1,0:T(8,128)S(1)}, u32[]{:S(2)}, u32[]{:S(2)}) %all-to-all-start) | async-done | bytes 262176 | tf_op jit(solution)/shard_map/all_to_all | solution.py:495
  38.2 3.8 %update.1 = (f32[2048,128]{1,0:T(8,128)}, f32[8,256]{1,0:T(8,128)}) custom-call(s32[4]{0:T(128)S(1)} %pad_add_fusion.place_ref, s32[1]{0:T(128)S(6)} %copy.24.count_ref, s32[1,32]{1,0:T(1,128)} %cells_hbm.3, s32[1,32]{1,0:T(1,128)} %probes_hbm.1, s32[1,32]{1,0:T(1,128)} %level_hbm.1, f32[32,2,8,128]{3,2,1,0:T(8,128)S(1)} %all-to-all-done.pred_ref, ...), custom_call_target="tpu_custom_call" | custom-call | tf_op jit(solution)/shard_map/update/pallas_call | solution.py:519
Async XLA Ops:
  3.0 14.1 %collective-permute-start = (f32[69,8,128]{2,1,0:T(8,128)S(1)}, f32[69,8,128]{2,1,0:T(8,128)S(1)}, u32[]{:S(2)}, u32[]{:S(2)}) collective-permute-start(f32[69,8,128]{2,1,0:T(8,128)S(1)} %get-tuple-element.20), channel_id=1, source_target_pairs={{0,8},{8,16},{16,24},{1,9},{9,17},{17,25},{2,10},{10,18},{18,26},{... | collective-permute-start | bytes 847880 | tf_op jit(solution)/shard_map/ppermute | solution.py:432
  7.9 10.1 %collective-permute-start.1 = (f32[69,8,128]{2,1,0:T(8,128)S(1)}, f32[69,8,128]{2,1,0:T(8,128)S(1)}, u32[]{:S(2)}, u32[]{:S(2)}) collective-permute-start(f32[69,8,128]{2,1,0:T(8,128)S(1)} %get-tuple-element.21), channel_id=1, source_target_pairs={{8,0},{16,8},{24,16},{9,1},{17,9},{25,17},{10,2},{18,10},{26,18},{... | collective-permute-start | bytes 847880 | tf_op jit(solution)/shard_map/ppermute | solution.py:433
  9.2 10.9 %collective-permute-start.2 = (f32[32,8,128]{2,1,0:T(8,128)}, f32[32,8,128]{2,1,0:T(8,128)S(1)}, u32[]{:S(2)}, u32[]{:S(2)}) collective-permute-start(f32[32,8,128]{2,1,0:T(8,128)} %get-tuple-element.26.refs_0_), channel_id=1, source_target_pairs={{0,2},{2,0},{4,6},{6,4},{1,3},{3,1},{5,7},{7,5},{8,10},{10,8},{12,... | collective-permute-start | bytes 393224 | tf_op jit(solution)/shard_map/ppermute | solution.py:464
  10.8 9.4 %collective-permute-start.3 = (f32[32,8,128]{2,1,0:T(8,128)}, f32[32,8,128]{2,1,0:T(8,128)S(1)}, u32[]{:S(2)}, u32[]{:S(2)}) collective-permute-start(f32[32,8,128]{2,1,0:T(8,128)} %get-tuple-element.26.refs_0_), channel_id=1, source_target_pairs={{0,4},{2,6},{4,0},{6,2},{1,5},{3,7},{5,1},{7,3},{8,12},{10,14},{12... | collective-permute-start | bytes 393224 | tf_op jit(solution)/shard_map/ppermute | solution.py:464
  12.3 7.9 %collective-permute-start.4 = (f32[32,8,128]{2,1,0:T(8,128)}, f32[32,8,128]{2,1,0:T(8,128)S(1)}, u32[]{:S(2)}, u32[]{:S(2)}) collective-permute-start(f32[32,8,128]{2,1,0:T(8,128)} %get-tuple-element.26.refs_0_), channel_id=1, source_target_pairs={{0,6},{2,4},{4,2},{6,0},{1,7},{3,5},{5,3},{7,1},{8,14},{10,12},{12... | collective-permute-start | bytes 393224 | tf_op jit(solution)/shard_map/ppermute | solution.py:464
  18.0 2.1 %copy-start = (f32[32,8,128]{2,1,0:T(8,128)S(1)}, f32[32,8,128]{2,1,0:T(8,128)}, u32[]{:S(2)}) copy-start(f32[32,8,128]{2,1,0:T(8,128)} %get-tuple-element.26.refs_0_) | copy-start | bytes 393220
  21.0 17.2 %all-to-all-start = ((f32[32,2,8,128]{3,2,1,0:T(8,128)}), f32[32,2,8,128]{3,2,1,0:T(8,128)S(1)}, u32[]{:S(2)}, u32[]{:S(2)}) async-start(f32[32,2,8,128]{3,2,1,0:T(8,128)} %send.1), calls=%async_computation | async-start | bytes 524288 | tf_op jit(solution)/shard_map/all_to_all | solution.py:495
  28.6 4.4 %collective-permute-start.6 = (f32[32,8,128]{2,1,0:T(8,128)S(1)}, f32[32,8,128]{2,1,0:T(8,128)S(1)}, u32[]{:S(2)}, u32[]{:S(2)}) collective-permute-start(f32[32,8,128]{2,1,0:T(8,128)S(1)} %get-tuple-element.31.refs_0_), channel_id=1, source_target_pairs={{0,1},{1,0},{2,3},{3,2},{4,5},{5,4},{6,7},{7,6},{8,9},{9,8},{10,11... | collective-permute-start | bytes 393224 | tf_op jit(solution)/shard_map/ppermute | solution.py:506
  28.9 4.2 %collective-permute-start.7 = (f32[32,8,128]{2,1,0:T(8,128)S(1)}, f32[32,8,128]{2,1,0:T(8,128)S(1)}, u32[]{:S(2)}, u32[]{:S(2)}) collective-permute-start(f32[32,8,128]{2,1,0:T(8,128)S(1)} %get-tuple-element.32.refs_1_), channel_id=1, source_target_pairs={{0,1},{1,0},{2,3},{3,2},{4,5},{5,4},{6,7},{7,6},{8,9},{9,8},{10,11... | collective-permute-start | bytes 393224 | tf_op jit(solution)/shard_map/ppermute | solution.py:506
  29.1 3.9 %collective-permute-start.8 = (f32[32,8,128]{2,1,0:T(8,128)S(1)}, f32[32,8,128]{2,1,0:T(8,128)S(1)}, u32[]{:S(2)}, u32[]{:S(2)}) collective-permute-start(f32[32,8,128]{2,1,0:T(8,128)S(1)} %get-tuple-element.33.refs_2_), channel_id=1, source_target_pairs={{0,1},{1,0},{2,3},{3,2},{4,5},{5,4},{6,7},{7,6},{8,9},{9,8},{10,11... | collective-permute-start | bytes 393224 | tf_op jit(solution)/shard_map/ppermute | solution.py:506
  29.4 3.7 %collective-permute-start.9 = (f32[32,8,128]{2,1,0:T(8,128)S(1)}, f32[32,8,128]{2,1,0:T(8,128)S(1)}, u32[]{:S(2)}, u32[]{:S(2)}) collective-permute-start(f32[32,8,128]{2,1,0:T(8,128)S(1)} %get-tuple-element.34.refs_3_), channel_id=1, source_target_pairs={{0,1},{1,0},{2,3},{3,2},{4,5},{5,4},{6,7},{7,6},{8,9},{9,8},{10,11... | collective-permute-start | bytes 393224 | tf_op jit(solution)/shard_map/ppermute | solution.py:506
  29.6 7.5 %collective-permute-start.5 = (f32[4,8,128]{2,1,0:T(8,128)S(1)}, f32[4,8,128]{2,1,0:T(8,128)S(1)}, u32[]{:S(2)}, u32[]{:S(2)}) collective-permute-start(f32[4,8,128]{2,1,0:T(8,128)S(1)} %get-tuple-element.29.own_ref), channel_id=1, source_target_pairs={{0,16},{8,24},{16,0},{24,8},{1,17},{9,25},{17,1},{25,9},{2,18},{10... | collective-permute-start | bytes 49160 | tf_op jit(solution)/shard_map/ppermute | solution.py:435

commit v10 on v9

--- a/solution.py
+++ b/solution.py
@@ -39,8 +39,8 @@
 
 
 def pack_kernel(planes, tiles, taper_hbm, u_hbm, t_hbm, noise_hbm, observed_hbm, var_hbm, cells_hbm,
-                low_ref, high_ref, obs_ref, t_ref, pick_hbm,
-                taper_ref, u_ref, noise_ref, row_ref, cells_ref, pick_ref, sems):
+                low_ref, high_ref, obs_ref, t_ref, pick_ref,
+                taper_ref, u_ref, noise_ref, row_ref, cells_ref, sems):
     stride = planes * tiles
     blocks = noise_ref.shape[1] // LANES
     copies = [
@@ -63,8 +63,6 @@
         block = cells_ref[0, slot]
         row = row_of(block // tiles, block % tiles, tiles)
         pick_ref[slot] = t_ref[pl.ds(row, ROWS, stride=stride), :]
-    picked = pltpu.make_async_copy(pick_ref, pick_hbm, sems.at[7])
-    picked.start()
     for kind, source in ((1, t_ref), (0, u_ref)):
         if kind == 0:
             copies[1].wait()
@@ -90,7 +88,6 @@
     for ref in (low_ref, high_ref):
         for at in range(obs_ref.shape[0]):
             ref[4 * tiles + 1 + at] = obs_ref[at]
-    picked.wait()
 
 
 def rot(value, by):
@@ -273,31 +270,6 @@
     each(0, planes, 4, store)
 
 
-def split_kernel(by_xor, chips, place_ref, *refs):
-    *parts, split_ref, theta_ref, sems = refs
-    chip, core = place_ref[2], place_ref[3]
-    same, other = parts[: len(parts) // 2], parts[len(parts) // 2 :]
-    if not by_xor:
-        same, other = ([ref.at[at] for at in range(chips)] for (ref,) in (same, other))
-    members = 2 * theta_ref.shape[0] * ROWS
-    copies = []
-    for at in range(chips):
-        where = chip ^ at if by_xor else at
-        copies.append(pltpu.make_async_copy(same[at], theta_ref.at[where, core], sems.at[2 * at]))
-        copies.append(pltpu.make_async_copy(other[at], theta_ref.at[where, 1 - core], sems.at[2 * at + 1]))
-    for copy in copies:
-        copy.start()
-    for copy in copies:
-        copy.wait()
-
-    def split(slot):
-        high, low = halves(theta_ref[:, :, slot].reshape(members, LANES))
-        split_ref[slot, :members, :] = high
-        split_ref[slot, members:, :] = low
-
-    each(0, split_ref.shape[0], 4, split)
-
-
 def stacked(value):
     high, low = halves(value)
     return jnp.concatenate([high.astype(jnp.float32), low.astype(jnp.float32)], axis=0).astype(jnp.bfloat16)
@@ -311,9 +283,14 @@
     return lax.dot_general(left, right, (((1,), (over,)), ((), ())), preferred_element_type=jnp.float32)
 
 
-def update_kernel(slabs, planes, tiles, place_ref, count_ref, cells_hbm, probes_hbm, level_hbm,
-                  pred_ref, before_2_ref, seen_ref, own_ref, after_2_ref, split_hbm, t_hbm,
-                  post_ref, gain_ref, reach, cells_ref, probes_ref, level_ref, split_ref, sems):
+def update_kernel(slabs, chips, planes, tiles, place_ref, count_ref, cells_hbm, probes_hbm, level_hbm,
+                  pred_ref, before_2_ref, seen_ref, own_ref, after_2_ref, t_hbm, *refs):
+    *parts, post_ref, gain_ref, reach, cells_ref, probes_ref, level_ref, theta_ref, sems = refs
+    chip, core = place_ref[2], place_ref[3]
+    same, other = parts[: len(parts) // 2], parts[len(parts) // 2 :]
+    by_xor = len(same) == chips
+    if not by_xor:
+        same, other = ([ref.at[at] for at in range(chips)] for (ref,) in (same, other))
     groups, blocks = pred_ref.shape[0] // slabs, pred_ref.shape[1]
     members = groups * ROWS
     share = 1.0 / (members - 1)
@@ -321,8 +298,12 @@
         pltpu.make_async_copy(source, target, sems.at[at])
         for at, (source, target) in enumerate((
             (cells_hbm, cells_ref), (probes_hbm, probes_ref), (level_hbm, level_ref),
-            (split_hbm, split_ref), (t_hbm, post_ref)))
+            (t_hbm, post_ref)))
     ]
+    for at in range(chips):
+        where = chip ^ at if by_xor else at
+        for side, source in ((core, same[at]), (1 - core, other[at])):
+            copies.append(pltpu.make_async_copy(source, theta_ref.at[where, side], sems.at[len(copies)]))
     for copy in copies:
         copy.start()
     slab, group = place_ref[0], place_ref[1]
@@ -367,9 +348,11 @@
             reach[(d - 1) * blocks + i] = jnp.concatenate([both, both], axis=1)
     for copy in copies:
         copy.wait()
-    for slot in range(split_ref.shape[0]):
+    for slot in range(theta_ref.shape[2]):
         weight = jnp.where(slot < count_ref[0], level_ref[0, slot].astype(jnp.float32) / 256.0, 0.0) * share
-        change = fold(dot(reach[probes_ref[0, slot]], split_ref[slot], 0)) * weight
+        high, low = halves(theta_ref[:, :, slot].reshape(members, LANES))
+        both = jnp.concatenate([high, low], axis=0)
+        change = fold(dot(reach[probes_ref[0, slot]], both, 0)) * weight
         block = cells_ref[0, slot]
         rows = pl.ds(row_of(block // tiles, block % tiles, tiles), ROWS, stride=planes * tiles)
         post_ref[rows, :] = post_ref[rows, :] + change
@@ -411,18 +394,17 @@
             edge,
             obs_shape,
             jax.ShapeDtypeStruct(u_rows.shape, f32),
-            pltpu.HBM((slots, ROWS, LANES), f32),
+            jax.ShapeDtypeStruct((slots, ROWS, LANES), f32),
         ),
         in_specs=[HBM] * 7,
-        out_specs=(VMEM,) * 4 + (HBM,),
+        out_specs=(VMEM,) * 5,
         scratch_shapes=[
             pltpu.SMEM(probe_taper.shape, i32),
             pltpu.VMEM(u_rows.shape, f32),
             pltpu.VMEM((ROWS, probes), f32),
             pltpu.VMEM((2, probes), f32),
             pltpu.SMEM(pair_cells.shape, i32),
-            pltpu.VMEM((slots, ROWS, LANES), f32),
-            pltpu.SemaphoreType.DMA((8,)),
+            pltpu.SemaphoreType.DMA((7,)),
         ],
         compiler_params=params,
         name="pack",
@@ -506,36 +488,26 @@
     swapped = [lax.ppermute(part, "core", [(0, 1), (1, 0)]) for part in parts]
     where = [lax.axis_index(axes) for axes in ("space", ("chip", "core"), "chip", "core")]
     place = jnp.stack(where).astype(i32)
-    split = pl.pallas_call(
-        functools.partial(split_kernel, by_xor, chips),
-        out_shape=pltpu.HBM((slots, 2 * groups * ROWS, LANES), jnp.bfloat16),
-        in_specs=[SMEM] + [ANY] * (2 * len(parts)),
-        out_specs=VMEM,
-        scratch_shapes=[pltpu.VMEM((chips, 2, slots, ROWS, LANES), f32), pltpu.SemaphoreType.DMA((2 * chips,))],
-        compiler_params=params,
-        cost_estimate=little,
-        name="split",
-    )(place, *parts, *swapped)
     post_rows, gain = pl.pallas_call(
-        functools.partial(update_kernel, slabs, planes, tiles),
+        functools.partial(update_kernel, slabs, chips, planes, tiles),
         out_shape=(
             jax.ShapeDtypeStruct(u_rows.shape, f32),
             jax.ShapeDtypeStruct((members, probes), f32),
         ),
-        in_specs=[SMEM] * 2 + [HBM] * 3 + [VMEM] * 5 + [HBM] * 2,
+        in_specs=[SMEM] * 2 + [HBM] * 3 + [VMEM] * 5 + [HBM] + [ANY] * (2 * len(parts)),
         out_specs=(VMEM,) * 2,
         scratch_shapes=[
             pltpu.VMEM((probe_taper.shape[2], 2 * ROWS, 2 * groups * ROWS), jnp.bfloat16),
             pltpu.SMEM(pair_cells.shape, i32),
             pltpu.SMEM(pair_cells.shape, i32),
             pltpu.SMEM(pair_cells.shape, i32),
-            pltpu.VMEM(split.shape, jnp.bfloat16),
-            pltpu.SemaphoreType.DMA((5,)),
+            pltpu.VMEM((chips, 2, slots, ROWS, LANES), f32),
+            pltpu.SemaphoreType.DMA((4 + groups,)),
         ],
         compiler_params=params,
         name="update",
     )(place, pair_counts, *map(stay, (pair_cells, pair_probes, pair_taper)), pred_all,
-      before_2, seen, obs, after_2, stay(split), stay(t_rows))
+      before_2, seen, obs, after_2, stay(t_rows), *parts, *swapped)
     return (from_rows(u2_rows, shape), from_rows(post_rows, shape), gain)
 
 

time: 42.3 us -> 42.6 us (level)
  waiting for transfers between devices: 2.94 us -> 6.08 us
  Pallas kernels: 18.1 us -> 15.3 us
    ppermute x1, waiting for transfers between devices: 0.9 us -> 4.06 us  [shards(): lax.ppermute(obs, 'space', [(i, (i + 2) % 4) for i in range(4)])]
    pallas_call x2 -> x1, Pallas kernels: 6.91 us -> 4.53 us  [shards(): pl.pallas_call(functools.partial(update_kernel, slabs, chips, planes, til...]
  transfers between devices with their start and end apart: 11 -> 11, of which waited for: 3 -> 3; matrix products, arithmetic and copies ran while one was open for 0% -> 0% of each run, Pallas kernels for 26% -> 19%
where the time goes in v10:
time: 42.6 us; the launch traced here: 42.3 us
  starting transfers between devices  19.5 us (46%)
  Pallas kernels  15.3 us (36%)
  waiting for transfers between devices  6.08 us (14%)
  between operations  1.39 us (3%)
    all_to_all x1, starting transfers between devices, shards(): pred_all = lax.all_to_all(sent, ('space', 'chip', 'core'), 0, 0)  5.99 us
    ppermute x1, starting transfers between devices, shards(): before = lax.ppermute(high, 'space', upward)  4.95 us
    pallas_call x1, Pallas kernels, shards(): pl.pallas_call(functools.partial(update_kernel, slabs, chips, planes, til...  4.53 us
    pallas_call x1, Pallas kernels, shards(): pl.pallas_call(functools.partial(inner_kernel, planes, tiles), out_shape=...  4.28 us
    ppermute x1, waiting for transfers between devices, shards(): lax.ppermute(obs, 'space', [(i, (i + 2) % 4) for i in range(4)])  4.06 us
    ppermute x3, starting transfers between devices, shards(): lax.ppermute(picked, 'chip', [(i, i ^ d) for i in range(chips)])  3.55 us
    ppermute x1, starting transfers between devices, shards(): lax.ppermute(obs, 'space', [(i, (i + 2) % 4) for i in range(4)])  2.67 us
    pallas_call x1, Pallas kernels, shards(): pl.pallas_call(functools.partial(outer_kernel, planes, tiles), out_shape=...  2.1 us
  transfers between devices with their start and end apart: 11, of which 3 were waited for; matrix products, arithmetic and copies ran while one was open for 0% of the time, Pallas kernels for 19%

profile of v10, /device:TPU:0, one launch (start us, length us, event | category | flops | bytes accessed | tf_op | source)
XLA Modules:
  0.0 42.3 jit_solution(9058365368917122545)
XLA Ops:
  0.6 2.0 %pack.1 = (f32[69,8,128]{2,1,0:T(8,128)S(1)}, f32[69,8,128]{2,1,0:T(8,128)S(1)}, f32[4,8,128]{2,1,0:T(8,128)S(1)}, f32[2048,128]{1,0:T(8,128)S(1)}, f32[32,8,128]{2,1,0:T(8,128)S(1)}) custom-call(s32[1,2,6]{2,1,0:T(2,128)} %taper_hbm.1, f32[2048,128]{1,0:T(8,128)} %bitcast.26, f32[2048,128]{1,0:T(8,128)} %bitcast.28, f32[8,256]{1,0:T(8,128)} %noise_hbm.1, ...), custom_call_target="tpu_custom_call" | custom-call | tf_op jit(solution)/shard_map/pack/pallas_call | solution.py:390
  2.6 4.9 %collective-permute-start = (f32[69,8,128]{2,1,0:T(8,128)S(1)}, f32[69,8,128]{2,1,0:T(8,128)S(1)}, u32[]{:S(2)}, u32[]{:S(2)}) collective-permute-start(f32[69,8,128]{2,1,0:T(8,128)S(1)} %get-tuple-element.20), channel_id=1, source_target_pairs={{0,8},{8,16},{16,24},{1,9},{9,17},{17,25},{2,10},{10,18},{18,26},{... | collective-permute-start | bytes 847880 | tf_op jit(solution)/shard_map/ppermute | solution.py:414
  7.6 1.3 %collective-permute-start.1 = (f32[69,8,128]{2,1,0:T(8,128)S(1)}, f32[69,8,128]{2,1,0:T(8,128)S(1)}, u32[]{:S(2)}, u32[]{:S(2)}) collective-permute-start(f32[69,8,128]{2,1,0:T(8,128)S(1)} %get-tuple-element.21), channel_id=1, source_target_pairs={{8,0},{16,8},{24,16},{9,1},{17,9},{25,17},{10,2},{18,10},{26,18},{... | collective-permute-start | bytes 847880 | tf_op jit(solution)/shard_map/ppermute | solution.py:415
  8.9 1.6 %collective-permute-start.2 = (f32[32,8,128]{2,1,0:T(8,128)S(1)}, f32[32,8,128]{2,1,0:T(8,128)S(1)}, u32[]{:S(2)}, u32[]{:S(2)}) collective-permute-start(f32[32,8,128]{2,1,0:T(8,128)S(1)} %get-tuple-element.26.refs_0_), channel_id=1, source_target_pairs={{0,2},{2,0},{4,6},{6,4},{1,3},{3,1},{5,7},{7,5},{8,10},{10,8},{12,... | collective-permute-start | bytes 393224 | tf_op jit(solution)/shard_map/ppermute | solution.py:446
  10.4 1.5 %collective-permute-start.3 = (f32[32,8,128]{2,1,0:T(8,128)S(1)}, f32[32,8,128]{2,1,0:T(8,128)S(1)}, u32[]{:S(2)}, u32[]{:S(2)}) collective-permute-start(f32[32,8,128]{2,1,0:T(8,128)S(1)} %get-tuple-element.26.refs_0_), channel_id=1, source_target_pairs={{0,4},{2,6},{4,0},{6,2},{1,5},{3,7},{5,1},{7,3},{8,12},{10,14},{12... | collective-permute-start | bytes 393224 | tf_op jit(solution)/shard_map/ppermute | solution.py:446
  11.9 0.5 %collective-permute-start.4 = (f32[32,8,128]{2,1,0:T(8,128)S(1)}, f32[32,8,128]{2,1,0:T(8,128)S(1)}, u32[]{:S(2)}, u32[]{:S(2)}) collective-permute-start(f32[32,8,128]{2,1,0:T(8,128)S(1)} %get-tuple-element.26.refs_0_), channel_id=1, source_target_pairs={{0,6},{2,4},{4,2},{6,0},{1,7},{3,5},{5,3},{7,1},{8,14},{10,12},{12... | collective-permute-start | bytes 393224 | tf_op jit(solution)/shard_map/ppermute | solution.py:446
  12.4 4.3 %inner_planes.1 = (f32[256,8,128]{2,1,0:T(8,128)S(1)}, f32[224,8,128]{2,1,0:T(8,128)S(1)}) custom-call(f32[2048,128]{1,0:T(8,128)} %bitcast.27, f32[2048,128]{1,0:T(8,128)S(1)} %get-tuple-element.22.t_ref), custom_call_target="tpu_custom_call" | custom-call | bytes 15000000 | tf_op jit(solution)/shard_map/inner_planes/pallas_call | solution.py:422
  16.7 0.0 collective-permute-done.before_ref
  16.7 0.9 %collective-permute-done.1.after_ref = f32[69,8,128]{2,1,0:T(8,128)S(1)} collective-permute-done((f32[69,8,128]{2,1,0:T(8,128)S(1)}, f32[69,8,128]{2,1,0:T(8,128)S(1)}, u32[]{:S(2)}, u32[]{:S(2)}) %collective-permute-start.1) | collective-permute-done | bytes 282656 | tf_op jit(solution)/shard_map/ppermute | solution.py:415
  17.7 2.1 %outer_planes.1 = (f32[256,8,128]{2,1,0:T(8,128)S(1)}, f32[2,8,128]{2,1,0:T(8,128)S(1)}, f32[8,8,128]{2,1,0:T(8,128)S(1)}) custom-call(s32[256]{0:T(256)} %probe_hbm.1, f32[69,8,128]{2,1,0:T(8,128)S(1)} %collective-permute-done.before_ref, f32[69,8,128]{2,1,0:T(8,128)S(1)} %collective-permute-done.1.after_ref, ...), custom_call_target="tpu_custom_call", output_to_operand_aliasing={{0}: (4, {})} | custom-call | flops 1000 | bytes 1000 | tf_op jit(solution)/shard_map/outer_planes/pallas_call | solution.py:449
  19.8 0.0 collective-permute-done.2.refs_1_
  19.8 0.0 collective-permute-done.3.refs_2_
  19.8 0.0 collective-permute-done.4.refs_3_
  19.8 0.8 %send.1 = f32[32,2,8,128]{3,2,1,0:T(8,128)} custom-call(f32[2,8,128]{2,1,0:T(8,128)S(1)} %get-tuple-element.28.found_ref, f32[32,8,128]{2,1,0:T(8,128)S(1)} %get-tuple-element.26.refs_0_, f32[32,8,128]{2,1,0:T(8,128)S(1)} %collective-permute-done.2.refs_1_, f32[32,8,128]{2,1,0:T(8,128)S(1)} %collective-permute-done.3.refs_2_, ...), custom_call_target="tpu_custom_call" | custom-call | flops 1000 | bytes 1000 | tf_op jit(solution)/shard_map/send/pallas_call | solution.py:467
  20.6 6.0 %all-to-all-start = ((f32[32,2,8,128]{3,2,1,0:T(8,128)}), f32[32,2,8,128]{3,2,1,0:T(8,128)S(1)}, u32[]{:S(2)}, u32[]{:S(2)}) async-start(f32[32,2,8,128]{3,2,1,0:T(8,128)} %send.1), calls=%async_computation | async-start | bytes 524288 | tf_op jit(solution)/shard_map/all_to_all | solution.py:477
  26.6 1.6 %store.1 = (f32[2048,128]{1,0:T(8,128)}, f32[32,8,128]{2,1,0:T(8,128)S(1)}, f32[32,8,128]{2,1,0:T(8,128)S(1)}, f32[32,8,128]{2,1,0:T(8,128)S(1)}, f32[32,8,128]{2,1,0:T(8,128)S(1)}) custom-call(f32[256,8,128]{2,1,0:T(8,128)S(1)} %get-tuple-element.25.u2_ref, ...), custom_call_target="tpu_custom_call", output_to_operand_aliasing={{1}: (1, {}), {2}: (2, {}), {3}: (3, {}), {4}: (4, {})} | custom-call | flops 1000 | bytes 1000 | tf_op jit(solution)/shard_map/store/pallas_call | solution.py:478
  28.2 0.3 collective-permute-start.6
  28.5 0.3 collective-permute-start.7
  28.7 0.3 collective-permute-start.8
  29.0 0.3 collective-permute-start.9
  29.2 2.7 %collective-permute-start.5 = (f32[4,8,128]{2,1,0:T(8,128)S(1)}, f32[4,8,128]{2,1,0:T(8,128)S(1)}, u32[]{:S(2)}, u32[]{:S(2)}) collective-permute-start(f32[4,8,128]{2,1,0:T(8,128)S(1)} %get-tuple-element.29.own_ref), channel_id=1, source_target_pairs={{0,16},{8,24},{16,0},{24,8},{1,17},{9,25},{17,1},{25,9},{2,18},{10... | collective-permute-start | bytes 49160 | tf_op jit(solution)/shard_map/ppermute | solution.py:417
  31.9 0.1 pad_add_fusion.place_ref
  32.6 4.1 %collective-permute-done.5.before_2_ref.after_2_ref = f32[4,8,128]{2,1,0:T(8,128)S(1)} collective-permute-done((f32[4,8,128]{2,1,0:T(8,128)S(1)}, f32[4,8,128]{2,1,0:T(8,128)S(1)}, u32[]{:S(2)}, u32[]{:S(2)}) %collective-permute-start.5) | collective-permute-done | bytes 16416 | tf_op jit(solution)/shard_map/ppermute | solution.py:417
  36.7 0.0 collective-permute-done.6.refs_4_
  36.7 0.0 collective-permute-done.7.refs_5_
  36.7 0.0 collective-permute-done.8.refs_6_
  36.7 0.0 collective-permute-done.9.refs_7_
  36.7 1.0 %all-to-all-done.pred_ref = f32[32,2,8,128]{3,2,1,0:T(8,128)S(1)} async-done(((f32[32,2,8,128]{3,2,1,0:T(8,128)}), f32[32,2,8,128]{3,2,1,0:T(8,128)S(1)}, u32[]{:S(2)}, u32[]{:S(2)}) %all-to-all-start) | async-done | bytes 262176 | tf_op jit(solution)/shard_map/all_to_all | solution.py:477
  37.8 4.5 %update.1 = (f32[2048,128]{1,0:T(8,128)}, f32[8,256]{1,0:T(8,128)}) custom-call(s32[4]{0:T(128)S(1)} %pad_add_fusion.place_ref, s32[1]{0:T(128)S(6)} %copy.24.count_ref, s32[1,32]{1,0:T(1,128)} %cells_hbm.3, s32[1,32]{1,0:T(1,128)} %probes_hbm.1, s32[1,32]{1,0:T(1,128)} %level_hbm.1, f32[32,2,8,128]{3,2,1,0:T(8,128)S(1)} %all-to-all-done.pred_ref, ...), custom_call_target="tpu_custom_call" | custom-call | tf_op jit(solution)/shard_map/update/pallas_call | solution.py:491
Async XLA Ops:
  2.6 14.1 %collective-permute-start = (f32[69,8,128]{2,1,0:T(8,128)S(1)}, f32[69,8,128]{2,1,0:T(8,128)S(1)}, u32[]{:S(2)}, u32[]{:S(2)}) collective-permute-start(f32[69,8,128]{2,1,0:T(8,128)S(1)} %get-tuple-element.20), channel_id=1, source_target_pairs={{0,8},{8,16},{16,24},{1,9},{9,17},{17,25},{2,10},{10,18},{18,26},{... | collective-permute-start | bytes 847880 | tf_op jit(solution)/shard_map/ppermute | solution.py:414
  7.6 10.1 %collective-permute-start.1 = (f32[69,8,128]{2,1,0:T(8,128)S(1)}, f32[69,8,128]{2,1,0:T(8,128)S(1)}, u32[]{:S(2)}, u32[]{:S(2)}) collective-permute-start(f32[69,8,128]{2,1,0:T(8,128)S(1)} %get-tuple-element.21), channel_id=1, source_target_pairs={{8,0},{16,8},{24,16},{9,1},{17,9},{25,17},{10,2},{18,10},{26,18},{... | collective-permute-start | bytes 847880 | tf_op jit(solution)/shard_map/ppermute | solution.py:415
  8.9 10.9 %collective-permute-start.2 = (f32[32,8,128]{2,1,0:T(8,128)S(1)}, f32[32,8,128]{2,1,0:T(8,128)S(1)}, u32[]{:S(2)}, u32[]{:S(2)}) collective-permute-start(f32[32,8,128]{2,1,0:T(8,128)S(1)} %get-tuple-element.26.refs_0_), channel_id=1, source_target_pairs={{0,2},{2,0},{4,6},{6,4},{1,3},{3,1},{5,7},{7,5},{8,10},{10,8},{12,... | collective-permute-start | bytes 393224 | tf_op jit(solution)/shard_map/ppermute | solution.py:446
  10.4 9.4 %collective-permute-start.3 = (f32[32,8,128]{2,1,0:T(8,128)S(1)}, f32[32,8,128]{2,1,0:T(8,128)S(1)}, u32[]{:S(2)}, u32[]{:S(2)}) collective-permute-start(f32[32,8,128]{2,1,0:T(8,128)S(1)} %get-tuple-element.26.refs_0_), channel_id=1, source_target_pairs={{0,4},{2,6},{4,0},{6,2},{1,5},{3,7},{5,1},{7,3},{8,12},{10,14},{12... | collective-permute-start | bytes 393224 | tf_op jit(solution)/shard_map/ppermute | solution.py:446
  11.9 7.9 %collective-permute-start.4 = (f32[32,8,128]{2,1,0:T(8,128)S(1)}, f32[32,8,128]{2,1,0:T(8,128)S(1)}, u32[]{:S(2)}, u32[]{:S(2)}) collective-permute-start(f32[32,8,128]{2,1,0:T(8,128)S(1)} %get-tuple-element.26.refs_0_), channel_id=1, source_target_pairs={{0,6},{2,4},{4,2},{6,0},{1,7},{3,5},{5,3},{7,1},{8,14},{10,12},{12... | collective-permute-start | bytes 393224 | tf_op jit(solution)/shard_map/ppermute | solution.py:446
  20.6 17.2 %all-to-all-start = ((f32[32,2,8,128]{3,2,1,0:T(8,128)}), f32[32,2,8,128]{3,2,1,0:T(8,128)S(1)}, u32[]{:S(2)}, u32[]{:S(2)}) async-start(f32[32,2,8,128]{3,2,1,0:T(8,128)} %send.1), calls=%async_computation | async-start | bytes 524288 | tf_op jit(solution)/shard_map/all_to_all | solution.py:477
  28.2 8.5 %collective-permute-start.6 = (f32[32,8,128]{2,1,0:T(8,128)S(1)}, f32[32,8,128]{2,1,0:T(8,128)S(1)}, u32[]{:S(2)}, u32[]{:S(2)}) collective-permute-start(f32[32,8,128]{2,1,0:T(8,128)S(1)} %get-tuple-element.31.refs_0_), channel_id=1, source_target_pairs={{0,1},{1,0},{2,3},{3,2},{4,5},{5,4},{6,7},{7,6},{8,9},{9,8},{10,11... | collective-permute-start | bytes 393224 | tf_op jit(solution)/shard_map/ppermute | solution.py:488
  28.5 8.2 %collective-permute-start.7 = (f32[32,8,128]{2,1,0:T(8,128)S(1)}, f32[32,8,128]{2,1,0:T(8,128)S(1)}, u32[]{:S(2)}, u32[]{:S(2)}) collective-permute-start(f32[32,8,128]{2,1,0:T(8,128)S(1)} %get-tuple-element.32.refs_1_), channel_id=1, source_target_pairs={{0,1},{1,0},{2,3},{3,2},{4,5},{5,4},{6,7},{7,6},{8,9},{9,8},{10,11... | collective-permute-start | bytes 393224 | tf_op jit(solution)/shard_map/ppermute | solution.py:488
  28.7 8.0 %collective-permute-start.8 = (f32[32,8,128]{2,1,0:T(8,128)S(1)}, f32[32,8,128]{2,1,0:T(8,128)S(1)}, u32[]{:S(2)}, u32[]{:S(2)}) collective-permute-start(f32[32,8,128]{2,1,0:T(8,128)S(1)} %get-tuple-element.33.refs_2_), channel_id=1, source_target_pairs={{0,1},{1,0},{2,3},{3,2},{4,5},{5,4},{6,7},{7,6},{8,9},{9,8},{10,11... | collective-permute-start | bytes 393224 | tf_op jit(solution)/shard_map/ppermute | solution.py:488
  29.0 7.7 %collective-permute-start.9 = (f32[32,8,128]{2,1,0:T(8,128)S(1)}, f32[32,8,128]{2,1,0:T(8,128)S(1)}, u32[]{:S(2)}, u32[]{:S(2)}) collective-permute-start(f32[32,8,128]{2,1,0:T(8,128)S(1)} %get-tuple-element.34.refs_3_), channel_id=1, source_target_pairs={{0,1},{1,0},{2,3},{3,2},{4,5},{5,4},{6,7},{7,6},{8,9},{9,8},{10,11... | collective-permute-start | bytes 393224 | tf_op jit(solution)/shard_map/ppermute | solution.py:488
  29.2 7.5 %collective-permute-start.5 = (f32[4,8,128]{2,1,0:T(8,128)S(1)}, f32[4,8,128]{2,1,0:T(8,128)S(1)}, u32[]{:S(2)}, u32[]{:S(2)}) collective-permute-start(f32[4,8,128]{2,1,0:T(8,128)S(1)} %get-tuple-element.29.own_ref), channel_id=1, source_target_pairs={{0,16},{8,24},{16,0},{24,8},{1,17},{9,25},{17,1},{25,9},{2,18},{10... | collective-permute-start | bytes 49160 | tf_op jit(solution)/shard_map/ppermute | solution.py:417

commit v11 on v9

--- a/solution.py
+++ b/solution.py
@@ -39,8 +39,8 @@
 
 
 def pack_kernel(planes, tiles, taper_hbm, u_hbm, t_hbm, noise_hbm, observed_hbm, var_hbm, cells_hbm,
-                low_ref, high_ref, obs_ref, t_ref, pick_hbm,
-                taper_ref, u_ref, noise_ref, row_ref, cells_ref, pick_ref, sems):
+                low_ref, high_ref, obs_ref, t_ref, pick_ref,
+                taper_ref, u_ref, noise_ref, row_ref, cells_ref, sems):
     stride = planes * tiles
     blocks = noise_ref.shape[1] // LANES
     copies = [
@@ -63,8 +63,6 @@
         block = cells_ref[0, slot]
         row = row_of(block // tiles, block % tiles, tiles)
         pick_ref[slot] = t_ref[pl.ds(row, ROWS, stride=stride), :]
-    picked = pltpu.make_async_copy(pick_ref, pick_hbm, sems.at[7])
-    picked.start()
     for kind, source in ((1, t_ref), (0, u_ref)):
         if kind == 0:
             copies[1].wait()
@@ -90,7 +88,6 @@
     for ref in (low_ref, high_ref):
         for at in range(obs_ref.shape[0]):
             ref[4 * tiles + 1 + at] = obs_ref[at]
-    picked.wait()
 
 
 def rot(value, by):
@@ -243,7 +240,7 @@
             turned = pltpu.roll(u2_ref[cell >> 7], (p - cell) & (LANES - 1), 1)
             found = jnp.where(lane == p, turned, found)
 
-        found_ref[part] = found
+        found_ref[part * ROWS : (part + 1) * ROWS, :] = found
 
 
 def send_kernel(found_ref, *refs):
@@ -274,28 +271,38 @@
 
 
 def split_kernel(by_xor, chips, place_ref, *refs):
-    *parts, split_ref, theta_ref, sems = refs
+    *parts, split_hbm, theta_ref, split_ref, sems = refs
     chip, core = place_ref[2], place_ref[3]
     same, other = parts[: len(parts) // 2], parts[len(parts) // 2 :]
     if not by_xor:
         same, other = ([ref.at[at] for at in range(chips)] for (ref,) in (same, other))
-    members = 2 * theta_ref.shape[0] * ROWS
-    copies = []
-    for at in range(chips):
-        where = chip ^ at if by_xor else at
-        copies.append(pltpu.make_async_copy(same[at], theta_ref.at[where, core], sems.at[2 * at]))
-        copies.append(pltpu.make_async_copy(other[at], theta_ref.at[where, 1 - core], sems.at[2 * at + 1]))
-    for copy in copies:
+    slots, members = theta_ref.shape[2], 2 * chips * ROWS
+    half = slots // 2
+    arriving, leaving = [[], []], []
+    for side in range(2):
+        cut = pl.ds(side * half, half)
+        for at in range(chips):
+            where = chip ^ at if by_xor else at
+            for slot, source in ((core, same[at]), (1 - core, other[at])):
+                target = theta_ref.at[where, slot, cut]
+                sem = sems.at[2 * chips * side + len(arriving[side])]
+                arriving[side].append(pltpu.make_async_copy(source.at[cut], target, sem))
+        leaving.append(pltpu.make_async_copy(split_ref.at[cut], split_hbm.at[cut], sems.at[4 * chips + side]))
+    for copy in arriving[0] + arriving[1]:
         copy.start()
-    for copy in copies:
-        copy.wait()
 
     def split(slot):
         high, low = halves(theta_ref[:, :, slot].reshape(members, LANES))
         split_ref[slot, :members, :] = high
         split_ref[slot, members:, :] = low
 
-    each(0, split_ref.shape[0], 4, split)
+    for side in range(2):
+        for copy in arriving[side]:
+            copy.wait()
+        each(side * half, (side + 1) * half, 4, split)
+        leaving[side].start()
+    for copy in leaving:
+        copy.wait()
 
 
 def stacked(value):
@@ -303,6 +310,10 @@
     return jnp.concatenate([high.astype(jnp.float32), low.astype(jnp.float32)], axis=0).astype(jnp.bfloat16)
 
 
+def beside(pair):
+    return jnp.concatenate(pair, axis=1)
+
+
 def fold(both):
     return both[:ROWS] + both[ROWS:]
 
@@ -312,16 +323,16 @@
 
 
 def update_kernel(slabs, planes, tiles, place_ref, count_ref, cells_hbm, probes_hbm, level_hbm,
-                  pred_ref, before_2_ref, seen_ref, own_ref, after_2_ref, split_hbm, t_hbm,
-                  post_ref, gain_ref, reach, cells_ref, probes_ref, level_ref, split_ref, sems):
-    groups, blocks = pred_ref.shape[0] // slabs, pred_ref.shape[1]
+                  pred_ref, before_2_ref, seen_ref, own_ref, after_2_ref, t_hbm, split_hbm, pick_hbm,
+                  post_ref, gain_ref, reach, cells_ref, probes_ref, level_ref, split_ref, pick_ref, sum_ref, sems):
+    groups, blocks = pred_ref.shape[0] // slabs, pred_ref.shape[1] // ROWS
     members = groups * ROWS
     share = 1.0 / (members - 1)
     copies = [
         pltpu.make_async_copy(source, target, sems.at[at])
         for at, (source, target) in enumerate((
             (cells_hbm, cells_ref), (probes_hbm, probes_ref), (level_hbm, level_ref),
-            (split_hbm, split_ref), (t_hbm, post_ref)))
+            (pick_hbm, pick_ref), (split_hbm, split_ref), (t_hbm, post_ref)))
     ]
     for copy in copies:
         copy.start()
@@ -341,38 +352,44 @@
         at = jnp.clip(wanted, 0, slabs - 1)
         live = jnp.where((wanted >= 0) & (wanted < slabs), 1.0, 0.0)
         for b in range(blocks):
-            predicted = pred_ref[pl.ds(at * groups, groups), b].reshape(members, LANES)
+            cut = slice(b * ROWS, (b + 1) * ROWS)
+            predicted = pred_ref[pl.ds(at * groups, groups), cut].reshape(members, LANES)
             mean = jnp.sum(predicted, axis=0, keepdims=True) / members
-            anomaly.append(halves((predicted - mean) * live))
+            anomaly.append(beside(halves((predicted - mean) * live)))
             variance.append(extra(d, blocks + b) + (1.0 - live))
             noise = seen[d][0][seen[d][1] + b]
-            scaled.append((extra(d, b) + noise - pred_ref[at * groups + group, b]) / variance[-1] * live)
-            left = stacked(scaled[-1])
-            high, low = anomaly[-1]
-            matches.append(fold(dot(left, high, 1) + dot(left, low, 1)))
+            scaled.append((extra(d, b) + noise - pred_ref[at * groups + group, cut]) / variance[-1] * live)
+            matches.append(fold(dot(beside([stacked(scaled[-1])] * 2), anomaly[-1], 1)))
     for d in range(1, 4):
         for i in range(blocks):
             total = jnp.zeros((ROWS, members), jnp.float32)
             for j in range(3 * blocks):
                 level = extra(d, 2 * blocks + i * 3 * blocks + j) / 256.0 * share
                 total = total + wide(level) * matches[(d - 1) * blocks + j]
-            high, low = anomaly[d * blocks + i]
+            both = anomaly[d * blocks + i]
             left = stacked(total)
-            correction = fold(dot(left, high, 0) + dot(left, low, 0))
+            correction = fold(dot(left, both[:, :LANES], 0) + dot(left, both[:, LANES:], 0))
             gain = scaled[d * blocks + i] - correction / variance[d * blocks + i]
             if d == 2:
                 gain_ref[:, i * LANES : (i + 1) * LANES] = gain
-            left = stacked(gain)
-            both = stacked(fold(dot(left, high, 1) + dot(left, low, 1)))
-            reach[(d - 1) * blocks + i] = jnp.concatenate([both, both], axis=1)
-    for copy in copies:
+            near = stacked(fold(dot(beside([stacked(gain)] * 2), both, 1)))
+            reach[(d - 1) * blocks + i] = beside([near, near])
+    for copy in copies[:4]:
         copy.wait()
-    for slot in range(split_ref.shape[0]):
+    slots = split_ref.shape[0]
+    blocks_of = [cells_ref[0, slot] for slot in range(slots)]
+    for slot in range(slots):
+        sum_ref[blocks_of[slot]] = pick_ref[slot]
+    copies[4].wait()
+    for slot in range(slots):
         weight = jnp.where(slot < count_ref[0], level_ref[0, slot].astype(jnp.float32) / 256.0, 0.0) * share
         change = fold(dot(reach[probes_ref[0, slot]], split_ref[slot], 0)) * weight
-        block = cells_ref[0, slot]
+        sum_ref[blocks_of[slot]] = sum_ref[blocks_of[slot]] + change
+    copies[5].wait()
+    for slot in range(slots):
+        block = blocks_of[slot]
         rows = pl.ds(row_of(block // tiles, block % tiles, tiles), ROWS, stride=planes * tiles)
-        post_ref[rows, :] = post_ref[rows, :] + change
+        post_ref[rows, :] = sum_ref[block]
 
 
 def shards(
@@ -411,18 +428,17 @@
             edge,
             obs_shape,
             jax.ShapeDtypeStruct(u_rows.shape, f32),
-            pltpu.HBM((slots, ROWS, LANES), f32),
+            jax.ShapeDtypeStruct((slots, ROWS, LANES), f32),
         ),
         in_specs=[HBM] * 7,
-        out_specs=(VMEM,) * 4 + (HBM,),
+        out_specs=(VMEM,) * 5,
         scratch_shapes=[
             pltpu.SMEM(probe_taper.shape, i32),
             pltpu.VMEM(u_rows.shape, f32),
             pltpu.VMEM((ROWS, probes), f32),
             pltpu.VMEM((2, probes), f32),
             pltpu.SMEM(pair_cells.shape, i32),
-            pltpu.VMEM((slots, ROWS, LANES), f32),
-            pltpu.SemaphoreType.DMA((8,)),
+            pltpu.SemaphoreType.DMA((7,)),
         ],
         compiler_params=params,
         name="pack",
@@ -468,7 +484,7 @@
         functools.partial(outer_kernel, planes, tiles),
         out_shape=(
             jax.ShapeDtypeStruct((planes * tiles, ROWS, LANES), f32),
-            jax.ShapeDtypeStruct((blocks, ROWS, LANES), f32),
+            jax.ShapeDtypeStruct((blocks * ROWS, LANES), f32),
             jax.ShapeDtypeStruct((2 * obs_tiles, ROWS, LANES), f32),
         ),
         in_specs=[HBM] + [VMEM] * 4,
@@ -484,7 +500,7 @@
     )(stay(probe_cells), before, after, edges, inner)
     sent = pl.pallas_call(
         send_kernel,
-        out_shape=pltpu.HBM((slabs * groups, blocks, ROWS, LANES), f32),
+        out_shape=pltpu.HBM((slabs * groups, blocks * ROWS, LANES), f32),
         in_specs=[VMEM] + [ANY] * len(parts),
         out_specs=HBM,
         scratch_shapes=[pltpu.SemaphoreType.DMA(())],
@@ -510,8 +526,12 @@
         functools.partial(split_kernel, by_xor, chips),
         out_shape=pltpu.HBM((slots, 2 * groups * ROWS, LANES), jnp.bfloat16),
         in_specs=[SMEM] + [ANY] * (2 * len(parts)),
-        out_specs=VMEM,
-        scratch_shapes=[pltpu.VMEM((chips, 2, slots, ROWS, LANES), f32), pltpu.SemaphoreType.DMA((2 * chips,))],
+        out_specs=HBM,
+        scratch_shapes=[
+            pltpu.VMEM((chips, 2, slots, ROWS, LANES), f32),
+            pltpu.VMEM((slots, 2 * groups * ROWS, LANES), jnp.bfloat16),
+            pltpu.SemaphoreType.DMA((4 * chips + 2,)),
+        ],
         compiler_params=params,
         cost_estimate=little,
         name="split",
@@ -522,7 +542,7 @@
             jax.ShapeDtypeStruct(u_rows.shape, f32),
             jax.ShapeDtypeStruct((members, probes), f32),
         ),
-        in_specs=[SMEM] * 2 + [HBM] * 3 + [VMEM] * 5 + [HBM] * 2,
+        in_specs=[SMEM] * 2 + [HBM] * 3 + [VMEM] * 5 + [HBM] * 2 + [ANY],
         out_specs=(VMEM,) * 2,
         scratch_shapes=[
             pltpu.VMEM((probe_taper.shape[2], 2 * ROWS, 2 * groups * ROWS), jnp.bfloat16),
@@ -530,12 +550,14 @@
             pltpu.SMEM(pair_cells.shape, i32),
             pltpu.SMEM(pair_cells.shape, i32),
             pltpu.VMEM(split.shape, jnp.bfloat16),
-            pltpu.SemaphoreType.DMA((5,)),
+            pltpu.VMEM(picked.shape, f32),
+            pltpu.VMEM((planes * tiles, ROWS, LANES), f32),
+            pltpu.SemaphoreType.DMA((6,)),
         ],
         compiler_params=params,
         name="update",
     )(place, pair_counts, *map(stay, (pair_cells, pair_probes, pair_taper)), pred_all,
-      before_2, seen, obs, after_2, stay(split), stay(t_rows))
+      before_2, seen, obs, after_2, stay(t_rows), stay(split), parts[0] if by_xor else picked)
     return (from_rows(u2_rows, shape), from_rows(post_rows, shape), gain)
 
 

time: 42.3 us -> 41.9 us (level)
  transfers between devices with their start and end apart: 11 -> 11, of which waited for: 3 -> 3; matrix products, arithmetic and copies ran while one was open for 0% -> 0% of each run, Pallas kernels for 26% -> 27%
where the time goes in v11:
time: 41.9 us; the launch traced here: 41.6 us
  starting transfers between devices  19.5 us (47%)
  Pallas kernels  17.7 us (42%)
  waiting for transfers between devices  2.93 us (7%)
  between operations  1.42 us (3%)
    all_to_all x1, starting transfers between devices, shards(): pred_all = lax.all_to_all(sent, ('space', 'chip', 'core'), 0, 0)  5.99 us
    ppermute x1, starting transfers between devices, shards(): before = lax.ppermute(high, 'space', upward)  4.95 us
    pallas_call x1, Pallas kernels, shards(): pl.pallas_call(functools.partial(inner_kernel, planes, tiles), out_shape=...  4.28 us
    pallas_call x1, Pallas kernels, shards(): pl.pallas_call(functools.partial(update_kernel, slabs, planes, tiles), ou...  3.81 us
    ppermute x3, starting transfers between devices, shards(): lax.ppermute(picked, 'chip', [(i, i ^ d) for i in range(chips)])  3.55 us
    pallas_call x1, Pallas kernels, shards(): pl.pallas_call(functools.partial(split_kernel, by_xor, chips), out_shape=...  3.12 us
    ppermute x1, starting transfers between devices, shards(): lax.ppermute(obs, 'space', [(i, (i + 2) % 4) for i in range(4)])  2.67 us
    pallas_call x1, Pallas kernels, shards(): pl.pallas_call(functools.partial(outer_kernel, planes, tiles), out_shape=...  2.1 us
  transfers between devices with their start and end apart: 11, of which 3 were waited for; matrix products, arithmetic and copies ran while one was open for 0% of the time, Pallas kernels for 27%

profile of v11, /device:TPU:0, one launch (start us, length us, event | category | flops | bytes accessed | tf_op | source)
XLA Modules:
  0.0 41.6 jit_solution(8204721904683593694)
XLA Ops:
  0.6 2.0 %pack.1 = (f32[69,8,128]{2,1,0:T(8,128)S(1)}, f32[69,8,128]{2,1,0:T(8,128)S(1)}, f32[4,8,128]{2,1,0:T(8,128)S(1)}, f32[2048,128]{1,0:T(8,128)S(1)}, f32[32,8,128]{2,1,0:T(8,128)S(1)}) custom-call(s32[1,2,6]{2,1,0:T(2,128)} %taper_hbm.1, f32[2048,128]{1,0:T(8,128)} %bitcast.26, f32[2048,128]{1,0:T(8,128)} %bitcast.28, f32[8,256]{1,0:T(8,128)} %noise_hbm.1, ...), custom_call_target="tpu_custom_call" | custom-call | tf_op jit(solution)/shard_map/pack/pallas_call | solution.py:424
  2.6 4.9 %collective-permute-start = (f32[69,8,128]{2,1,0:T(8,128)S(1)}, f32[69,8,128]{2,1,0:T(8,128)S(1)}, u32[]{:S(2)}, u32[]{:S(2)}) collective-permute-start(f32[69,8,128]{2,1,0:T(8,128)S(1)} %get-tuple-element.20), channel_id=1, source_target_pairs={{0,8},{8,16},{16,24},{1,9},{9,17},{17,25},{2,10},{10,18},{18,26},{... | collective-permute-start | bytes 847880 | tf_op jit(solution)/shard_map/ppermute | solution.py:448
  7.6 1.3 %collective-permute-start.1 = (f32[69,8,128]{2,1,0:T(8,128)S(1)}, f32[69,8,128]{2,1,0:T(8,128)S(1)}, u32[]{:S(2)}, u32[]{:S(2)}) collective-permute-start(f32[69,8,128]{2,1,0:T(8,128)S(1)} %get-tuple-element.21), channel_id=1, source_target_pairs={{8,0},{16,8},{24,16},{9,1},{17,9},{25,17},{10,2},{18,10},{26,18},{... | collective-permute-start | bytes 847880 | tf_op jit(solution)/shard_map/ppermute | solution.py:449
  8.9 1.6 %collective-permute-start.2 = (f32[32,8,128]{2,1,0:T(8,128)S(1)}, f32[32,8,128]{2,1,0:T(8,128)S(1)}, u32[]{:S(2)}, u32[]{:S(2)}) collective-permute-start(f32[32,8,128]{2,1,0:T(8,128)S(1)} %get-tuple-element.26.refs_0_), channel_id=1, source_target_pairs={{0,2},{2,0},{4,6},{6,4},{1,3},{3,1},{5,7},{7,5},{8,10},{10,8},{12,... | collective-permute-start | bytes 393224 | tf_op jit(solution)/shard_map/ppermute | solution.py:480
  10.4 1.5 %collective-permute-start.3 = (f32[32,8,128]{2,1,0:T(8,128)S(1)}, f32[32,8,128]{2,1,0:T(8,128)S(1)}, u32[]{:S(2)}, u32[]{:S(2)}) collective-permute-start(f32[32,8,128]{2,1,0:T(8,128)S(1)} %get-tuple-element.26.refs_0_), channel_id=1, source_target_pairs={{0,4},{2,6},{4,0},{6,2},{1,5},{3,7},{5,1},{7,3},{8,12},{10,14},{12... | collective-permute-start | bytes 393224 | tf_op jit(solution)/shard_map/ppermute | solution.py:480
  11.9 0.5 %collective-permute-start.4 = (f32[32,8,128]{2,1,0:T(8,128)S(1)}, f32[32,8,128]{2,1,0:T(8,128)S(1)}, u32[]{:S(2)}, u32[]{:S(2)}) collective-permute-start(f32[32,8,128]{2,1,0:T(8,128)S(1)} %get-tuple-element.26.refs_0_), channel_id=1, source_target_pairs={{0,6},{2,4},{4,2},{6,0},{1,7},{3,5},{5,3},{7,1},{8,14},{10,12},{12... | collective-permute-start | bytes 393224 | tf_op jit(solution)/shard_map/ppermute | solution.py:480
  12.4 4.3 %inner_planes.1 = (f32[256,8,128]{2,1,0:T(8,128)S(1)}, f32[224,8,128]{2,1,0:T(8,128)S(1)}) custom-call(f32[2048,128]{1,0:T(8,128)} %bitcast.27, f32[2048,128]{1,0:T(8,128)S(1)} %get-tuple-element.22.t_ref), custom_call_target="tpu_custom_call" | custom-call | bytes 15000000 | tf_op jit(solution)/shard_map/inner_planes/pallas_call | solution.py:456
  16.7 0.0 collective-permute-done.before_ref
  16.7 0.9 %collective-permute-done.1.after_ref = f32[69,8,128]{2,1,0:T(8,128)S(1)} collective-permute-done((f32[69,8,128]{2,1,0:T(8,128)S(1)}, f32[69,8,128]{2,1,0:T(8,128)S(1)}, u32[]{:S(2)}, u32[]{:S(2)}) %collective-permute-start.1) | collective-permute-done | bytes 282656 | tf_op jit(solution)/shard_map/ppermute | solution.py:449
  17.7 2.1 %outer_planes.1 = (f32[256,8,128]{2,1,0:T(8,128)S(1)}, f32[16,128]{1,0:T(8,128)S(1)}, f32[8,8,128]{2,1,0:T(8,128)S(1)}) custom-call(s32[256]{0:T(256)} %probe_hbm.1, f32[69,8,128]{2,1,0:T(8,128)S(1)} %collective-permute-done.before_ref, f32[69,8,128]{2,1,0:T(8,128)S(1)} %collective-permute-done.1.after_ref, ...), custom_call_target="tpu_custom_call", output_to_operand_aliasing={{0}: (4, {})} | custom-call | flops 1000 | bytes 1000 | tf_op jit(solution)/shard_map/outer_planes/pallas_call | solution.py:483
  19.8 0.0 collective-permute-done.2.refs_1_
  19.8 0.0 collective-permute-done.3.refs_2_
  19.8 0.0 collective-permute-done.4.refs_3_
  19.8 0.8 %send.1 = f32[32,16,128]{2,1,0:T(8,128)} custom-call(f32[16,128]{1,0:T(8,128)S(1)} %get-tuple-element.28.found_ref, f32[32,8,128]{2,1,0:T(8,128)S(1)} %get-tuple-element.26.refs_0_, f32[32,8,128]{2,1,0:T(8,128)S(1)} %collective-permute-done.2.refs_1_, f32[32,8,128]{2,1,0:T(8,128)S(1)} %collective-permute-done.3.refs_2_, ...), custom_call_target="tpu_custom_call" | custom-call | flops 1000 | bytes 1000 | tf_op jit(solution)/shard_map/send/pallas_call | solution.py:501
  20.6 6.0 %all-to-all-start = ((f32[32,16,128]{2,1,0:T(8,128)}), f32[32,16,128]{2,1,0:T(8,128)S(1)}, u32[]{:S(2)}, u32[]{:S(2)}) async-start(f32[32,16,128]{2,1,0:T(8,128)} %send.1), calls=%async_computation | async-start | bytes 524288 | tf_op jit(solution)/shard_map/all_to_all | solution.py:511
  26.6 1.6 %store.1 = (f32[2048,128]{1,0:T(8,128)}, f32[32,8,128]{2,1,0:T(8,128)S(1)}, f32[32,8,128]{2,1,0:T(8,128)S(1)}, f32[32,8,128]{2,1,0:T(8,128)S(1)}, f32[32,8,128]{2,1,0:T(8,128)S(1)}) custom-call(f32[256,8,128]{2,1,0:T(8,128)S(1)} %get-tuple-element.25.u2_ref, ...), custom_call_target="tpu_custom_call", output_to_operand_aliasing={{1}: (1, {}), {2}: (2, {}), {3}: (3, {}), {4}: (4, {})} | custom-call | flops 1000 | bytes 1000 | tf_op jit(solution)/shard_map/store/pallas_call | solution.py:512
  28.2 0.3 collective-permute-start.6
  28.5 0.3 collective-permute-start.7
  28.7 0.3 collective-permute-start.8
  29.0 0.3 collective-permute-start.9
  29.2 2.7 %collective-permute-start.5 = (f32[4,8,128]{2,1,0:T(8,128)S(1)}, f32[4,8,128]{2,1,0:T(8,128)S(1)}, u32[]{:S(2)}, u32[]{:S(2)}) collective-permute-start(f32[4,8,128]{2,1,0:T(8,128)S(1)} %get-tuple-element.29.own_ref), channel_id=1, source_target_pairs={{0,16},{8,24},{16,0},{24,8},{1,17},{9,25},{17,1},{25,9},{2,18},{10... | collective-permute-start | bytes 49160 | tf_op jit(solution)/shard_map/ppermute | solution.py:451
  31.9 0.1 pad_add_fusion.place_ref
  32.6 0.0 collective-permute-done.6.refs_4_
  32.7 0.0 collective-permute-done.7.refs_5_
  32.7 0.0 collective-permute-done.8.refs_6_
  32.7 0.0 collective-permute-done.9.refs_7_
  32.7 3.1 %split.1.split_hbm = bf16[32,128,128]{2,1,0:T(8,128)(2,1)} custom-call(s32[4]{0:T(128)S(1)} %pad_add_fusion.place_ref, f32[32,8,128]{2,1,0:T(8,128)S(1)} %get-tuple-element.31.refs_0_.pick_hbm, f32[32,8,128]{2,1,0:T(8,128)S(1)} %get-tuple-element.32.refs_1_, f32[32,8,128]{2,1,0:T(8,128)S(1)} %get-tuple-element.33.refs_2_, ...), custom_call_target="tpu_custom_call" | custom-call | flops 1000 | bytes 1000 | tf_op jit(solution)/shard_map/split/pallas_call | solution.py:525
  35.8 0.9 %collective-permute-done.5.before_2_ref.after_2_ref = f32[4,8,128]{2,1,0:T(8,128)S(1)} collective-permute-done((f32[4,8,128]{2,1,0:T(8,128)S(1)}, f32[4,8,128]{2,1,0:T(8,128)S(1)}, u32[]{:S(2)}, u32[]{:S(2)}) %collective-permute-start.5) | collective-permute-done | bytes 16416 | tf_op jit(solution)/shard_map/ppermute | solution.py:451
  36.7 1.1 %all-to-all-done.pred_ref = f32[32,16,128]{2,1,0:T(8,128)S(1)} async-done(((f32[32,16,128]{2,1,0:T(8,128)}), f32[32,16,128]{2,1,0:T(8,128)S(1)}, u32[]{:S(2)}, u32[]{:S(2)}) %all-to-all-start) | async-done | bytes 262176 | tf_op jit(solution)/shard_map/all_to_all | solution.py:511
  37.8 3.8 %update.1 = (f32[2048,128]{1,0:T(8,128)}, f32[8,256]{1,0:T(8,128)}) custom-call(s32[4]{0:T(128)S(1)} %pad_add_fusion.place_ref, s32[1]{0:T(128)S(6)} %copy.24.count_ref, s32[1,32]{1,0:T(1,128)} %cells_hbm.3, s32[1,32]{1,0:T(1,128)} %probes_hbm.1, s32[1,32]{1,0:T(1,128)} %level_hbm.1, f32[32,16,128]{2,1,0:T(8,128)S(1)} %all-to-all-done.pred_ref, ...), custom_call_target="tpu_custom_call" | custom-call | tf_op jit(solution)/shard_map/update/pallas_call | solution.py:539
Async XLA Ops:
  2.6 14.1 %collective-permute-start = (f32[69,8,128]{2,1,0:T(8,128)S(1)}, f32[69,8,128]{2,1,0:T(8,128)S(1)}, u32[]{:S(2)}, u32[]{:S(2)}) collective-permute-start(f32[69,8,128]{2,1,0:T(8,128)S(1)} %get-tuple-element.20), channel_id=1, source_target_pairs={{0,8},{8,16},{16,24},{1,9},{9,17},{17,25},{2,10},{10,18},{18,26},{... | collective-permute-start | bytes 847880 | tf_op jit(solution)/shard_map/ppermute | solution.py:448
  7.6 10.1 %collective-permute-start.1 = (f32[69,8,128]{2,1,0:T(8,128)S(1)}, f32[69,8,128]{2,1,0:T(8,128)S(1)}, u32[]{:S(2)}, u32[]{:S(2)}) collective-permute-start(f32[69,8,128]{2,1,0:T(8,128)S(1)} %get-tuple-element.21), channel_id=1, source_target_pairs={{8,0},{16,8},{24,16},{9,1},{17,9},{25,17},{10,2},{18,10},{26,18},{... | collective-permute-start | bytes 847880 | tf_op jit(solution)/shard_map/ppermute | solution.py:449
  8.9 10.9 %collective-permute-start.2 = (f32[32,8,128]{2,1,0:T(8,128)S(1)}, f32[32,8,128]{2,1,0:T(8,128)S(1)}, u32[]{:S(2)}, u32[]{:S(2)}) collective-permute-start(f32[32,8,128]{2,1,0:T(8,128)S(1)} %get-tuple-element.26.refs_0_), channel_id=1, source_target_pairs={{0,2},{2,0},{4,6},{6,4},{1,3},{3,1},{5,7},{7,5},{8,10},{10,8},{12,... | collective-permute-start | bytes 393224 | tf_op jit(solution)/shard_map/ppermute | solution.py:480
  10.4 9.4 %collective-permute-start.3 = (f32[32,8,128]{2,1,0:T(8,128)S(1)}, f32[32,8,128]{2,1,0:T(8,128)S(1)}, u32[]{:S(2)}, u32[]{:S(2)}) collective-permute-start(f32[32,8,128]{2,1,0:T(8,128)S(1)} %get-tuple-element.26.refs_0_), channel_id=1, source_target_pairs={{0,4},{2,6},{4,0},{6,2},{1,5},{3,7},{5,1},{7,3},{8,12},{10,14},{12... | collective-permute-start | bytes 393224 | tf_op jit(solution)/shard_map/ppermute | solution.py:480
  11.9 7.9 %collective-permute-start.4 = (f32[32,8,128]{2,1,0:T(8,128)S(1)}, f32[32,8,128]{2,1,0:T(8,128)S(1)}, u32[]{:S(2)}, u32[]{:S(2)}) collective-permute-start(f32[32,8,128]{2,1,0:T(8,128)S(1)} %get-tuple-element.26.refs_0_), channel_id=1, source_target_pairs={{0,6},{2,4},{4,2},{6,0},{1,7},{3,5},{5,3},{7,1},{8,14},{10,12},{12... | collective-permute-start | bytes 393224 | tf_op jit(solution)/shard_map/ppermute | solution.py:480
  20.6 17.2 %all-to-all-start = ((f32[32,16,128]{2,1,0:T(8,128)}), f32[32,16,128]{2,1,0:T(8,128)S(1)}, u32[]{:S(2)}, u32[]{:S(2)}) async-start(f32[32,16,128]{2,1,0:T(8,128)} %send.1), calls=%async_computation | async-start | bytes 524288 | tf_op jit(solution)/shard_map/all_to_all | solution.py:511
  28.2 4.4 %collective-permute-start.6 = (f32[32,8,128]{2,1,0:T(8,128)S(1)}, f32[32,8,128]{2,1,0:T(8,128)S(1)}, u32[]{:S(2)}, u32[]{:S(2)}) collective-permute-start(f32[32,8,128]{2,1,0:T(8,128)S(1)} %get-tuple-element.31.refs_0_.pick_hbm), channel_id=1, source_target_pairs={{0,1},{1,0},{2,3},{3,2},{4,5},{5,4},{6,7},{7,6},{8,9},{9,8},{10,11... | collective-permute-start | bytes 393224 | tf_op jit(solution)/shard_map/ppermute | solution.py:522
  28.5 4.2 %collective-permute-start.7 = (f32[32,8,128]{2,1,0:T(8,128)S(1)}, f32[32,8,128]{2,1,0:T(8,128)S(1)}, u32[]{:S(2)}, u32[]{:S(2)}) collective-permute-start(f32[32,8,128]{2,1,0:T(8,128)S(1)} %get-tuple-element.32.refs_1_), channel_id=1, source_target_pairs={{0,1},{1,0},{2,3},{3,2},{4,5},{5,4},{6,7},{7,6},{8,9},{9,8},{10,11... | collective-permute-start | bytes 393224 | tf_op jit(solution)/shard_map/ppermute | solution.py:522
  28.7 3.9 %collective-permute-start.8 = (f32[32,8,128]{2,1,0:T(8,128)S(1)}, f32[32,8,128]{2,1,0:T(8,128)S(1)}, u32[]{:S(2)}, u32[]{:S(2)}) collective-permute-start(f32[32,8,128]{2,1,0:T(8,128)S(1)} %get-tuple-element.33.refs_2_), channel_id=1, source_target_pairs={{0,1},{1,0},{2,3},{3,2},{4,5},{5,4},{6,7},{7,6},{8,9},{9,8},{10,11... | collective-permute-start | bytes 393224 | tf_op jit(solution)/shard_map/ppermute | solution.py:522
  29.0 3.7 %collective-permute-start.9 = (f32[32,8,128]{2,1,0:T(8,128)S(1)}, f32[32,8,128]{2,1,0:T(8,128)S(1)}, u32[]{:S(2)}, u32[]{:S(2)}) collective-permute-start(f32[32,8,128]{2,1,0:T(8,128)S(1)} %get-tuple-element.34.refs_3_), channel_id=1, source_target_pairs={{0,1},{1,0},{2,3},{3,2},{4,5},{5,4},{6,7},{7,6},{8,9},{9,8},{10,11... | collective-permute-start | bytes 393224 | tf_op jit(solution)/shard_map/ppermute | solution.py:522
  29.2 7.5 %collective-permute-start.5 = (f32[4,8,128]{2,1,0:T(8,128)S(1)}, f32[4,8,128]{2,1,0:T(8,128)S(1)}, u32[]{:S(2)}, u32[]{:S(2)}) collective-permute-start(f32[4,8,128]{2,1,0:T(8,128)S(1)} %get-tuple-element.29.own_ref), channel_id=1, source_target_pairs={{0,16},{8,24},{16,0},{24,8},{1,17},{9,25},{17,1},{25,9},{2,18},{10... | collective-permute-start | bytes 49160 | tf_op jit(solution)/shard_map/ppermute | solution.py:451

commit v12 on v11

--- a/solution.py
+++ b/solution.py
@@ -100,40 +100,48 @@
     return lane < NZ, height == 0, height == NZ - 1
 
 
-def coefficients(masks, low, here, high):
+def around(tiles, value):
+    here = first = value(0)
+    before, turned = rot(value(tiles - 1), NZ), rot(here, NZ)
+    first_turned = turned
+    for tile in range(tiles):
+        last = tile == tiles - 1
+        ahead = first if last else value(tile + 1)
+        after = first_turned if last else rot(ahead, NZ)
+        yield here, turned, before, after
+        here, before, turned = ahead, turned, after
+
+
+def weigh(masks, parts, low, high):
     first_half, floor, roof = masks
-    tiles = len(here)
-    turned = [rot(value, NZ) for value in here]
-    out = []
-    for tile in range(tiles):
-        mid = here[tile]
-        near = mid + turned[tile]
-        far = mid + jnp.where(first_half, turned[tile - 1], turned[(tile + 1) % tiles])
-        up = mid + jnp.where(roof, HALF_DT, rot(mid, -1))
-        down = mid + jnp.where(floor, HALF_DT, rot(mid, 1))
-        below = mid + low[tile]
-        above = mid + high[tile]
-        diag = 1.0 - ((near + far) + (up + down) + (below + above))
-        out.append((diag, near, far, jnp.where(roof, 0.0, up), jnp.where(floor, 0.0, down), below, above))
-    return out
-
-
-def step(masks, weights, low, here, high):
-    first_half = masks[0]
-    tiles = len(here)
-    turned = [rot(value, NZ) for value in here]
-    out = []
-    for tile in range(tiles):
-        diag, near, far, up, down, below, above = weights[tile]
-        mid = here[tile]
-        beyond = jnp.where(first_half, turned[tile - 1], turned[(tile + 1) % tiles])
-        out.append(
-            (diag * mid + near * turned[tile])
-            + (far * beyond + up * rot(mid, -1))
-            + (down * rot(mid, 1) + below * low[tile])
-            + above * high[tile]
-        )
-    return out
+    mid, turned, before, after = parts
+    near = mid + turned
+    far = mid + jnp.where(first_half, before, after)
+    up = mid + jnp.where(roof, HALF_DT, rot(mid, -1))
+    down = mid + jnp.where(floor, HALF_DT, rot(mid, 1))
+    below = mid + low
+    above = mid + high
+    diag = 1.0 - ((near + far) + (up + down) + (below + above))
+    return diag, near, far, jnp.where(roof, 0.0, up), jnp.where(floor, 0.0, down), below, above
+
+
+def blend(masks, weights, parts, low, high):
+    diag, near, far, up, down, below, above = weights
+    mid, turned, before, after = parts
+    beyond = jnp.where(masks[0], before, after)
+    return (
+        (diag * mid + near * turned)
+        + (far * beyond + up * rot(mid, -1))
+        + (down * rot(mid, 1) + below * low)
+        + above * high
+    )
+
+
+def advance(masks, tiles, v, u, emit):
+    pairs = zip(around(tiles, functools.partial(v, 0)), around(tiles, functools.partial(u, 0)))
+    for tile, (v_parts, u_parts) in enumerate(pairs):
+        weights = weigh(masks, v_parts, v(-1, tile), v(1, tile))
+        emit(tile, weights, blend(masks, weights, u_parts, u(-1, tile), u(1, tile)))
 
 
 def plane_of(ref, at, tiles):
@@ -176,19 +184,19 @@
             u0[x * tiles + tile] = u_ref[rows_at(x, tile), :]
 
     def first_step(x):
-        weights = coefficients(masks, *[plane_of(hv, x + d, tiles) for d in (-1, 0, 1)])
-        for tile in range(tiles):
+        def emit(tile, weights, value):
             for kind in range(5):
-                held[kind, x * tiles + tile] = weights[tile][kind]
-        put(u1, x, step(masks, weights, *[plane_of(u0, x + d, tiles) for d in (-1, 0, 1)]))
+                held[kind, x * tiles + tile] = weights[kind]
+            u1[x * tiles + tile] = value
+
+        advance(masks, tiles, lambda d, tile: hv[(x + d) * tiles + tile], lambda d, tile: u0[(x + d) * tiles + tile], emit)
 
     def second_step(x):
-        weights = []
-        for tile in range(tiles):
+        for tile, parts in enumerate(around(tiles, lambda tile: u1[x * tiles + tile])):
             at = x * tiles + tile
             here = hv[at]
-            weights.append([held[kind, at] for kind in range(5)] + [here + hv[at - tiles], here + hv[at + tiles]])
-        put(u2_ref, x, step(masks, weights, *[plane_of(u1, x + d, tiles) for d in (-1, 0, 1)]))
+            weights = [held[kind, at] for kind in range(5)] + [here + hv[at - tiles], here + hv[at + tiles]]
+            u2_ref[at] = blend(masks, weights, parts, u1[at - tiles], u1[at + tiles])
 
     each(0, planes, 4, load_t)
     copy.wait()
@@ -205,7 +213,7 @@
 
 
 def outer_kernel(planes, tiles, probe_hbm, before_ref, after_ref, edge_ref, inner_ref,
-                 u2_ref, found_ref, seen_ref, probe_ref, sem):
+                 u2_ref, found_ref, seen_ref, probe_ref, v_ref, n_ref, sem):
     probe_copy = pltpu.make_async_copy(probe_hbm, probe_ref, sem)
     probe_copy.start()
     masks = lane_masks()
@@ -214,22 +222,35 @@
     for at in range(count):
         seen_ref[at] = before_ref[4 * tiles + 1 + at]
         seen_ref[count + at] = after_ref[4 * tiles + 1 + at]
-    edge = [plane_of(edge_ref, at, tiles) for at in range(14)]
     last = planes - 1
-    for ref, own_u, own_v, own_1, where in (
-        (before_ref, edge[0:2], edge[4:7], edge[10:12], (0, 1)),
-        (after_ref, edge[3:1:-1], edge[9:6:-1], edge[13:11:-1], (last, last - 1)),
+    for ref, own_u, own_v, own_1, where, order in (
+        (before_ref, (0, 1), (4, 5, 6), (10, 11), (0, 1), (0, 1)),
+        (after_ref, (3, 2), (9, 8, 7), (13, 12), (last, last - 1), (1, 0)),
     ):
-        order = (0, 1) if ref is before_ref else (1, 0)
-        u = [plane_of(ref, d, tiles) for d in order] + own_u
-        v = [[HALF_DT * jnp.exp(t) for t in plane_of(ref, 2 + d, tiles)] for d in order] + own_v
+        for d in range(2):
+            for tile in range(tiles):
+                v_ref[d * tiles + tile] = HALF_DT * jnp.exp(ref[(2 + order[d]) * tiles + tile])
         live = ref[4 * tiles]
-        weights = [coefficients(masks, v[d], v[d + 1], v[d + 2]) for d in range(3)]
-        next_u = [step(masks, weights[d], u[d], u[d + 1], u[d + 2]) for d in range(2)]
-        next_u[0] = [value * live for value in next_u[0]]
-        next_u = next_u + own_1
+
+        def v(d, tile):
+            return v_ref[d * tiles + tile] if d < 2 else edge_ref[own_v[d - 2] * tiles + tile]
+
+        def u(d, tile):
+            return ref[order[d] * tiles + tile] if d < 2 else edge_ref[own_u[d - 2] * tiles + tile]
+
+        def u1(d, tile):
+            return n_ref[d * tiles + tile] if d < 2 else edge_ref[own_1[d - 2] * tiles + tile]
+
+        def first(d, tile, weights, value):
+            n_ref[d * tiles + tile] = value * live if d == 0 else value
+
+        def second(d, tile, weights, value):
+            u2_ref[where[d] * tiles + tile] = value
+
         for d in range(2):
-            put(u2_ref, where[d], step(masks, weights[d + 1], next_u[d], next_u[d + 1], next_u[d + 2]))
+            advance(masks, tiles, lambda s, t: v(d + 1 + s, t), lambda s, t: u(d + 1 + s, t), functools.partial(first, d))
+        for d in range(2):
+            advance(masks, tiles, lambda s, t: v(d + 2 + s, t), lambda s, t: u1(d + 1 + s, t), functools.partial(second, d))
 
     probe_copy.wait()
     lane = lax.broadcasted_iota(jnp.int32, (ROWS, LANES), 1)
@@ -491,6 +512,8 @@
         out_specs=(VMEM,) * 3,
         scratch_shapes=[
             pltpu.SMEM(probe_cells.shape, i32),
+            pltpu.VMEM((2 * tiles, ROWS, LANES), f32),
+            pltpu.VMEM((2 * tiles, ROWS, LANES), f32),
             pltpu.SemaphoreType.DMA(()),
         ],
         input_output_aliases={4: 0},

time: 41.9 us -> 42.1 us (level)
  no operation moved by 1% of the time
where the time goes in v12:
time: 42.1 us; the launch traced here: 41.7 us
  starting transfers between devices  19.5 us (46%)
  Pallas kernels  17.8 us (42%)
  waiting for transfers between devices  2.91 us (7%)
  between operations  1.42 us (3%)
    all_to_all x1, starting transfers between devices, shards(): pred_all = lax.all_to_all(sent, ('space', 'chip', 'core'), 0, 0)  6.02 us
    ppermute x1, starting transfers between devices, shards(): before = lax.ppermute(high, 'space', upward)  4.95 us
    pallas_call x1, Pallas kernels, shards(): pl.pallas_call(functools.partial(inner_kernel, planes, tiles), out_shape=...  4.31 us
    pallas_call x1, Pallas kernels, shards(): pl.pallas_call(functools.partial(update_kernel, slabs, planes, tiles), ou...  3.81 us
    ppermute x3, starting transfers between devices, shards(): lax.ppermute(picked, 'chip', [(i, i ^ d) for i in range(chips)])  3.55 us
    pallas_call x1, Pallas kernels, shards(): pl.pallas_call(functools.partial(split_kernel, by_xor, chips), out_shape=...  3.12 us
    ppermute x1, starting transfers between devices, shards(): lax.ppermute(obs, 'space', [(i, (i + 2) % 4) for i in range(4)])  2.67 us
    pallas_call x1, Pallas kernels, shards(): pl.pallas_call(functools.partial(outer_kernel, planes, tiles), out_shape=...  2.21 us
  transfers between devices with their start and end apart: 11, of which 3 were waited for; matrix products, arithmetic and copies ran while one was open for 0% of the time, Pallas kernels for 27%

profile of v12, /device:TPU:0, one launch (start us, length us, event | category | flops | bytes accessed | tf_op | source)
XLA Modules:
  0.0 41.7 jit_solution(7390259025644234867)
XLA Ops:
  0.6 2.0 %pack.1 = (f32[69,8,128]{2,1,0:T(8,128)S(1)}, f32[69,8,128]{2,1,0:T(8,128)S(1)}, f32[4,8,128]{2,1,0:T(8,128)S(1)}, f32[2048,128]{1,0:T(8,128)S(1)}, f32[32,8,128]{2,1,0:T(8,128)S(1)}) custom-call(s32[1,2,6]{2,1,0:T(2,128)} %taper_hbm.1, f32[2048,128]{1,0:T(8,128)} %bitcast.26, f32[2048,128]{1,0:T(8,128)} %bitcast.28, f32[8,256]{1,0:T(8,128)} %noise_hbm.1, ...), custom_call_target="tpu_custom_call" | custom-call | tf_op jit(solution)/shard_map/pack/pallas_call | solution.py:445
  2.6 4.9 %collective-permute-start = (f32[69,8,128]{2,1,0:T(8,128)S(1)}, f32[69,8,128]{2,1,0:T(8,128)S(1)}, u32[]{:S(2)}, u32[]{:S(2)}) collective-permute-start(f32[69,8,128]{2,1,0:T(8,128)S(1)} %get-tuple-element.20), channel_id=1, source_target_pairs={{0,8},{8,16},{16,24},{1,9},{9,17},{17,25},{2,10},{10,18},{18,26},{... | collective-permute-start | bytes 847880 | tf_op jit(solution)/shard_map/ppermute | solution.py:469
  7.6 1.3 %collective-permute-start.1 = (f32[69,8,128]{2,1,0:T(8,128)S(1)}, f32[69,8,128]{2,1,0:T(8,128)S(1)}, u32[]{:S(2)}, u32[]{:S(2)}) collective-permute-start(f32[69,8,128]{2,1,0:T(8,128)S(1)} %get-tuple-element.21), channel_id=1, source_target_pairs={{8,0},{16,8},{24,16},{9,1},{17,9},{25,17},{10,2},{18,10},{26,18},{... | collective-permute-start | bytes 847880 | tf_op jit(solution)/shard_map/ppermute | solution.py:470
  8.9 1.6 %collective-permute-start.2 = (f32[32,8,128]{2,1,0:T(8,128)S(1)}, f32[32,8,128]{2,1,0:T(8,128)S(1)}, u32[]{:S(2)}, u32[]{:S(2)}) collective-permute-start(f32[32,8,128]{2,1,0:T(8,128)S(1)} %get-tuple-element.26.refs_0_), channel_id=1, source_target_pairs={{0,2},{2,0},{4,6},{6,4},{1,3},{3,1},{5,7},{7,5},{8,10},{10,8},{12,... | collective-permute-start | bytes 393224 | tf_op jit(solution)/shard_map/ppermute | solution.py:501
  10.4 1.5 %collective-permute-start.3 = (f32[32,8,128]{2,1,0:T(8,128)S(1)}, f32[32,8,128]{2,1,0:T(8,128)S(1)}, u32[]{:S(2)}, u32[]{:S(2)}) collective-permute-start(f32[32,8,128]{2,1,0:T(8,128)S(1)} %get-tuple-element.26.refs_0_), channel_id=1, source_target_pairs={{0,4},{2,6},{4,0},{6,2},{1,5},{3,7},{5,1},{7,3},{8,12},{10,14},{12... | collective-permute-start | bytes 393224 | tf_op jit(solution)/shard_map/ppermute | solution.py:501
  11.9 0.5 %collective-permute-start.4 = (f32[32,8,128]{2,1,0:T(8,128)S(1)}, f32[32,8,128]{2,1,0:T(8,128)S(1)}, u32[]{:S(2)}, u32[]{:S(2)}) collective-permute-start(f32[32,8,128]{2,1,0:T(8,128)S(1)} %get-tuple-element.26.refs_0_), channel_id=1, source_target_pairs={{0,6},{2,4},{4,2},{6,0},{1,7},{3,5},{5,3},{7,1},{8,14},{10,12},{12... | collective-permute-start | bytes 393224 | tf_op jit(solution)/shard_map/ppermute | solution.py:501
  12.4 4.3 %inner_planes.1 = (f32[256,8,128]{2,1,0:T(8,128)S(1)}, f32[224,8,128]{2,1,0:T(8,128)S(1)}) custom-call(f32[2048,128]{1,0:T(8,128)} %bitcast.27, f32[2048,128]{1,0:T(8,128)S(1)} %get-tuple-element.22.t_ref), custom_call_target="tpu_custom_call" | custom-call | bytes 15000000 | tf_op jit(solution)/shard_map/inner_planes/pallas_call | solution.py:477
  16.7 0.0 collective-permute-done.before_ref
  16.8 0.9 %collective-permute-done.1.after_ref = f32[69,8,128]{2,1,0:T(8,128)S(1)} collective-permute-done((f32[69,8,128]{2,1,0:T(8,128)S(1)}, f32[69,8,128]{2,1,0:T(8,128)S(1)}, u32[]{:S(2)}, u32[]{:S(2)}) %collective-permute-start.1) | collective-permute-done | bytes 282656 | tf_op jit(solution)/shard_map/ppermute | solution.py:470
  17.7 2.2 %outer_planes.1 = (f32[256,8,128]{2,1,0:T(8,128)S(1)}, f32[16,128]{1,0:T(8,128)S(1)}, f32[8,8,128]{2,1,0:T(8,128)S(1)}) custom-call(s32[256]{0:T(256)} %probe_hbm.1, f32[69,8,128]{2,1,0:T(8,128)S(1)} %collective-permute-done.before_ref, f32[69,8,128]{2,1,0:T(8,128)S(1)} %collective-permute-done.1.after_ref, ...), custom_call_target="tpu_custom_call", output_to_operand_aliasing={{0}: (4, {})} | custom-call | flops 1000 | bytes 1000 | tf_op jit(solution)/shard_map/outer_planes/pallas_call | solution.py:504
  19.9 0.0 collective-permute-done.2.refs_1_
  19.9 0.0 collective-permute-done.3.refs_2_
  19.9 0.0 collective-permute-done.4.refs_3_
  19.9 0.8 %send.1 = f32[32,16,128]{2,1,0:T(8,128)} custom-call(f32[16,128]{1,0:T(8,128)S(1)} %get-tuple-element.28.found_ref, f32[32,8,128]{2,1,0:T(8,128)S(1)} %get-tuple-element.26.refs_0_, f32[32,8,128]{2,1,0:T(8,128)S(1)} %collective-permute-done.2.refs_1_, f32[32,8,128]{2,1,0:T(8,128)S(1)} %collective-permute-done.3.refs_2_, ...), custom_call_target="tpu_custom_call" | custom-call | flops 1000 | bytes 1000 | tf_op jit(solution)/shard_map/send/pallas_call | solution.py:524
  20.7 6.0 %all-to-all-start = ((f32[32,16,128]{2,1,0:T(8,128)}), f32[32,16,128]{2,1,0:T(8,128)S(1)}, u32[]{:S(2)}, u32[]{:S(2)}) async-start(f32[32,16,128]{2,1,0:T(8,128)} %send.1), calls=%async_computation | async-start | bytes 524288 | tf_op jit(solution)/shard_map/all_to_all | solution.py:534
  26.8 1.6 %store.1 = (f32[2048,128]{1,0:T(8,128)}, f32[32,8,128]{2,1,0:T(8,128)S(1)}, f32[32,8,128]{2,1,0:T(8,128)S(1)}, f32[32,8,128]{2,1,0:T(8,128)S(1)}, f32[32,8,128]{2,1,0:T(8,128)S(1)}) custom-call(f32[256,8,128]{2,1,0:T(8,128)S(1)} %get-tuple-element.25.u2_ref, ...), custom_call_target="tpu_custom_call", output_to_operand_aliasing={{1}: (1, {}), {2}: (2, {}), {3}: (3, {}), {4}: (4, {})} | custom-call | flops 1000 | bytes 1000 | tf_op jit(solution)/shard_map/store/pallas_call | solution.py:535
  28.4 0.3 collective-permute-start.6
  28.6 0.3 collective-permute-start.7
  28.9 0.3 collective-permute-start.8
  29.1 0.3 collective-permute-start.9
  29.4 2.7 %collective-permute-start.5 = (f32[4,8,128]{2,1,0:T(8,128)S(1)}, f32[4,8,128]{2,1,0:T(8,128)S(1)}, u32[]{:S(2)}, u32[]{:S(2)}) collective-permute-start(f32[4,8,128]{2,1,0:T(8,128)S(1)} %get-tuple-element.29.own_ref), channel_id=1, source_target_pairs={{0,16},{8,24},{16,0},{24,8},{1,17},{9,25},{17,1},{25,9},{2,18},{10... | collective-permute-start | bytes 49160 | tf_op jit(solution)/shard_map/ppermute | solution.py:472
  32.0 0.1 pad_add_fusion.place_ref
  32.8 0.0 collective-permute-done.6.refs_4_
  32.8 0.0 collective-permute-done.7.refs_5_
  32.8 0.0 collective-permute-done.8.refs_6_
  32.8 0.0 collective-permute-done.9.refs_7_
  32.8 3.1 %split.1.split_hbm = bf16[32,128,128]{2,1,0:T(8,128)(2,1)} custom-call(s32[4]{0:T(128)S(1)} %pad_add_fusion.place_ref, f32[32,8,128]{2,1,0:T(8,128)S(1)} %get-tuple-element.31.refs_0_.pick_hbm, f32[32,8,128]{2,1,0:T(8,128)S(1)} %get-tuple-element.32.refs_1_, f32[32,8,128]{2,1,0:T(8,128)S(1)} %get-tuple-element.33.refs_2_, ...), custom_call_target="tpu_custom_call" | custom-call | flops 1000 | bytes 1000 | tf_op jit(solution)/shard_map/split/pallas_call | solution.py:548
  35.9 0.9 %collective-permute-done.5.before_2_ref.after_2_ref = f32[4,8,128]{2,1,0:T(8,128)S(1)} collective-permute-done((f32[4,8,128]{2,1,0:T(8,128)S(1)}, f32[4,8,128]{2,1,0:T(8,128)S(1)}, u32[]{:S(2)}, u32[]{:S(2)}) %collective-permute-start.5) | collective-permute-done | bytes 16416 | tf_op jit(solution)/shard_map/ppermute | solution.py:472
  36.8 1.1 %all-to-all-done.pred_ref = f32[32,16,128]{2,1,0:T(8,128)S(1)} async-done(((f32[32,16,128]{2,1,0:T(8,128)}), f32[32,16,128]{2,1,0:T(8,128)S(1)}, u32[]{:S(2)}, u32[]{:S(2)}) %all-to-all-start) | async-done | bytes 262176 | tf_op jit(solution)/shard_map/all_to_all | solution.py:534
  37.9 3.8 %update.1 = (f32[2048,128]{1,0:T(8,128)}, f32[8,256]{1,0:T(8,128)}) custom-call(s32[4]{0:T(128)S(1)} %pad_add_fusion.place_ref, s32[1]{0:T(128)S(6)} %copy.24.count_ref, s32[1,32]{1,0:T(1,128)} %cells_hbm.3, s32[1,32]{1,0:T(1,128)} %probes_hbm.1, s32[1,32]{1,0:T(1,128)} %level_hbm.1, f32[32,16,128]{2,1,0:T(8,128)S(1)} %all-to-all-done.pred_ref, ...), custom_call_target="tpu_custom_call" | custom-call | tf_op jit(solution)/shard_map/update/pallas_call | solution.py:562
Async XLA Ops:
  2.6 14.1 %collective-permute-start = (f32[69,8,128]{2,1,0:T(8,128)S(1)}, f32[69,8,128]{2,1,0:T(8,128)S(1)}, u32[]{:S(2)}, u32[]{:S(2)}) collective-permute-start(f32[69,8,128]{2,1,0:T(8,128)S(1)} %get-tuple-element.20), channel_id=1, source_target_pairs={{0,8},{8,16},{16,24},{1,9},{9,17},{17,25},{2,10},{10,18},{18,26},{... | collective-permute-start | bytes 847880 | tf_op jit(solution)/shard_map/ppermute | solution.py:469
  7.6 10.1 %collective-permute-start.1 = (f32[69,8,128]{2,1,0:T(8,128)S(1)}, f32[69,8,128]{2,1,0:T(8,128)S(1)}, u32[]{:S(2)}, u32[]{:S(2)}) collective-permute-start(f32[69,8,128]{2,1,0:T(8,128)S(1)} %get-tuple-element.21), channel_id=1, source_target_pairs={{8,0},{16,8},{24,16},{9,1},{17,9},{25,17},{10,2},{18,10},{26,18},{... | collective-permute-start | bytes 847880 | tf_op jit(solution)/shard_map/ppermute | solution.py:470
  8.9 11.0 %collective-permute-start.2 = (f32[32,8,128]{2,1,0:T(8,128)S(1)}, f32[32,8,128]{2,1,0:T(8,128)S(1)}, u32[]{:S(2)}, u32[]{:S(2)}) collective-permute-start(f32[32,8,128]{2,1,0:T(8,128)S(1)} %get-tuple-element.26.refs_0_), channel_id=1, source_target_pairs={{0,2},{2,0},{4,6},{6,4},{1,3},{3,1},{5,7},{7,5},{8,10},{10,8},{12,... | collective-permute-start | bytes 393224 | tf_op jit(solution)/shard_map/ppermute | solution.py:501
  10.4 9.5 %collective-permute-start.3 = (f32[32,8,128]{2,1,0:T(8,128)S(1)}, f32[32,8,128]{2,1,0:T(8,128)S(1)}, u32[]{:S(2)}, u32[]{:S(2)}) collective-permute-start(f32[32,8,128]{2,1,0:T(8,128)S(1)} %get-tuple-element.26.refs_0_), channel_id=1, source_target_pairs={{0,4},{2,6},{4,0},{6,2},{1,5},{3,7},{5,1},{7,3},{8,12},{10,14},{12... | collective-permute-start | bytes 393224 | tf_op jit(solution)/shard_map/ppermute | solution.py:501
  11.9 8.0 %collective-permute-start.4 = (f32[32,8,128]{2,1,0:T(8,128)S(1)}, f32[32,8,128]{2,1,0:T(8,128)S(1)}, u32[]{:S(2)}, u32[]{:S(2)}) collective-permute-start(f32[32,8,128]{2,1,0:T(8,128)S(1)} %get-tuple-element.26.refs_0_), channel_id=1, source_target_pairs={{0,6},{2,4},{4,2},{6,0},{1,7},{3,5},{5,3},{7,1},{8,14},{10,12},{12... | collective-permute-start | bytes 393224 | tf_op jit(solution)/shard_map/ppermute | solution.py:501
  20.7 17.2 %all-to-all-start = ((f32[32,16,128]{2,1,0:T(8,128)}), f32[32,16,128]{2,1,0:T(8,128)S(1)}, u32[]{:S(2)}, u32[]{:S(2)}) async-start(f32[32,16,128]{2,1,0:T(8,128)} %send.1), calls=%async_computation | async-start | bytes 524288 | tf_op jit(solution)/shard_map/all_to_all | solution.py:534
  28.4 4.4 %collective-permute-start.6 = (f32[32,8,128]{2,1,0:T(8,128)S(1)}, f32[32,8,128]{2,1,0:T(8,128)S(1)}, u32[]{:S(2)}, u32[]{:S(2)}) collective-permute-start(f32[32,8,128]{2,1,0:T(8,128)S(1)} %get-tuple-element.31.refs_0_.pick_hbm), channel_id=1, source_target_pairs={{0,1},{1,0},{2,3},{3,2},{4,5},{5,4},{6,7},{7,6},{8,9},{9,8},{10,11... | collective-permute-start | bytes 393224 | tf_op jit(solution)/shard_map/ppermute | solution.py:545
  28.6 4.2 %collective-permute-start.7 = (f32[32,8,128]{2,1,0:T(8,128)S(1)}, f32[32,8,128]{2,1,0:T(8,128)S(1)}, u32[]{:S(2)}, u32[]{:S(2)}) collective-permute-start(f32[32,8,128]{2,1,0:T(8,128)S(1)} %get-tuple-element.32.refs_1_), channel_id=1, source_target_pairs={{0,1},{1,0},{2,3},{3,2},{4,5},{5,4},{6,7},{7,6},{8,9},{9,8},{10,11... | collective-permute-start | bytes 393224 | tf_op jit(solution)/shard_map/ppermute | solution.py:545
  28.9 3.9 %collective-permute-start.8 = (f32[32,8,128]{2,1,0:T(8,128)S(1)}, f32[32,8,128]{2,1,0:T(8,128)S(1)}, u32[]{:S(2)}, u32[]{:S(2)}) collective-permute-start(f32[32,8,128]{2,1,0:T(8,128)S(1)} %get-tuple-element.33.refs_2_), channel_id=1, source_target_pairs={{0,1},{1,0},{2,3},{3,2},{4,5},{5,4},{6,7},{7,6},{8,9},{9,8},{10,11... | collective-permute-start | bytes 393224 | tf_op jit(solution)/shard_map/ppermute | solution.py:545
  29.1 3.7 %collective-permute-start.9 = (f32[32,8,128]{2,1,0:T(8,128)S(1)}, f32[32,8,128]{2,1,0:T(8,128)S(1)}, u32[]{:S(2)}, u32[]{:S(2)}) collective-permute-start(f32[32,8,128]{2,1,0:T(8,128)S(1)} %get-tuple-element.34.refs_3_), channel_id=1, source_target_pairs={{0,1},{1,0},{2,3},{3,2},{4,5},{5,4},{6,7},{7,6},{8,9},{9,8},{10,11... | collective-permute-start | bytes 393224 | tf_op jit(solution)/shard_map/ppermute | solution.py:545
  29.4 7.5 %collective-permute-start.5 = (f32[4,8,128]{2,1,0:T(8,128)S(1)}, f32[4,8,128]{2,1,0:T(8,128)S(1)}, u32[]{:S(2)}, u32[]{:S(2)}) collective-permute-start(f32[4,8,128]{2,1,0:T(8,128)S(1)} %get-tuple-element.29.own_ref), channel_id=1, source_target_pairs={{0,16},{8,24},{16,0},{24,8},{1,17},{9,25},{17,1},{25,9},{2,18},{10... | collective-permute-start | bytes 49160 | tf_op jit(solution)/shard_map/ppermute | solution.py:472

commit v13 on v11

--- a/solution.py
+++ b/solution.py
@@ -39,8 +39,8 @@
 
 
 def pack_kernel(planes, tiles, taper_hbm, u_hbm, t_hbm, noise_hbm, observed_hbm, var_hbm, cells_hbm,
-                low_ref, high_ref, obs_ref, t_ref, pick_ref,
-                taper_ref, u_ref, noise_ref, row_ref, cells_ref, sems):
+                low_ref, high_ref, obs_ref, t_ref, u_ref, pick_ref,
+                taper_ref, noise_ref, row_ref, cells_ref, sems):
     stride = planes * tiles
     blocks = noise_ref.shape[1] // LANES
     copies = [
@@ -158,21 +158,16 @@
         body(x)
 
 
-def inner_kernel(planes, tiles, u_hbm, t_ref, u2_ref, edge_ref, u_ref, u0, hv, u1, held, sem):
+def inner_kernel(planes, tiles, u_ref, t_ref, u2_ref, edge_ref, u0, hv, u1, held):
     stride = planes * tiles
     masks = lane_masks()
-    copy = pltpu.make_async_copy(u_hbm, u_ref, sem)
-    copy.start()
 
     def rows_at(x, tile):
         return pl.ds((x // ROWS) * tiles * ROWS + x % ROWS + tile * ROWS, ROWS, stride=stride)
 
-    def load_t(x):
+    def load(x):
         for tile in range(tiles):
             hv[x * tiles + tile] = HALF_DT * jnp.exp(t_ref[rows_at(x, tile), :])
-
-    def load_u(x):
-        for tile in range(tiles):
             u0[x * tiles + tile] = u_ref[rows_at(x, tile), :]
 
     def first_step(x):
@@ -190,9 +185,7 @@
             weights.append([held[kind, at] for kind in range(5)] + [here + hv[at - tiles], here + hv[at + tiles]])
         put(u2_ref, x, step(masks, weights, *[plane_of(u1, x + d, tiles) for d in (-1, 0, 1)]))
 
-    each(0, planes, 4, load_t)
-    copy.wait()
-    each(0, planes, 4, load_u)
+    each(0, planes, 4, load)
     each(1, planes - 1, 7, first_step)
     each(2, planes - 2, 6, second_step)
     last = planes - 1
@@ -377,19 +370,25 @@
     for copy in copies[:4]:
         copy.wait()
     slots = split_ref.shape[0]
-    blocks_of = [cells_ref[0, slot] for slot in range(slots)]
-    for slot in range(slots):
-        sum_ref[blocks_of[slot]] = pick_ref[slot]
-    copies[4].wait()
-    for slot in range(slots):
+
+    def begin(slot):
+        sum_ref[cells_ref[0, slot]] = pick_ref[slot]
+
+    def add(slot):
         weight = jnp.where(slot < count_ref[0], level_ref[0, slot].astype(jnp.float32) / 256.0, 0.0) * share
         change = fold(dot(reach[probes_ref[0, slot]], split_ref[slot], 0)) * weight
-        sum_ref[blocks_of[slot]] = sum_ref[blocks_of[slot]] + change
-    copies[5].wait()
-    for slot in range(slots):
-        block = blocks_of[slot]
+        sum_ref[cells_ref[0, slot]] = sum_ref[cells_ref[0, slot]] + change
+
+    def finish(slot):
+        block = cells_ref[0, slot]
         rows = pl.ds(row_of(block // tiles, block % tiles, tiles), ROWS, stride=planes * tiles)
         post_ref[rows, :] = sum_ref[block]
+
+    each(0, slots, 8, begin)
+    copies[4].wait()
+    each(0, slots, 8, add)
+    copies[5].wait()
+    each(0, slots, 8, finish)
 
 
 def shards(
@@ -421,20 +420,20 @@
     obs_shape = jax.ShapeDtypeStruct((obs_tiles, ROWS, LANES), f32)
     params = pltpu.CompilerParams(vmem_limit_bytes=32 * 1024 * 1024)
     stack = pltpu.VMEM((planes * tiles, ROWS, LANES), f32)
-    low, high, obs, t_near, picked = pl.pallas_call(
+    low, high, obs, t_near, u_near, picked = pl.pallas_call(
         functools.partial(pack_kernel, planes, tiles),
         out_shape=(
             edge,
             edge,
             obs_shape,
             jax.ShapeDtypeStruct(u_rows.shape, f32),
+            jax.ShapeDtypeStruct(u_rows.shape, f32),
             jax.ShapeDtypeStruct((slots, ROWS, LANES), f32),
         ),
         in_specs=[HBM] * 7,
-        out_specs=(VMEM,) * 5,
+        out_specs=(VMEM,) * 6,
         scratch_shapes=[
             pltpu.SMEM(probe_taper.shape, i32),
-            pltpu.VMEM(u_rows.shape, f32),
             pltpu.VMEM((ROWS, probes), f32),
             pltpu.VMEM((2, probes), f32),
             pltpu.SMEM(pair_cells.shape, i32),
@@ -459,20 +458,13 @@
             jax.ShapeDtypeStruct((planes * tiles, ROWS, LANES), f32),
             jax.ShapeDtypeStruct((14 * tiles, ROWS, LANES), f32),
         ),
-        in_specs=[HBM, VMEM],
+        in_specs=[VMEM, VMEM],
         out_specs=(VMEM, VMEM),
-        scratch_shapes=[
-            pltpu.VMEM(u_rows.shape, f32),
-            stack,
-            stack,
-            stack,
-            pltpu.VMEM((5, planes * tiles, ROWS, LANES), f32),
-            pltpu.SemaphoreType.DMA(()),
-        ],
+        scratch_shapes=[stack, stack, stack, pltpu.VMEM((5, planes * tiles, ROWS, LANES), f32)],
         compiler_params=params,
         cost_estimate=pl.CostEstimate(flops=0, bytes_accessed=15_000_000, transcendentals=0),
         name="inner_planes",
-    )(stay(u_rows), t_near)
+    )(u_near, t_near)
     by_xor = chips <= 4 and chips & (chips - 1) == 0
     if by_xor:
         parts = [picked]

time: 41.9 us -> 41.7 us (level)
  starting transfers between devices: 19.5 us -> 18.9 us
  waiting for transfers between devices: 2.93 us -> 3.5 us
    ppermute x1, waiting for transfers between devices: 0.94 us -> 1.51 us  [shards(): after = lax.ppermute(low, 'space', [(j, i) for i, j in upward])]
    pallas_call x1, Pallas kernels: 4.28 us -> 3.71 us  [shards(): pl.pallas_call(functools.partial(inner_kernel, planes, tiles), out_shape=...]
    all_to_all x1, starting transfers between devices: 5.99 us -> 5.42 us  [shards(): pred_all = lax.all_to_all(sent, ('space', 'chip', 'core'), 0, 0)]
    pallas_call x1, Pallas kernels: 3.81 us -> 4.24 us  [shards(): pl.pallas_call(functools.partial(update_kernel, slabs, planes, tiles), ou...]
  transfers between devices with their start and end apart: 11 -> 11, of which waited for: 3 -> 3; matrix products, arithmetic and copies ran while one was open for 0% -> 0% of each run, Pallas kernels for 27% -> 25%
where the time goes in v13:
time: 41.7 us; the launch traced here: 41.4 us
  starting transfers between devices  18.9 us (45%)
  Pallas kernels  17.5 us (42%)
  waiting for transfers between devices  3.5 us (8%)
  between operations  1.42 us (3%)
    all_to_all x1, starting transfers between devices, shards(): pred_all = lax.all_to_all(sent, ('space', 'chip', 'core'), 0, 0)  5.42 us
    ppermute x1, starting transfers between devices, shards(): before = lax.ppermute(high, 'space', upward)  4.95 us
    pallas_call x1, Pallas kernels, shards(): pl.pallas_call(functools.partial(update_kernel, slabs, planes, tiles), ou...  4.24 us
    pallas_call x1, Pallas kernels, shards(): pl.pallas_call(functools.partial(inner_kernel, planes, tiles), out_shape=...  3.71 us
    ppermute x3, starting transfers between devices, shards(): lax.ppermute(picked, 'chip', [(i, i ^ d) for i in range(chips)])  3.55 us
    pallas_call x1, Pallas kernels, shards(): pl.pallas_call(functools.partial(split_kernel, by_xor, chips), out_shape=...  3.12 us
    ppermute x1, starting transfers between devices, shards(): lax.ppermute(obs, 'space', [(i, (i + 2) % 4) for i in range(4)])  2.67 us
    pallas_call x1, Pallas kernels, shards(): pl.pallas_call(functools.partial(outer_kernel, planes, tiles), out_shape=...  2.09 us
  transfers between devices with their start and end apart: 11, of which 3 were waited for; matrix products, arithmetic and copies ran while one was open for 0% of the time, Pallas kernels for 25%

profile of v13, /device:TPU:0, one launch (start us, length us, event | category | flops | bytes accessed | tf_op | source)
XLA Modules:
  0.0 41.4 jit_solution(11447609546504542964)
XLA Ops:
  0.6 2.0 %pack.1 = (f32[69,8,128]{2,1,0:T(8,128)S(1)}, f32[69,8,128]{2,1,0:T(8,128)S(1)}, f32[4,8,128]{2,1,0:T(8,128)S(1)}, f32[2048,128]{1,0:T(8,128)S(1)}, f32[2048,128]{1,0:T(8,128)S(1)}, /*index=5*/f32[32,8,128]{2,1,0:T(8,128)S(1)}) custom-call(s32[1,2,6]{2,1,0:T(2,128)} %taper_hbm.1, f32[2048,128]{1,0:T(8,128)} %bitcast.28, f32[2048,128]{1,0:T(8,128)} %bitcast.26, ...), custom_call_target="tpu_custom_call" | custom-call | tf_op jit(solution)/shard_map/pack/pallas_call | solution.py:423
  2.6 4.9 %collective-permute-start = (f32[69,8,128]{2,1,0:T(8,128)S(1)}, f32[69,8,128]{2,1,0:T(8,128)S(1)}, u32[]{:S(2)}, u32[]{:S(2)}) collective-permute-start(f32[69,8,128]{2,1,0:T(8,128)S(1)} %get-tuple-element.21), channel_id=1, source_target_pairs={{0,8},{8,16},{16,24},{1,9},{9,17},{17,25},{2,10},{10,18},{18,26},{... | collective-permute-start | bytes 847880 | tf_op jit(solution)/shard_map/ppermute | solution.py:447
  7.6 1.3 %collective-permute-start.1 = (f32[69,8,128]{2,1,0:T(8,128)S(1)}, f32[69,8,128]{2,1,0:T(8,128)S(1)}, u32[]{:S(2)}, u32[]{:S(2)}) collective-permute-start(f32[69,8,128]{2,1,0:T(8,128)S(1)} %get-tuple-element.22), channel_id=1, source_target_pairs={{8,0},{16,8},{24,16},{9,1},{17,9},{25,17},{10,2},{18,10},{26,18},{... | collective-permute-start | bytes 847880 | tf_op jit(solution)/shard_map/ppermute | solution.py:448
  8.9 1.6 %collective-permute-start.2 = (f32[32,8,128]{2,1,0:T(8,128)S(1)}, f32[32,8,128]{2,1,0:T(8,128)S(1)}, u32[]{:S(2)}, u32[]{:S(2)}) collective-permute-start(f32[32,8,128]{2,1,0:T(8,128)S(1)} %get-tuple-element.28.refs_0_), channel_id=1, source_target_pairs={{0,2},{2,0},{4,6},{6,4},{1,3},{3,1},{5,7},{7,5},{8,10},{10,8},{12,... | collective-permute-start | bytes 393224 | tf_op jit(solution)/shard_map/ppermute | solution.py:472
  10.4 1.5 %collective-permute-start.3 = (f32[32,8,128]{2,1,0:T(8,128)S(1)}, f32[32,8,128]{2,1,0:T(8,128)S(1)}, u32[]{:S(2)}, u32[]{:S(2)}) collective-permute-start(f32[32,8,128]{2,1,0:T(8,128)S(1)} %get-tuple-element.28.refs_0_), channel_id=1, source_target_pairs={{0,4},{2,6},{4,0},{6,2},{1,5},{3,7},{5,1},{7,3},{8,12},{10,14},{12... | collective-permute-start | bytes 393224 | tf_op jit(solution)/shard_map/ppermute | solution.py:472
  12.0 0.5 %collective-permute-start.4 = (f32[32,8,128]{2,1,0:T(8,128)S(1)}, f32[32,8,128]{2,1,0:T(8,128)S(1)}, u32[]{:S(2)}, u32[]{:S(2)}) collective-permute-start(f32[32,8,128]{2,1,0:T(8,128)S(1)} %get-tuple-element.28.refs_0_), channel_id=1, source_target_pairs={{0,6},{2,4},{4,2},{6,0},{1,7},{3,5},{5,3},{7,1},{8,14},{10,12},{12... | collective-permute-start | bytes 393224 | tf_op jit(solution)/shard_map/ppermute | solution.py:472
  12.4 3.7 %inner_planes.1 = (f32[256,8,128]{2,1,0:T(8,128)S(1)}, f32[224,8,128]{2,1,0:T(8,128)S(1)}) custom-call(f32[2048,128]{1,0:T(8,128)S(1)} %get-tuple-element.23.u_ref, f32[2048,128]{1,0:T(8,128)S(1)} %get-tuple-element.24.t_ref), custom_call_target="tpu_custom_call" | custom-call | bytes 15000000 | tf_op jit(solution)/shard_map/inner_planes/pallas_call | solution.py:455
  16.2 0.0 collective-permute-done.before_ref
  16.2 1.5 %collective-permute-done.1.after_ref = f32[69,8,128]{2,1,0:T(8,128)S(1)} collective-permute-done((f32[69,8,128]{2,1,0:T(8,128)S(1)}, f32[69,8,128]{2,1,0:T(8,128)S(1)}, u32[]{:S(2)}, u32[]{:S(2)}) %collective-permute-start.1) | collective-permute-done | bytes 282656 | tf_op jit(solution)/shard_map/ppermute | solution.py:448
  17.7 2.1 %outer_planes.1 = (f32[256,8,128]{2,1,0:T(8,128)S(1)}, f32[16,128]{1,0:T(8,128)S(1)}, f32[8,8,128]{2,1,0:T(8,128)S(1)}) custom-call(s32[256]{0:T(256)} %probe_hbm.1, f32[69,8,128]{2,1,0:T(8,128)S(1)} %collective-permute-done.before_ref, f32[69,8,128]{2,1,0:T(8,128)S(1)} %collective-permute-done.1.after_ref, ...), custom_call_target="tpu_custom_call", output_to_operand_aliasing={{0}: (4, {})} | custom-call | flops 1000 | bytes 1000 | tf_op jit(solution)/shard_map/outer_planes/pallas_call | solution.py:475
  19.8 0.0 collective-permute-done.2.refs_1_
  19.8 0.0 collective-permute-done.3.refs_2_
  19.8 0.0 collective-permute-done.4.refs_3_
  19.8 0.8 %send.1 = f32[32,16,128]{2,1,0:T(8,128)} custom-call(f32[16,128]{1,0:T(8,128)S(1)} %get-tuple-element.30.found_ref, f32[32,8,128]{2,1,0:T(8,128)S(1)} %get-tuple-element.28.refs_0_, f32[32,8,128]{2,1,0:T(8,128)S(1)} %collective-permute-done.2.refs_1_, f32[32,8,128]{2,1,0:T(8,128)S(1)} %collective-permute-done.3.refs_2_, ...), custom_call_target="tpu_custom_call" | custom-call | flops 1000 | bytes 1000 | tf_op jit(solution)/shard_map/send/pallas_call | solution.py:493
  20.6 5.4 %all-to-all-start = ((f32[32,16,128]{2,1,0:T(8,128)}), f32[32,16,128]{2,1,0:T(8,128)S(1)}, u32[]{:S(2)}, u32[]{:S(2)}) async-start(f32[32,16,128]{2,1,0:T(8,128)} %send.1), calls=%async_computation | async-start | bytes 524288 | tf_op jit(solution)/shard_map/all_to_all | solution.py:503
  26.0 1.6 %store.1 = (f32[2048,128]{1,0:T(8,128)}, f32[32,8,128]{2,1,0:T(8,128)S(1)}, f32[32,8,128]{2,1,0:T(8,128)S(1)}, f32[32,8,128]{2,1,0:T(8,128)S(1)}, f32[32,8,128]{2,1,0:T(8,128)S(1)}) custom-call(f32[256,8,128]{2,1,0:T(8,128)S(1)} %get-tuple-element.27.u2_ref, ...), custom_call_target="tpu_custom_call", output_to_operand_aliasing={{1}: (1, {}), {2}: (2, {}), {3}: (3, {}), {4}: (4, {})} | custom-call | flops 1000 | bytes 1000 | tf_op jit(solution)/shard_map/store/pallas_call | solution.py:504
  27.6 0.3 collective-permute-start.6
  27.9 0.3 collective-permute-start.7
  28.2 0.3 collective-permute-start.8
  28.4 0.3 collective-permute-start.9
  28.7 2.7 %collective-permute-start.5 = (f32[4,8,128]{2,1,0:T(8,128)S(1)}, f32[4,8,128]{2,1,0:T(8,128)S(1)}, u32[]{:S(2)}, u32[]{:S(2)}) collective-permute-start(f32[4,8,128]{2,1,0:T(8,128)S(1)} %get-tuple-element.31.own_ref), channel_id=1, source_target_pairs={{0,16},{8,24},{16,0},{24,8},{1,17},{9,25},{17,1},{25,9},{2,18},{10... | collective-permute-start | bytes 49160 | tf_op jit(solution)/shard_map/ppermute | solution.py:450
  31.3 0.1 pad_add_fusion.place_ref
  32.1 0.0 collective-permute-done.6.refs_4_
  32.1 0.0 collective-permute-done.7.refs_5_
  32.1 0.0 collective-permute-done.8.refs_6_
  32.1 0.0 collective-permute-done.9.refs_7_
  32.1 3.1 %split.1.split_hbm = bf16[32,128,128]{2,1,0:T(8,128)(2,1)} custom-call(s32[4]{0:T(128)S(1)} %pad_add_fusion.place_ref, f32[32,8,128]{2,1,0:T(8,128)S(1)} %get-tuple-element.33.refs_0_.pick_hbm, f32[32,8,128]{2,1,0:T(8,128)S(1)} %get-tuple-element.34.refs_1_, f32[32,8,128]{2,1,0:T(8,128)S(1)} %get-tuple-element.35.refs_2_, ...), custom_call_target="tpu_custom_call" | custom-call | flops 1000 | bytes 1000 | tf_op jit(solution)/shard_map/split/pallas_call | solution.py:517
  35.2 0.9 %collective-permute-done.5.before_2_ref.after_2_ref = f32[4,8,128]{2,1,0:T(8,128)S(1)} collective-permute-done((f32[4,8,128]{2,1,0:T(8,128)S(1)}, f32[4,8,128]{2,1,0:T(8,128)S(1)}, u32[]{:S(2)}, u32[]{:S(2)}) %collective-permute-start.5) | collective-permute-done | bytes 16416 | tf_op jit(solution)/shard_map/ppermute | solution.py:450
  36.1 1.1 %all-to-all-done.pred_ref = f32[32,16,128]{2,1,0:T(8,128)S(1)} async-done(((f32[32,16,128]{2,1,0:T(8,128)}), f32[32,16,128]{2,1,0:T(8,128)S(1)}, u32[]{:S(2)}, u32[]{:S(2)}) %all-to-all-start) | async-done | bytes 262176 | tf_op jit(solution)/shard_map/all_to_all | solution.py:503
  37.2 4.2 %update.1 = (f32[2048,128]{1,0:T(8,128)}, f32[8,256]{1,0:T(8,128)}) custom-call(s32[4]{0:T(128)S(1)} %pad_add_fusion.place_ref, s32[1]{0:T(128)S(6)} %copy.24.count_ref, s32[1,32]{1,0:T(1,128)} %cells_hbm.3, s32[1,32]{1,0:T(1,128)} %probes_hbm.1, s32[1,32]{1,0:T(1,128)} %level_hbm.1, f32[32,16,128]{2,1,0:T(8,128)S(1)} %all-to-all-done.pred_ref, ...), custom_call_target="tpu_custom_call" | custom-call | tf_op jit(solution)/shard_map/update/pallas_call | solution.py:531
Async XLA Ops:
  2.6 13.5 %collective-permute-start = (f32[69,8,128]{2,1,0:T(8,128)S(1)}, f32[69,8,128]{2,1,0:T(8,128)S(1)}, u32[]{:S(2)}, u32[]{:S(2)}) collective-permute-start(f32[69,8,128]{2,1,0:T(8,128)S(1)} %get-tuple-element.21), channel_id=1, source_target_pairs={{0,8},{8,16},{16,24},{1,9},{9,17},{17,25},{2,10},{10,18},{18,26},{... | collective-permute-start | bytes 847880 | tf_op jit(solution)/shard_map/ppermute | solution.py:447
  7.6 10.1 %collective-permute-start.1 = (f32[69,8,128]{2,1,0:T(8,128)S(1)}, f32[69,8,128]{2,1,0:T(8,128)S(1)}, u32[]{:S(2)}, u32[]{:S(2)}) collective-permute-start(f32[69,8,128]{2,1,0:T(8,128)S(1)} %get-tuple-element.22), channel_id=1, source_target_pairs={{8,0},{16,8},{24,16},{9,1},{17,9},{25,17},{10,2},{18,10},{26,18},{... | collective-permute-start | bytes 847880 | tf_op jit(solution)/shard_map/ppermute | solution.py:448
  8.9 10.9 %collective-permute-start.2 = (f32[32,8,128]{2,1,0:T(8,128)S(1)}, f32[32,8,128]{2,1,0:T(8,128)S(1)}, u32[]{:S(2)}, u32[]{:S(2)}) collective-permute-start(f32[32,8,128]{2,1,0:T(8,128)S(1)} %get-tuple-element.28.refs_0_), channel_id=1, source_target_pairs={{0,2},{2,0},{4,6},{6,4},{1,3},{3,1},{5,7},{7,5},{8,10},{10,8},{12,... | collective-permute-start | bytes 393224 | tf_op jit(solution)/shard_map/ppermute | solution.py:472
  10.4 9.4 %collective-permute-start.3 = (f32[32,8,128]{2,1,0:T(8,128)S(1)}, f32[32,8,128]{2,1,0:T(8,128)S(1)}, u32[]{:S(2)}, u32[]{:S(2)}) collective-permute-start(f32[32,8,128]{2,1,0:T(8,128)S(1)} %get-tuple-element.28.refs_0_), channel_id=1, source_target_pairs={{0,4},{2,6},{4,0},{6,2},{1,5},{3,7},{5,1},{7,3},{8,12},{10,14},{12... | collective-permute-start | bytes 393224 | tf_op jit(solution)/shard_map/ppermute | solution.py:472
  12.0 7.8 %collective-permute-start.4 = (f32[32,8,128]{2,1,0:T(8,128)S(1)}, f32[32,8,128]{2,1,0:T(8,128)S(1)}, u32[]{:S(2)}, u32[]{:S(2)}) collective-permute-start(f32[32,8,128]{2,1,0:T(8,128)S(1)} %get-tuple-element.28.refs_0_), channel_id=1, source_target_pairs={{0,6},{2,4},{4,2},{6,0},{1,7},{3,5},{5,3},{7,1},{8,14},{10,12},{12... | collective-permute-start | bytes 393224 | tf_op jit(solution)/shard_map/ppermute | solution.py:472
  20.6 16.6 %all-to-all-start = ((f32[32,16,128]{2,1,0:T(8,128)}), f32[32,16,128]{2,1,0:T(8,128)S(1)}, u32[]{:S(2)}, u32[]{:S(2)}) async-start(f32[32,16,128]{2,1,0:T(8,128)} %send.1), calls=%async_computation | async-start | bytes 524288 | tf_op jit(solution)/shard_map/all_to_all | solution.py:503
  27.6 4.4 %collective-permute-start.6 = (f32[32,8,128]{2,1,0:T(8,128)S(1)}, f32[32,8,128]{2,1,0:T(8,128)S(1)}, u32[]{:S(2)}, u32[]{:S(2)}) collective-permute-start(f32[32,8,128]{2,1,0:T(8,128)S(1)} %get-tuple-element.33.refs_0_.pick_hbm), channel_id=1, source_target_pairs={{0,1},{1,0},{2,3},{3,2},{4,5},{5,4},{6,7},{7,6},{8,9},{9,8},{10,11... | collective-permute-start | bytes 393224 | tf_op jit(solution)/shard_map/ppermute | solution.py:514
  27.9 4.2 %collective-permute-start.7 = (f32[32,8,128]{2,1,0:T(8,128)S(1)}, f32[32,8,128]{2,1,0:T(8,128)S(1)}, u32[]{:S(2)}, u32[]{:S(2)}) collective-permute-start(f32[32,8,128]{2,1,0:T(8,128)S(1)} %get-tuple-element.34.refs_1_), channel_id=1, source_target_pairs={{0,1},{1,0},{2,3},{3,2},{4,5},{5,4},{6,7},{7,6},{8,9},{9,8},{10,11... | collective-permute-start | bytes 393224 | tf_op jit(solution)/shard_map/ppermute | solution.py:514
  28.2 3.9 %collective-permute-start.8 = (f32[32,8,128]{2,1,0:T(8,128)S(1)}, f32[32,8,128]{2,1,0:T(8,128)S(1)}, u32[]{:S(2)}, u32[]{:S(2)}) collective-permute-start(f32[32,8,128]{2,1,0:T(8,128)S(1)} %get-tuple-element.35.refs_2_), channel_id=1, source_target_pairs={{0,1},{1,0},{2,3},{3,2},{4,5},{5,4},{6,7},{7,6},{8,9},{9,8},{10,11... | collective-permute-start | bytes 393224 | tf_op jit(solution)/shard_map/ppermute | solution.py:514
  28.4 3.7 %collective-permute-start.9 = (f32[32,8,128]{2,1,0:T(8,128)S(1)}, f32[32,8,128]{2,1,0:T(8,128)S(1)}, u32[]{:S(2)}, u32[]{:S(2)}) collective-permute-start(f32[32,8,128]{2,1,0:T(8,128)S(1)} %get-tuple-element.36.refs_3_), channel_id=1, source_target_pairs={{0,1},{1,0},{2,3},{3,2},{4,5},{5,4},{6,7},{7,6},{8,9},{9,8},{10,11... | collective-permute-start | bytes 393224 | tf_op jit(solution)/shard_map/ppermute | solution.py:514
  28.7 7.5 %collective-permute-start.5 = (f32[4,8,128]{2,1,0:T(8,128)S(1)}, f32[4,8,128]{2,1,0:T(8,128)S(1)}, u32[]{:S(2)}, u32[]{:S(2)}) collective-permute-start(f32[4,8,128]{2,1,0:T(8,128)S(1)} %get-tuple-element.31.own_ref), channel_id=1, source_target_pairs={{0,16},{8,24},{16,0},{24,8},{1,17},{9,25},{17,1},{25,9},{2,18},{10... | collective-permute-start | bytes 49160 | tf_op jit(solution)/shard_map/ppermute | solution.py:450

commit v14 on v13

--- a/solution.py
+++ b/solution.py
@@ -371,24 +371,31 @@
         copy.wait()
     slots = split_ref.shape[0]
 
-    def begin(slot):
-        sum_ref[cells_ref[0, slot]] = pick_ref[slot]
-
-    def add(slot):
+    blocks_of = [cells_ref[0, slot] for slot in range(slots)]
+    for slot in range(slots):
+        sum_ref[blocks_of[slot]] = pick_ref[slot]
+    copies[4].wait()
+
+    def add(slot, both):
         weight = jnp.where(slot < count_ref[0], level_ref[0, slot].astype(jnp.float32) / 256.0, 0.0) * share
-        change = fold(dot(reach[probes_ref[0, slot]], split_ref[slot], 0)) * weight
-        sum_ref[cells_ref[0, slot]] = sum_ref[cells_ref[0, slot]] + change
-
-    def finish(slot):
-        block = cells_ref[0, slot]
+        sum_ref[blocks_of[slot]] = sum_ref[blocks_of[slot]] + fold(both) * weight
+
+    nothing = jnp.zeros(reach.shape[1:], jnp.bfloat16)
+    for slot in range(0, slots - slots % 4, 4):
+        gains = [reach[probes_ref[0, slot + k]] for k in range(4)]
+        left = [beside([gain, nothing] if k % 2 == 0 else [nothing, gain]) for k, gain in enumerate(gains)]
+        right = [jnp.concatenate([split_ref[slot + k], split_ref[slot + k + 1]], axis=0) for k in (0, 2)]
+        both = dot(jnp.concatenate(left, axis=0), beside(right), 0)
+        for k in range(4):
+            columns = slice(k // 2 * LANES, (k // 2 + 1) * LANES)
+            add(slot + k, both[k * 2 * ROWS : (k + 1) * 2 * ROWS, columns])
+    for slot in range(slots - slots % 4, slots):
+        add(slot, dot(reach[probes_ref[0, slot]], split_ref[slot], 0))
+    copies[5].wait()
+    for slot in range(slots):
+        block = blocks_of[slot]
         rows = pl.ds(row_of(block // tiles, block % tiles, tiles), ROWS, stride=planes * tiles)
         post_ref[rows, :] = sum_ref[block]
-
-    each(0, slots, 8, begin)
-    copies[4].wait()
-    each(0, slots, 8, add)
-    copies[5].wait()
-    each(0, slots, 8, finish)
 
 
 def shards(

time: 41.7 us -> 41.3 us (level)
    pallas_call x1, Pallas kernels: 4.24 us -> 3.75 us  [shards(): pl.pallas_call(functools.partial(update_kernel, slabs, planes, tiles), ou...]
  transfers between devices with their start and end apart: 11 -> 11, of which waited for: 3 -> 3; matrix products, arithmetic and copies ran while one was open for 0% -> 0% of each run, Pallas kernels for 25% -> 26%
where the time goes in v14:
time: 41.3 us; the launch traced here: 41 us
  starting transfers between devices  18.9 us (46%)
  Pallas kernels  17.1 us (41%)
  waiting for transfers between devices  3.5 us (8%)
  between operations  1.42 us (3%)
    all_to_all x1, starting transfers between devices, shards(): pred_all = lax.all_to_all(sent, ('space', 'chip', 'core'), 0, 0)  5.42 us
    ppermute x1, starting transfers between devices, shards(): before = lax.ppermute(high, 'space', upward)  4.95 us
    pallas_call x1, Pallas kernels, shards(): pl.pallas_call(functools.partial(update_kernel, slabs, planes, tiles), ou...  3.75 us
    pallas_call x1, Pallas kernels, shards(): pl.pallas_call(functools.partial(inner_kernel, planes, tiles), out_shape=...  3.71 us
    ppermute x3, starting transfers between devices, shards(): lax.ppermute(picked, 'chip', [(i, i ^ d) for i in range(chips)])  3.55 us
    pallas_call x1, Pallas kernels, shards(): pl.pallas_call(functools.partial(split_kernel, by_xor, chips), out_shape=...  3.12 us
    ppermute x1, starting transfers between devices, shards(): lax.ppermute(obs, 'space', [(i, (i + 2) % 4) for i in range(4)])  2.67 us
    pallas_call x1, Pallas kernels, shards(): pl.pallas_call(functools.partial(outer_kernel, planes, tiles), out_shape=...  2.09 us
  transfers between devices with their start and end apart: 11, of which 3 were waited for; matrix products, arithmetic and copies ran while one was open for 0% of the time, Pallas kernels for 26%

profile of v14, /device:TPU:0, one launch (start us, length us, event | category | flops | bytes accessed | tf_op | source)
XLA Modules:
  0.0 41.0 jit_solution(1601035223102306496)
XLA Ops:
  0.6 2.0 %pack.1 = (f32[69,8,128]{2,1,0:T(8,128)S(1)}, f32[69,8,128]{2,1,0:T(8,128)S(1)}, f32[4,8,128]{2,1,0:T(8,128)S(1)}, f32[2048,128]{1,0:T(8,128)S(1)}, f32[2048,128]{1,0:T(8,128)S(1)}, /*index=5*/f32[32,8,128]{2,1,0:T(8,128)S(1)}) custom-call(s32[1,2,6]{2,1,0:T(2,128)} %taper_hbm.1, f32[2048,128]{1,0:T(8,128)} %bitcast.28, f32[2048,128]{1,0:T(8,128)} %bitcast.26, ...), custom_call_target="tpu_custom_call" | custom-call | tf_op jit(solution)/shard_map/pack/pallas_call | solution.py:430
  2.6 4.9 %collective-permute-start = (f32[69,8,128]{2,1,0:T(8,128)S(1)}, f32[69,8,128]{2,1,0:T(8,128)S(1)}, u32[]{:S(2)}, u32[]{:S(2)}) collective-permute-start(f32[69,8,128]{2,1,0:T(8,128)S(1)} %get-tuple-element.21), channel_id=1, source_target_pairs={{0,8},{8,16},{16,24},{1,9},{9,17},{17,25},{2,10},{10,18},{18,26},{... | collective-permute-start | bytes 847880 | tf_op jit(solution)/shard_map/ppermute | solution.py:454
  7.6 1.3 %collective-permute-start.1 = (f32[69,8,128]{2,1,0:T(8,128)S(1)}, f32[69,8,128]{2,1,0:T(8,128)S(1)}, u32[]{:S(2)}, u32[]{:S(2)}) collective-permute-start(f32[69,8,128]{2,1,0:T(8,128)S(1)} %get-tuple-element.22), channel_id=1, source_target_pairs={{8,0},{16,8},{24,16},{9,1},{17,9},{25,17},{10,2},{18,10},{26,18},{... | collective-permute-start | bytes 847880 | tf_op jit(solution)/shard_map/ppermute | solution.py:455
  8.9 1.6 %collective-permute-start.2 = (f32[32,8,128]{2,1,0:T(8,128)S(1)}, f32[32,8,128]{2,1,0:T(8,128)S(1)}, u32[]{:S(2)}, u32[]{:S(2)}) collective-permute-start(f32[32,8,128]{2,1,0:T(8,128)S(1)} %get-tuple-element.28.refs_0_), channel_id=1, source_target_pairs={{0,2},{2,0},{4,6},{6,4},{1,3},{3,1},{5,7},{7,5},{8,10},{10,8},{12,... | collective-permute-start | bytes 393224 | tf_op jit(solution)/shard_map/ppermute | solution.py:479
  10.4 1.5 %collective-permute-start.3 = (f32[32,8,128]{2,1,0:T(8,128)S(1)}, f32[32,8,128]{2,1,0:T(8,128)S(1)}, u32[]{:S(2)}, u32[]{:S(2)}) collective-permute-start(f32[32,8,128]{2,1,0:T(8,128)S(1)} %get-tuple-element.28.refs_0_), channel_id=1, source_target_pairs={{0,4},{2,6},{4,0},{6,2},{1,5},{3,7},{5,1},{7,3},{8,12},{10,14},{12... | collective-permute-start | bytes 393224 | tf_op jit(solution)/shard_map/ppermute | solution.py:479
  12.0 0.5 %collective-permute-start.4 = (f32[32,8,128]{2,1,0:T(8,128)S(1)}, f32[32,8,128]{2,1,0:T(8,128)S(1)}, u32[]{:S(2)}, u32[]{:S(2)}) collective-permute-start(f32[32,8,128]{2,1,0:T(8,128)S(1)} %get-tuple-element.28.refs_0_), channel_id=1, source_target_pairs={{0,6},{2,4},{4,2},{6,0},{1,7},{3,5},{5,3},{7,1},{8,14},{10,12},{12... | collective-permute-start | bytes 393224 | tf_op jit(solution)/shard_map/ppermute | solution.py:479
  12.4 3.7 %inner_planes.1 = (f32[256,8,128]{2,1,0:T(8,128)S(1)}, f32[224,8,128]{2,1,0:T(8,128)S(1)}) custom-call(f32[2048,128]{1,0:T(8,128)S(1)} %get-tuple-element.23.u_ref, f32[2048,128]{1,0:T(8,128)S(1)} %get-tuple-element.24.t_ref), custom_call_target="tpu_custom_call" | custom-call | bytes 15000000 | tf_op jit(solution)/shard_map/inner_planes/pallas_call | solution.py:462
  16.2 0.0 collective-permute-done.before_ref
  16.2 1.5 %collective-permute-done.1.after_ref = f32[69,8,128]{2,1,0:T(8,128)S(1)} collective-permute-done((f32[69,8,128]{2,1,0:T(8,128)S(1)}, f32[69,8,128]{2,1,0:T(8,128)S(1)}, u32[]{:S(2)}, u32[]{:S(2)}) %collective-permute-start.1) | collective-permute-done | bytes 282656 | tf_op jit(solution)/shard_map/ppermute | solution.py:455
  17.7 2.1 %outer_planes.1 = (f32[256,8,128]{2,1,0:T(8,128)S(1)}, f32[16,128]{1,0:T(8,128)S(1)}, f32[8,8,128]{2,1,0:T(8,128)S(1)}) custom-call(s32[256]{0:T(256)} %probe_hbm.1, f32[69,8,128]{2,1,0:T(8,128)S(1)} %collective-permute-done.before_ref, f32[69,8,128]{2,1,0:T(8,128)S(1)} %collective-permute-done.1.after_ref, ...), custom_call_target="tpu_custom_call", output_to_operand_aliasing={{0}: (4, {})} | custom-call | flops 1000 | bytes 1000 | tf_op jit(solution)/shard_map/outer_planes/pallas_call | solution.py:482
  19.8 0.0 collective-permute-done.2.refs_1_
  19.8 0.0 collective-permute-done.3.refs_2_
  19.8 0.0 collective-permute-done.4.refs_3_
  19.8 0.8 %send.1 = f32[32,16,128]{2,1,0:T(8,128)} custom-call(f32[16,128]{1,0:T(8,128)S(1)} %get-tuple-element.30.found_ref, f32[32,8,128]{2,1,0:T(8,128)S(1)} %get-tuple-element.28.refs_0_, f32[32,8,128]{2,1,0:T(8,128)S(1)} %collective-permute-done.2.refs_1_, f32[32,8,128]{2,1,0:T(8,128)S(1)} %collective-permute-done.3.refs_2_, ...), custom_call_target="tpu_custom_call" | custom-call | flops 1000 | bytes 1000 | tf_op jit(solution)/shard_map/send/pallas_call | solution.py:500
  20.6 5.4 %all-to-all-start = ((f32[32,16,128]{2,1,0:T(8,128)}), f32[32,16,128]{2,1,0:T(8,128)S(1)}, u32[]{:S(2)}, u32[]{:S(2)}) async-start(f32[32,16,128]{2,1,0:T(8,128)} %send.1), calls=%async_computation | async-start | bytes 524288 | tf_op jit(solution)/shard_map/all_to_all | solution.py:510
  26.0 1.6 %store.1 = (f32[2048,128]{1,0:T(8,128)}, f32[32,8,128]{2,1,0:T(8,128)S(1)}, f32[32,8,128]{2,1,0:T(8,128)S(1)}, f32[32,8,128]{2,1,0:T(8,128)S(1)}, f32[32,8,128]{2,1,0:T(8,128)S(1)}) custom-call(f32[256,8,128]{2,1,0:T(8,128)S(1)} %get-tuple-element.27.u2_ref, ...), custom_call_target="tpu_custom_call", output_to_operand_aliasing={{1}: (1, {}), {2}: (2, {}), {3}: (3, {}), {4}: (4, {})} | custom-call | flops 1000 | bytes 1000 | tf_op jit(solution)/shard_map/store/pallas_call | solution.py:511
  27.6 0.3 collective-permute-start.6
  27.9 0.3 collective-permute-start.7
  28.2 0.3 collective-permute-start.8
  28.4 0.3 collective-permute-start.9
  28.7 2.7 %collective-permute-start.5 = (f32[4,8,128]{2,1,0:T(8,128)S(1)}, f32[4,8,128]{2,1,0:T(8,128)S(1)}, u32[]{:S(2)}, u32[]{:S(2)}) collective-permute-start(f32[4,8,128]{2,1,0:T(8,128)S(1)} %get-tuple-element.31.own_ref), channel_id=1, source_target_pairs={{0,16},{8,24},{16,0},{24,8},{1,17},{9,25},{17,1},{25,9},{2,18},{10... | collective-permute-start | bytes 49160 | tf_op jit(solution)/shard_map/ppermute | solution.py:457
  31.3 0.1 pad_add_fusion.place_ref
  32.1 0.0 collective-permute-done.6.refs_4_
  32.1 0.0 collective-permute-done.7.refs_5_
  32.1 0.0 collective-permute-done.8.refs_6_
  32.1 0.0 collective-permute-done.9.refs_7_
  32.1 3.1 %split.1.split_hbm = bf16[32,128,128]{2,1,0:T(8,128)(2,1)} custom-call(s32[4]{0:T(128)S(1)} %pad_add_fusion.place_ref, f32[32,8,128]{2,1,0:T(8,128)S(1)} %get-tuple-element.33.refs_0_.pick_hbm, f32[32,8,128]{2,1,0:T(8,128)S(1)} %get-tuple-element.34.refs_1_, f32[32,8,128]{2,1,0:T(8,128)S(1)} %get-tuple-element.35.refs_2_, ...), custom_call_target="tpu_custom_call" | custom-call | flops 1000 | bytes 1000 | tf_op jit(solution)/shard_map/split/pallas_call | solution.py:524
  35.2 0.9 %collective-permute-done.5.before_2_ref.after_2_ref = f32[4,8,128]{2,1,0:T(8,128)S(1)} collective-permute-done((f32[4,8,128]{2,1,0:T(8,128)S(1)}, f32[4,8,128]{2,1,0:T(8,128)S(1)}, u32[]{:S(2)}, u32[]{:S(2)}) %collective-permute-start.5) | collective-permute-done | bytes 16416 | tf_op jit(solution)/shard_map/ppermute | solution.py:457
  36.1 1.1 %all-to-all-done.pred_ref = f32[32,16,128]{2,1,0:T(8,128)S(1)} async-done(((f32[32,16,128]{2,1,0:T(8,128)}), f32[32,16,128]{2,1,0:T(8,128)S(1)}, u32[]{:S(2)}, u32[]{:S(2)}) %all-to-all-start) | async-done | bytes 262176 | tf_op jit(solution)/shard_map/all_to_all | solution.py:510
  37.2 3.8 %update.1 = (f32[2048,128]{1,0:T(8,128)}, f32[8,256]{1,0:T(8,128)}) custom-call(s32[4]{0:T(128)S(1)} %pad_add_fusion.place_ref, s32[1]{0:T(128)S(6)} %copy.24.count_ref, s32[1,32]{1,0:T(1,128)} %cells_hbm.3, s32[1,32]{1,0:T(1,128)} %probes_hbm.1, s32[1,32]{1,0:T(1,128)} %level_hbm.1, f32[32,16,128]{2,1,0:T(8,128)S(1)} %all-to-all-done.pred_ref, ...), custom_call_target="tpu_custom_call" | custom-call | tf_op jit(solution)/shard_map/update/pallas_call | solution.py:538
Async XLA Ops:
  2.6 13.5 %collective-permute-start = (f32[69,8,128]{2,1,0:T(8,128)S(1)}, f32[69,8,128]{2,1,0:T(8,128)S(1)}, u32[]{:S(2)}, u32[]{:S(2)}) collective-permute-start(f32[69,8,128]{2,1,0:T(8,128)S(1)} %get-tuple-element.21), channel_id=1, source_target_pairs={{0,8},{8,16},{16,24},{1,9},{9,17},{17,25},{2,10},{10,18},{18,26},{... | collective-permute-start | bytes 847880 | tf_op jit(solution)/shard_map/ppermute | solution.py:454
  7.6 10.1 %collective-permute-start.1 = (f32[69,8,128]{2,1,0:T(8,128)S(1)}, f32[69,8,128]{2,1,0:T(8,128)S(1)}, u32[]{:S(2)}, u32[]{:S(2)}) collective-permute-start(f32[69,8,128]{2,1,0:T(8,128)S(1)} %get-tuple-element.22), channel_id=1, source_target_pairs={{8,0},{16,8},{24,16},{9,1},{17,9},{25,17},{10,2},{18,10},{26,18},{... | collective-permute-start | bytes 847880 | tf_op jit(solution)/shard_map/ppermute | solution.py:455
  8.9 10.9 %collective-permute-start.2 = (f32[32,8,128]{2,1,0:T(8,128)S(1)}, f32[32,8,128]{2,1,0:T(8,128)S(1)}, u32[]{:S(2)}, u32[]{:S(2)}) collective-permute-start(f32[32,8,128]{2,1,0:T(8,128)S(1)} %get-tuple-element.28.refs_0_), channel_id=1, source_target_pairs={{0,2},{2,0},{4,6},{6,4},{1,3},{3,1},{5,7},{7,5},{8,10},{10,8},{12,... | collective-permute-start | bytes 393224 | tf_op jit(solution)/shard_map/ppermute | solution.py:479
  10.4 9.4 %collective-permute-start.3 = (f32[32,8,128]{2,1,0:T(8,128)S(1)}, f32[32,8,128]{2,1,0:T(8,128)S(1)}, u32[]{:S(2)}, u32[]{:S(2)}) collective-permute-start(f32[32,8,128]{2,1,0:T(8,128)S(1)} %get-tuple-element.28.refs_0_), channel_id=1, source_target_pairs={{0,4},{2,6},{4,0},{6,2},{1,5},{3,7},{5,1},{7,3},{8,12},{10,14},{12... | collective-permute-start | bytes 393224 | tf_op jit(solution)/shard_map/ppermute | solution.py:479
  12.0 7.8 %collective-permute-start.4 = (f32[32,8,128]{2,1,0:T(8,128)S(1)}, f32[32,8,128]{2,1,0:T(8,128)S(1)}, u32[]{:S(2)}, u32[]{:S(2)}) collective-permute-start(f32[32,8,128]{2,1,0:T(8,128)S(1)} %get-tuple-element.28.refs_0_), channel_id=1, source_target_pairs={{0,6},{2,4},{4,2},{6,0},{1,7},{3,5},{5,3},{7,1},{8,14},{10,12},{12... | collective-permute-start | bytes 393224 | tf_op jit(solution)/shard_map/ppermute | solution.py:479
  20.6 16.6 %all-to-all-start = ((f32[32,16,128]{2,1,0:T(8,128)}), f32[32,16,128]{2,1,0:T(8,128)S(1)}, u32[]{:S(2)}, u32[]{:S(2)}) async-start(f32[32,16,128]{2,1,0:T(8,128)} %send.1), calls=%async_computation | async-start | bytes 524288 | tf_op jit(solution)/shard_map/all_to_all | solution.py:510
  27.6 4.4 %collective-permute-start.6 = (f32[32,8,128]{2,1,0:T(8,128)S(1)}, f32[32,8,128]{2,1,0:T(8,128)S(1)}, u32[]{:S(2)}, u32[]{:S(2)}) collective-permute-start(f32[32,8,128]{2,1,0:T(8,128)S(1)} %get-tuple-element.33.refs_0_.pick_hbm), channel_id=1, source_target_pairs={{0,1},{1,0},{2,3},{3,2},{4,5},{5,4},{6,7},{7,6},{8,9},{9,8},{10,11... | collective-permute-start | bytes 393224 | tf_op jit(solution)/shard_map/ppermute | solution.py:521
  27.9 4.2 %collective-permute-start.7 = (f32[32,8,128]{2,1,0:T(8,128)S(1)}, f32[32,8,128]{2,1,0:T(8,128)S(1)}, u32[]{:S(2)}, u32[]{:S(2)}) collective-permute-start(f32[32,8,128]{2,1,0:T(8,128)S(1)} %get-tuple-element.34.refs_1_), channel_id=1, source_target_pairs={{0,1},{1,0},{2,3},{3,2},{4,5},{5,4},{6,7},{7,6},{8,9},{9,8},{10,11... | collective-permute-start | bytes 393224 | tf_op jit(solution)/shard_map/ppermute | solution.py:521
  28.2 3.9 %collective-permute-start.8 = (f32[32,8,128]{2,1,0:T(8,128)S(1)}, f32[32,8,128]{2,1,0:T(8,128)S(1)}, u32[]{:S(2)}, u32[]{:S(2)}) collective-permute-start(f32[32,8,128]{2,1,0:T(8,128)S(1)} %get-tuple-element.35.refs_2_), channel_id=1, source_target_pairs={{0,1},{1,0},{2,3},{3,2},{4,5},{5,4},{6,7},{7,6},{8,9},{9,8},{10,11... | collective-permute-start | bytes 393224 | tf_op jit(solution)/shard_map/ppermute | solution.py:521
  28.4 3.7 %collective-permute-start.9 = (f32[32,8,128]{2,1,0:T(8,128)S(1)}, f32[32,8,128]{2,1,0:T(8,128)S(1)}, u32[]{:S(2)}, u32[]{:S(2)}) collective-permute-start(f32[32,8,128]{2,1,0:T(8,128)S(1)} %get-tuple-element.36.refs_3_), channel_id=1, source_target_pairs={{0,1},{1,0},{2,3},{3,2},{4,5},{5,4},{6,7},{7,6},{8,9},{9,8},{10,11... | collective-permute-start | bytes 393224 | tf_op jit(solution)/shard_map/ppermute | solution.py:521
  28.7 7.5 %collective-permute-start.5 = (f32[4,8,128]{2,1,0:T(8,128)S(1)}, f32[4,8,128]{2,1,0:T(8,128)S(1)}, u32[]{:S(2)}, u32[]{:S(2)}) collective-permute-start(f32[4,8,128]{2,1,0:T(8,128)S(1)} %get-tuple-element.31.own_ref), channel_id=1, source_target_pairs={{0,16},{8,24},{16,0},{24,8},{1,17},{9,25},{17,1},{25,9},{2,18},{10... | collective-permute-start | bytes 49160 | tf_op jit(solution)/shard_map/ppermute | solution.py:457

commit v15 on v14

--- a/solution.py
+++ b/solution.py
@@ -237,13 +237,15 @@
 
 
 def send_kernel(found_ref, *refs):
-    sent_hbm, sem = refs[-2:]
-
-    def send(device, _):
-        pltpu.make_async_copy(found_ref, sent_hbm.at[device], sem).start()
-        return 0
-
-    lax.fori_loop(0, sent_hbm.shape[0], send, 0)
+    sent_hbm, many_ref, sem = refs[-3:]
+    many = many_ref.shape[0]
+    for device in range(many):
+        many_ref[device] = found_ref[...]
+
+    def send(at):
+        pltpu.make_async_copy(many_ref, sent_hbm.at[pl.ds(at * many, many)], sem).start()
+
+    each(0, sent_hbm.shape[0] // many, 4, send)
     pltpu.make_async_copy(sent_hbm, sent_hbm, sem).wait()
 
 
@@ -502,7 +504,7 @@
         out_shape=pltpu.HBM((slabs * groups, blocks * ROWS, LANES), f32),
         in_specs=[VMEM] + [ANY] * len(parts),
         out_specs=HBM,
-        scratch_shapes=[pltpu.SemaphoreType.DMA(())],
+        scratch_shapes=[pltpu.VMEM((groups, blocks * ROWS, LANES), f32), pltpu.SemaphoreType.DMA(())],
         compiler_params=params,
         cost_estimate=little,
         name="send",

time: 41.3 us -> 41.2 us (level)
  no operation moved by 1% of the time
where the time goes in v15:
time: 41.2 us; the launch traced here: 40.9 us
  starting transfers between devices  18.9 us (46%)
  Pallas kernels  17 us (41%)
  waiting for transfers between devices  3.5 us (8%)
  between operations  1.42 us (3%)
    all_to_all x1, starting transfers between devices, shards(): pred_all = lax.all_to_all(sent, ('space', 'chip', 'core'), 0, 0)  5.42 us
    ppermute x1, starting transfers between devices, shards(): before = lax.ppermute(high, 'space', upward)  4.94 us
    pallas_call x1, Pallas kernels, shards(): pl.pallas_call(functools.partial(update_kernel, slabs, planes, tiles), ou...  3.75 us
    pallas_call x1, Pallas kernels, shards(): pl.pallas_call(functools.partial(inner_kernel, planes, tiles), out_shape=...  3.71 us
    ppermute x3, starting transfers between devices, shards(): lax.ppermute(picked, 'chip', [(i, i ^ d) for i in range(chips)])  3.55 us
    pallas_call x1, Pallas kernels, shards(): pl.pallas_call(functools.partial(split_kernel, by_xor, chips), out_shape=...  3.12 us
    ppermute x1, starting transfers between devices, shards(): lax.ppermute(obs, 'space', [(i, (i + 2) % 4) for i in range(4)])  2.67 us
    pallas_call x1, Pallas kernels, shards(): pl.pallas_call(functools.partial(outer_kernel, planes, tiles), out_shape=...  2.09 us
  transfers between devices with their start and end apart: 11, of which 3 were waited for; matrix products, arithmetic and copies ran while one was open for 0% of the time, Pallas kernels for 26%

profile of v15, /device:TPU:0, one launch (start us, length us, event | category | flops | bytes accessed | tf_op | source)
XLA Modules:
  0.0 40.9 jit_solution(3579876269917225953)
XLA Ops:
  0.6 2.0 %pack.1 = (f32[69,8,128]{2,1,0:T(8,128)S(1)}, f32[69,8,128]{2,1,0:T(8,128)S(1)}, f32[4,8,128]{2,1,0:T(8,128)S(1)}, f32[2048,128]{1,0:T(8,128)S(1)}, f32[2048,128]{1,0:T(8,128)S(1)}, /*index=5*/f32[32,8,128]{2,1,0:T(8,128)S(1)}) custom-call(s32[1,2,6]{2,1,0:T(2,128)} %taper_hbm.1, f32[2048,128]{1,0:T(8,128)} %bitcast.28, f32[2048,128]{1,0:T(8,128)} %bitcast.26, ...), custom_call_target="tpu_custom_call" | custom-call | tf_op jit(solution)/shard_map/pack/pallas_call | solution.py:432
  2.6 4.9 %collective-permute-start = (f32[69,8,128]{2,1,0:T(8,128)S(1)}, f32[69,8,128]{2,1,0:T(8,128)S(1)}, u32[]{:S(2)}, u32[]{:S(2)}) collective-permute-start(f32[69,8,128]{2,1,0:T(8,128)S(1)} %get-tuple-element.21), channel_id=1, source_target_pairs={{0,8},{8,16},{16,24},{1,9},{9,17},{17,25},{2,10},{10,18},{18,26},{... | collective-permute-start | bytes 847880 | tf_op jit(solution)/shard_map/ppermute | solution.py:456
  7.6 1.3 %collective-permute-start.1 = (f32[69,8,128]{2,1,0:T(8,128)S(1)}, f32[69,8,128]{2,1,0:T(8,128)S(1)}, u32[]{:S(2)}, u32[]{:S(2)}) collective-permute-start(f32[69,8,128]{2,1,0:T(8,128)S(1)} %get-tuple-element.22), channel_id=1, source_target_pairs={{8,0},{16,8},{24,16},{9,1},{17,9},{25,17},{10,2},{18,10},{26,18},{... | collective-permute-start | bytes 847880 | tf_op jit(solution)/shard_map/ppermute | solution.py:457
  8.9 1.6 %collective-permute-start.2 = (f32[32,8,128]{2,1,0:T(8,128)S(1)}, f32[32,8,128]{2,1,0:T(8,128)S(1)}, u32[]{:S(2)}, u32[]{:S(2)}) collective-permute-start(f32[32,8,128]{2,1,0:T(8,128)S(1)} %get-tuple-element.28.refs_0_), channel_id=1, source_target_pairs={{0,2},{2,0},{4,6},{6,4},{1,3},{3,1},{5,7},{7,5},{8,10},{10,8},{12,... | collective-permute-start | bytes 393224 | tf_op jit(solution)/shard_map/ppermute | solution.py:481
  10.4 1.5 %collective-permute-start.3 = (f32[32,8,128]{2,1,0:T(8,128)S(1)}, f32[32,8,128]{2,1,0:T(8,128)S(1)}, u32[]{:S(2)}, u32[]{:S(2)}) collective-permute-start(f32[32,8,128]{2,1,0:T(8,128)S(1)} %get-tuple-element.28.refs_0_), channel_id=1, source_target_pairs={{0,4},{2,6},{4,0},{6,2},{1,5},{3,7},{5,1},{7,3},{8,12},{10,14},{12... | collective-permute-start | bytes 393224 | tf_op jit(solution)/shard_map/ppermute | solution.py:481
  11.9 0.5 %collective-permute-start.4 = (f32[32,8,128]{2,1,0:T(8,128)S(1)}, f32[32,8,128]{2,1,0:T(8,128)S(1)}, u32[]{:S(2)}, u32[]{:S(2)}) collective-permute-start(f32[32,8,128]{2,1,0:T(8,128)S(1)} %get-tuple-element.28.refs_0_), channel_id=1, source_target_pairs={{0,6},{2,4},{4,2},{6,0},{1,7},{3,5},{5,3},{7,1},{8,14},{10,12},{12... | collective-permute-start | bytes 393224 | tf_op jit(solution)/shard_map/ppermute | solution.py:481
  12.4 3.7 %inner_planes.1 = (f32[256,8,128]{2,1,0:T(8,128)S(1)}, f32[224,8,128]{2,1,0:T(8,128)S(1)}) custom-call(f32[2048,128]{1,0:T(8,128)S(1)} %get-tuple-element.23.u_ref, f32[2048,128]{1,0:T(8,128)S(1)} %get-tuple-element.24.t_ref), custom_call_target="tpu_custom_call" | custom-call | bytes 15000000 | tf_op jit(solution)/shard_map/inner_planes/pallas_call | solution.py:464
  16.1 0.0 collective-permute-done.before_ref
  16.2 1.5 %collective-permute-done.1.after_ref = f32[69,8,128]{2,1,0:T(8,128)S(1)} collective-permute-done((f32[69,8,128]{2,1,0:T(8,128)S(1)}, f32[69,8,128]{2,1,0:T(8,128)S(1)}, u32[]{:S(2)}, u32[]{:S(2)}) %collective-permute-start.1) | collective-permute-done | bytes 282656 | tf_op jit(solution)/shard_map/ppermute | solution.py:457
  17.7 2.1 %outer_planes.1 = (f32[256,8,128]{2,1,0:T(8,128)S(1)}, f32[16,128]{1,0:T(8,128)S(1)}, f32[8,8,128]{2,1,0:T(8,128)S(1)}) custom-call(s32[256]{0:T(256)} %probe_hbm.1, f32[69,8,128]{2,1,0:T(8,128)S(1)} %collective-permute-done.before_ref, f32[69,8,128]{2,1,0:T(8,128)S(1)} %collective-permute-done.1.after_ref, ...), custom_call_target="tpu_custom_call", output_to_operand_aliasing={{0}: (4, {})} | custom-call | flops 1000 | bytes 1000 | tf_op jit(solution)/shard_map/outer_planes/pallas_call | solution.py:484
  19.8 0.0 collective-permute-done.2.refs_1_
  19.8 0.0 collective-permute-done.3.refs_2_
  19.8 0.0 collective-permute-done.4.refs_3_
  19.8 0.7 %send.1 = f32[32,16,128]{2,1,0:T(8,128)} custom-call(f32[16,128]{1,0:T(8,128)S(1)} %get-tuple-element.30.found_ref, f32[32,8,128]{2,1,0:T(8,128)S(1)} %get-tuple-element.28.refs_0_, f32[32,8,128]{2,1,0:T(8,128)S(1)} %collective-permute-done.2.refs_1_, f32[32,8,128]{2,1,0:T(8,128)S(1)} %collective-permute-done.3.refs_2_, ...), custom_call_target="tpu_custom_call" | custom-call | flops 1000 | bytes 1000 | tf_op jit(solution)/shard_map/send/pallas_call | solution.py:502
  20.5 5.4 %all-to-all-start = ((f32[32,16,128]{2,1,0:T(8,128)}), f32[32,16,128]{2,1,0:T(8,128)S(1)}, u32[]{:S(2)}, u32[]{:S(2)}) async-start(f32[32,16,128]{2,1,0:T(8,128)} %send.1), calls=%async_computation | async-start | bytes 524288 | tf_op jit(solution)/shard_map/all_to_all | solution.py:512
  26.0 1.6 %store.1 = (f32[2048,128]{1,0:T(8,128)}, f32[32,8,128]{2,1,0:T(8,128)S(1)}, f32[32,8,128]{2,1,0:T(8,128)S(1)}, f32[32,8,128]{2,1,0:T(8,128)S(1)}, f32[32,8,128]{2,1,0:T(8,128)S(1)}) custom-call(f32[256,8,128]{2,1,0:T(8,128)S(1)} %get-tuple-element.27.u2_ref, ...), custom_call_target="tpu_custom_call", output_to_operand_aliasing={{1}: (1, {}), {2}: (2, {}), {3}: (3, {}), {4}: (4, {})} | custom-call | flops 1000 | bytes 1000 | tf_op jit(solution)/shard_map/store/pallas_call | solution.py:513
  27.5 0.3 collective-permute-start.6
  27.8 0.3 collective-permute-start.7
  28.1 0.3 collective-permute-start.8
  28.3 0.3 collective-permute-start.9
  28.6 2.7 %collective-permute-start.5 = (f32[4,8,128]{2,1,0:T(8,128)S(1)}, f32[4,8,128]{2,1,0:T(8,128)S(1)}, u32[]{:S(2)}, u32[]{:S(2)}) collective-permute-start(f32[4,8,128]{2,1,0:T(8,128)S(1)} %get-tuple-element.31.own_ref), channel_id=1, source_target_pairs={{0,16},{8,24},{16,0},{24,8},{1,17},{9,25},{17,1},{25,9},{2,18},{10... | collective-permute-start | bytes 49160 | tf_op jit(solution)/shard_map/ppermute | solution.py:459
  31.2 0.1 pad_add_fusion.place_ref
  32.0 0.0 collective-permute-done.6.refs_4_
  32.0 0.0 collective-permute-done.7.refs_5_
  32.0 0.0 collective-permute-done.8.refs_6_
  32.0 0.0 collective-permute-done.9.refs_7_
  32.0 3.1 %split.1.split_hbm = bf16[32,128,128]{2,1,0:T(8,128)(2,1)} custom-call(s32[4]{0:T(128)S(1)} %pad_add_fusion.place_ref, f32[32,8,128]{2,1,0:T(8,128)S(1)} %get-tuple-element.33.refs_0_.pick_hbm, f32[32,8,128]{2,1,0:T(8,128)S(1)} %get-tuple-element.34.refs_1_, f32[32,8,128]{2,1,0:T(8,128)S(1)} %get-tuple-element.35.refs_2_, ...), custom_call_target="tpu_custom_call" | custom-call | flops 1000 | bytes 1000 | tf_op jit(solution)/shard_map/split/pallas_call | solution.py:526
  35.1 0.9 %collective-permute-done.5.before_2_ref.after_2_ref = f32[4,8,128]{2,1,0:T(8,128)S(1)} collective-permute-done((f32[4,8,128]{2,1,0:T(8,128)S(1)}, f32[4,8,128]{2,1,0:T(8,128)S(1)}, u32[]{:S(2)}, u32[]{:S(2)}) %collective-permute-start.5) | collective-permute-done | bytes 16416 | tf_op jit(solution)/shard_map/ppermute | solution.py:459
  36.0 1.1 %all-to-all-done.pred_ref = f32[32,16,128]{2,1,0:T(8,128)S(1)} async-done(((f32[32,16,128]{2,1,0:T(8,128)}), f32[32,16,128]{2,1,0:T(8,128)S(1)}, u32[]{:S(2)}, u32[]{:S(2)}) %all-to-all-start) | async-done | bytes 262176 | tf_op jit(solution)/shard_map/all_to_all | solution.py:512
  37.1 3.8 %update.1 = (f32[2048,128]{1,0:T(8,128)}, f32[8,256]{1,0:T(8,128)}) custom-call(s32[4]{0:T(128)S(1)} %pad_add_fusion.place_ref, s32[1]{0:T(128)S(6)} %copy.24.count_ref, s32[1,32]{1,0:T(1,128)} %cells_hbm.3, s32[1,32]{1,0:T(1,128)} %probes_hbm.1, s32[1,32]{1,0:T(1,128)} %level_hbm.1, f32[32,16,128]{2,1,0:T(8,128)S(1)} %all-to-all-done.pred_ref, ...), custom_call_target="tpu_custom_call" | custom-call | tf_op jit(solution)/shard_map/update/pallas_call | solution.py:540
Async XLA Ops:
  2.6 13.5 %collective-permute-start = (f32[69,8,128]{2,1,0:T(8,128)S(1)}, f32[69,8,128]{2,1,0:T(8,128)S(1)}, u32[]{:S(2)}, u32[]{:S(2)}) collective-permute-start(f32[69,8,128]{2,1,0:T(8,128)S(1)} %get-tuple-element.21), channel_id=1, source_target_pairs={{0,8},{8,16},{16,24},{1,9},{9,17},{17,25},{2,10},{10,18},{18,26},{... | collective-permute-start | bytes 847880 | tf_op jit(solution)/shard_map/ppermute | solution.py:456
  7.6 10.1 %collective-permute-start.1 = (f32[69,8,128]{2,1,0:T(8,128)S(1)}, f32[69,8,128]{2,1,0:T(8,128)S(1)}, u32[]{:S(2)}, u32[]{:S(2)}) collective-permute-start(f32[69,8,128]{2,1,0:T(8,128)S(1)} %get-tuple-element.22), channel_id=1, source_target_pairs={{8,0},{16,8},{24,16},{9,1},{17,9},{25,17},{10,2},{18,10},{26,18},{... | collective-permute-start | bytes 847880 | tf_op jit(solution)/shard_map/ppermute | solution.py:457
  8.9 10.9 %collective-permute-start.2 = (f32[32,8,128]{2,1,0:T(8,128)S(1)}, f32[32,8,128]{2,1,0:T(8,128)S(1)}, u32[]{:S(2)}, u32[]{:S(2)}) collective-permute-start(f32[32,8,128]{2,1,0:T(8,128)S(1)} %get-tuple-element.28.refs_0_), channel_id=1, source_target_pairs={{0,2},{2,0},{4,6},{6,4},{1,3},{3,1},{5,7},{7,5},{8,10},{10,8},{12,... | collective-permute-start | bytes 393224 | tf_op jit(solution)/shard_map/ppermute | solution.py:481
  10.4 9.4 %collective-permute-start.3 = (f32[32,8,128]{2,1,0:T(8,128)S(1)}, f32[32,8,128]{2,1,0:T(8,128)S(1)}, u32[]{:S(2)}, u32[]{:S(2)}) collective-permute-start(f32[32,8,128]{2,1,0:T(8,128)S(1)} %get-tuple-element.28.refs_0_), channel_id=1, source_target_pairs={{0,4},{2,6},{4,0},{6,2},{1,5},{3,7},{5,1},{7,3},{8,12},{10,14},{12... | collective-permute-start | bytes 393224 | tf_op jit(solution)/shard_map/ppermute | solution.py:481
  11.9 7.8 %collective-permute-start.4 = (f32[32,8,128]{2,1,0:T(8,128)S(1)}, f32[32,8,128]{2,1,0:T(8,128)S(1)}, u32[]{:S(2)}, u32[]{:S(2)}) collective-permute-start(f32[32,8,128]{2,1,0:T(8,128)S(1)} %get-tuple-element.28.refs_0_), channel_id=1, source_target_pairs={{0,6},{2,4},{4,2},{6,0},{1,7},{3,5},{5,3},{7,1},{8,14},{10,12},{12... | collective-permute-start | bytes 393224 | tf_op jit(solution)/shard_map/ppermute | solution.py:481
  20.5 16.6 %all-to-all-start = ((f32[32,16,128]{2,1,0:T(8,128)}), f32[32,16,128]{2,1,0:T(8,128)S(1)}, u32[]{:S(2)}, u32[]{:S(2)}) async-start(f32[32,16,128]{2,1,0:T(8,128)} %send.1), calls=%async_computation | async-start | bytes 524288 | tf_op jit(solution)/shard_map/all_to_all | solution.py:512
  27.5 4.4 %collective-permute-start.6 = (f32[32,8,128]{2,1,0:T(8,128)S(1)}, f32[32,8,128]{2,1,0:T(8,128)S(1)}, u32[]{:S(2)}, u32[]{:S(2)}) collective-permute-start(f32[32,8,128]{2,1,0:T(8,128)S(1)} %get-tuple-element.33.refs_0_.pick_hbm), channel_id=1, source_target_pairs={{0,1},{1,0},{2,3},{3,2},{4,5},{5,4},{6,7},{7,6},{8,9},{9,8},{10,11... | collective-permute-start | bytes 393224 | tf_op jit(solution)/shard_map/ppermute | solution.py:523
  27.8 4.2 %collective-permute-start.7 = (f32[32,8,128]{2,1,0:T(8,128)S(1)}, f32[32,8,128]{2,1,0:T(8,128)S(1)}, u32[]{:S(2)}, u32[]{:S(2)}) collective-permute-start(f32[32,8,128]{2,1,0:T(8,128)S(1)} %get-tuple-element.34.refs_1_), channel_id=1, source_target_pairs={{0,1},{1,0},{2,3},{3,2},{4,5},{5,4},{6,7},{7,6},{8,9},{9,8},{10,11... | collective-permute-start | bytes 393224 | tf_op jit(solution)/shard_map/ppermute | solution.py:523
  28.1 3.9 %collective-permute-start.8 = (f32[32,8,128]{2,1,0:T(8,128)S(1)}, f32[32,8,128]{2,1,0:T(8,128)S(1)}, u32[]{:S(2)}, u32[]{:S(2)}) collective-permute-start(f32[32,8,128]{2,1,0:T(8,128)S(1)} %get-tuple-element.35.refs_2_), channel_id=1, source_target_pairs={{0,1},{1,0},{2,3},{3,2},{4,5},{5,4},{6,7},{7,6},{8,9},{9,8},{10,11... | collective-permute-start | bytes 393224 | tf_op jit(solution)/shard_map/ppermute | solution.py:523
  28.3 3.7 %collective-permute-start.9 = (f32[32,8,128]{2,1,0:T(8,128)S(1)}, f32[32,8,128]{2,1,0:T(8,128)S(1)}, u32[]{:S(2)}, u32[]{:S(2)}) collective-permute-start(f32[32,8,128]{2,1,0:T(8,128)S(1)} %get-tuple-element.36.refs_3_), channel_id=1, source_target_pairs={{0,1},{1,0},{2,3},{3,2},{4,5},{5,4},{6,7},{7,6},{8,9},{9,8},{10,11... | collective-permute-start | bytes 393224 | tf_op jit(solution)/shard_map/ppermute | solution.py:523
  28.6 7.5 %collective-permute-start.5 = (f32[4,8,128]{2,1,0:T(8,128)S(1)}, f32[4,8,128]{2,1,0:T(8,128)S(1)}, u32[]{:S(2)}, u32[]{:S(2)}) collective-permute-start(f32[4,8,128]{2,1,0:T(8,128)S(1)} %get-tuple-element.31.own_ref), channel_id=1, source_target_pairs={{0,16},{8,24},{16,0},{24,8},{1,17},{9,25},{17,1},{25,9},{2,18},{10... | collective-permute-start | bytes 49160 | tf_op jit(solution)/shard_map/ppermute | solution.py:459

commit v16 on v15

--- a/solution.py
+++ b/solution.py
@@ -189,6 +189,18 @@
     each(1, planes - 1, 7, first_step)
     each(2, planes - 2, 6, second_step)
     last = planes - 1
+    nothing = [jnp.zeros((ROWS, LANES), jnp.float32)] * tiles
+    for x, low, high, at in ((0, None, 1, 34), (last, last - 1, None, 35)):
+        sides = [[nothing if near is None else plane_of(ref, near, tiles) for near in (low, high)] for ref in (hv, u0)]
+        weights = coefficients(masks, sides[0][0], plane_of(hv, x, tiles), sides[0][1])
+        for tile in range(tiles):
+            for kind in range(5):
+                held[kind, x * tiles + tile] = weights[tile][kind]
+        put(edge_ref, at, step(masks, weights, sides[1][0], plane_of(u0, x, tiles), sides[1][1]))
+    for number, x in enumerate((0, 1, last - 1, last)):
+        for kind in range(5):
+            for tile in range(tiles):
+                edge_ref[(14 + number * 5 + kind) * tiles + tile] = held[kind, x * tiles + tile]
     at = 0
     for ref, kept in ((u0, (0, 1, last - 1, last)), (hv, (0, 1, 2, last - 2, last - 1, last)),
                       (u1, (1, 2, last - 2, last - 1))):
@@ -207,19 +219,28 @@
     for at in range(count):
         seen_ref[at] = before_ref[4 * tiles + 1 + at]
         seen_ref[count + at] = after_ref[4 * tiles + 1 + at]
-    edge = [plane_of(edge_ref, at, tiles) for at in range(14)]
+    edge = [plane_of(edge_ref, at, tiles) for at in range(36)]
     last = planes - 1
-    for ref, own_u, own_v, own_1, where in (
-        (before_ref, edge[0:2], edge[4:7], edge[10:12], (0, 1)),
-        (after_ref, edge[3:1:-1], edge[9:6:-1], edge[13:11:-1], (last, last - 1)),
+    for ref, own_u, own_v, own_1, own_w, partial, where in (
+        (before_ref, edge[0:2], edge[4:7], edge[10:12], (14, 19), edge[34], (0, 1)),
+        (after_ref, edge[3:1:-1], edge[9:6:-1], edge[13:11:-1], (29, 24), edge[35], (last, last - 1)),
     ):
         order = (0, 1) if ref is before_ref else (1, 0)
         u = [plane_of(ref, d, tiles) for d in order] + own_u
         v = [[HALF_DT * jnp.exp(t) for t in plane_of(ref, 2 + d, tiles)] for d in order] + own_v
         live = ref[4 * tiles]
-        weights = [coefficients(masks, v[d], v[d + 1], v[d + 2]) for d in range(3)]
-        next_u = [step(masks, weights[d], u[d], u[d + 1], u[d + 2]) for d in range(2)]
-        next_u[0] = [value * live for value in next_u[0]]
+        weights = [coefficients(masks, v[0], v[1], v[2])]
+        for d in (1, 2):
+            kinds = edge[own_w[d - 1] : own_w[d - 1] + 5]
+            weights.append([
+                (kinds[0][t] - v[1][t] if d == 1 else kinds[0][t], *(kinds[k][t] for k in range(1, 5)),
+                 v[d + 1][t] + v[d][t], v[d + 1][t] + v[d + 2][t])
+                for t in range(tiles)
+            ])
+        next_u = [[value * live for value in step(masks, weights[0], u[0], u[1], u[2])]]
+        next_u.append([
+            partial[t] - v[1][t] * u[2][t] + (v[2][t] + v[1][t]) * u[1][t] for t in range(tiles)
+        ])
         next_u = next_u + own_1
         for d in range(2):
             put(u2_ref, where[d], step(masks, weights[d + 1], next_u[d], next_u[d + 1], next_u[d + 2]))
@@ -465,7 +486,7 @@
         functools.partial(inner_kernel, planes, tiles),
         out_shape=(
             jax.ShapeDtypeStruct((planes * tiles, ROWS, LANES), f32),
-            jax.ShapeDtypeStruct((14 * tiles, ROWS, LANES), f32),
+            jax.ShapeDtypeStruct((36 * tiles, ROWS, LANES), f32),
         ),
         in_specs=[VMEM, VMEM],
         out_specs=(VMEM, VMEM),

time: 41.2 us -> 40.5 us (0.983)
  Pallas kernels: 17 us -> 16.3 us
    pallas_call x1, Pallas kernels: 2.09 us -> 1.17 us  [shards(): pl.pallas_call(functools.partial(outer_kernel, planes, tiles), out_shape=...]
  transfers between devices with their start and end apart: 11 -> 11, of which waited for: 3 -> 3; matrix products, arithmetic and copies ran while one was open for 0% -> 0% of each run, Pallas kernels for 26% -> 25%
where the time goes in v16:
time: 40.5 us; the launch traced here: 40.2 us
  starting transfers between devices  19.2 us (47%)
  Pallas kernels  16.3 us (40%)
  waiting for transfers between devices  3.21 us (8%)
  between operations  1.42 us (4%)
    all_to_all x1, starting transfers between devices, shards(): pred_all = lax.all_to_all(sent, ('space', 'chip', 'core'), 0, 0)  5.71 us
    ppermute x1, starting transfers between devices, shards(): before = lax.ppermute(high, 'space', upward)  4.95 us
    pallas_call x1, Pallas kernels, shards(): pl.pallas_call(functools.partial(inner_kernel, planes, tiles), out_shape=...  4 us
    pallas_call x1, Pallas kernels, shards(): pl.pallas_call(functools.partial(update_kernel, slabs, planes, tiles), ou...  3.75 us
    ppermute x3, starting transfers between devices, shards(): lax.ppermute(picked, 'chip', [(i, i ^ d) for i in range(chips)])  3.55 us
    pallas_call x1, Pallas kernels, shards(): pl.pallas_call(functools.partial(split_kernel, by_xor, chips), out_shape=...  3.12 us
    ppermute x1, starting transfers between devices, shards(): lax.ppermute(obs, 'space', [(i, (i + 2) % 4) for i in range(4)])  2.67 us
    pallas_call x1, Pallas kernels, shards(): pl.pallas_call(functools.partial(pack_kernel, planes, tiles), out_shape=(...  1.98 us
  transfers between devices with their start and end apart: 11, of which 3 were waited for; matrix products, arithmetic and copies ran while one was open for 0% of the time, Pallas kernels for 25%

profile of v16, /device:TPU:0, one launch (start us, length us, event | category | flops | bytes accessed | tf_op | source)
XLA Modules:
  0.0 40.2 jit_solution(18231541475219990995)
XLA Ops:
  0.6 2.0 %pack.1 = (f32[69,8,128]{2,1,0:T(8,128)S(1)}, f32[69,8,128]{2,1,0:T(8,128)S(1)}, f32[4,8,128]{2,1,0:T(8,128)S(1)}, f32[2048,128]{1,0:T(8,128)S(1)}, f32[2048,128]{1,0:T(8,128)S(1)}, /*index=5*/f32[32,8,128]{2,1,0:T(8,128)S(1)}) custom-call(s32[1,2,6]{2,1,0:T(2,128)} %taper_hbm.1, f32[2048,128]{1,0:T(8,128)} %bitcast.28, f32[2048,128]{1,0:T(8,128)} %bitcast.26, ...), custom_call_target="tpu_custom_call" | custom-call | tf_op jit(solution)/shard_map/pack/pallas_call | solution.py:453
  2.6 4.9 %collective-permute-start = (f32[69,8,128]{2,1,0:T(8,128)S(1)}, f32[69,8,128]{2,1,0:T(8,128)S(1)}, u32[]{:S(2)}, u32[]{:S(2)}) collective-permute-start(f32[69,8,128]{2,1,0:T(8,128)S(1)} %get-tuple-element.21), channel_id=1, source_target_pairs={{0,8},{8,16},{16,24},{1,9},{9,17},{17,25},{2,10},{10,18},{18,26},{... | collective-permute-start | bytes 847880 | tf_op jit(solution)/shard_map/ppermute | solution.py:477
  7.6 1.3 %collective-permute-start.1 = (f32[69,8,128]{2,1,0:T(8,128)S(1)}, f32[69,8,128]{2,1,0:T(8,128)S(1)}, u32[]{:S(2)}, u32[]{:S(2)}) collective-permute-start(f32[69,8,128]{2,1,0:T(8,128)S(1)} %get-tuple-element.22), channel_id=1, source_target_pairs={{8,0},{16,8},{24,16},{9,1},{17,9},{25,17},{10,2},{18,10},{26,18},{... | collective-permute-start | bytes 847880 | tf_op jit(solution)/shard_map/ppermute | solution.py:478
  8.9 1.6 %collective-permute-start.2 = (f32[32,8,128]{2,1,0:T(8,128)S(1)}, f32[32,8,128]{2,1,0:T(8,128)S(1)}, u32[]{:S(2)}, u32[]{:S(2)}) collective-permute-start(f32[32,8,128]{2,1,0:T(8,128)S(1)} %get-tuple-element.28.refs_0_), channel_id=1, source_target_pairs={{0,2},{2,0},{4,6},{6,4},{1,3},{3,1},{5,7},{7,5},{8,10},{10,8},{12,... | collective-permute-start | bytes 393224 | tf_op jit(solution)/shard_map/ppermute | solution.py:502
  10.4 1.5 %collective-permute-start.3 = (f32[32,8,128]{2,1,0:T(8,128)S(1)}, f32[32,8,128]{2,1,0:T(8,128)S(1)}, u32[]{:S(2)}, u32[]{:S(2)}) collective-permute-start(f32[32,8,128]{2,1,0:T(8,128)S(1)} %get-tuple-element.28.refs_0_), channel_id=1, source_target_pairs={{0,4},{2,6},{4,0},{6,2},{1,5},{3,7},{5,1},{7,3},{8,12},{10,14},{12... | collective-permute-start | bytes 393224 | tf_op jit(solution)/shard_map/ppermute | solution.py:502
  12.0 0.5 %collective-permute-start.4 = (f32[32,8,128]{2,1,0:T(8,128)S(1)}, f32[32,8,128]{2,1,0:T(8,128)S(1)}, u32[]{:S(2)}, u32[]{:S(2)}) collective-permute-start(f32[32,8,128]{2,1,0:T(8,128)S(1)} %get-tuple-element.28.refs_0_), channel_id=1, source_target_pairs={{0,6},{2,4},{4,2},{6,0},{1,7},{3,5},{5,3},{7,1},{8,14},{10,12},{12... | collective-permute-start | bytes 393224 | tf_op jit(solution)/shard_map/ppermute | solution.py:502
  12.4 4.0 %inner_planes.1 = (f32[256,8,128]{2,1,0:T(8,128)S(1)}, f32[576,8,128]{2,1,0:T(8,128)S(1)}) custom-call(f32[2048,128]{1,0:T(8,128)S(1)} %get-tuple-element.23.u_ref, f32[2048,128]{1,0:T(8,128)S(1)} %get-tuple-element.24.t_ref), custom_call_target="tpu_custom_call" | custom-call | bytes 15000000 | tf_op jit(solution)/shard_map/inner_planes/pallas_call | solution.py:485
  16.4 0.0 collective-permute-done.before_ref
  16.4 1.2 %collective-permute-done.1.after_ref = f32[69,8,128]{2,1,0:T(8,128)S(1)} collective-permute-done((f32[69,8,128]{2,1,0:T(8,128)S(1)}, f32[69,8,128]{2,1,0:T(8,128)S(1)}, u32[]{:S(2)}, u32[]{:S(2)}) %collective-permute-start.1) | collective-permute-done | bytes 282656 | tf_op jit(solution)/shard_map/ppermute | solution.py:478
  17.7 1.2 %outer_planes.1 = (f32[256,8,128]{2,1,0:T(8,128)S(1)}, f32[16,128]{1,0:T(8,128)S(1)}, f32[8,8,128]{2,1,0:T(8,128)S(1)}) custom-call(s32[256]{0:T(256)} %probe_hbm.1, f32[69,8,128]{2,1,0:T(8,128)S(1)} %collective-permute-done.before_ref, f32[69,8,128]{2,1,0:T(8,128)S(1)} %collective-permute-done.1.after_ref, ...), custom_call_target="tpu_custom_call", output_to_operand_aliasing={{0}: (4, {})} | custom-call | flops 1000 | bytes 1000 | tf_op jit(solution)/shard_map/outer_planes/pallas_call | solution.py:505
  18.9 0.0 collective-permute-done.2.refs_1_
  18.9 0.0 collective-permute-done.3.refs_2_
  18.9 0.0 collective-permute-done.4.refs_3_
  18.9 0.7 %send.1 = f32[32,16,128]{2,1,0:T(8,128)} custom-call(f32[16,128]{1,0:T(8,128)S(1)} %get-tuple-element.30.found_ref, f32[32,8,128]{2,1,0:T(8,128)S(1)} %get-tuple-element.28.refs_0_, f32[32,8,128]{2,1,0:T(8,128)S(1)} %collective-permute-done.2.refs_1_, f32[32,8,128]{2,1,0:T(8,128)S(1)} %collective-permute-done.3.refs_2_, ...), custom_call_target="tpu_custom_call" | custom-call | flops 1000 | bytes 1000 | tf_op jit(solution)/shard_map/send/pallas_call | solution.py:523
  19.6 5.7 %all-to-all-start = ((f32[32,16,128]{2,1,0:T(8,128)}), f32[32,16,128]{2,1,0:T(8,128)S(1)}, u32[]{:S(2)}, u32[]{:S(2)}) async-start(f32[32,16,128]{2,1,0:T(8,128)} %send.1), calls=%async_computation | async-start | bytes 524288 | tf_op jit(solution)/shard_map/all_to_all | solution.py:533
  25.3 1.6 %store.1 = (f32[2048,128]{1,0:T(8,128)}, f32[32,8,128]{2,1,0:T(8,128)S(1)}, f32[32,8,128]{2,1,0:T(8,128)S(1)}, f32[32,8,128]{2,1,0:T(8,128)S(1)}, f32[32,8,128]{2,1,0:T(8,128)S(1)}) custom-call(f32[256,8,128]{2,1,0:T(8,128)S(1)} %get-tuple-element.27.u2_ref, ...), custom_call_target="tpu_custom_call", output_to_operand_aliasing={{1}: (1, {}), {2}: (2, {}), {3}: (3, {}), {4}: (4, {})} | custom-call | flops 1000 | bytes 1000 | tf_op jit(solution)/shard_map/store/pallas_call | solution.py:534
  26.9 0.3 collective-permute-start.6
  27.2 0.3 collective-permute-start.7
  27.4 0.3 collective-permute-start.8
  27.7 0.3 collective-permute-start.9
  27.9 2.7 %collective-permute-start.5 = (f32[4,8,128]{2,1,0:T(8,128)S(1)}, f32[4,8,128]{2,1,0:T(8,128)S(1)}, u32[]{:S(2)}, u32[]{:S(2)}) collective-permute-start(f32[4,8,128]{2,1,0:T(8,128)S(1)} %get-tuple-element.31.own_ref), channel_id=1, source_target_pairs={{0,16},{8,24},{16,0},{24,8},{1,17},{9,25},{17,1},{25,9},{2,18},{10... | collective-permute-start | bytes 49160 | tf_op jit(solution)/shard_map/ppermute | solution.py:480
  30.6 0.1 pad_add_fusion.place_ref
  31.3 0.0 collective-permute-done.6.refs_4_
  31.3 0.0 collective-permute-done.7.refs_5_
  31.4 0.0 collective-permute-done.8.refs_6_
  31.4 0.0 collective-permute-done.9.refs_7_
  31.4 3.1 %split.1.split_hbm = bf16[32,128,128]{2,1,0:T(8,128)(2,1)} custom-call(s32[4]{0:T(128)S(1)} %pad_add_fusion.place_ref, f32[32,8,128]{2,1,0:T(8,128)S(1)} %get-tuple-element.33.refs_0_.pick_hbm, f32[32,8,128]{2,1,0:T(8,128)S(1)} %get-tuple-element.34.refs_1_, f32[32,8,128]{2,1,0:T(8,128)S(1)} %get-tuple-element.35.refs_2_, ...), custom_call_target="tpu_custom_call" | custom-call | flops 1000 | bytes 1000 | tf_op jit(solution)/shard_map/split/pallas_call | solution.py:547
  34.5 0.9 %collective-permute-done.5.before_2_ref.after_2_ref = f32[4,8,128]{2,1,0:T(8,128)S(1)} collective-permute-done((f32[4,8,128]{2,1,0:T(8,128)S(1)}, f32[4,8,128]{2,1,0:T(8,128)S(1)}, u32[]{:S(2)}, u32[]{:S(2)}) %collective-permute-start.5) | collective-permute-done | bytes 16416 | tf_op jit(solution)/shard_map/ppermute | solution.py:480
  35.4 1.1 %all-to-all-done.pred_ref = f32[32,16,128]{2,1,0:T(8,128)S(1)} async-done(((f32[32,16,128]{2,1,0:T(8,128)}), f32[32,16,128]{2,1,0:T(8,128)S(1)}, u32[]{:S(2)}, u32[]{:S(2)}) %all-to-all-start) | async-done | bytes 262176 | tf_op jit(solution)/shard_map/all_to_all | solution.py:533
  36.5 3.8 %update.1 = (f32[2048,128]{1,0:T(8,128)}, f32[8,256]{1,0:T(8,128)}) custom-call(s32[4]{0:T(128)S(1)} %pad_add_fusion.place_ref, s32[1]{0:T(128)S(6)} %copy.24.count_ref, s32[1,32]{1,0:T(1,128)} %cells_hbm.3, s32[1,32]{1,0:T(1,128)} %probes_hbm.1, s32[1,32]{1,0:T(1,128)} %level_hbm.1, f32[32,16,128]{2,1,0:T(8,128)S(1)} %all-to-all-done.pred_ref, ...), custom_call_target="tpu_custom_call" | custom-call | tf_op jit(solution)/shard_map/update/pallas_call | solution.py:561
Async XLA Ops:
  2.6 13.8 %collective-permute-start = (f32[69,8,128]{2,1,0:T(8,128)S(1)}, f32[69,8,128]{2,1,0:T(8,128)S(1)}, u32[]{:S(2)}, u32[]{:S(2)}) collective-permute-start(f32[69,8,128]{2,1,0:T(8,128)S(1)} %get-tuple-element.21), channel_id=1, source_target_pairs={{0,8},{8,16},{16,24},{1,9},{9,17},{17,25},{2,10},{10,18},{18,26},{... | collective-permute-start | bytes 847880 | tf_op jit(solution)/shard_map/ppermute | solution.py:477
  7.6 10.1 %collective-permute-start.1 = (f32[69,8,128]{2,1,0:T(8,128)S(1)}, f32[69,8,128]{2,1,0:T(8,128)S(1)}, u32[]{:S(2)}, u32[]{:S(2)}) collective-permute-start(f32[69,8,128]{2,1,0:T(8,128)S(1)} %get-tuple-element.22), channel_id=1, source_target_pairs={{8,0},{16,8},{24,16},{9,1},{17,9},{25,17},{10,2},{18,10},{26,18},{... | collective-permute-start | bytes 847880 | tf_op jit(solution)/shard_map/ppermute | solution.py:478
  8.9 10.0 %collective-permute-start.2 = (f32[32,8,128]{2,1,0:T(8,128)S(1)}, f32[32,8,128]{2,1,0:T(8,128)S(1)}, u32[]{:S(2)}, u32[]{:S(2)}) collective-permute-start(f32[32,8,128]{2,1,0:T(8,128)S(1)} %get-tuple-element.28.refs_0_), channel_id=1, source_target_pairs={{0,2},{2,0},{4,6},{6,4},{1,3},{3,1},{5,7},{7,5},{8,10},{10,8},{12,... | collective-permute-start | bytes 393224 | tf_op jit(solution)/shard_map/ppermute | solution.py:502
  10.4 8.4 %collective-permute-start.3 = (f32[32,8,128]{2,1,0:T(8,128)S(1)}, f32[32,8,128]{2,1,0:T(8,128)S(1)}, u32[]{:S(2)}, u32[]{:S(2)}) collective-permute-start(f32[32,8,128]{2,1,0:T(8,128)S(1)} %get-tuple-element.28.refs_0_), channel_id=1, source_target_pairs={{0,4},{2,6},{4,0},{6,2},{1,5},{3,7},{5,1},{7,3},{8,12},{10,14},{12... | collective-permute-start | bytes 393224 | tf_op jit(solution)/shard_map/ppermute | solution.py:502
  12.0 6.9 %collective-permute-start.4 = (f32[32,8,128]{2,1,0:T(8,128)S(1)}, f32[32,8,128]{2,1,0:T(8,128)S(1)}, u32[]{:S(2)}, u32[]{:S(2)}) collective-permute-start(f32[32,8,128]{2,1,0:T(8,128)S(1)} %get-tuple-element.28.refs_0_), channel_id=1, source_target_pairs={{0,6},{2,4},{4,2},{6,0},{1,7},{3,5},{5,3},{7,1},{8,14},{10,12},{12... | collective-permute-start | bytes 393224 | tf_op jit(solution)/shard_map/ppermute | solution.py:502
  19.6 16.9 %all-to-all-start = ((f32[32,16,128]{2,1,0:T(8,128)}), f32[32,16,128]{2,1,0:T(8,128)S(1)}, u32[]{:S(2)}, u32[]{:S(2)}) async-start(f32[32,16,128]{2,1,0:T(8,128)} %send.1), calls=%async_computation | async-start | bytes 524288 | tf_op jit(solution)/shard_map/all_to_all | solution.py:533
  26.9 4.4 %collective-permute-start.6 = (f32[32,8,128]{2,1,0:T(8,128)S(1)}, f32[32,8,128]{2,1,0:T(8,128)S(1)}, u32[]{:S(2)}, u32[]{:S(2)}) collective-permute-start(f32[32,8,128]{2,1,0:T(8,128)S(1)} %get-tuple-element.33.refs_0_.pick_hbm), channel_id=1, source_target_pairs={{0,1},{1,0},{2,3},{3,2},{4,5},{5,4},{6,7},{7,6},{8,9},{9,8},{10,11... | collective-permute-start | bytes 393224 | tf_op jit(solution)/shard_map/ppermute | solution.py:544
  27.2 4.2 %collective-permute-start.7 = (f32[32,8,128]{2,1,0:T(8,128)S(1)}, f32[32,8,128]{2,1,0:T(8,128)S(1)}, u32[]{:S(2)}, u32[]{:S(2)}) collective-permute-start(f32[32,8,128]{2,1,0:T(8,128)S(1)} %get-tuple-element.34.refs_1_), channel_id=1, source_target_pairs={{0,1},{1,0},{2,3},{3,2},{4,5},{5,4},{6,7},{7,6},{8,9},{9,8},{10,11... | collective-permute-start | bytes 393224 | tf_op jit(solution)/shard_map/ppermute | solution.py:544
  27.4 3.9 %collective-permute-start.8 = (f32[32,8,128]{2,1,0:T(8,128)S(1)}, f32[32,8,128]{2,1,0:T(8,128)S(1)}, u32[]{:S(2)}, u32[]{:S(2)}) collective-permute-start(f32[32,8,128]{2,1,0:T(8,128)S(1)} %get-tuple-element.35.refs_2_), channel_id=1, source_target_pairs={{0,1},{1,0},{2,3},{3,2},{4,5},{5,4},{6,7},{7,6},{8,9},{9,8},{10,11... | collective-permute-start | bytes 393224 | tf_op jit(solution)/shard_map/ppermute | solution.py:544
  27.7 3.7 %collective-permute-start.9 = (f32[32,8,128]{2,1,0:T(8,128)S(1)}, f32[32,8,128]{2,1,0:T(8,128)S(1)}, u32[]{:S(2)}, u32[]{:S(2)}) collective-permute-start(f32[32,8,128]{2,1,0:T(8,128)S(1)} %get-tuple-element.36.refs_3_), channel_id=1, source_target_pairs={{0,1},{1,0},{2,3},{3,2},{4,5},{5,4},{6,7},{7,6},{8,9},{9,8},{10,11... | collective-permute-start | bytes 393224 | tf_op jit(solution)/shard_map/ppermute | solution.py:544
  27.9 7.5 %collective-permute-start.5 = (f32[4,8,128]{2,1,0:T(8,128)S(1)}, f32[4,8,128]{2,1,0:T(8,128)S(1)}, u32[]{:S(2)}, u32[]{:S(2)}) collective-permute-start(f32[4,8,128]{2,1,0:T(8,128)S(1)} %get-tuple-element.31.own_ref), channel_id=1, source_target_pairs={{0,16},{8,24},{16,0},{24,8},{1,17},{9,25},{17,1},{25,9},{2,18},{10... | collective-permute-start | bytes 49160 | tf_op jit(solution)/shard_map/ppermute | solution.py:480
